TPU v7x, 32 devices: a whole 2x2x4 slice. The times are simulated.
32 devices in a mesh: dp: 8 (over z, x), cls: 4 (over y, core).
Axes of the slice: x: 2, y: 2, z: 4, core: 2. Of those that a mesh axis runs over, the one named last changes fastest.
Arguments:
- particles: bfloat16 [64, 2, 288, 128], P('dp'), may hold values from -20 to 20
- references: bfloat16 [288, 2, 200, 128], P('dp', None, 'cls'), may hold values from -9 to 9
- ctf_table: float32 [16, 128], replicated, may hold values from -0.1 to 0.1
- rot_offset: int32 [200], P('cls'), may hold values from 0 to 7
- prior_shift: int32 [64, 2], P('dp'), may hold values from -8 to 8
- defocus_group: int32 [64], P('dp'), may hold values from 0 to 15
Outputs:
- log_evidence: float32 [64], P('dp')
- class_posterior: float32 [64, 200], P('dp', 'cls')
- class_sums: float32 [288, 2, 200, 128], P('dp', None, 'cls')
All inputs are finite; a program needn't handle non-finite values.
Results may differ from a plain program's by a relative error of at most 0.0056.
Values may be sent and summed in bfloat16 or wider, within the bound.
No kernel may reach another device: no remote copies, remote signals or barrier semaphores. Data moves between devices by JAX's collectives and lax.ppermute only.
A program may use at most 384 MiB of HBM per device.

v0:
```python
import math

import jax
import jax.numpy as jnp
from jax import lax
from jax.sharding import PartitionSpec as P

ROTS = 36
ANG_STEP = 8
SHIFT_SIDE = 5


two_pi = 2.0 * math.pi


def fourier_rows(angles):
    index_grid = jnp.arange(angles, dtype=jnp.int32)
    phase_index = index_grid[:, None] * index_grid[None, :] % angles
    radians = phase_index.astype(jnp.float32) * (two_pi / angles)
    cosine = jnp.cos(radians)
    sine_part = jnp.sin(radians)
    table_full = jnp.stack(
        [jnp.stack([cosine, sine_part], 1), jnp.stack([-sine_part, cosine], 1)], 1
    )
    return table_full.reshape(2 * angles, 2 * angles).astype(jnp.bfloat16)


def rotation_tables(freq_rows, offsets, angles):
    rotation_steps = jnp.arange(ROTS, dtype=jnp.int32) * ANG_STEP
    angle_grid = rotation_steps[None, :] + offsets[:, None]
    phase_index = freq_rows[:, None, None] * angle_grid[None, :, :] % angles
    radians = phase_index.astype(jnp.float32) * (two_pi / angles)
    return (jnp.cos(radians), jnp.sin(radians))


def local(particles, references, ctf_table, rot_offset, prior_shift, defocus_group):
    top_score_value = lax.Precision.HIGHEST
    particle_count = particles.shape[0]
    angles = particles.shape[2]
    cycles = particles.shape[3]
    classes_here = references.shape[2]
    group_count = ctf_table.shape[0]
    shifts = SHIFT_SIDE * SHIFT_SIDE
    queries = particle_count * shifts
    shift_index = jnp.arange(shifts, dtype=jnp.int32)
    along_x = shift_index // SHIFT_SIDE - SHIFT_SIDE // 2
    along_y = shift_index % SHIFT_SIDE - SHIFT_SIDE // 2
    theta_grid = jnp.arange(angles, dtype=jnp.int32).astype(jnp.float32) * (two_pi / angles)
    radius = (jnp.arange(cycles, dtype=jnp.int32) + 1).astype(jnp.float32) / (2.0 * cycles)
    table_wide = fourier_rows(angles)
    onehot = (defocus_group[:, None] == jnp.arange(group_count, dtype=jnp.int32)[None, :]).astype(
        jnp.float32
    )
    ctf_rows = jnp.dot(onehot, ctf_table, precision=top_score_value)

    def transform(inputs):
        image, offset, ctf_row = inputs
        shift_x = (offset[0] + along_x).astype(jnp.float32)
        shift_y = (offset[1] + along_y).astype(jnp.float32)
        argument = (
            two_pi
            * radius[None, None, :]
            * (
                shift_x[None, :, None] * jnp.cos(theta_grid)[:, None, None]
                + shift_y[None, :, None] * jnp.sin(theta_grid)[:, None, None]
            )
        )
        cosine = jnp.cos(argument)
        sine_part = jnp.sin(argument)
        real_part = image[0].astype(jnp.float32)[:, None, :]
        imag_part = image[1].astype(jnp.float32)[:, None, :]
        shifted = jnp.stack(
            [real_part * cosine + imag_part * sine_part, imag_part * cosine - real_part * sine_part]
        ).astype(jnp.bfloat16)
        spectrum = jnp.dot(
            table_wide,
            shifted.reshape(2 * angles, shifts * cycles),
            preferred_element_type=jnp.float32,
        )
        spectrum = spectrum.reshape(angles, 2, shifts, cycles) * ctf_row[None, None, None, :]
        return spectrum.astype(jnp.bfloat16)

    per_particle = lax.map(transform, (particles, prior_shift, ctf_rows))
    weighted = jnp.transpose(per_particle, (1, 2, 0, 3, 4)).reshape(angles, 2, queries, cycles)
    shard_piece = lax.all_gather(references, "dp", axis=0, tiled=True)
    rows_here = shard_piece.shape[0]
    query_block = weighted.reshape(rows_here, 2 * queries, cycles)
    class_block = shard_piece.reshape(rows_here, 2 * classes_here, cycles)
    product = lax.dot_general(
        query_block, class_block, (((2,), (2,)), ((0,), (0,))), preferred_element_type=jnp.float32
    )
    product = product.reshape(rows_here, 2, queries, 2, classes_here)
    real_correlation = product[:, 0, :, 0] + product[:, 1, :, 1]
    imag_correlation = product[:, 1, :, 0] - product[:, 0, :, 1]
    freq_rows = jnp.arange(rows_here, dtype=jnp.int32)
    cos_table, sin_table = rotation_tables(freq_rows, rot_offset, angles)
    stacked_table = jnp.transpose(jnp.concatenate([cos_table, -sin_table], 0), (1, 0, 2))
    stacked_corr = jnp.transpose(
        jnp.concatenate([real_correlation, imag_correlation], 0), (2, 1, 0)
    )
    cross_sums = lax.dot_general(
        stacked_corr, stacked_table, (((2,), (1,)), ((0,), (0,))), precision=top_score_value
    )
    piece_values = shard_piece.astype(jnp.float32)
    cycle_power = jnp.sum(piece_values * piece_values, axis=(0, 1))
    power_sums = jnp.dot(cycle_power, (ctf_table * ctf_table).T, precision=top_score_value)
    cross_sums, power_sums = (cross_sums, power_sums)
    class_power = jnp.dot(onehot, power_sums.T, precision=top_score_value)
    cross_ordered = jnp.transpose(cross_sums, (1, 0, 2))
    scores = (
        cross_ordered.reshape(particle_count, shifts, classes_here, ROTS) / angles
        - 0.5 * class_power[:, None, :, None] / angles
    )
    local_peak = jnp.max(scores, axis=(1, 2, 3))
    peak_score = lax.pmax(local_peak, "cls")
    total_mass = lax.psum(
        jnp.sum(jnp.exp(scores - peak_score[:, None, None, None]), axis=(1, 2, 3)), "cls"
    )
    log_evidence = peak_score + jnp.log(total_mass)
    weights = jnp.exp(scores - log_evidence[:, None, None, None])
    class_posterior = jnp.sum(weights, axis=(1, 3))
    class_weights = jnp.transpose(weights.reshape(queries, classes_here, ROTS), (1, 0, 2))
    own_rows = angles // lax.axis_size("dp")
    freq_rows = jnp.arange(angles, dtype=jnp.int32)
    cos_table, sin_table = rotation_tables(freq_rows, rot_offset, angles)
    stacked_table = jnp.transpose(jnp.concatenate([cos_table, sin_table], 0), (1, 2, 0))
    returned = lax.dot_general(
        class_weights, stacked_table, (((2,), (1,)), ((0,), (0,))), precision=top_score_value
    ).astype(jnp.bfloat16)
    real_returned = jnp.transpose(returned[:, :, :angles], (2, 1, 0))
    imag_returned = jnp.transpose(returned[:, :, angles:], (2, 1, 0))
    mixing = jnp.stack(
        [
            jnp.stack([real_returned, -imag_returned], 1),
            jnp.stack([imag_returned, real_returned], 1),
        ],
        1,
    )
    query_block = weighted
    summed = lax.psum(
        lax.dot_general(
            mixing,
            query_block,
            (((2, 3), (1, 2)), ((0,), (0,))),
            preferred_element_type=jnp.float32,
        ),
        "dp",
    )
    class_sums = lax.dynamic_slice_in_dim(summed, lax.axis_index("dp") * own_rows, own_rows, 0)
    return (log_evidence, class_posterior, class_sums)


def solution(mesh):
    placed = (
        P("dp", None, None, None),
        P("dp", None, "cls", None),
        P(),
        P("cls"),
        P("dp", None),
        P("dp"),
    )
    return jax.shard_map(
        local,
        mesh=mesh,
        in_specs=placed,
        out_specs=(P("dp"), P("dp", "cls"), P("dp", None, "cls", None)),
        check_vma=False,
    )
```

profile of v0, /device:TPU:8, one launch (start us, length us, event | category | flops | bytes accessed | tf_op | source)
XLA Modules:
  0.0 1302.4 jit_solution(3212088044611333508)
XLA Ops:
  13.5 15.9 %fusion.55 = (f32[288,50,36]{0,2,1:T(8,128)}, f32[288,50,36]{0,2,1:T(8,128)}, f32[288,50,36]{0,2,1:T(8,128)}) fusion(s32[50,36]{1,0:T(8,128)S(1)} %broadcast_add_fusion), kind=kLoop, calls=%fused_computation.83 | loop fusion | flops 5184000 | bytes 6228000 | tf_op jit(solution)/shard_map/sin | solution.py:33
  29.5 380.7 %while.13 = (s32[]{:T(128)}, bf16[8,288,2,25,128]{4,1,3,0,2:T(8,128)(2,1)}, bf16[8,2,288,128]{3,2,1,0:T(8,128)(2,1)}, s32[8,2]{0,1:T(2,128)S(1)}, bf16[576,576]{...) while((s32[]{:T(128)}, ...), condition=%wide.region_1.2_spmd.clone, body=%wide.region_0.1_spmd.clone.sunk | while | flops 2137287680 | bytes 56820304 | solution.py:83
  33.0 18.5 %fusion.100 = (bf16[1,288,25,128]{3,2,1,0:T(8,128)(2,1)S(1)}, bf16[1,288,25,128]{3,2,1,0:T(8,128)(2,1)S(1)}) fusion(f32[288,128]{1,0:T(8,128)S(1)} %get-tuple-element.241, f32[288,25]{1,0:T(8,128)S(1)} %copy.127, f32[128]{0:T(128)S(1)} %convert_multiply_fusion.3, f32[288,128]{1,0:T(8,128)S(1)} %get-tuple-element.246), kind=kLoop, calls=%fused_computation.14.clone.1 | loop fusion | flops 8294400 | bytes 4010624 | tf_op jit(solution)/shard_map/convert.2
  58.8 9.3 reshape.331
  80.8 18.5 %fusion.100 = (bf16[1,288,25,128]{3,2,1,0:T(8,128)(2,1)S(1)}, bf16[1,288,25,128]{3,2,1,0:T(8,128)(2,1)S(1)}) fusion(f32[288,128]{1,0:T(8,128)S(1)} %get-tuple-element.241, f32[288,25]{1,0:T(8,128)S(1)} %copy.127, f32[128]{0:T(128)S(1)} %convert_multiply_fusion.3, f32[288,128]{1,0:T(8,128)S(1)} %get-tuple-element.246), kind=kLoop, calls=%fused_computation.14.clone.1 | loop fusion | flops 8294400 | bytes 4010624 | tf_op jit(solution)/shard_map/convert.2
  106.6 9.1 reshape.331
  128.2 18.5 %fusion.100 = (bf16[1,288,25,128]{3,2,1,0:T(8,128)(2,1)S(1)}, bf16[1,288,25,128]{3,2,1,0:T(8,128)(2,1)S(1)}) fusion(f32[288,128]{1,0:T(8,128)S(1)} %get-tuple-element.241, f32[288,25]{1,0:T(8,128)S(1)} %copy.127, f32[128]{0:T(128)S(1)} %convert_multiply_fusion.3, f32[288,128]{1,0:T(8,128)S(1)} %get-tuple-element.246), kind=kLoop, calls=%fused_computation.14.clone.1 | loop fusion | flops 8294400 | bytes 4010624 | tf_op jit(solution)/shard_map/convert.2
  154.1 9.1 reshape.331
  175.8 18.5 %fusion.100 = (bf16[1,288,25,128]{3,2,1,0:T(8,128)(2,1)S(1)}, bf16[1,288,25,128]{3,2,1,0:T(8,128)(2,1)S(1)}) fusion(f32[288,128]{1,0:T(8,128)S(1)} %get-tuple-element.241, f32[288,25]{1,0:T(8,128)S(1)} %copy.127, f32[128]{0:T(128)S(1)} %convert_multiply_fusion.3, f32[288,128]{1,0:T(8,128)S(1)} %get-tuple-element.246), kind=kLoop, calls=%fused_computation.14.clone.1 | loop fusion | flops 8294400 | bytes 4010624 | tf_op jit(solution)/shard_map/convert.2
  201.7 9.1 reshape.331
  223.4 18.5 %fusion.100 = (bf16[1,288,25,128]{3,2,1,0:T(8,128)(2,1)S(1)}, bf16[1,288,25,128]{3,2,1,0:T(8,128)(2,1)S(1)}) fusion(f32[288,128]{1,0:T(8,128)S(1)} %get-tuple-element.241, f32[288,25]{1,0:T(8,128)S(1)} %copy.127, f32[128]{0:T(128)S(1)} %convert_multiply_fusion.3, f32[288,128]{1,0:T(8,128)S(1)} %get-tuple-element.246), kind=kLoop, calls=%fused_computation.14.clone.1 | loop fusion | flops 8294400 | bytes 4010624 | tf_op jit(solution)/shard_map/convert.2
  249.2 9.1 reshape.331
  270.9 18.5 %fusion.100 = (bf16[1,288,25,128]{3,2,1,0:T(8,128)(2,1)S(1)}, bf16[1,288,25,128]{3,2,1,0:T(8,128)(2,1)S(1)}) fusion(f32[288,128]{1,0:T(8,128)S(1)} %get-tuple-element.241, f32[288,25]{1,0:T(8,128)S(1)} %copy.127, f32[128]{0:T(128)S(1)} %convert_multiply_fusion.3, f32[288,128]{1,0:T(8,128)S(1)} %get-tuple-element.246), kind=kLoop, calls=%fused_computation.14.clone.1 | loop fusion | flops 8294400 | bytes 4010624 | tf_op jit(solution)/shard_map/convert.2
  296.8 9.1 reshape.331
  318.4 18.5 %fusion.100 = (bf16[1,288,25,128]{3,2,1,0:T(8,128)(2,1)S(1)}, bf16[1,288,25,128]{3,2,1,0:T(8,128)(2,1)S(1)}) fusion(f32[288,128]{1,0:T(8,128)S(1)} %get-tuple-element.241, f32[288,25]{1,0:T(8,128)S(1)} %copy.127, f32[128]{0:T(128)S(1)} %convert_multiply_fusion.3, f32[288,128]{1,0:T(8,128)S(1)} %get-tuple-element.246), kind=kLoop, calls=%fused_computation.14.clone.1 | loop fusion | flops 8294400 | bytes 4010624 | tf_op jit(solution)/shard_map/convert.2
  344.3 9.1 reshape.331
  366.1 18.5 %fusion.100 = (bf16[1,288,25,128]{3,2,1,0:T(8,128)(2,1)S(1)}, bf16[1,288,25,128]{3,2,1,0:T(8,128)(2,1)S(1)}) fusion(f32[288,128]{1,0:T(8,128)S(1)} %get-tuple-element.241, f32[288,25]{1,0:T(8,128)S(1)} %copy.127, f32[128]{0:T(128)S(1)} %convert_multiply_fusion.3, f32[288,128]{1,0:T(8,128)S(1)} %get-tuple-element.246), kind=kLoop, calls=%fused_computation.14.clone.1 | loop fusion | flops 8294400 | bytes 4010624 | tf_op jit(solution)/shard_map/convert.2
  391.9 9.1 reshape.331
  410.3 7.2 copy.84
  417.5 37.9 %fusion.31 = f32[288,400,100]{2,1,0:T(8,128)} fusion(bf16[288,400,128]{2,0,1:T(8,128)(2,1)} %bitcast.123, bf16[288,100,128]{2,0,1:T(8,128)(2,1)} %bitcast.125), kind=kOutput, calls=%fused_computation.47 | convolution fusion | flops 2949120000 | bytes 82944000 | tf_op jit(solution)/shard_map/dot_general | solution.py:89
  455.4 68.2 %copy.87 = f32[288,400,100]{0,1,2:T(8,128)} copy(f32[288,400,100]{2,1,0:T(8,128)} %fusion.31) | data formatting | bytes 92160000 | tf_op jit(solution)/shard_map/dot_general | solution.py:89
  523.6 30.8 %fusion.39 = (f32[288,200,50]{0,1,2:T(8,128)}, f32[288,200,50]{0,1,2:T(8,128)}) fusion(f32[288,2,200,2,50]{0,2,1,4,3:T(8,128)} %bitcast.121), kind=kLoop, calls=%fused_computation.59 | loop fusion | flops 5760000 | bytes 69120000 | tf_op jit(solution)/shard_map/add | solution.py:93
  554.5 9.4 multiply_reduce_fusion
  564.4 36.2 %fusion.62 = (f32[200]{0:T(256)S(1)}, f32[50,200,36]{1,2,0:T(8,128)S(1)}) fusion(f32[200,50]{0,1:T(8,128)S(1)} %copy.92, f32[288,50,36]{0,2,1:T(8,128)} %get-tuple-element.191, f32[288,50,36]{0,2,1:T(8,128)} %get-tuple-element.190, f32[288,200,50]{0,1,2:T(8,128)} %get-tuple-element.182, f32[288,200,50]{0,1,2:T(8,128)} %get-tuple-element.181), kind=kOutput, calls=%fused_computation.93 | convolution fusion | flops 2496196608 | bytes 28668000 | tf_op jit(solution)/shard_map/dot_general | solution.py:101
  614.9 26.7 %convolution_convert_fusion = bf16[50,200,576]{2,1,0:T(8,128)(2,1)S(1)} fusion(f32[288,50,36]{0,2,1:T(8,128)} %get-tuple-element.191, f32[288,50,36]{0,2,1:T(8,128)} %get-tuple-element.189, f32[50,200,36]{1,2,0:T(8,128)S(1)} %get-tuple-element.193, f32[200]{0:T(256)S(1)} %sub.97, f32[50,200]{1,0:T(8,128)S(1)} %copy.94), kind=kOutput, calls=%fused_computation.64 | convolution fusion | flops 2496196864 | bytes 17148000 | tf_op jit(solution)/shard_map/dot_general | solution.py:127
  646.2 7.3 slice_bitcast_fusion.5
  653.5 9.0 fusion.43
  662.4 25.1 %maximum_bitcast_fusion.2 = (bf16[288,1,2,200,50]{0,3,4,2,1:T(8,128)(2,1)}, bf16[288,1,2,200,50]{0,3,4,2,1:T(8,128)(2,1)}) fusion(bf16[288,1,200,50]{0,2,3,1:T(8,128)(2,1)} %fusion.43, bf16[288,1,200,50]{0,2,3,1:T(8,128)(2,1)} %get-tuple-element.184, bf16[288,1,200,50]{0,2,3,1:T(8,128)(2,1)} %get-tuple-element.183), kind=kLoop, calls=%fused_computation.61 | loop fusion | flops 11520000 | bytes 40320000 | tf_op jit(solution)/shard_map/stack | solution.py:132
  687.6 21.4 %pad_maximum_fusion.1 = bf16[288,2,2,200,50]{0,3,4,2,1:T(8,128)(2,1)} fusion(bf16[288,1,2,200,50]{0,3,4,2,1:T(8,128)(2,1)} %get-tuple-element.186, bf16[288,1,2,200,50]{0,3,4,2,1:T(8,128)(2,1)} %get-tuple-element.185), kind=kLoop, calls=%fused_computation.44 | loop fusion | flops 11520000 | bytes 46080000 | tf_op jit(solution)/shard_map/stack | solution.py:132
  708.9 50.3 %copy.95 = bf16[288,2,2,200,50]{3,4,2,1,0:T(8,128)(2,1)} copy(bf16[288,2,2,200,50]{0,3,4,2,1:T(8,128)(2,1)} %pad_maximum_fusion.1) | data formatting | bytes 46080000 | tf_op jit(solution)/shard_map/stack | solution.py:132
  759.3 32.1 %fusion.40 = f32[288,2,50,128]{3,2,1,0:T(8,128)} fusion(bf16[288,2,2,200,50]{3,4,2,1,0:T(8,128)(2,1)} %copy.95, bf16[288,2,200,128,1]{3,0,2,1,4:T(8,128)(2,1)} %bitcast.124), kind=kOutput, calls=%fused_computation.65 | convolution fusion | flops 2949120000 | bytes 67276800 | tf_op jit(solution)/shard_map/dot_general | solution.py:141
  792.7 498.8 %all-reduce.2.cloned.1.call-done = f32[288,2,50,128]{3,2,1,0:T(8,128)} async-done(((f32[288,2,50,128]{3,2,1,0:T(8,128)}), f32[288,2,50,128]{3,2,1,0:T(8,128)}) %all-reduce.2.cloned.1.call-update) | async-done | bytes 14745616 | tf_op jit(solution)/shard_map/psum | solution.py:140
  (167 shorter events, 189.8 us)
Async XLA Ops:
  7.2 6.2 copy-start.5
  7.2 403.1 %all-gather.2.cloned.1.call-start = ((), (), s32[]{:S(2)}) async-start(), calls=%async_computation | async-start | bytes 8294400 | tf_op jit(solution)/shard_map/all_gather | solution.py:85
  7.9 1283.5 %all-reduce.2.cloned.1.call-start = ((), (), s32[]{:S(2)}) async-start(), calls=%async_computation.1 | async-start | bytes 33030144 | tf_op jit(solution)/shard_map/psum | solution.py:140
  12.7 16.6 %copy-start.2 = (f32[16,128]{1,0:T(8,128)S(1)}, f32[16,128]{1,0:T(8,128)}, u32[]{:S(2)}) copy-start(f32[16,128]{1,0:T(8,128)} %param.10) | copy-start | bytes 24580
  12.7 16.6 %copy-start.6 = (s32[8]{0:T(128)S(1)}, s32[8]{0:T(128)}, u32[]{:S(2)}) copy-start(s32[8]{0:T(128)} %param.13) | copy-start | bytes 100
  12.7 16.8 %copy-start.1 = (s32[8,2]{0,1:T(2,128)S(1)}, s32[8,2]{0,1:T(2,128)}, u32[]{:S(2)}) copy-start(s32[8,2]{0,1:T(2,128)} %param.12) | copy-start | bytes 196
  554.4 9.4 copy-start.3
  554.5 9.6 copy-start.7
  614.6 27.0 %copy-start.4 = (f32[8]{0:T(128)}, f32[8]{0:T(128)S(1)}, u32[]{:S(2)}) copy-start(f32[8]{0:T(128)S(1)} %log_add_fusion) | copy-start | bytes 100
  641.6 4.6 copy-start
Sparse Core Ops, SparseCore 0:
  10.2 111.7 all-gather.1
  791.5 499.9 all-reduce.1
where the time goes:
time: 1310 us; the launch traced here: 1300 us
  waiting for transfers between devices  499 us (38%)
  other arithmetic  331 us (25%)
  local copies, waits for them, and re-layouts  257 us (20%)
  matrix products  187 us (14%)
  between operations  14.5 us (1%)
    psum x1, waiting for transfers between devices, local(): lax.psum(lax.dot_general(mixing, query_block, (((2, 3), (1, 2)), ((0,), (...  499 us
    another operation x10, other arithmetic  152 us
    reshape x8, local copies, waits for them, and re-layouts, transform(): spectrum.reshape(angles, 2, shifts, cycles) * ctf_row[None, None, None, :]  73 us
    dot_general x1, local copies, waits for them, and re-layouts, local(): lax.dot_general(query_block, class_block, (((2,), (2,)), ((0,), (0,))), p...  68.2 us
    dot_general x8, matrix products, transform(): jnp.dot(table_wide, shifted.reshape(2 * angles, shifts * cycles), preferr...  53.4 us
    another operation x1, local copies, waits for them, and re-layouts, local(): jnp.stack([jnp.stack([real_returned, -imag_returned], 1), jnp.stack([imag...  50.3 us
    another operation x2, other arithmetic, local(): jnp.stack([jnp.stack([real_returned, -imag_returned], 1), jnp.stack([imag...  46.5 us
    convert_element_type x8, other arithmetic, transform(): return spectrum.astype(jnp.bfloat16)  40.2 us
  transfers between devices with their start and end apart: 2, of which 1 were waited for; matrix products, arithmetic and copies ran while one was open for 31% of the time, Pallas kernels for 0%

commit v1 on v0

v1 whole, which is shorter than its diff:
```python
import functools
import math

import jax
import jax.numpy as jnp
import ml_dtypes
import numpy as np
from jax import lax
from jax.experimental import pallas as pl
from jax.experimental.pallas import tpu as pltpu
from jax.sharding import PartitionSpec as P

ROTS = 36
ANG_STEP = 8
SHIFT_SIDE = 5
SHIFTS = SHIFT_SIDE * SHIFT_SIDE
LANES = 128
HALF = 64
GROUP = 4
ROWS = 16
FOLD = ROTS // 2 + 1

two_pi = 2.0 * math.pi
f32 = jnp.float32
bf16 = jnp.bfloat16
VMEM_LIMIT = 56 * 1024 * 1024


def fourier_rows(angles):
    index_grid = np.arange(angles)
    radians = (index_grid[:, None] * index_grid[None, :] % angles) * (two_pi / angles)
    cosine, sine_part = np.cos(radians), np.sin(radians)
    table_full = np.concatenate(
        [np.concatenate([cosine, sine_part], 1), np.concatenate([-sine_part, cosine], 1)], 0
    )
    return table_full.astype(np.float32).astype(ml_dtypes.bfloat16)


def shift_tables(angles, cycles):
    theta = np.arange(angles) * (two_pi / angles)
    radius = (np.arange(cycles) + 1) / (2.0 * cycles)
    turns = np.stack([np.cos(theta), np.sin(theta)])[:, :, None] * radius
    steps = np.arange(SHIFT_SIDE) - SHIFT_SIDE // 2
    phase = two_pi * turns[:, None] * steps[None, :, None, None]
    factors = np.stack([np.cos(phase), -np.sin(phase)], 2)
    return turns.astype(np.float32), factors.astype(np.float32)


def fold_tables():
    k = np.arange(FOLD // 2 + 1)[:, None]
    m = np.arange(FOLD)[None, :]
    radians = (k * m % ROTS) * (two_pi / ROTS)
    cosine = np.repeat(np.cos(radians)[:, :, None], HALF, 2)
    sine_part = np.repeat(np.sin(radians)[:, :, None], HALF, 2)
    to_score = np.concatenate([cosine, -sine_part], 2).astype(np.float32)
    to_back = np.concatenate([cosine, sine_part], 2).astype(np.float32)
    return to_score.reshape(-1, LANES), to_back.reshape(-1, LANES)


def cos_sin_of_turns(turns):
    frac = turns - jnp.floor(turns + 0.5)
    w = frac * two_pi
    w2 = w * w
    cosine = jnp.full_like(w, 1.0 / math.factorial(16))
    for n in range(14, -1, -2):
        cosine = cosine * w2 + (-1.0) ** (n // 2) / math.factorial(n)
    sine_part = jnp.full_like(w, 1.0 / math.factorial(17))
    for n in range(15, 0, -2):
        sine_part = sine_part * w2 + (-1.0) ** (n // 2) / math.factorial(n)
    return cosine, sine_part * w


def spectra_kernel(
    shift_ref, part_ref, ctf_ref, table_ref, turns_ref, factor_ref, out_ref, base_ref, data_ref, re_ref, im_ref
):
    step = pl.program_id(0)
    count, _, angles, cycles = part_ref.shape
    chunk = 32
    per_step = ROWS // count if count < ROWS else 1

    @pl.when(step == 0)
    def _():
        for p in range(count):
            sx = shift_ref[p, 0].astype(f32)
            sy = shift_ref[p, 1].astype(f32)

            def turn(n, carry):
                rows = pl.ds(pl.multiple_of(n * chunk, chunk), chunk)
                cosine, sine_part = cos_sin_of_turns(sx * turns_ref[0, rows, :] + sy * turns_ref[1, rows, :])
                re = part_ref[p, 0, rows, :].astype(f32)
                im = part_ref[p, 1, rows, :].astype(f32)
                base_ref[p, 0, rows, :] = re * cosine + im * sine_part
                base_ref[p, 1, rows, :] = im * cosine - re * sine_part
                return carry

            lax.fori_loop(0, angles // chunk, turn, 0)

    for g in range(per_step):
        s = jnp.minimum(step * per_step + g, SHIFTS - 1)
        a = lax.div(s, SHIFT_SIDE)
        b = s - a * SHIFT_SIDE

        def shift(n, carry):
            rows = pl.ds(pl.multiple_of(n * chunk, chunk), chunk)
            low = pl.ds(pl.multiple_of(angles + n * chunk, chunk), chunk)
            xr, xi = factor_ref[0, a, 0, rows, :], factor_ref[0, a, 1, rows, :]
            yr, yi = factor_ref[1, b, 0, rows, :], factor_ref[1, b, 1, rows, :]
            tr = xr * yr - xi * yi
            ti = xr * yi + xi * yr
            for p in range(count):
                gr, gi = base_ref[p, 0, rows, :], base_ref[p, 1, rows, :]
                lanes = pl.ds((g * count + p) * cycles, cycles)
                data_ref[rows, lanes] = (gr * tr - gi * ti).astype(bf16)
                data_ref[low, lanes] = (gr * ti + gi * tr).astype(bf16)
            return carry

        lax.fori_loop(0, angles // chunk, shift, 0)

    for n in range(ROWS // 2):
        spectrum = jnp.dot(
            table_ref[...], data_ref[:, n * 2 * cycles : (n + 1) * 2 * cycles], preferred_element_type=f32
        )
        for j in range(2):
            row = 2 * n + j
            ctf_row = ctf_ref[row % count, :][None, :]
            part = spectrum[:, j * cycles : (j + 1) * cycles] * ctf_row
            re_ref[pl.ds(row, angles, stride=ROWS), :] = part[:angles]
            im_ref[pl.ds(row, angles, stride=ROWS), :] = part[angles:]
    out_ref[:, :, :cycles] = re_ref[...].reshape(angles, ROWS, cycles).astype(bf16)
    out_ref[:, :, cycles:] = im_ref[...].reshape(angles, ROWS, cycles).astype(bf16)


def make_spectra(particles, prior_shift, ctf_rows):
    count, _, angles, cycles = particles.shape
    per_step = ROWS // count if count < ROWS else 1
    steps = -(-SHIFTS // per_step)
    turns, factors = shift_tables(angles, cycles)
    full = lambda shape: pl.BlockSpec(shape, lambda i: (0,) * len(shape))
    return pl.pallas_call(
        spectra_kernel,
        grid=(steps,),
        in_specs=[
            pl.BlockSpec(memory_space=pltpu.SMEM),
            full(particles.shape),
            full(ctf_rows.shape),
            full((2 * angles, 2 * angles)),
            full(turns.shape),
            full(factors.shape),
        ],
        out_specs=pl.BlockSpec((angles, ROWS, 2 * cycles), lambda i: (0, i, 0)),
        out_shape=jax.ShapeDtypeStruct((angles, steps * ROWS, 2 * cycles), bf16),
        scratch_shapes=[
            pltpu.VMEM((count, 2, angles, cycles), f32),
            pltpu.VMEM((2 * angles, ROWS * cycles), bf16),
            pltpu.VMEM((angles * ROWS, cycles), f32),
            pltpu.VMEM((angles * ROWS, cycles), f32),
        ],
        compiler_params=pltpu.CompilerParams(vmem_limit_bytes=VMEM_LIMIT),
        name="spectra",
    )(prior_shift, particles, ctf_rows, fourier_rows(angles), turns, factors)


def folded_dft(values, coef_ref, sign):
    half = FOLD // 2
    outputs = [None] * FOLD
    for k in range(half + 1):
        even = values[0] * coef_ref[pl.ds(k * FOLD, 1), :]
        for m in range(2, FOLD, 2):
            even = even + values[m] * coef_ref[pl.ds(k * FOLD + m, 1), :]
        odd = values[1] * coef_ref[pl.ds(k * FOLD + 1, 1), :]
        for m in range(3, FOLD, 2):
            odd = odd + values[m] * coef_ref[pl.ds(k * FOLD + m, 1), :]
        outputs[k] = even + odd
        if k != half:
            outputs[FOLD - 1 - k] = (even - odd) * sign
    return outputs


def score_kernel(
    slot_ref,
    weighted_ref,
    pieces_ref,
    ctf_ref,
    score_coef_ref,
    back_coef_ref,
    rot_ref,
    back_ref,
    stat_ref,
    corr_ref,
    score_ref,
    right_ref,
    wide_ref,
    power_ref,
    *,
    classes,
    count,
):
    group = pl.program_id(0)
    slots = pieces_ref.shape[0]
    cycles = pieces_ref.shape[2]
    queries = weighted_ref.shape[2]

    @pl.when(group == 0)
    def _():
        right_ref[...] = jnp.zeros_like(right_ref)
        power_ref[...] = jnp.zeros_like(power_ref)

    for j in range(slots):
        wide_ref[j, :, :] = pieces_ref[j, :, :].astype(f32)
    for i in range(GROUP):
        total = None
        power = power_ref[:classes, :]
        for j in range(slots):
            re = wide_ref[j, 2 * i * classes : (2 * i + 1) * classes, :]
            im = wide_ref[j, (2 * i + 1) * classes : (2 * i + 2) * classes, :]
            power = power + (re * re + im * im)
            right_ref[i, j, :classes, :cycles] = re.astype(bf16)
            right_ref[i, j, :classes, cycles:] = im.astype(bf16)
            right_ref[i, j, HALF : HALF + classes, :cycles] = (-im).astype(bf16)
            right_ref[i, j, HALF : HALF + classes, cycles:] = re.astype(bf16)
            part = lax.dot_general(
                weighted_ref[slot_ref[j], i],
                right_ref[i, j],
                (((1,), (1,)), ((), ())),
                preferred_element_type=f32,
            )
            total = part if total is None else total + part
        power_ref[:classes, :] = power
        corr_ref[group * GROUP + i] = total

    @pl.when(group == pl.num_programs(0) - 1)
    def _():
        angles = ROTS * slots
        lane = lax.broadcasted_iota(jnp.int32, (count, LANES), 1)
        sign = jnp.where(lane < HALF, 1.0, -1.0).astype(f32)
        used = (lane & (HALF - 1)) < classes
        used_once = used & (lane < HALF)
        power = power_ref[...]
        ctf_row = ctf_ref[...]
        bias = lax.dot_general(
            ctf_row * ctf_row,
            jnp.concatenate([power, power], 0),
            (((1,), (1,)), ((), ())),
            precision=lax.Precision.HIGHEST,
            preferred_element_type=f32,
        ) * (0.5 / angles)

        def scores(s, peak):
            rows = pl.ds(pl.multiple_of(s * count, 8), count)
            values = [corr_ref[0, rows, :]]
            for m in range(1, ROTS // 2):
                values.append(corr_ref[m, rows, :] + corr_ref[ROTS - m, rows, :] * sign)
            values.append(corr_ref[ROTS // 2, rows, :])
            for k, y in enumerate(folded_dft(values, score_coef_ref, sign)):
                z = (pltpu.roll(y, HALF, 1) + y * sign) * (1.0 / angles) - bias
                z = jnp.where(used_once if k in (0, FOLD - 1) else used, z, -1e30)
                score_ref[k, rows, :] = z
                peak = jnp.maximum(peak, z)
            return peak

        peak = lax.fori_loop(0, SHIFTS, scores, jnp.full((count, LANES), -1e30, f32))
        peak = jnp.broadcast_to(jnp.max(peak, axis=1, keepdims=True), (count, LANES))

        def backs(s, mass):
            rows = pl.ds(pl.multiple_of(s * count, 8), count)
            values = []
            for k in range(FOLD):
                e = jnp.exp(score_ref[k, rows, :] - peak)
                mass = mass + e
                values.append(pltpu.roll(e, HALF, 1) + e * sign)
            for m, y in enumerate(folded_dft(values, back_coef_ref, sign)):
                y_rolled = pltpu.roll(y, HALF, 1)
                back_ref[m, rows, :] = y * rot_ref[m, 0:1, :] + y_rolled * rot_ref[m, 1:2, :]
                if m not in (0, FOLD - 1):
                    y, y_rolled = y * sign, y_rolled * -sign
                    back_ref[ROTS - m, rows, :] = (
                        y * rot_ref[ROTS - m, 0:1, :] + y_rolled * rot_ref[ROTS - m, 1:2, :]
                    )
            return mass

        mass = lax.fori_loop(0, SHIFTS, backs, jnp.zeros((count, LANES), f32))
        if queries > SHIFTS * count:
            back_ref[:, SHIFTS * count :, :] = jnp.zeros((ROTS, queries - SHIFTS * count, LANES), f32)
        stat_ref[0] = peak
        stat_ref[1] = mass


def make_scores(slot_of, weighted, pieces, ctf_rows, rot_lanes, classes):
    slots, _, queries, _ = weighted.shape
    cycles = pieces.shape[2]
    count = ctf_rows.shape[0]
    to_score, to_back = fold_tables()
    block = 2 * GROUP * classes
    full = lambda shape: pl.BlockSpec(shape, lambda g: (0,) * len(shape))
    return pl.pallas_call(
        functools.partial(score_kernel, classes=classes, count=count),
        grid=(ROTS // GROUP,),
        in_specs=[
            pl.BlockSpec(memory_space=pltpu.SMEM),
            pl.BlockSpec((slots, GROUP, queries, 2 * cycles), lambda g: (0, g, 0, 0)),
            pl.BlockSpec((slots, block, cycles), lambda g: (0, g, 0)),
            full(ctf_rows.shape),
            full(to_score.shape),
            full(to_back.shape),
            full(rot_lanes.shape),
        ],
        out_specs=[full((ROTS, queries, LANES)), full((2, count, LANES))],
        out_shape=[
            jax.ShapeDtypeStruct((ROTS, queries, LANES), f32),
            jax.ShapeDtypeStruct((2, count, LANES), f32),
        ],
        scratch_shapes=[
            pltpu.VMEM((ROTS, queries, LANES), f32),
            pltpu.VMEM((FOLD, queries, LANES), f32),
            pltpu.VMEM((GROUP, slots, 2 * HALF, 2 * cycles), bf16),
            pltpu.VMEM((slots, block, cycles), f32),
            pltpu.VMEM((HALF, cycles), f32),
        ],
        compiler_params=pltpu.CompilerParams(vmem_limit_bytes=VMEM_LIMIT),
        name="scores",
    )(slot_of, weighted, pieces, ctf_rows, to_score, to_back, rot_lanes)


def scale_kernel(back_ref, scale_ref, out_ref):
    queries = back_ref.shape[1]
    padded = -(-queries // LANES) * LANES
    for i in range(GROUP):
        value = back_ref[i] * scale_ref[...]
        if padded > queries:
            value = jnp.concatenate([value, jnp.zeros((padded - queries, LANES), f32)], 0)
        out_ref[i] = value.T[:, :queries].astype(bf16)


def scale_back(back, scale):
    _, queries, _ = back.shape
    return pl.pallas_call(
        scale_kernel,
        grid=(ROTS // GROUP,),
        in_specs=[
            pl.BlockSpec((GROUP, queries, LANES), lambda g: (g, 0, 0)),
            pl.BlockSpec((queries, LANES), lambda g: (0, 0)),
        ],
        out_specs=pl.BlockSpec((GROUP, LANES, queries), lambda g: (g, 0, 0)),
        out_shape=jax.ShapeDtypeStruct((ROTS, LANES, queries), bf16),
        compiler_params=pltpu.CompilerParams(vmem_limit_bytes=VMEM_LIMIT),
        name="scale_back",
    )(back, scale)


def sums_kernel(back_ref, weighted_ref, turn_ref, out_ref, wide_ref, *, classes):
    cycles = out_ref.shape[2]
    cosine = turn_ref[0, 0]
    sine_part = turn_ref[0, 1]
    for i in range(GROUP):
        product = jnp.dot(back_ref[i], weighted_ref[0, i], preferred_element_type=f32)
        re = product[:HALF, :cycles] - product[HALF:, cycles:]
        im = product[:HALF, cycles:] + product[HALF:, :cycles]
        wide_ref[2 * i * classes : (2 * i + 1) * classes, :] = (re * cosine - im * sine_part)[:classes]
        wide_ref[(2 * i + 1) * classes : (2 * i + 2) * classes, :] = (re * sine_part + im * cosine)[:classes]
    out_ref[0] = wide_ref[...].astype(bf16)


def make_sums(back, weighted, turn_columns, classes):
    slots, _, queries, double = weighted.shape
    cycles = double // 2
    block = 2 * GROUP * classes
    return pl.pallas_call(
        functools.partial(sums_kernel, classes=classes),
        grid=(slots, ROTS // GROUP),
        in_specs=[
            pl.BlockSpec((GROUP, LANES, queries), lambda u, g: (g, 0, 0)),
            pl.BlockSpec((1, GROUP, queries, double), lambda u, g: (u, g, 0, 0)),
            pl.BlockSpec((1, 2, HALF, LANES), lambda u, g: (u, 0, 0, 0)),
        ],
        out_specs=pl.BlockSpec((1, block, cycles), lambda u, g: (u, g, 0)),
        out_shape=jax.ShapeDtypeStruct((slots, ROTS * 2 * classes, cycles), bf16),
        scratch_shapes=[pltpu.VMEM((block, cycles), f32)],
        compiler_params=pltpu.CompilerParams(vmem_limit_bytes=VMEM_LIMIT),
        name="class_sums",
    )(back, weighted, turn_columns)


def phase_of(index, period):
    radians = (index % period).astype(f32) * (two_pi / period)
    return jnp.cos(radians), jnp.sin(radians)


def local(particles, references, ctf_table, rot_offset, prior_shift, defocus_group):
    count, _, angles, cycles = particles.shape
    own_rows, _, classes, _ = references.shape
    slots = angles // ROTS
    group_count = ctf_table.shape[0]
    parts = lax.axis_size("cls")
    onehot = (defocus_group[:, None] == jnp.arange(group_count, dtype=jnp.int32)[None, :]).astype(f32)
    ctf_rows = jnp.dot(onehot, ctf_table, precision=lax.Precision.HIGHEST)

    freq = lax.axis_index("dp") * own_rows + jnp.arange(own_rows, dtype=jnp.int32)
    cosine, sine_part = phase_of(freq[:, None] * rot_offset[None, :], angles)
    cosine, sine_part = cosine[:, :, None], sine_part[:, :, None]
    wide = references.astype(f32)
    turned = jnp.stack(
        [
            wide[:, 0] * cosine + wide[:, 1] * sine_part,
            wide[:, 1] * cosine - wide[:, 0] * sine_part,
        ],
        1,
    ).astype(bf16)
    piece = turned.reshape(own_rows * 2 * classes, cycles)
    pieces = lax.all_gather(piece, "dp", axis=0, tiled=True).reshape(slots, ROTS * 2 * classes, cycles)

    weighted = make_spectra(particles, prior_shift, ctf_rows)
    queries = weighted.shape[1]
    weighted = weighted.reshape(slots, ROTS, queries, 2 * cycles)

    lanes = jnp.pad(rot_offset, (0, HALF - classes))
    cosine, sine_part = phase_of(jnp.arange(ROTS, dtype=jnp.int32)[:, None] * lanes[None, :], angles)
    rot_lanes = jnp.stack(
        [jnp.concatenate([cosine, cosine], 1), jnp.concatenate([-sine_part, sine_part], 1)], 1
    )
    cosine, sine_part = phase_of(jnp.arange(slots, dtype=jnp.int32)[:, None] * lanes[None, :], slots)
    turn_columns = jnp.broadcast_to(
        jnp.stack([cosine, sine_part], 1)[:, :, :, None], (slots, 2, HALF, LANES)
    )

    back, stat = make_scores(
        jnp.arange(slots, dtype=jnp.int32), weighted, pieces, ctf_rows, rot_lanes, classes
    )
    peak = stat[0, :, 0]
    mass_lanes = stat[1]
    mine = jnp.stack([peak, jnp.sum(mass_lanes, axis=1)])
    place = (jnp.arange(parts) == lax.axis_index("cls")).astype(f32)
    everyone = lax.psum(place[:, None, None] * mine[None], "cls")
    top = jnp.max(everyone[:, 0], axis=0)
    total_mass = jnp.sum(everyone[:, 1] * jnp.exp(everyone[:, 0] - top[None]), axis=0)
    log_evidence = top + jnp.log(total_mass)
    scale = jnp.exp(peak - log_evidence)
    class_posterior = (mass_lanes[:, :classes] + mass_lanes[:, HALF : HALF + classes]) * scale[:, None]

    scale_rows = jnp.broadcast_to(
        jnp.tile(scale, queries // count)[:, None], (queries, LANES)
    )
    back = scale_back(back, scale_rows)
    sums = make_sums(back, weighted, turn_columns, classes)
    summed = lax.psum_scatter(
        sums.reshape(slots * ROTS * 2 * classes, cycles), "dp", scatter_dimension=0, tiled=True
    )
    class_sums = summed.astype(f32).reshape(own_rows, 2, classes, cycles)
    return (log_evidence, class_posterior, class_sums)


def solution(mesh):
    placed = (
        P("dp", None, None, None),
        P("dp", None, "cls", None),
        P(),
        P("cls"),
        P("dp", None),
        P("dp"),
    )
    return jax.shard_map(
        local,
        mesh=mesh,
        in_specs=placed,
        out_specs=(P("dp"), P("dp", "cls"), P("dp", None, "cls", None)),
        check_vma=False,
    )
```

time: 1310 us -> 376 us (0.29)
  other arithmetic: 331 us -> 11.9 us
  waiting for transfers between devices: 499 us -> 182 us
  local copies, waits for them, and re-layouts: 257 us -> 8.68 us
  matrix products: 187 us -> 0.78 us
  Pallas kernels: 0 us -> 148 us
    psum x1 -> x0, waiting for transfers between devices: 499 us -> none  [local(): lax.psum(lax.dot_general(mixing, query_block, (((2, 3), (1, 2)), ((0,), (...]
    another operation x23 -> x6, other arithmetic: 213 us -> 7.56 us
    dot_general x15 -> x1, matrix products: 187 us -> 0.78 us  [local(): ctf_rows = jnp.dot(onehot, ctf_table, precision=lax.Precision.HIGHEST)]
    pallas_call x0 -> x4, Pallas kernels: none -> 148 us  [the longest x1 59.6 us: make_spectra(): pl.pallas_call(spectra_kernel, grid=(steps,), in_specs=[pl.BlockSpec(memo...]
    reduce_scatter x0 -> x1, waiting for transfers between devices: none -> 132 us  [local(): lax.psum_scatter(sums.reshape(slots * ROTS * 2 * classes, cycles), 'dp',...]
    reshape x8 -> x1, local copies, waits for them, and re-layouts: 73 us -> 1.3 us  [local(): class_sums = summed.astype(f32).reshape(own_rows, 2, classes, cycles)]
    dot_general x1 -> x0, local copies, waits for them, and re-layouts: 68.2 us -> none  [local(): lax.dot_general(query_block, class_block, (((2,), (2,)), ((0,), (0,))), p...]
    another operation x3 -> x5, local copies, waits for them, and re-layouts: 58.3 us -> 0.18 us  [the longest x1 0.14 us: local(): jnp.stack([wide[:, 0] * cosine + wide[:, 1] * sine_part, wide[:, 1] * cos...]
  transfers between devices with their start and end apart: 2 -> 2, of which waited for: 1 -> 2; matrix products, arithmetic and copies ran while one was open for 31% -> 1% of each run, Pallas kernels for 0% -> 16%
where the time goes in v1:
time: 376 us; the launch traced here: 371 us
  waiting for transfers between devices  182 us (48%)
  Pallas kernels  148 us (39%)
  between operations  14.2 us (4%)
  other arithmetic  11.9 us (3%)
  local copies, waits for them, and re-layouts  8.68 us (2%)
  blocking collectives  6.07 us (2%)
    reduce_scatter x1, waiting for transfers between devices, local(): lax.psum_scatter(sums.reshape(slots * ROTS * 2 * classes, cycles), 'dp',...  132 us
    pallas_call x1, Pallas kernels, make_spectra(): pl.pallas_call(spectra_kernel, grid=(steps,), in_specs=[pl.BlockSpec(memo...  59.6 us
    pallas_call x1, Pallas kernels, make_sums(): pl.pallas_call(functools.partial(sums_kernel, classes=classes), grid=(slo...  52.5 us
    all_gather x1, waiting for transfers between devices, local(): lax.all_gather(piece, 'dp', axis=0, tiled=True)  49.8 us
    pallas_call x1, Pallas kernels, make_scores(): pl.pallas_call(functools.partial(score_kernel, classes=classes, count=cou...  28.6 us
  transfers between devices with their start and end apart: 2, of which 2 were waited for; matrix products, arithmetic and copies ran while one was open for 1% of the time, Pallas kernels for 16%

profile of v1, /device:TPU:8, one launch (start us, length us, event | category | flops | bytes accessed | tf_op | source)
XLA Modules:
  0.0 371.3 jit_solution(1483446864689567847)
XLA Ops:
  7.3 1.8 convert_element_type.45
  9.1 0.2 fusion.11
  9.3 4.7 %add_convert_fusion = (bf16[36,1,50,128]{3,1,2,0:T(2,128)(2,1)S(1)}, bf16[36,1,50,128]{3,1,2,0:T(2,128)(2,1)S(1)}) fusion(f32[36,2,50,128]{3,1,2,0:T(2,128)S(1)} %convert_element_type.45, f32[36,50]{1,0:T(8,128)S(1)} %get-tuple-element.20, f32[36,50]{1,0:T(8,128)S(1)} %get-tuple-element.19), kind=kLoop, calls=%fused_computation.2 | loop fusion | flops 1843200 | bytes 2779200 | tf_op jit(solution)/shard_map/convert.1
  14.0 2.1 pad_maximum_fusion
  16.1 0.1 copy.21
  16.3 1.2 convert_element_type.47
  17.5 0.0 reduce-scatter.2.cloned.1.call-start
  17.5 0.1 fusion.7
  17.6 0.1 pad_maximum_fusion.2
  17.7 0.1 maximum_bitcast_fusion
  17.8 0.7 copy.20.shift_ref
  18.5 0.1 fusion.26
  18.6 0.8 fusion.21.ctf_ref
  19.4 59.6 %spectra.1 = bf16[288,208,256]{2,1,0:T(8,128)(2,1)} custom-call(s32[8,2]{1,0:T(8,128)} %copy.20.shift_ref, bf16[8,2,288,128]{3,2,1,0:T(8,128)(2,1)} %part_ref.1, f32[8,128]{1,0:T(8,128)} %fusion.21.ctf_ref, bf16[576,576]{1,0:T(8,128)(2,1)} %constant.63.clone.table_ref, f32[2,288,128]{2,1,0:T(8,128)} %constant.64.clone.turns_ref, ...), custom_call_target="tpu_custom_call" | custom-call | tf_op jit(solution)/shard_map/spectra/pallas_call | solution.py:139
  79.0 0.7 pad_maximum_fusion.1.rot_ref
  79.6 49.8 %all-gather.2.cloned.1.call-done = bf16[28800,128]{1,0:T(8,128)(2,1)} async-done(((bf16[3600,128]{1,0:T(8,128)(2,1)}), bf16[28800,128]{1,0:T(8,128)(2,1)}) %all-gather.2.cloned.1.call-update) | async-done | bytes 7372816 | tf_op jit(solution)/shard_map/all_gather | solution.py:409
  129.4 0.5 iota.31.slot_ref
  129.9 28.6 %scores.1 = (f32[36,208,128]{2,1,0:T(8,128)}, f32[2,8,128]{2,1,0:T(8,128)}) custom-call(s32[8]{0:T(128)} %iota.31.slot_ref, bf16[8,36,208,256]{3,2,1,0:T(8,128)(2,1)} %bitcast.22, bf16[8,3600,128]{2,1,0:T(8,128)(2,1)} %bitcast.25, f32[8,128]{1,0:T(8,128)} %fusion.21.ctf_ref, f32[190,128]{1,0:T(8,128)} %constant.66.clone.score_coef_ref, ...), custom_call_target="tpu_custom_call" | custom-call | tf_op jit(solution)/shard_map/scores/pallas_call | solution.py:295
  158.5 0.8 slice_bitcast_fusion
  159.3 0.8 slice_reduce_fusion
  160.1 0.1 broadcast_multiply_fusion
  160.2 6.1 %psum.7 = f32[4,2,8]{2,0,1:T(4,128)S(1)} all-reduce(f32[4,2,8]{2,0,1:T(4,128)S(1)} %broadcast_multiply_fusion), channel_id=1, replica_groups=mesh['dp'=8,'cls'=4] {'cls'}, use_global_device_ids=true, to_apply=%region_1.2 | all-reduce | flops 64 | bytes 512 | tf_op jit(solution)/shard_map/psum | solution.py:432
  166.3 0.5 subtract_exponential_fusion
  166.8 0.1 broadcast_in_dim.6
  166.9 0.7 broadcast_in_dim.7.scale_ref
  167.7 7.1 %scale_back.1.back_ref = bf16[36,128,208]{2,1,0:T(8,128)(2,1)} custom-call(f32[36,208,128]{2,1,0:T(8,128)} %get-tuple-element.6.back_ref, f32[208,128]{1,0:T(8,128)} %broadcast_in_dim.7.scale_ref), custom_call_target="tpu_custom_call" | custom-call | tf_op jit(solution)/shard_map/scale_back/pallas_call | solution.py:336
  174.8 1.0 broadcast_in_dim.8.turn_ref
  175.8 52.5 %class_sums.1 = bf16[8,3600,128]{2,1,0:T(8,128)(2,1)} custom-call(bf16[36,128,208]{2,1,0:T(8,128)(2,1)} %scale_back.1.back_ref, bf16[8,36,208,256]{3,2,1,0:T(8,128)(2,1)} %bitcast.23, f32[8,2,64,128]{3,2,1,0:T(8,128)} %broadcast_in_dim.8.turn_ref), custom_call_target="tpu_custom_call" | custom-call | tf_op jit(solution)/shard_map/class_sums/pallas_call | solution.py:367
  228.3 0.7 add_multiply_fusion
  229.0 132.0 %reduce-scatter.2.cloned.1.call-done = bf16[3600,128]{1,0:T(8,128)(2,1)} async-done(((bf16[28800,128]{1,0:T(8,128)(2,1)}), bf16[3600,128]{1,0:T(8,128)(2,1)}) %reduce-scatter.2.cloned.1.call-update) | async-done | bytes 921616 | tf_op jit(solution)/shard_map/reduce_scatter | solution.py:444
  361.0 1.3 reshape.217
  362.3 2.2 copy.24
  (24 shorter events, 0.2 us)
Async XLA Ops:
  7.2 11.4 %copy-start = (f32[16,128]{1,0:T(8,128)S(1)}, f32[16,128]{1,0:T(8,128)}, u32[]{:S(2)}) copy-start(f32[16,128]{1,0:T(8,128)} %param.13) | copy-start | bytes 24580
  7.2 1.9 copy-start.3
  7.2 122.2 %all-gather.2.cloned.1.call-start = ((), (), s32[]{:S(2)}) async-start(), calls=%async_computation.1 | async-start | bytes 8294400 | tf_op jit(solution)/shard_map/all_gather | solution.py:409
  16.1 1.7 copy-start.2
  16.2 2.4 copy-start.4
  17.5 343.5 %reduce-scatter.2.cloned.1.call-start = ((), (), s32[]{:S(2)}) async-start(), calls=%async_computation.2 | async-start | bytes 8294400 | tf_op jit(solution)/shard_map/reduce_scatter | solution.py:444
  361.0 3.5 copy-start.1
Sparse Core Ops, SparseCore 0:
  17.6 111.7 all-gather.1
  228.4 132.5 reduce-scatter.1

commit v2 on v1

v2 whole, which is shorter than its diff:
```python
import functools
import math

import jax
import jax.numpy as jnp
import ml_dtypes
import numpy as np
from jax import lax
from jax.experimental import pallas as pl
from jax.experimental.pallas import tpu as pltpu
from jax.sharding import PartitionSpec as P

ROTS = 36
ANG_STEP = 8
SHIFT_SIDE = 5
SHIFTS = SHIFT_SIDE * SHIFT_SIDE
LANES = 128
GROUP = 12
ROWS = 16
FOLD = ROTS // 2 + 1

two_pi = 2.0 * math.pi
f32 = jnp.float32
bf16 = jnp.bfloat16
VMEM_LIMIT = 56 * 1024 * 1024


def fourier_rows(angles):
    index_grid = np.arange(angles)
    radians = (index_grid[:, None] * index_grid[None, :] % angles) * (two_pi / angles)
    cosine, sine_part = np.cos(radians), np.sin(radians)
    table_full = np.concatenate(
        [np.concatenate([cosine, sine_part], 1), np.concatenate([-sine_part, cosine], 1)], 0
    )
    return table_full.astype(np.float32).astype(ml_dtypes.bfloat16)


def shift_tables(angles, cycles):
    theta = np.arange(angles) * (two_pi / angles)
    radius = (np.arange(cycles) + 1) / (2.0 * cycles)
    turns = np.stack([np.cos(theta), np.sin(theta)])[:, :, None] * radius
    steps = np.arange(SHIFT_SIDE) - SHIFT_SIDE // 2
    phase = two_pi * turns[:, None] * steps[None, :, None, None]
    factors = np.stack([np.cos(phase), -np.sin(phase)], 2)
    return turns.astype(np.float32), factors.astype(np.float32)


def cos_sin_of_turns(turns):
    frac = turns - jnp.floor(turns + 0.5)
    w = frac * two_pi
    w2 = w * w
    cosine = jnp.full_like(w, 1.0 / math.factorial(16))
    for n in range(14, -1, -2):
        cosine = cosine * w2 + (-1.0) ** (n // 2) / math.factorial(n)
    sine_part = jnp.full_like(w, 1.0 / math.factorial(17))
    for n in range(15, 0, -2):
        sine_part = sine_part * w2 + (-1.0) ** (n // 2) / math.factorial(n)
    return cosine, sine_part * w


def spectra_kernel(
    shift_ref, part_ref, ctf_ref, table_ref, turns_ref, factor_ref, out_ref, base_ref, data_ref, re_ref, im_ref
):
    step = pl.program_id(0)
    count, _, angles, cycles = part_ref.shape
    chunk = 32
    per_step = ROWS // count if count < ROWS else 1

    @pl.when(step == 0)
    def _():
        for p in range(count):
            sx = shift_ref[p, 0].astype(f32)
            sy = shift_ref[p, 1].astype(f32)

            def turn(n, carry):
                rows = pl.ds(pl.multiple_of(n * chunk, chunk), chunk)
                cosine, sine_part = cos_sin_of_turns(sx * turns_ref[0, rows, :] + sy * turns_ref[1, rows, :])
                re = part_ref[p, 0, rows, :].astype(f32)
                im = part_ref[p, 1, rows, :].astype(f32)
                base_ref[p, 0, rows, :] = re * cosine + im * sine_part
                base_ref[p, 1, rows, :] = im * cosine - re * sine_part
                return carry

            lax.fori_loop(0, angles // chunk, turn, 0)

    for g in range(per_step):
        s = jnp.minimum(step * per_step + g, SHIFTS - 1)
        a = lax.div(s, SHIFT_SIDE)
        b = s - a * SHIFT_SIDE

        def shift(n, carry):
            rows = pl.ds(pl.multiple_of(n * chunk, chunk), chunk)
            low = pl.ds(pl.multiple_of(angles + n * chunk, chunk), chunk)
            xr, xi = factor_ref[0, a, 0, rows, :], factor_ref[0, a, 1, rows, :]
            yr, yi = factor_ref[1, b, 0, rows, :], factor_ref[1, b, 1, rows, :]
            tr = xr * yr - xi * yi
            ti = xr * yi + xi * yr
            for p in range(count):
                gr, gi = base_ref[p, 0, rows, :], base_ref[p, 1, rows, :]
                lanes = pl.ds((g * count + p) * cycles, cycles)
                data_ref[rows, lanes] = (gr * tr - gi * ti).astype(bf16)
                data_ref[low, lanes] = (gr * ti + gi * tr).astype(bf16)
            return carry

        lax.fori_loop(0, angles // chunk, shift, 0)

    for n in range(ROWS // 2):
        spectrum = jnp.dot(
            table_ref[...], data_ref[:, n * 2 * cycles : (n + 1) * 2 * cycles], preferred_element_type=f32
        )
        for j in range(2):
            row = 2 * n + j
            ctf_row = ctf_ref[row % count, :][None, :]
            part = spectrum[:, j * cycles : (j + 1) * cycles] * ctf_row
            re_ref[pl.ds(row, angles, stride=ROWS), :] = part[:angles]
            im_ref[pl.ds(row, angles, stride=ROWS), :] = part[angles:]
    out_ref[:, :, :cycles] = re_ref[...].reshape(angles, ROWS, cycles).astype(bf16)
    out_ref[:, :, cycles:] = im_ref[...].reshape(angles, ROWS, cycles).astype(bf16)


def make_spectra(particles, prior_shift, ctf_rows):
    count, _, angles, cycles = particles.shape
    per_step = ROWS // count if count < ROWS else 1
    steps = -(-SHIFTS // per_step)
    turns, factors = shift_tables(angles, cycles)
    full = lambda shape: pl.BlockSpec(shape, lambda i: (0,) * len(shape))
    return pl.pallas_call(
        spectra_kernel,
        grid=(steps,),
        in_specs=[
            pl.BlockSpec(memory_space=pltpu.SMEM),
            full(particles.shape),
            full(ctf_rows.shape),
            full((2 * angles, 2 * angles)),
            full(turns.shape),
            full(factors.shape),
        ],
        out_specs=pl.BlockSpec((angles, ROWS, 2 * cycles), lambda i: (0, i, 0)),
        out_shape=jax.ShapeDtypeStruct((angles, steps * ROWS, 2 * cycles), bf16),
        scratch_shapes=[
            pltpu.VMEM((count, 2, angles, cycles), f32),
            pltpu.VMEM((2 * angles, ROWS * cycles), bf16),
            pltpu.VMEM((angles * ROWS, cycles), f32),
            pltpu.VMEM((angles * ROWS, cycles), f32),
        ],
        compiler_params=pltpu.CompilerParams(vmem_limit_bytes=VMEM_LIMIT),
        name="spectra",
    )(prior_shift, particles, ctf_rows, fourier_rows(angles), turns, factors)


def half_dft(even_values, odd_values):
    half = FOLD // 2
    cos_sums, sin_sums = [None] * FOLD, [None] * FOLD

    def weighted_sum(values, k, table, start):
        total = None
        for m in range(start, FOLD, 2):
            weight = float(table((k * m % ROTS) * two_pi / ROTS))
            if values[m] is None or abs(weight) < 1e-9:
                continue
            if abs(abs(weight) - 1.0) < 1e-9:
                term = values[m] if weight > 0 else -values[m]
            else:
                term = values[m] * weight
            total = term if total is None else total + term
        return jnp.zeros_like(values[1]) if total is None else total

    for k in range(half + 1):
        even = weighted_sum(even_values, k, math.cos, 0)
        odd = weighted_sum(even_values, k, math.cos, 1)
        cos_sums[k] = even + odd
        if k != half:
            cos_sums[FOLD - 1 - k] = even - odd
        if k:
            even = weighted_sum(odd_values, k, math.sin, 0)
            odd = weighted_sum(odd_values, k, math.sin, 1)
            sin_sums[k] = even + odd
            if k != half:
                sin_sums[FOLD - 1 - k] = odd - even
    return cos_sums, sin_sums


def turn_kernel(first_ref, references_ref, offset_ref, out_ref, wide_ref):
    own_rows, _, classes, _ = references_ref.shape
    batch = wide_ref.shape[1] // (2 * classes)
    offsets = offset_ref[:classes, :]

    def some(n, carry):
        for i in range(batch):
            m = batch * n + i
            freq = (first_ref[0] + m).astype(f32)
            cosine, sine_part = cos_sin_of_turns(offsets * freq * (1.0 / (ROTS * ANG_STEP)))
            re = references_ref[m, 0].astype(f32)
            im = references_ref[m, 1].astype(f32)
            wide_ref[n, 2 * i * classes : (2 * i + 1) * classes, :] = re * cosine + im * sine_part
            wide_ref[n, (2 * i + 1) * classes : (2 * i + 2) * classes, :] = im * cosine - re * sine_part
        return carry

    lax.fori_loop(0, own_rows // batch, some, 0)
    out_ref[...] = wide_ref[...].reshape(out_ref.shape).astype(bf16)


def turn_references(first, references, offsets):
    own_rows, _, classes, cycles = references.shape
    batch = own_rows if own_rows % 2 else 2
    return pl.pallas_call(
        turn_kernel,
        in_specs=[
            pl.BlockSpec(memory_space=pltpu.SMEM),
            pl.BlockSpec(memory_space=pltpu.VMEM),
            pl.BlockSpec(memory_space=pltpu.VMEM),
        ],
        out_shape=jax.ShapeDtypeStruct((own_rows * 2 * classes, cycles), bf16),
        scratch_shapes=[pltpu.VMEM((own_rows // batch, batch * 2 * classes, cycles), f32)],
        compiler_params=pltpu.CompilerParams(vmem_limit_bytes=VMEM_LIMIT),
        name="turn_references",
    )(first, references, offsets)


def correlate_kernel(slot_ref, *refs, slots, classes, padded, finish):
    weighted_refs, refs = refs[:slots], refs[slots:]
    piece_refs, refs = refs[:slots], refs[slots:]
    if finish:
        before_ref, power_before_ref, ctf_ref, weight_ref, stat_ref = refs[:5]
        corr_ref, wide_ref, power_ref = refs[5:]
    else:
        corr_ref, power_ref, wide_ref = refs
    group = pl.program_id(0)
    cycles = piece_refs[0].shape[1]
    queries = weighted_refs[0].shape[2]
    block = piece_refs[0].shape[0]

    @pl.when(group == 0)
    def _():
        wide_ref[:, block:, :] = jnp.zeros((slots, wide_ref.shape[1] - block, cycles), f32)
        power_ref[...] = power_before_ref[...] if finish else jnp.zeros_like(power_ref)

    for j in range(slots):
        wide_ref[j, :block, :] = piece_refs[j][...].astype(f32)
    power = power_ref[...]
    for i in range(GROUP):
        total = before_ref[i, :, :queries] if finish else None
        for j in range(slots):
            start = 2 * i * classes
            re = wide_ref[j, start : start + padded, :]
            im = wide_ref[j, start + classes : start + classes + padded, :]
            power = power + (re * re + im * im)
            left = jnp.concatenate(
                [jnp.concatenate([re, im], 1), jnp.concatenate([-im, re], 1)], 0
            ).astype(bf16)
            part = lax.dot_general(
                left, weighted_refs[j][0, i], (((1,), (1,)), ((), ())), preferred_element_type=f32
            )
            total = part if total is None else total + part
        row = group * GROUP + i if finish else i
        corr_ref[row, :, :queries] = total
    power_ref[...] = power

    if not finish:
        return

    @pl.when(group == pl.num_programs(0) - 1)
    def _():
        count = ctf_ref.shape[0]
        angles = ROTS * ANG_STEP
        used = SHIFTS * count
        tiles = weight_ref.shape[2] // LANES
        ctf_row = ctf_ref[...]
        ctf_rows = jnp.concatenate([ctf_row * ctf_row] * (LANES // count), 0)
        bias = lax.dot_general(
            power_ref[...],
            ctf_rows,
            (((1,), (1,)), ((), ())),
            precision=lax.Precision.HIGHEST,
            preferred_element_type=f32,
        ) * (0.5 / angles)
        wide_ref[0, :padded, :] = bias
        rows_of = lambda base: lax.broadcasted_iota(jnp.int32, (8, LANES), 0) + base
        lanes_of = lambda base: lax.broadcasted_iota(jnp.int32, (8, LANES), 1) + base

        peak = jnp.full((8, LANES), -1e30, f32)
        for tile in range(tiles):
            lanes = slice(tile * LANES, (tile + 1) * LANES)

            def scores(n, peak):
                start = pl.multiple_of(n * 8, 8)
                rows = pl.ds(start, 8)
                low = pl.ds(padded + start, 8)
                valid = (rows_of(start) < classes) & (lanes_of(tile * LANES) < used)
                even_values = [corr_ref[0, rows, lanes]]
                odd_values = [None]
                for m in range(1, ROTS // 2):
                    even_values.append(corr_ref[m, rows, lanes] + corr_ref[ROTS - m, rows, lanes])
                    odd_values.append(corr_ref[m, low, lanes] - corr_ref[ROTS - m, low, lanes])
                even_values.append(corr_ref[ROTS // 2, rows, lanes])
                odd_values.append(None)
                cos_sums, sin_sums = half_dft(even_values, odd_values)
                bias = wide_ref[0, rows, :]
                for k in range(FOLD):
                    if k in (0, FOLD - 1):
                        results = [(k, cos_sums[k])]
                    else:
                        results = [(k, cos_sums[k] - sin_sums[k]), (ROTS - k, cos_sums[k] + sin_sums[k])]
                    for place, value in results:
                        value = jnp.where(valid, value * (1.0 / angles) - bias, -1e30)
                        weight_ref[place, rows, lanes] = value
                        peak = jnp.maximum(peak, value)
                return peak

            peak = lax.fori_loop(0, padded // 8, scores, peak)

        peak = jnp.broadcast_to(jnp.max(peak, axis=0, keepdims=True), (8, LANES))
        step = count
        while step < LANES:
            peak = jnp.maximum(peak, pltpu.roll(peak, step, 1))
            step *= 2
        stat_ref[0:8, :] = peak

        def masses(n, carry):
            rows = pl.ds(pl.multiple_of(n * 8, 8), 8)
            mass = jnp.zeros((8, LANES), f32)
            for tile in range(tiles):
                lanes = slice(tile * LANES, (tile + 1) * LANES)
                for k in range(ROTS):
                    value = jnp.exp(weight_ref[k, rows, lanes] - peak)
                    weight_ref[k, rows, lanes] = value
                    mass = mass + value
            step = count
            while step < LANES:
                mass = mass + pltpu.roll(mass, step, 1)
                step *= 2
            stat_ref[pl.ds(pl.multiple_of(8 + n * 8, 8), 8), :] = mass
            return carry

        lax.fori_loop(0, padded // 8, masses, 0)


def correlate(slot_of, weighted, pieces, classes, before=None, power=None, ctf_rows=None):
    _, _, queries, double = weighted.shape
    cycles = double // 2
    slots = len(pieces)
    padded = -(-classes // 8) * 8
    wide_lanes = -(-queries // LANES) * LANES
    block = 2 * GROUP * classes
    finish = ctf_rows is not None
    full = lambda shape: pl.BlockSpec(shape, lambda g, u: (0,) * len(shape))
    in_specs = [
        pl.BlockSpec((1, GROUP, queries, double), functools.partial(lambda j, g, u: (u[j], g, 0, 0), j))
        for j in range(slots)
    ] + [pl.BlockSpec((block, cycles), lambda g, u: (g, 0))] * slots
    corr_block = pl.BlockSpec((GROUP, 2 * padded, wide_lanes), lambda g, u: (g, 0, 0))
    corr_shape = (ROTS, 2 * padded, wide_lanes)
    wide = pltpu.VMEM((slots, block + 8, cycles), f32)
    operands = [slot_of] + [weighted] * slots + list(pieces)
    if finish:
        in_specs += [corr_block, full((padded, cycles)), full(ctf_rows.shape)]
        operands += [before, power, ctf_rows]
        out_shapes = [(ROTS, padded, wide_lanes), (8 + padded, LANES)]
        out_specs = [full(shape) for shape in out_shapes]
        scratch = [pltpu.VMEM(corr_shape, f32), wide, pltpu.VMEM((padded, cycles), f32)]
    else:
        out_shapes = [corr_shape, (padded, cycles)]
        out_specs = [corr_block, full((padded, cycles))]
        scratch = [wide]
    return pl.pallas_call(
        functools.partial(correlate_kernel, slots=slots, classes=classes, padded=padded, finish=finish),
        grid_spec=pltpu.PrefetchScalarGridSpec(
            num_scalar_prefetch=1,
            grid=(ROTS // GROUP,),
            in_specs=in_specs,
            out_specs=out_specs,
            scratch_shapes=scratch,
        ),
        out_shape=[jax.ShapeDtypeStruct(shape, f32) for shape in out_shapes],
        compiler_params=pltpu.CompilerParams(vmem_limit_bytes=VMEM_LIMIT),
        name="scores" if finish else "correlate",
    )(*operands)


def back_kernel(weight_ref, scale_ref, offset_ref, out_ref, sum_ref):
    padded = weight_ref.shape[1]
    queries = out_ref.shape[2]
    scale = scale_ref[...]
    for tile in range(weight_ref.shape[2] // LANES):
        lanes = slice(tile * LANES, (tile + 1) * LANES)

        def transform(n, carry):
            start = pl.multiple_of(n * 8, 8)
            rows = pl.ds(start, 8)
            low = pl.ds(padded + start, 8)
            values = [weight_ref[k, rows, lanes] * scale for k in range(ROTS)]
            even_values = [values[0]] + [values[k] + values[ROTS - k] for k in range(1, ROTS // 2)]
            odd_values = [None] + [values[k] - values[ROTS - k] for k in range(1, ROTS // 2)] + [None]
            cos_sums, sin_sums = half_dft(even_values + [values[ROTS // 2]], odd_values)
            for m in range(FOLD):
                sine_part = jnp.zeros_like(scale) if m in (0, FOLD - 1) else sin_sums[m]
                sum_ref[m, rows, lanes] = cos_sums[m]
                sum_ref[m, low, lanes] = sine_part
                if m not in (0, FOLD - 1):
                    sum_ref[ROTS - m, rows, lanes] = cos_sums[m]
                    sum_ref[ROTS - m, low, lanes] = -sine_part
            return carry

        lax.fori_loop(0, padded // 8, transform, 0)

    step_cos, step_sin = cos_sin_of_turns(offset_ref[...] * (1.0 / (ROTS * ANG_STEP)))

    def turn(m, carry):
        cosine, sine_part = carry
        wide_cos, wide_sin = cosine[:, :1], sine_part[:, :1]
        re, im = sum_ref[m, :padded, :], sum_ref[m, padded:, :]
        turned = jnp.concatenate([re * wide_cos - im * wide_sin, re * wide_sin + im * wide_cos], 0)
        out_ref[m] = turned[:, :queries].astype(bf16)
        return cosine * step_cos - sine_part * step_sin, sine_part * step_cos + cosine * step_sin

    lax.fori_loop(0, ROTS, turn, (jnp.ones_like(step_cos), jnp.zeros_like(step_cos)))


def make_back(weights, scale, offsets, queries):
    _, padded, wide_lanes = weights.shape
    return pl.pallas_call(
        back_kernel,
        out_shape=jax.ShapeDtypeStruct((ROTS, 2 * padded, queries), bf16),
        scratch_shapes=[pltpu.VMEM((ROTS, 2 * padded, wide_lanes), f32)],
        compiler_params=pltpu.CompilerParams(vmem_limit_bytes=VMEM_LIMIT),
        name="back",
    )(weights, scale, offsets)


def sums_kernel(slot_ref, back_ref, weighted_ref, offset_ref, *refs, classes, extra):
    added, (out_ref, wide_ref) = refs[:extra], refs[extra:]
    padded = offset_ref.shape[0]
    cycles = wide_ref.shape[1]
    turns = offset_ref[...] * (slot_ref[0].astype(f32) * (1.0 / ANG_STEP))
    cosine, sine_part = cos_sin_of_turns(turns)
    for i in range(GROUP):
        product = jnp.dot(back_ref[i], weighted_ref[0, i], preferred_element_type=f32)
        re = product[:padded, :cycles] - product[padded:, cycles:]
        im = product[:padded, cycles:] + product[padded:, :cycles]
        start = 2 * i * classes
        wide_ref[start : start + classes, :] = (re * cosine - im * sine_part)[:classes]
        wide_ref[start + classes : start + 2 * classes, :] = (re * sine_part + im * cosine)[:classes]
    if len(out_ref.shape) == 2:
        total = wide_ref[...]
        for ref in added:
            total = total + ref[...].astype(f32)
        out_ref[...] = total.astype(out_ref.dtype)
    else:
        total = wide_ref[...]
        for ref in added:
            total = total + ref[...].astype(f32)
        wide_ref[...] = total
        for i in range(GROUP):
            for x in range(2):
                start = (2 * i + x) * classes
                out_ref[i, x] = wide_ref[start : start + classes, :]


def class_sums_of(slot, back, weighted, offsets, added, classes, last=False):
    _, _, queries, double = weighted.shape
    cycles = double // 2
    rows = back.shape[1]
    block = 2 * GROUP * classes
    piece = pl.BlockSpec((block, cycles), lambda g, u: (g, 0))
    if last:
        out_spec = pl.BlockSpec((GROUP, 2, classes, cycles), lambda g, u: (g, 0, 0, 0))
        out_shape = jax.ShapeDtypeStruct((ROTS, 2, classes, cycles), f32)
    else:
        out_spec = piece
        out_shape = jax.ShapeDtypeStruct((ROTS * 2 * classes, cycles), bf16)
    return pl.pallas_call(
        functools.partial(sums_kernel, classes=classes, extra=len(added)),
        grid_spec=pltpu.PrefetchScalarGridSpec(
            num_scalar_prefetch=1,
            grid=(ROTS // GROUP,),
            in_specs=[
                pl.BlockSpec((GROUP, rows, queries), lambda g, u: (g, 0, 0)),
                pl.BlockSpec((1, GROUP, queries, double), lambda g, u: (u[0], g, 0, 0)),
                pl.BlockSpec(offsets.shape, lambda g, u: (0, 0)),
            ]
            + [piece] * len(added),
            out_specs=out_spec,
            scratch_shapes=[pltpu.VMEM((block, cycles), f32)],
        ),
        out_shape=out_shape,
        compiler_params=pltpu.CompilerParams(vmem_limit_bytes=VMEM_LIMIT),
        name="class_sums",
    )(jnp.reshape(slot, (1,)).astype(jnp.int32), back, weighted, offsets, *added)


def pick(index, table):
    return jnp.take(jnp.asarray(table, jnp.int32), index)


def reduce_on_line(back, weighted, offsets, classes):
    index = lax.axis_index("dp")
    line, side = index // 2, index % 2
    order = [pick(line, row) for row in ((3, 3, 0, 0), (2, 2, 1, 1), (1, 0, 3, 2), (0, 1, 2, 3))]

    def sums(target, added, last=False):
        return class_sums_of(target, back, weighted, offsets, added, classes, last)

    def across(piece):
        return lax.ppermute(piece, "dp", [(d, d ^ 1) for d in range(8)])

    def along(piece, pairs):
        return lax.ppermute(piece, "dp", [(2 * a + x, 2 * b + x) for a, b in pairs for x in range(2)])

    crossed = [across(sums(2 * z + 1 - side, ())) for z in order]
    first = along(sums(2 * order[0] + side, (crossed[0],)), ((0, 1), (3, 2)))
    end = (line == 0) | (line == 3)
    chosen = jnp.where(end, order[1], order[0])
    chosen_crossed = jnp.where(end, crossed[1], crossed[0])
    second = sums(2 * chosen + side, (chosen_crossed, first))
    from_ends = along(second, ((0, 1), (3, 2)))
    from_middle = along(second, ((1, 2), (2, 1)))
    third_middle = along(sums(2 * order[1] + side, (crossed[1], from_ends)), ((1, 2), (2, 1)))
    third_pairs = along(
        sums(2 * order[2] + side, (crossed[2], from_middle)), ((0, 1), (1, 0), (2, 3), (3, 2))
    )
    return sums(2 * order[3] + side, (crossed[3], third_middle, third_pairs), last=True)


def local(particles, references, ctf_table, rot_offset, prior_shift, defocus_group):
    count, _, angles, cycles = particles.shape
    own_rows, _, classes, _ = references.shape
    slots = angles // ROTS
    padded = -(-classes // 8) * 8
    group_count = ctf_table.shape[0]
    parts = lax.axis_size("cls")
    devices = lax.axis_size("dp")
    offsets = jnp.broadcast_to(
        jnp.pad(rot_offset, (0, padded - classes)).astype(f32)[:, None], (padded, LANES)
    )

    first = (lax.axis_index("dp") * own_rows).astype(jnp.int32).reshape(1)
    piece = turn_references(first, references, offsets)
    gathered = lax.all_gather(piece, "dp", axis=0, tiled=True).reshape(slots, ROTS * 2 * classes, cycles)
    pieces = [gathered[j] for j in range(slots)]
    slot_of = jnp.arange(slots, dtype=jnp.int32)

    onehot = (defocus_group[:, None] == jnp.arange(group_count, dtype=jnp.int32)[None, :]).astype(f32)
    ctf_rows = jnp.dot(onehot, ctf_table, precision=lax.Precision.HIGHEST)
    weighted = make_spectra(particles, prior_shift, ctf_rows)
    queries = weighted.shape[1]
    weighted = weighted.reshape(slots, ROTS, queries, 2 * cycles)

    half = slots // 2
    corr, power = correlate(slot_of[:half], weighted, pieces[:half], classes)
    weights, stat = correlate(slot_of[half:], weighted, pieces[half:], classes, corr, power, ctf_rows)

    peak = stat[0, :count]
    mass = stat[8 : 8 + classes, :count]
    mine = jnp.stack([peak, jnp.sum(mass, axis=0)])
    place = (jnp.arange(parts) == lax.axis_index("cls")).astype(f32)
    everyone = lax.psum(place[:, None, None] * mine[None], "cls")
    top = jnp.max(everyone[:, 0], axis=0)
    total_mass = jnp.sum(everyone[:, 1] * jnp.exp(everyone[:, 0] - top[None]), axis=0)
    log_evidence = top + jnp.log(total_mass)
    scale = jnp.exp(peak - log_evidence)
    class_posterior = (mass * scale[None, :]).T

    scale_lanes = jnp.broadcast_to(jnp.tile(scale, LANES // count)[None, :], (8, LANES))
    back = make_back(weights, scale_lanes, offsets, queries)
    if devices == 8 and own_rows == ROTS:
        class_sums = reduce_on_line(back, weighted, offsets, classes)
    else:
        sums = [class_sums_of(slot_of[u], back, weighted, offsets, (), classes) for u in range(slots)]
        summed = lax.psum_scatter(jnp.concatenate(sums, 0), "dp", scatter_dimension=0, tiled=True)
        class_sums = summed.astype(f32).reshape(own_rows, 2, classes, cycles)
    return (log_evidence, class_posterior, class_sums)


def solution(mesh):
    placed = (
        P("dp", None, None, None),
        P("dp", None, "cls", None),
        P(),
        P("cls"),
        P("dp", None),
        P("dp"),
    )
    return jax.shard_map(
        local,
        mesh=mesh,
        in_specs=placed,
        out_specs=(P("dp"), P("dp", "cls"), P("dp", None, "cls", None)),
        check_vma=False,
    )
```

time: 376 us -> 316 us (0.84)
  waiting for transfers between devices: 182 us -> 100 us
  starting transfers between devices: 0.08 us -> 13.8 us
  local copies, waits for them, and re-layouts: 8.68 us -> 22.3 us
  other arithmetic: 11.9 us -> 5.36 us
    reduce_scatter x1 -> x0, waiting for transfers between devices: 132 us -> none  [local(): lax.psum_scatter(sums.reshape(slots * ROTS * 2 * classes, cycles), 'dp',...]
    ppermute x0 -> x9, waiting for transfers between devices: none -> 52.7 us  [the longest x5 30.3 us: along(): lax.ppermute(piece, 'dp', [(2 * a + x, 2 * b + x) for a, b in pairs for x...]
    ppermute x0 -> x9, starting transfers between devices: none -> 13.8 us  [the longest x5 10.6 us: along(): lax.ppermute(piece, 'dp', [(2 * a + x, 2 * b + x) for a, b in pairs for x...]
    unnamed x12 -> x36, local copies, waits for them, and re-layouts: 2.89 us -> 11.2 us
    another operation x6 -> x1, other arithmetic: 7.56 us -> 0.01 us  [local(): mine = jnp.stack([peak, jnp.sum(mass, axis=0)])]
    slice x1 -> x3, local copies, waits for them, and re-layouts: 0.8 us -> 7.47 us  [the longest x1 6.21 us: local(): pieces = [gathered[j] for j in range(slots)]]
    pallas_call x3 -> x13, Pallas kernels: 88.2 us -> 89.6 us  [the longest x9 47.4 us: class_sums_of(): pl.pallas_call(functools.partial(sums_kernel, classes=classes, extra=len(...]
  transfers between devices with their start and end apart: 2 -> 10, of which waited for: 2 -> 7; matrix products, arithmetic and copies ran while one was open for 1% -> 2% of each run, Pallas kernels for 16% -> 30%
where the time goes in v2:
time: 316 us; the launch traced here: 314 us
  Pallas kernels  149 us (47%)
  waiting for transfers between devices  100 us (32%)
  local copies, waits for them, and re-layouts  22.3 us (7%)
  between operations  16.2 us (5%)
  starting transfers between devices  13.8 us (4%)
  blocking collectives  6.07 us (2%)
  other arithmetic  5.36 us (2%)
    pallas_call x1, Pallas kernels, make_spectra(): pl.pallas_call(spectra_kernel, grid=(steps,), in_specs=[pl.BlockSpec(memo...  59.6 us
    all_gather x1, waiting for transfers between devices, local(): lax.all_gather(piece, 'dp', axis=0, tiled=True)  47.8 us
    pallas_call x9, Pallas kernels, class_sums_of(): pl.pallas_call(functools.partial(sums_kernel, classes=classes, extra=len(...  47.4 us
    pallas_call x2, Pallas kernels, correlate(): pl.pallas_call(functools.partial(correlate_kernel, slots=slots, classes=c...  30.3 us
    ppermute x5, waiting for transfers between devices, along(): lax.ppermute(piece, 'dp', [(2 * a + x, 2 * b + x) for a, b in pairs for x...  30.3 us
    ppermute x4, waiting for transfers between devices, across(): return lax.ppermute(piece, 'dp', [(d, d ^ 1) for d in range(8)])  22.4 us
    unnamed x36, local copies, waits for them, and re-layouts  11.2 us
    ppermute x5, starting transfers between devices, along(): lax.ppermute(piece, 'dp', [(2 * a + x, 2 * b + x) for a, b in pairs for x...  10.6 us
  transfers between devices with their start and end apart: 10, of which 7 were waited for; matrix products, arithmetic and copies ran while one was open for 2% of the time, Pallas kernels for 30%

profile of v2, /device:TPU:8, one launch (start us, length us, event | category | flops | bytes accessed | tf_op | source)
XLA Modules:
  0.0 314.2 jit_solution(13010565236201335470)
XLA Ops:
  7.9 2.3 copy.21.references_ref
  10.9 4.2 %turn_references.1 = bf16[3600,128]{1,0:T(8,128)(2,1)} custom-call(s32[1]{0:T(128)} %bitcast.1.first_ref, bf16[36,2,50,128]{3,2,1,0:T(8,128)(2,1)} %copy.21.references_ref, f32[56,128]{1,0:T(8,128)} %broadcast_in_dim.12.offset_ref), custom_call_target="tpu_custom_call" | custom-call | tf_op jit(solution)/shard_map/turn_references/pallas_call | solution.py:206
  19.7 59.6 %spectra.1 = bf16[288,208,256]{2,1,0:T(8,128)(2,1)} custom-call(s32[8,2]{1,0:T(8,128)} %copy.20.shift_ref, bf16[8,2,288,128]{3,2,1,0:T(8,128)(2,1)} %part_ref.1, f32[8,128]{1,0:T(8,128)} %fusion.ctf_ref.refs_10_, bf16[576,576]{1,0:T(8,128)(2,1)} %constant.91.clone.table_ref, f32[2,288,128]{2,1,0:T(8,128)} %constant.92.clone.turns_ref, ...), custom_call_target="tpu_custom_call" | custom-call | tf_op jit(solution)/shard_map/spectra/pallas_call | solution.py:127
  79.2 47.8 %all-gather.2.cloned.1.call-done = bf16[28800,128]{1,0:T(8,128)(2,1)} async-done(((bf16[3600,128]{1,0:T(8,128)(2,1)}), bf16[28800,128]{1,0:T(8,128)(2,1)}) %all-gather.2.cloned.1.call-update) | async-done | bytes 7372816 | tf_op jit(solution)/shard_map/all_gather | solution.py:538
  127.0 6.2 %fusion.7 = (bf16[3600,128]{1,0:T(8,128)(2,1)}, bf16[3600,128]{1,0:T(8,128)(2,1)}, bf16[3600,128]{1,0:T(8,128)(2,1)}, bf16[3600,128]{1,0:T(8,128)(2,1)}, bf16[36...) fusion(bf16[28800,128]{1,0:T(8,128)(2,1)} %all-gather.2.cloned.1.call-done), kind=kLoop, calls=%fused_computation.20 | loop fusion | bytes 14745600 | tf_op jit(solution)/shard_map/slice | solution.py:539
  133.7 12.2 %correlate.1 = (f32[36,112,256]{2,1,0:T(8,128)}, f32[56,128]{1,0:T(8,128)}) custom-call(s32[4]{0:T(128)} %bitcast.60, bf16[8,36,208,256]{3,2,1,0:T(8,128)(2,1)} %bitcast.42, bf16[8,36,208,256]{3,2,1,0:T(8,128)(2,1)} %bitcast.43, bf16[8,36,208,256]{3,2,1,0:T(8,128)(2,1)} %bitcast.44, bf16[8,36,208,256]{3,2,1,0:T(8,128)(2,1)} %bitcast.45, ...), custom_call_target="tpu_custom_call" | custom-call | tf_op jit(solution)/shard_map/correlate/pallas_call | solution.py:365
  145.9 18.1 %scores.1 = (f32[36,56,256]{2,1,0:T(8,128)}, f32[64,128]{1,0:T(8,128)}) custom-call(s32[4]{0:T(128)} %slice.51.slot_ref, bf16[8,36,208,256]{3,2,1,0:T(8,128)(2,1)} %bitcast.46, bf16[8,36,208,256]{3,2,1,0:T(8,128)(2,1)} %bitcast.47, bf16[8,36,208,256]{3,2,1,0:T(8,128)(2,1)} %bitcast.48, bf16[8,36,208,256]{3,2,1,0:T(8,128)(2,1)} %bitcast.49, ...), custom_call_target="tpu_custom_call" | custom-call | tf_op jit(solution)/shard_map/scores/pallas_call | solution.py:365
  165.6 6.1 %psum.7 = f32[4,2,8]{2,0,1:T(4,128)S(1)} all-reduce(f32[4,2,8]{2,0,1:T(4,128)S(1)} %broadcast_multiply_fusion), channel_id=1, replica_groups=mesh['dp'=8,'cls'=4] {'cls'}, use_global_device_ids=true, to_apply=%region_1.2 | all-reduce | flops 64 | bytes 512 | tf_op jit(solution)/shard_map/psum | solution.py:556
  171.7 1.2 fusion.6
  173.6 7.7 %back.1.back_ref = bf16[36,112,208]{2,1,0:T(8,128)(2,1)} custom-call(f32[36,56,256]{2,1,0:T(8,128)} %get-tuple-element.10.weight_ref, f32[8,128]{1,0:T(8,128)} %broadcast_in_dim.29.scale_ref, f32[56,128]{1,0:T(8,128)} %broadcast_in_dim.12.offset_ref), custom_call_target="tpu_custom_call" | custom-call | tf_op jit(solution)/shard_map/back/pallas_call | solution.py:421
  181.3 4.8 %class_sums.11 = bf16[3600,128]{1,0:T(8,128)(2,1)} custom-call(s32[1]{0:T(128)} %bitcast.18.slot_ref, bf16[36,112,208]{2,1,0:T(8,128)(2,1)} %back.1.back_ref, bf16[8,36,208,256]{3,2,1,0:T(8,128)(2,1)} %bitcast.50, f32[56,128]{1,0:T(8,128)} %broadcast_in_dim.12.offset_ref), custom_call_target="tpu_custom_call" | custom-call | tf_op jit(solution)/shard_map/class_sums/pallas_call | solution.py:471
  186.7 4.8 %class_sums.10 = bf16[3600,128]{1,0:T(8,128)(2,1)} custom-call(s32[1]{0:T(128)} %bitcast.15.slot_ref, bf16[36,112,208]{2,1,0:T(8,128)(2,1)} %back.1.back_ref, bf16[8,36,208,256]{3,2,1,0:T(8,128)(2,1)} %bitcast.51, f32[56,128]{1,0:T(8,128)} %broadcast_in_dim.12.offset_ref), custom_call_target="tpu_custom_call" | custom-call | tf_op jit(solution)/shard_map/class_sums/pallas_call | solution.py:471
  191.5 1.5 collective-permute-start.1
  194.2 4.8 %class_sums.15 = bf16[3600,128]{1,0:T(8,128)(2,1)} custom-call(s32[1]{0:T(128)} %bitcast.22.slot_ref, bf16[36,112,208]{2,1,0:T(8,128)(2,1)} %back.1.back_ref, bf16[8,36,208,256]{3,2,1,0:T(8,128)(2,1)} %bitcast.52, f32[56,128]{1,0:T(8,128)} %broadcast_in_dim.12.offset_ref), custom_call_target="tpu_custom_call" | custom-call | tf_op jit(solution)/shard_map/class_sums/pallas_call | solution.py:471
  199.6 10.1 %collective-permute-done.2.refs_0_ = bf16[3600,128]{1,0:T(8,128)(2,1)S(1)} collective-permute-done((bf16[3600,128]{1,0:T(8,128)(2,1)}, bf16[3600,128]{1,0:T(8,128)(2,1)S(1)}, u32[]{:S(2)}, u32[]{:S(2)}) %collective-permute-start.2) | collective-permute-done | bytes 921632 | tf_op jit(solution)/shard_map/ppermute | solution.py:504
  210.7 5.2 %class_sums.12 = bf16[3600,128]{1,0:T(8,128)(2,1)} custom-call(s32[1]{0:T(128)} %bitcast.19.slot_ref, bf16[36,112,208]{2,1,0:T(8,128)(2,1)} %back.1.back_ref, bf16[8,36,208,256]{3,2,1,0:T(8,128)(2,1)} %bitcast.53, f32[56,128]{1,0:T(8,128)} %broadcast_in_dim.12.offset_ref, bf16[3600,128]{1,0:T(8,128)(2,1)} %copy-done.2), custom_call_target="tpu_custom_call" | custom-call | tf_op jit(solution)/shard_map/class_sums/pallas_call | solution.py:471
  215.9 1.3 collective-permute-start.3
  217.2 12.3 %collective-permute-done.1.refs_0_ = bf16[3600,128]{1,0:T(8,128)(2,1)S(1)} collective-permute-done((bf16[3600,128]{1,0:T(8,128)(2,1)}, bf16[3600,128]{1,0:T(8,128)(2,1)S(1)}, u32[]{:S(2)}, u32[]{:S(2)}) %collective-permute-start.1) | collective-permute-done | bytes 921632 | tf_op jit(solution)/shard_map/ppermute | solution.py:504
  229.5 2.6 broadcast_select_fusion.refs_0_
  232.1 5.1 %collective-permute-done.3.refs_1_ = bf16[3600,128]{1,0:T(8,128)(2,1)S(1)} collective-permute-done((bf16[3600,128]{1,0:T(8,128)(2,1)}, bf16[3600,128]{1,0:T(8,128)(2,1)S(1)}, u32[]{:S(2)}, u32[]{:S(2)}) %collective-permute-start.3) | collective-permute-done | bytes 921632 | tf_op jit(solution)/shard_map/ppermute | solution.py:507
  238.2 5.5 %class_sums.13 = bf16[3600,128]{1,0:T(8,128)(2,1)} custom-call(s32[1]{0:T(128)} %bitcast.17.slot_ref, bf16[36,112,208]{2,1,0:T(8,128)(2,1)} %back.1.back_ref, bf16[8,36,208,256]{3,2,1,0:T(8,128)(2,1)} %bitcast.54, f32[56,128]{1,0:T(8,128)} %broadcast_in_dim.12.offset_ref, bf16[3600,128]{1,0:T(8,128)(2,1)} %broadcast_select_fusion.refs_0_, ...), custom_call_target="tpu_custom_call" | custom-call | tf_op jit(solution)/shard_map/class_sums/pallas_call | solution.py:471
  243.6 4.2 %collective-permute-start.7 = (bf16[3600,128]{1,0:T(8,128)(2,1)}, bf16[3600,128]{1,0:T(8,128)(2,1)S(1)}, u32[]{:S(2)}, u32[]{:S(2)}) collective-permute-start(bf16[3600,128]{1,0:T(8,128)(2,1)} %class_sums.13), channel_id=1, source_target_pairs={{8,16},{12,20},{16,8},{20,12},{9,17},{13,21},{17,9},{21,13},{10,18... | collective-permute-start | bytes 2764808 | tf_op jit(solution)/shard_map/ppermute | solution.py:507
  247.8 1.3 collective-permute-start.4
  249.2 4.8 %class_sums.9 = bf16[3600,128]{1,0:T(8,128)(2,1)} custom-call(s32[1]{0:T(128)} %bitcast.12.slot_ref, bf16[36,112,208]{2,1,0:T(8,128)(2,1)} %back.1.back_ref, bf16[8,36,208,256]{3,2,1,0:T(8,128)(2,1)} %bitcast.55, f32[56,128]{1,0:T(8,128)} %broadcast_in_dim.12.offset_ref), custom_call_target="tpu_custom_call" | custom-call | tf_op jit(solution)/shard_map/class_sums/pallas_call | solution.py:471
  254.6 9.9 %collective-permute-done.7.refs_1_ = bf16[3600,128]{1,0:T(8,128)(2,1)S(1)} collective-permute-done((bf16[3600,128]{1,0:T(8,128)(2,1)}, bf16[3600,128]{1,0:T(8,128)(2,1)S(1)}, u32[]{:S(2)}, u32[]{:S(2)}) %collective-permute-start.7) | collective-permute-done | bytes 921632 | tf_op jit(solution)/shard_map/ppermute | solution.py:507
  265.4 5.5 %class_sums.16 = bf16[3600,128]{1,0:T(8,128)(2,1)} custom-call(s32[1]{0:T(128)} %bitcast.21.slot_ref, bf16[36,112,208]{2,1,0:T(8,128)(2,1)} %back.1.back_ref, bf16[8,36,208,256]{3,2,1,0:T(8,128)(2,1)} %bitcast.56, f32[56,128]{1,0:T(8,128)} %broadcast_in_dim.12.offset_ref, bf16[3600,128]{1,0:T(8,128)(2,1)} %copy-done.7, bf16[3600,128]{1,0:T(8,128)(2,1)} %copy-done.8), custom_call_target="tpu_custom_call" | custom-call | tf_op jit(solution)/shard_map/class_sums/pallas_call | solution.py:471
  270.9 5.5 %class_sums.14 = bf16[3600,128]{1,0:T(8,128)(2,1)} custom-call(s32[1]{0:T(128)} %bitcast.14.slot_ref, bf16[36,112,208]{2,1,0:T(8,128)(2,1)} %back.1.back_ref, bf16[8,36,208,256]{3,2,1,0:T(8,128)(2,1)} %bitcast.57, f32[56,128]{1,0:T(8,128)} %broadcast_in_dim.12.offset_ref, bf16[3600,128]{1,0:T(8,128)(2,1)} %copy-done.3, ...), custom_call_target="tpu_custom_call" | custom-call | tf_op jit(solution)/shard_map/class_sums/pallas_call | solution.py:471
  276.4 3.8 %collective-permute-start.5 = (bf16[3600,128]{1,0:T(8,128)(2,1)}, bf16[3600,128]{1,0:T(8,128)(2,1)S(1)}, u32[]{:S(2)}, u32[]{:S(2)}) collective-permute-start(bf16[3600,128]{1,0:T(8,128)(2,1)} %class_sums.14), channel_id=1, source_target_pairs={{8,16},{12,20},{16,8},{20,12},{9,17},{13,21},{17,9},{21,13},{10,18... | collective-permute-start | bytes 2764808 | tf_op jit(solution)/shard_map/ppermute | solution.py:507
  281.0 7.8 %collective-permute-done.8.refs_2_ = bf16[3600,128]{1,0:T(8,128)(2,1)S(1)} collective-permute-done((bf16[3600,128]{1,0:T(8,128)(2,1)}, bf16[3600,128]{1,0:T(8,128)(2,1)S(1)}, u32[]{:S(2)}, u32[]{:S(2)}) %collective-permute-start.8) | collective-permute-done | bytes 921632 | tf_op jit(solution)/shard_map/ppermute | solution.py:507
  288.8 7.4 %collective-permute-done.5.refs_1_ = bf16[3600,128]{1,0:T(8,128)(2,1)S(1)} collective-permute-done((bf16[3600,128]{1,0:T(8,128)(2,1)}, bf16[3600,128]{1,0:T(8,128)(2,1)S(1)}, u32[]{:S(2)}, u32[]{:S(2)}) %collective-permute-start.5) | collective-permute-done | bytes 921632 | tf_op jit(solution)/shard_map/ppermute | solution.py:507
  297.1 6.4 %class_sums.17 = f32[36,2,50,128]{3,2,1,0:T(8,128)} custom-call(s32[1]{0:T(128)} %bitcast.11.slot_ref, bf16[36,112,208]{2,1,0:T(8,128)(2,1)} %back.1.back_ref, bf16[8,36,208,256]{3,2,1,0:T(8,128)(2,1)} %bitcast.58, f32[56,128]{1,0:T(8,128)} %broadcast_in_dim.12.offset_ref, bf16[3600,128]{1,0:T(8,128)(2,1)} %copy-done.4, bf16[3600,128]{1,0:T(8,128)(2,1)} %copy-done.6, ...), custom_call_target="tpu_custom_call" | custom-call | tf_op jit(solution)/shard_map/class_sums/pallas_call | solution.py:471
  303.6 3.8 %copy.23 = f32[36,2,50,128]{3,1,2,0:T(2,128)} copy(f32[36,2,50,128]{3,2,1,0:T(8,128)} %class_sums.17) | data formatting | bytes 3686400
  (63 shorter events, 14.2 us)
Async XLA Ops:
  7.2 11.7 %copy-start = (f32[16,128]{1,0:T(8,128)S(1)}, f32[16,128]{1,0:T(8,128)}, u32[]{:S(2)}) copy-start(f32[16,128]{1,0:T(8,128)} %param.15) | copy-start | bytes 24580
  7.2 9.2 %copy-start.15 = (s32[4]{0:T(128)S(1)}, s32[4]{0:T(128)}, u32[]{:S(2)}) copy-start(s32[4]{0:T(128)} %constant.94.clone..sunk.2) | copy-start | bytes 52
  7.2 10.4 %copy-start.14 = (s32[4]{0:T(128)S(1)}, s32[4]{0:T(128)}, u32[]{:S(2)}) copy-start(s32[4]{0:T(128)} %constant.95.clone..sunk.2) | copy-start | bytes 52
  7.2 7.9 %copy-start.11 = (s32[8,2]{0,1:T(2,128)S(1)}, s32[8,2]{0,1:T(2,128)}, u32[]{:S(2)}) copy-start(s32[8,2]{0,1:T(2,128)} %param.17) | copy-start | bytes 196
  7.2 11.6 %copy-start.12 = (s32[8]{0:T(128)S(1)}, s32[8]{0:T(128)}, u32[]{:S(2)}) copy-start(s32[8]{0:T(128)} %param.18) | copy-start | bytes 100
  7.2 119.8 %all-gather.2.cloned.1.call-start = ((), (), s32[]{:S(2)}) async-start(), calls=%async_computation | async-start | bytes 8294400 | tf_op jit(solution)/shard_map/all_gather | solution.py:538
  186.1 23.6 %collective-permute-start.2 = (bf16[3600,128]{1,0:T(8,128)(2,1)}, bf16[3600,128]{1,0:T(8,128)(2,1)S(1)}, u32[]{:S(2)}, u32[]{:S(2)}) collective-permute-start(bf16[3600,128]{1,0:T(8,128)(2,1)} %class_sums.11), channel_id=1, source_target_pairs={{0,4},{4,0},{8,12},{12,8},{16,20},{20,16},{24,28},{28,24},{1,5},{5... | collective-permute-start | bytes 2764808 | tf_op jit(solution)/shard_map/ppermute | solution.py:504
  186.7 6.3 %copy-start.13 = (s32[4]{0:T(128)S(1)}, s32[4]{0:T(128)}, u32[]{:S(2)}) copy-start(s32[4]{0:T(128)} %constant.96.clone..sunk.2) | copy-start | bytes 52
  191.5 38.0 %collective-permute-start.1 = (bf16[3600,128]{1,0:T(8,128)(2,1)}, bf16[3600,128]{1,0:T(8,128)(2,1)S(1)}, u32[]{:S(2)}, u32[]{:S(2)}) collective-permute-start(bf16[3600,128]{1,0:T(8,128)(2,1)} %class_sums.10), channel_id=1, source_target_pairs={{0,4},{4,0},{8,12},{12,8},{16,20},{20,16},{24,28},{28,24},{1,5},{5... | collective-permute-start | bytes 2764808 | tf_op jit(solution)/shard_map/ppermute | solution.py:504
  199.0 55.6 %collective-permute-start.6 = (bf16[3600,128]{1,0:T(8,128)(2,1)}, bf16[3600,128]{1,0:T(8,128)(2,1)S(1)}, u32[]{:S(2)}, u32[]{:S(2)}) collective-permute-start(bf16[3600,128]{1,0:T(8,128)(2,1)} %class_sums.15), channel_id=1, source_target_pairs={{0,4},{4,0},{8,12},{12,8},{16,20},{20,16},{24,28},{28,24},{1,5},{5... | collective-permute-start | bytes 2764808 | tf_op jit(solution)/shard_map/ppermute | solution.py:504
  209.7 1.0 copy-start.2
  215.9 21.3 %collective-permute-start.3 = (bf16[3600,128]{1,0:T(8,128)(2,1)}, bf16[3600,128]{1,0:T(8,128)(2,1)S(1)}, u32[]{:S(2)}, u32[]{:S(2)}) collective-permute-start(bf16[3600,128]{1,0:T(8,128)(2,1)} %class_sums.12), channel_id=1, source_target_pairs={{0,8},{4,12},{24,16},{28,20},{1,9},{5,13},{25,17},{29,21},{2,10},{... | collective-permute-start | bytes 2764808 | tf_op jit(solution)/shard_map/ppermute | solution.py:507
  229.5 14.2 %copy-start.3 = (bf16[3600,128]{1,0:T(8,128)(2,1)}, bf16[3600,128]{1,0:T(8,128)(2,1)S(1)}, u32[]{:S(2)}) copy-start(bf16[3600,128]{1,0:T(8,128)(2,1)S(1)} %collective-permute-done.1.refs_0_) | copy-start | bytes 2764804
  237.2 1.0 copy-start.9
  243.6 20.9 %collective-permute-start.7 = (bf16[3600,128]{1,0:T(8,128)(2,1)}, bf16[3600,128]{1,0:T(8,128)(2,1)S(1)}, u32[]{:S(2)}, u32[]{:S(2)}) collective-permute-start(bf16[3600,128]{1,0:T(8,128)(2,1)} %class_sums.13), channel_id=1, source_target_pairs={{8,16},{12,20},{16,8},{20,12},{9,17},{13,21},{17,9},{21,13},{10,18... | collective-permute-start | bytes 2764808 | tf_op jit(solution)/shard_map/ppermute | solution.py:507
  247.8 23.1 %collective-permute-start.4 = (bf16[3600,128]{1,0:T(8,128)(2,1)}, bf16[3600,128]{1,0:T(8,128)(2,1)}, u32[]{:S(2)}, u32[]{:S(2)}) collective-permute-start(bf16[3600,128]{1,0:T(8,128)(2,1)} %class_sums.13), channel_id=1, source_target_pairs={{0,8},{4,12},{24,16},{28,20},{1,9},{5,13},{25,17},{29,21},{2,10},{... | collective-permute-start | bytes 2764808 | tf_op jit(solution)/shard_map/ppermute | solution.py:507
  254.0 27.0 %collective-permute-start = (bf16[3600,128]{1,0:T(8,128)(2,1)}, bf16[3600,128]{1,0:T(8,128)(2,1)S(1)}, u32[]{:S(2)}, u32[]{:S(2)}) collective-permute-start(bf16[3600,128]{1,0:T(8,128)(2,1)} %class_sums.9), channel_id=1, source_target_pairs={{0,4},{4,0},{8,12},{12,8},{16,20},{20,16},{24,28},{28,24},{1,5},{5... | collective-permute-start | bytes 2764808 | tf_op jit(solution)/shard_map/ppermute | solution.py:504
  254.6 9.9 %copy-start.7 = (bf16[3600,128]{1,0:T(8,128)(2,1)}, bf16[3600,128]{1,0:T(8,128)(2,1)S(1)}, u32[]{:S(2)}) copy-start(bf16[3600,128]{1,0:T(8,128)(2,1)S(1)} %collective-permute-done.6.refs_0_) | copy-start | bytes 2764804
  264.5 0.9 copy-start.8
  270.9 17.9 %collective-permute-start.8 = (bf16[3600,128]{1,0:T(8,128)(2,1)}, bf16[3600,128]{1,0:T(8,128)(2,1)S(1)}, u32[]{:S(2)}, u32[]{:S(2)}) collective-permute-start(bf16[3600,128]{1,0:T(8,128)(2,1)} %class_sums.16), channel_id=1, source_target_pairs={{0,8},{4,12},{8,0},{12,4},{16,24},{20,28},{24,16},{28,20},{1,9},{5... | collective-permute-start | bytes 2764808 | tf_op jit(solution)/shard_map/ppermute | solution.py:507
  270.9 9.3 %copy-start.10 = (f32[64,128]{1,0:T(8,128)S(1)}, f32[64,128]{1,0:T(8,128)}, u32[]{:S(2)}) copy-start(f32[64,128]{1,0:T(8,128)} %get-tuple-element.9) | copy-start | bytes 98308
  276.4 19.8 %collective-permute-start.5 = (bf16[3600,128]{1,0:T(8,128)(2,1)}, bf16[3600,128]{1,0:T(8,128)(2,1)S(1)}, u32[]{:S(2)}, u32[]{:S(2)}) collective-permute-start(bf16[3600,128]{1,0:T(8,128)(2,1)} %class_sums.14), channel_id=1, source_target_pairs={{8,16},{12,20},{16,8},{20,12},{9,17},{13,21},{17,9},{21,13},{10,18... | collective-permute-start | bytes 2764808 | tf_op jit(solution)/shard_map/ppermute | solution.py:507
  281.0 15.2 %copy-start.4 = (bf16[3600,128]{1,0:T(8,128)(2,1)}, bf16[3600,128]{1,0:T(8,128)(2,1)S(1)}, u32[]{:S(2)}) copy-start(bf16[3600,128]{1,0:T(8,128)(2,1)S(1)} %collective-permute-done.refs_0_) | copy-start | bytes 2764804
  288.8 7.4 %copy-start.5 = (bf16[3600,128]{1,0:T(8,128)(2,1)}, bf16[3600,128]{1,0:T(8,128)(2,1)S(1)}, u32[]{:S(2)}) copy-start(bf16[3600,128]{1,0:T(8,128)(2,1)S(1)} %collective-permute-done.8.refs_2_) | copy-start | bytes 2764804
  296.2 0.9 copy-start.6
  297.1 10.2 %copy-start.1 = (f32[16,128]{1,0:T(8,128)S(1)}, f32[16,128]{1,0:T(8,128)}, u32[]{:S(2)}) copy-start(f32[16,128]{1,0:T(8,128)} %param.15) | copy-start | bytes 24580
Sparse Core Ops, SparseCore 0:
  15.2 111.7 all-gather.1

commit v3 on v2

v3 whole, which is shorter than its diff:
```python
import functools
import math

import jax
import jax.numpy as jnp
import ml_dtypes
import numpy as np
from jax import lax
from jax.experimental import pallas as pl
from jax.experimental.pallas import tpu as pltpu
from jax.sharding import PartitionSpec as P

ROTS = 36
ANG_STEP = 8
SHIFT_SIDE = 5
SHIFTS = SHIFT_SIDE * SHIFT_SIDE
LANES = 128
GROUP = 12
ROWS = 16
FOLD = ROTS // 2 + 1

two_pi = 2.0 * math.pi
f32 = jnp.float32
bf16 = jnp.bfloat16
VMEM_LIMIT = 56 * 1024 * 1024


def fourier_rows(angles):
    index_grid = np.arange(angles)
    radians = (index_grid[:, None] * index_grid[None, :] % angles) * (two_pi / angles)
    cosine, sine_part = np.cos(radians), np.sin(radians)
    table_full = np.concatenate(
        [np.concatenate([cosine, sine_part], 1), np.concatenate([-sine_part, cosine], 1)], 0
    )
    return table_full.astype(np.float32).astype(ml_dtypes.bfloat16)


def shift_tables(angles, cycles):
    theta = np.arange(angles) * (two_pi / angles)
    radius = (np.arange(cycles) + 1) / (2.0 * cycles)
    turns = np.stack([np.cos(theta), np.sin(theta)])[:, :, None] * radius
    steps = np.arange(SHIFT_SIDE) - SHIFT_SIDE // 2
    phase = two_pi * turns[:, None] * steps[None, :, None, None]
    factors = np.stack([np.cos(phase), -np.sin(phase)], 2)
    return turns.astype(np.float32), factors.astype(np.float32)


def cos_sin_of_turns(turns):
    frac = turns - jnp.floor(turns + 0.5)
    w = frac * two_pi
    w2 = w * w
    cosine = jnp.full_like(w, 1.0 / math.factorial(16))
    for n in range(14, -1, -2):
        cosine = cosine * w2 + (-1.0) ** (n // 2) / math.factorial(n)
    sine_part = jnp.full_like(w, 1.0 / math.factorial(17))
    for n in range(15, 0, -2):
        sine_part = sine_part * w2 + (-1.0) ** (n // 2) / math.factorial(n)
    return cosine, sine_part * w


def base_kernel(shift_ref, part_ref, turns_ref, base_ref):
    p = pl.program_id(0)
    sx = shift_ref[0, p].astype(f32)
    sy = shift_ref[1, p].astype(f32)
    chunk = 32

    def turn(n, carry):
        rows = pl.ds(pl.multiple_of(n * chunk, chunk), chunk)
        cosine, sine_part = cos_sin_of_turns(sx * turns_ref[0, rows, :] + sy * turns_ref[1, rows, :])
        re = part_ref[0, 0, rows, :].astype(f32)
        im = part_ref[0, 1, rows, :].astype(f32)
        base_ref[0, 0, rows, :] = re * cosine + im * sine_part
        base_ref[0, 1, rows, :] = im * cosine - re * sine_part
        return carry

    lax.fori_loop(0, part_ref.shape[2] // chunk, turn, 0)


def make_base(particles, prior_shift):
    count, _, angles, cycles = particles.shape
    turns, _ = shift_tables(angles, cycles)
    image = pl.BlockSpec((1, 2, angles, cycles), lambda p: (p, 0, 0, 0))
    return pl.pallas_call(
        base_kernel,
        grid=(count,),
        in_specs=[
            pl.BlockSpec(memory_space=pltpu.SMEM),
            image,
            pl.BlockSpec(turns.shape, lambda p: (0, 0, 0)),
        ],
        out_specs=image,
        out_shape=jax.ShapeDtypeStruct(particles.shape, f32),
        compiler_params=pltpu.CompilerParams(vmem_limit_bytes=VMEM_LIMIT),
        name="centre",
    )(prior_shift.T, particles, turns)


def spectra_kernel(base_ref, ctf_ref, table_ref, *refs, per_step):
    factor_refs, refs = refs[: 2 * per_step], refs[2 * per_step :]
    out_ref, data_ref, re_ref, im_ref = refs[-4:]
    count, _, angles, cycles = base_ref.shape
    chunk = 32

    for g in range(per_step):
        x_ref, y_ref = factor_refs[2 * g], factor_refs[2 * g + 1]

        def shift(n, carry):
            rows = pl.ds(pl.multiple_of(n * chunk, chunk), chunk)
            low = pl.ds(pl.multiple_of(angles + n * chunk, chunk), chunk)
            xr, xi = x_ref[0, 0, 0, rows, :], x_ref[0, 0, 1, rows, :]
            yr, yi = y_ref[0, 0, 0, rows, :], y_ref[0, 0, 1, rows, :]
            tr = xr * yr - xi * yi
            ti = xr * yi + xi * yr
            for p in range(count):
                gr, gi = base_ref[p, 0, rows, :], base_ref[p, 1, rows, :]
                lanes = pl.ds((g * count + p) * cycles, cycles)
                data_ref[rows, lanes] = (gr * tr - gi * ti).astype(bf16)
                data_ref[low, lanes] = (gr * ti + gi * tr).astype(bf16)
            return carry

        lax.fori_loop(0, angles // chunk, shift, 0)

    for n in range(ROWS // 2):
        spectrum = jnp.dot(
            table_ref[...], data_ref[:, n * 2 * cycles : (n + 1) * 2 * cycles], preferred_element_type=f32
        )
        for j in range(2):
            row = 2 * n + j
            ctf_row = ctf_ref[row % count, :][None, :]
            part = spectrum[:, j * cycles : (j + 1) * cycles] * ctf_row
            re_ref[pl.ds(row, angles, stride=ROWS), :] = part[:angles]
            im_ref[pl.ds(row, angles, stride=ROWS), :] = part[angles:]
    out_ref[:, :, :cycles] = re_ref[...].reshape(angles, ROWS, cycles).astype(bf16)
    out_ref[:, :, cycles:] = im_ref[...].reshape(angles, ROWS, cycles).astype(bf16)


def spectra_steps(count):
    per_step = ROWS // count if count < ROWS else 1
    return per_step, -(-SHIFTS // per_step)


def make_spectra(base, ctf_rows, first, last, before=None, after=()):
    count, _, angles, cycles = base.shape
    per_step, steps = spectra_steps(count)
    _, factors = shift_tables(angles, cycles)
    full = lambda shape: pl.BlockSpec(shape, lambda i: (0,) * len(shape))

    def factor_spec(g, axis):
        def place(i):
            s = jnp.minimum((i + first) * per_step + g, SHIFTS - 1)
            a = lax.div(s, jnp.int32(SHIFT_SIDE))
            return (axis, s - a * SHIFT_SIDE if axis else a, 0, 0, 0)

        return pl.BlockSpec((1, 1, 2, angles, cycles), place)

    untouched = ([] if before is None else [before]) + list(after)
    in_specs = (
        [full(base.shape), full(ctf_rows.shape), full((2 * angles, 2 * angles))]
        + [factor_spec(g, axis) for g in range(per_step) for axis in range(2)]
        + [pl.BlockSpec(memory_space=pl.ANY)] * len(untouched)
    )
    return pl.pallas_call(
        functools.partial(spectra_kernel, per_step=per_step),
        grid=(last - first,),
        in_specs=in_specs,
        out_specs=pl.BlockSpec((angles, ROWS, 2 * cycles), lambda i: (0, i + first, 0)),
        out_shape=jax.ShapeDtypeStruct((angles, steps * ROWS, 2 * cycles), bf16),
        scratch_shapes=[
            pltpu.VMEM((2 * angles, ROWS * cycles), bf16),
            pltpu.VMEM((angles * ROWS, cycles), f32),
            pltpu.VMEM((angles * ROWS, cycles), f32),
        ],
        input_output_aliases={} if before is None else {3 + 2 * per_step: 0},
        compiler_params=pltpu.CompilerParams(vmem_limit_bytes=VMEM_LIMIT),
        name="spectra",
    )(base, ctf_rows, fourier_rows(angles), *[factors] * (2 * per_step), *untouched)


def half_dft(even_values, odd_values):
    half = FOLD // 2
    cos_sums, sin_sums = [None] * FOLD, [None] * FOLD

    def weighted_sum(values, k, table, start):
        total = None
        for m in range(start, FOLD, 2):
            weight = float(table((k * m % ROTS) * two_pi / ROTS))
            if values[m] is None or abs(weight) < 1e-9:
                continue
            if abs(abs(weight) - 1.0) < 1e-9:
                term = values[m] if weight > 0 else -values[m]
            else:
                term = values[m] * weight
            total = term if total is None else total + term
        return jnp.zeros_like(values[1]) if total is None else total

    for k in range(half + 1):
        even = weighted_sum(even_values, k, math.cos, 0)
        odd = weighted_sum(even_values, k, math.cos, 1)
        cos_sums[k] = even + odd
        if k != half:
            cos_sums[FOLD - 1 - k] = even - odd
        if k:
            even = weighted_sum(odd_values, k, math.sin, 0)
            odd = weighted_sum(odd_values, k, math.sin, 1)
            sin_sums[k] = even + odd
            if k != half:
                sin_sums[FOLD - 1 - k] = odd - even
    return cos_sums, sin_sums


def turn_kernel(first_ref, offset_ref, references_ref, out_ref, column_ref, in_ref, wide_ref):
    rows, cycles = references_ref.shape
    classes = offset_ref.shape[0]
    own_rows = rows // (2 * classes)
    in_ref[...] = references_ref[...].astype(f32)
    row = lax.broadcasted_iota(jnp.int32, (8, LANES), 0)
    lane = lax.broadcasted_iota(jnp.int32, (8, LANES), 1)
    freq = (lane + first_ref[0]).astype(f32) * (1.0 / (ROTS * ANG_STEP))
    tables = []
    for start in range(0, classes, 8):
        column = jnp.zeros((8, LANES), jnp.int32)
        for c in range(start, min(start + 8, classes)):
            column = jnp.where(row == c - start, offset_ref[c], column)
        column = column.astype(f32)
        column_ref[start : start + 8, :] = column
        tables.append(cos_sin_of_turns(column * freq))
    cosine = jnp.concatenate([c for c, _ in tables], 0)
    sine_part = jnp.concatenate([s for _, s in tables], 0)
    for m in range(own_rows):
        re_rows = pl.ds(2 * m * classes, classes, stride=2)
        im_rows = pl.ds(2 * m * classes + 1, classes, stride=2)
        c, s = cosine[:classes, m : m + 1], sine_part[:classes, m : m + 1]
        re, im = in_ref[re_rows, :], in_ref[im_rows, :]
        wide_ref[re_rows, :] = re * c + im * s
        wide_ref[im_rows, :] = im * c - re * s
    out_ref[...] = wide_ref[...].astype(bf16)


def turn_references(first, offsets, references):
    padded = -(-offsets.shape[0] // 8) * 8
    return pl.pallas_call(
        turn_kernel,
        in_specs=[
            pl.BlockSpec(memory_space=pltpu.SMEM),
            pl.BlockSpec(memory_space=pltpu.SMEM),
            pl.BlockSpec(memory_space=pltpu.VMEM),
        ],
        out_shape=[
            jax.ShapeDtypeStruct(references.shape, bf16),
            jax.ShapeDtypeStruct((padded, LANES), f32),
        ],
        scratch_shapes=[pltpu.VMEM(references.shape, f32)] * 2,
        compiler_params=pltpu.CompilerParams(vmem_limit_bytes=VMEM_LIMIT),
        name="turn_references",
    )(first, offsets, references)


def correlate_kernel(*refs, slots, classes, padded, finish):
    part_ref, refs = refs[slots], refs[slots + 1 :]
    weighted_refs, refs = refs[:slots], refs[slots:]
    piece_refs, refs = refs[:slots], refs[slots:]
    if finish:
        before_ref, power_before_ref, ctf_ref, weight_ref, stat_ref, share_ref = refs[:6]
        corr_ref, wide_ref, power_ref = refs[6:]
    else:
        corr_ref, power_ref, wide_ref = refs
    group = pl.program_id(0)
    cycles = piece_refs[0].shape[1]
    queries = weighted_refs[0].shape[2]
    block = piece_refs[0].shape[0]

    @pl.when(group == 0)
    def _():
        wide_ref[:, block:, :] = jnp.zeros((slots, wide_ref.shape[1] - block, cycles), f32)
        power_ref[...] = power_before_ref[...] if finish else jnp.zeros_like(power_ref)

    for j in range(slots):
        wide_ref[j, :block, :] = piece_refs[j][...].astype(f32)
    power = power_ref[...]
    for i in range(GROUP):
        total = before_ref[i, :, :queries] if finish else None
        for j in range(slots):
            re = wide_ref[j, pl.ds(2 * i * classes, padded, stride=2), :]
            im = wide_ref[j, pl.ds(2 * i * classes + 1, padded, stride=2), :]
            power = power + (re * re + im * im)
            left = jnp.concatenate(
                [jnp.concatenate([re, im], 1), jnp.concatenate([-im, re], 1)], 0
            ).astype(bf16)
            part = lax.dot_general(
                left, weighted_refs[j][0, i], (((1,), (1,)), ((), ())), preferred_element_type=f32
            )
            total = part if total is None else total + part
        row = group * GROUP + i if finish else i
        corr_ref[row, :, :queries] = total
    power_ref[...] = power

    if not finish:
        return

    @pl.when(group == pl.num_programs(0) - 1)
    def _():
        count = ctf_ref.shape[0]
        angles = ROTS * ANG_STEP
        used = SHIFTS * count
        tiles = weight_ref.shape[2] // LANES
        ctf_row = ctf_ref[...]
        ctf_rows = jnp.concatenate([ctf_row * ctf_row] * (LANES // count), 0)
        bias = lax.dot_general(
            power_ref[...],
            ctf_rows,
            (((1,), (1,)), ((), ())),
            precision=lax.Precision.HIGHEST,
            preferred_element_type=f32,
        ) * (0.5 / angles)
        wide_ref[0, :padded, :] = bias
        rows_of = lambda base: lax.broadcasted_iota(jnp.int32, (8, LANES), 0) + base
        lanes_of = lambda base: lax.broadcasted_iota(jnp.int32, (8, LANES), 1) + base

        peak = jnp.full((8, LANES), -1e30, f32)
        for tile in range(tiles):
            lanes = slice(tile * LANES, (tile + 1) * LANES)

            def scores(n, peak):
                start = pl.multiple_of(n * 8, 8)
                rows = pl.ds(start, 8)
                low = pl.ds(padded + start, 8)
                valid = (rows_of(start) < classes) & (lanes_of(tile * LANES) < used)
                even_values = [corr_ref[0, rows, lanes]]
                odd_values = [None]
                for m in range(1, ROTS // 2):
                    even_values.append(corr_ref[m, rows, lanes] + corr_ref[ROTS - m, rows, lanes])
                    odd_values.append(corr_ref[m, low, lanes] - corr_ref[ROTS - m, low, lanes])
                even_values.append(corr_ref[ROTS // 2, rows, lanes])
                odd_values.append(None)
                cos_sums, sin_sums = half_dft(even_values, odd_values)
                bias = wide_ref[0, rows, :]
                for k in range(FOLD):
                    if k in (0, FOLD - 1):
                        results = [(k, cos_sums[k])]
                    else:
                        results = [(k, cos_sums[k] - sin_sums[k]), (ROTS - k, cos_sums[k] + sin_sums[k])]
                    for place, value in results:
                        value = jnp.where(valid, value * (1.0 / angles) - bias, -1e30)
                        weight_ref[place, rows, lanes] = value
                        peak = jnp.maximum(peak, value)
                return peak

            peak = lax.fori_loop(0, padded // 8, scores, peak)

        peak = jnp.broadcast_to(jnp.max(peak, axis=0, keepdims=True), (8, LANES))
        step = count
        while step < LANES:
            peak = jnp.maximum(peak, pltpu.roll(peak, step, 1))
            step *= 2
        stat_ref[0:8, :] = peak

        def masses(n, whole):
            rows = pl.ds(pl.multiple_of(n * 8, 8), 8)
            mass = jnp.zeros((8, LANES), f32)
            for tile in range(tiles):
                lanes = slice(tile * LANES, (tile + 1) * LANES)
                for k in range(ROTS):
                    value = jnp.exp(weight_ref[k, rows, lanes] - peak)
                    weight_ref[k, rows, lanes] = value
                    mass = mass + value
            step = count
            while step < LANES:
                mass = mass + pltpu.roll(mass, step, 1)
                step *= 2
            stat_ref[pl.ds(pl.multiple_of(8 + n * 8, 8), 8), :] = mass
            return whole + mass

        whole = lax.fori_loop(0, padded // 8, masses, jnp.zeros((8, LANES), f32))
        share = jnp.concatenate([peak[:1], jnp.sum(whole, axis=0, keepdims=True)], 0)
        for j in range(share_ref.shape[0]):
            share_ref[j] = jnp.where(part_ref[0] == j, share, 0.0)


def correlate(slot_of, weighted, pieces, classes, part, before=None, power=None, ctf_rows=None, parts=1):
    _, _, queries, double = weighted.shape
    cycles = double // 2
    slots = len(pieces)
    padded = -(-classes // 8) * 8
    wide_lanes = -(-queries // LANES) * LANES
    block = 2 * GROUP * classes
    finish = ctf_rows is not None
    full = lambda shape: pl.BlockSpec(shape, lambda g, *u: (0,) * len(shape))
    in_specs = [
        pl.BlockSpec((1, GROUP, queries, double), functools.partial(lambda j, g, *u: (u[j][0], g, 0, 0), j))
        for j in range(slots)
    ] + [pl.BlockSpec((block, cycles), lambda g, *u: (g, 0))] * slots
    corr_block = pl.BlockSpec((GROUP, 2 * padded, wide_lanes), lambda g, *u: (g, 0, 0))
    corr_shape = (ROTS, 2 * padded, wide_lanes)
    wide = pltpu.VMEM((slots, block + ROWS, cycles), f32)
    scalars = [jnp.reshape(n, (1,)).astype(jnp.int32) for n in (*slot_of, part)]
    operands = scalars + [weighted] * slots + list(pieces)
    if finish:
        in_specs += [corr_block, full((padded, cycles)), full(ctf_rows.shape)]
        operands += [before, power, ctf_rows]
        out_shapes = [(ROTS, padded, wide_lanes), (8 + padded, LANES), (parts, 2, LANES)]
        out_specs = [full(shape) for shape in out_shapes]
        scratch = [pltpu.VMEM(corr_shape, f32), wide, pltpu.VMEM((padded, cycles), f32)]
    else:
        out_shapes = [corr_shape, (padded, cycles)]
        out_specs = [corr_block, full((padded, cycles))]
        scratch = [wide]
    return pl.pallas_call(
        functools.partial(correlate_kernel, slots=slots, classes=classes, padded=padded, finish=finish),
        grid_spec=pltpu.PrefetchScalarGridSpec(
            num_scalar_prefetch=len(scalars),
            grid=(ROTS // GROUP,),
            in_specs=in_specs,
            out_specs=out_specs,
            scratch_shapes=scratch,
        ),
        out_shape=[jax.ShapeDtypeStruct(shape, f32) for shape in out_shapes],
        compiler_params=pltpu.CompilerParams(vmem_limit_bytes=VMEM_LIMIT),
        name="scores" if finish else "correlate",
    )(*operands)


def back_kernel(weight_ref, stat_ref, share_ref, offset_ref, out_ref, evidence_ref, posterior_ref, sum_ref):
    padded = weight_ref.shape[1]
    queries = out_ref.shape[2]
    shares = [share_ref[j] for j in range(share_ref.shape[0])]
    top = shares[0][:1]
    for share in shares[1:]:
        top = jnp.maximum(top, share[:1])
    mass = sum(share[1:] * jnp.exp(share[:1] - top) for share in shares)
    evidence = jnp.broadcast_to(top + jnp.log(mass), (8, LANES))
    scale = jnp.exp(stat_ref[:8, :] - evidence)
    evidence_ref[...] = evidence
    posterior_ref[...] = stat_ref[8:, :] * scale[:1]
    for tile in range(weight_ref.shape[2] // LANES):
        lanes = slice(tile * LANES, (tile + 1) * LANES)

        def transform(n, carry):
            start = pl.multiple_of(n * 8, 8)
            rows = pl.ds(start, 8)
            low = pl.ds(padded + start, 8)
            values = [weight_ref[k, rows, lanes] * scale for k in range(ROTS)]
            even_values = [values[0]] + [values[k] + values[ROTS - k] for k in range(1, ROTS // 2)]
            odd_values = [None] + [values[k] - values[ROTS - k] for k in range(1, ROTS // 2)] + [None]
            cos_sums, sin_sums = half_dft(even_values + [values[ROTS // 2]], odd_values)
            for m in range(FOLD):
                sine_part = jnp.zeros_like(scale) if m in (0, FOLD - 1) else sin_sums[m]
                sum_ref[m, rows, lanes] = cos_sums[m]
                sum_ref[m, low, lanes] = sine_part
                if m not in (0, FOLD - 1):
                    sum_ref[ROTS - m, rows, lanes] = cos_sums[m]
                    sum_ref[ROTS - m, low, lanes] = -sine_part
            return carry

        lax.fori_loop(0, padded // 8, transform, 0)

    step_cos, step_sin = cos_sin_of_turns(offset_ref[...] * (1.0 / (ROTS * ANG_STEP)))

    def turn(m, carry):
        cosine, sine_part = carry
        for tile in range(weight_ref.shape[2] // LANES):
            lanes = slice(tile * LANES, (tile + 1) * LANES)
            kept = slice(tile * LANES, min((tile + 1) * LANES, queries))
            re, im = sum_ref[m, :padded, lanes], sum_ref[m, padded:, lanes]
            turned = jnp.concatenate([re * cosine - im * sine_part, re * sine_part + im * cosine], 0)
            out_ref[m, :, kept] = turned[:, : kept.stop - kept.start].astype(bf16)
        return cosine * step_cos - sine_part * step_sin, sine_part * step_cos + cosine * step_sin

    lax.fori_loop(0, ROTS, turn, (jnp.ones_like(step_cos), jnp.zeros_like(step_cos)))


def make_back(weights, stat, shares, offsets, queries):
    _, padded, wide_lanes = weights.shape
    return pl.pallas_call(
        back_kernel,
        out_shape=[
            jax.ShapeDtypeStruct((ROTS, 2 * padded, queries), bf16),
            jax.ShapeDtypeStruct((8, LANES), f32),
            jax.ShapeDtypeStruct((padded, LANES), f32),
        ],
        scratch_shapes=[pltpu.VMEM((ROTS, 2 * padded, wide_lanes), f32)],
        compiler_params=pltpu.CompilerParams(vmem_limit_bytes=VMEM_LIMIT),
        name="back",
    )(weights, stat, shares, offsets)


def sums_kernel(slot_ref, back_ref, weighted_ref, offset_ref, out_ref, wide_ref, *, classes):
    padded = offset_ref.shape[0]
    cycles = wide_ref.shape[1]
    turns = offset_ref[...] * (slot_ref[0].astype(f32) * (1.0 / ANG_STEP))
    cosine, sine_part = cos_sin_of_turns(turns)
    for i in range(GROUP):
        product = jnp.dot(back_ref[i], weighted_ref[0, i], preferred_element_type=f32)
        re = product[:padded, :cycles] - product[padded:, cycles:]
        im = product[:padded, cycles:] + product[padded:, :cycles]
        start = 2 * i * classes
        wide_ref[pl.ds(start, classes, stride=2), :] = (re * cosine - im * sine_part)[:classes]
        wide_ref[pl.ds(start + 1, classes, stride=2), :] = (re * sine_part + im * cosine)[:classes]
    out_ref[...] = wide_ref[...].astype(out_ref.dtype)


def class_sums_of(slot, back, weighted, offsets, classes, dtype):
    _, _, queries, double = weighted.shape
    cycles = double // 2
    rows = back.shape[1]
    block = 2 * GROUP * classes
    piece = pl.BlockSpec((block, cycles), lambda g, u: (g, 0))
    return pl.pallas_call(
        functools.partial(sums_kernel, classes=classes),
        grid_spec=pltpu.PrefetchScalarGridSpec(
            num_scalar_prefetch=1,
            grid=(ROTS // GROUP,),
            in_specs=[
                pl.BlockSpec((GROUP, rows, queries), lambda g, u: (g, 0, 0)),
                pl.BlockSpec((1, GROUP, queries, double), lambda g, u: (u[0], g, 0, 0)),
                pl.BlockSpec(offsets.shape, lambda g, u: (0, 0)),
            ],
            out_specs=piece,
            scratch_shapes=[pltpu.VMEM((block, cycles), f32)],
        ),
        out_shape=jax.ShapeDtypeStruct((ROTS * 2 * classes, cycles), dtype),
        compiler_params=pltpu.CompilerParams(vmem_limit_bytes=VMEM_LIMIT),
        name="class_sums",
    )(jnp.reshape(slot, (1,)).astype(jnp.int32), back, weighted, offsets)


def across(piece):
    return lax.ppermute(piece, "dp", [(d, d ^ 1) for d in range(8)])


def along(piece, pairs):
    return lax.ppermute(piece, "dp", [(2 * a + x, 2 * b + x) for a, b in pairs for x in range(2)])


def gather_on_line(piece, base, ctf_rows):
    index = lax.axis_index("dp")
    line, side = index // 2, index % 2
    _, steps = spectra_steps(base.shape[0])
    cuts = [0, 3 * steps // 13, 7 * steps // 13, 11 * steps // 13, steps]

    own_crossed = across(piece)
    near = along(piece, ((0, 1), (1, 0), (2, 3), (3, 2)))
    middle = along(piece, ((1, 2), (2, 1)))
    weighted = make_spectra(base, ctf_rows, cuts[0], cuts[1])
    weighted, near, middle, own_crossed = lax.optimization_barrier((weighted, near, middle, own_crossed))
    near_crossed = across(near)
    far_middle = along(near, ((1, 2), (2, 1)))
    end = along(middle, ((1, 0), (2, 3)))
    weighted = make_spectra(base, ctf_rows, cuts[1], cuts[2], weighted)
    weighted, far_middle, end, near_crossed = lax.optimization_barrier(
        (weighted, far_middle, end, near_crossed)
    )
    third = middle + end
    third_crossed = across(third)
    far_end = along(far_middle, ((1, 0), (2, 3)))
    weighted = make_spectra(base, ctf_rows, cuts[2], cuts[3], weighted)
    weighted, far_end, third_crossed = lax.optimization_barrier((weighted, far_end, third_crossed))
    fourth = far_middle + far_end
    fourth_crossed = across(fourth)
    weighted = make_spectra(base, ctf_rows, cuts[3], cuts[4], weighted)

    pieces = [piece, own_crossed, near, near_crossed, third, third_crossed, fourth, fourth_crossed]
    places = [line, line ^ 1, jnp.where(line < 2, 2, 1), jnp.where(line < 2, 3, 0)]
    slot_of = [2 * place + s for place in places for s in (side, 1 - side)]
    return weighted, pieces, slot_of


def reduce_on_line(back, weighted, offsets, classes):
    index = lax.axis_index("dp")
    line, side = index // 2, index % 2
    order = [jnp.where(line < 2, 3, 0), jnp.where(line < 2, 2, 1), line ^ 1, line]
    theirs = [class_sums_of(2 * z + 1 - side, back, weighted, offsets, classes, bf16) for z in order]
    ours = [class_sums_of(2 * z + side, back, weighted, offsets, classes, f32) for z in order]
    at_end = (line == 0) | (line == 3)

    crossed = [across(theirs[0])]
    crossed[0], theirs[1], theirs[2], ours[0] = lax.optimization_barrier(
        (crossed[0], theirs[1], theirs[2], ours[0])
    )
    crossed.append(across(theirs[1]))
    farthest = ours[0] + crossed[0].astype(f32)
    first = along(farthest.astype(bf16), ((0, 1), (3, 2)))
    crossed[1], theirs[2], theirs[3], ours[1], ours[2] = lax.optimization_barrier(
        (crossed[1], theirs[2], theirs[3], ours[1], ours[2])
    )
    crossed.append(across(theirs[2]))
    next_farthest = ours[1] + crossed[1].astype(f32)
    second = (jnp.where(at_end, next_farthest, farthest) + first.astype(f32)).astype(bf16)
    from_ends = along(second, ((0, 1), (3, 2)))
    from_middle = along(second, ((1, 2), (2, 1)))
    crossed[2], theirs[3], ours[3] = lax.optimization_barrier((crossed[2], theirs[3], ours[3]))
    crossed.append(across(theirs[3]))
    third = (next_farthest + from_ends.astype(f32)).astype(bf16)
    third = along(third, ((1, 2), (2, 1)))
    fourth = (ours[2] + crossed[2].astype(f32) + from_middle.astype(f32)).astype(bf16)
    fourth = along(fourth, ((0, 1), (1, 0), (2, 3), (3, 2)))
    return ours[3] + crossed[3].astype(f32) + third.astype(f32) + fourth.astype(f32)


def local(particles, references, ctf_table, rot_offset, prior_shift, defocus_group):
    count, _, angles, cycles = particles.shape
    own_rows, _, classes, _ = references.shape
    slots = angles // ROTS
    group_count = ctf_table.shape[0]
    devices = lax.axis_size("dp")

    first = (lax.axis_index("dp") * own_rows).astype(jnp.int32).reshape(1)
    rows = jnp.transpose(references, (0, 2, 1, 3)).reshape(own_rows * 2 * classes, cycles)
    piece, offsets = turn_references(first, rot_offset, rows)

    onehot = (defocus_group[:, None] == jnp.arange(group_count, dtype=jnp.int32)[None, :]).astype(f32)
    ctf_rows = jnp.dot(onehot, ctf_table, precision=lax.Precision.HIGHEST)
    base = make_base(particles, prior_shift)
    on_line = devices == 8 and own_rows == ROTS
    if on_line:
        weighted, pieces, slot_of = gather_on_line(piece, base, ctf_rows)
    else:
        gathered = lax.all_gather(piece, "dp", axis=0, tiled=True)
        gathered = gathered.reshape(slots, ROTS * 2 * classes, cycles)
        pieces = [gathered[j] for j in range(slots)]
        slot_of = list(range(slots))
        weighted = make_spectra(base, ctf_rows, 0, spectra_steps(count)[1])
    queries = weighted.shape[1]
    weighted = weighted.reshape(slots, ROTS, queries, 2 * cycles)

    half = slots // 2
    part = lax.axis_index("cls")
    corr, power = correlate(slot_of[:half], weighted, pieces[:half], classes, part)
    weights, stat, share = correlate(
        slot_of[half:], weighted, pieces[half:], classes, part, corr, power, ctf_rows, lax.axis_size("cls")
    )
    shares = lax.psum(share, "cls")
    back, evidence, posterior = make_back(weights, stat, shares, offsets, queries)
    log_evidence = evidence[0, :count]
    class_posterior = posterior[:classes, :count].T
    if on_line:
        class_rows = reduce_on_line(back, weighted, offsets, classes)
    else:
        sums = [class_sums_of(slot_of[u], back, weighted, offsets, classes, bf16) for u in range(slots)]
        summed = lax.psum_scatter(jnp.concatenate(sums, 0), "dp", scatter_dimension=0, tiled=True)
        class_rows = summed.astype(f32)
    class_sums = jnp.transpose(class_rows.reshape(own_rows, classes, 2, cycles), (0, 2, 1, 3))
    return (log_evidence, class_posterior, class_sums)


def solution(mesh):
    placed = (
        P("dp", None, None, None),
        P("dp", None, "cls", None),
        P(),
        P("cls"),
        P("dp", None),
        P("dp"),
    )
    return jax.shard_map(
        local,
        mesh=mesh,
        in_specs=placed,
        out_specs=(P("dp"), P("dp", "cls"), P("dp", None, "cls", None)),
        check_vma=False,
    )
```

time: 316 us -> 252 us (0.80)
  waiting for transfers between devices: 100 us -> 44.4 us
  local copies, waits for them, and re-layouts: 22.3 us -> 2.85 us
  starting transfers between devices: 13.8 us -> 30.3 us
  between operations: 16.2 us -> 0.91 us
  other arithmetic: 5.36 us -> 12.9 us
  Pallas kernels: 149 us -> 153 us
    all_gather x1 -> x0, waiting for transfers between devices: 47.8 us -> none  [local(): lax.all_gather(piece, 'dp', axis=0, tiled=True)]
    ppermute x4 -> x8, waiting for transfers between devices: 22.4 us -> 11 us  [across(): return lax.ppermute(piece, 'dp', [(d, d ^ 1) for d in range(8)])]
    unnamed x36 -> x33, local copies, waits for them, and re-layouts: 11.2 us -> 1.65 us
    ppermute x5 -> x10, starting transfers between devices: 10.6 us -> 20.1 us  [along(): lax.ppermute(piece, 'dp', [(2 * a + x, 2 * b + x) for a, b in pairs for x...]
    convert_element_type x2 -> x4, other arithmetic: 0.66 us -> 9.29 us  [the longest x1 3.09 us: reduce_on_line(): (jnp.where(at_end, next_farthest, farthest) + first.astype(f32)).astype(b...]
    slice x3 -> x0, local copies, waits for them, and re-layouts: 7.47 us -> none  [the longest x1 6.21 us: local(): pieces = [gathered[j] for j in range(slots)]]
    ppermute x4 -> x8, starting transfers between devices: 3.18 us -> 10.2 us  [across(): return lax.ppermute(piece, 'dp', [(d, d ^ 1) for d in range(8)])]
    pallas_call x11 -> x14, Pallas kernels: 115 us -> 121 us  [the longest x4 68.3 us: make_spectra(): pl.pallas_call(functools.partial(spectra_kernel, per_step=per_step), grid...]
  transfers between devices with their start and end apart: 10 -> 18, of which waited for: 7 -> 8; matrix products, arithmetic and copies ran while one was open for 2% -> 5% of each run, Pallas kernels for 30% -> 49%
where the time goes in v3:
time: 252 us; the launch traced here: 251 us
  Pallas kernels  153 us (61%)
  waiting for transfers between devices  44.4 us (18%)
  starting transfers between devices  30.3 us (12%)
  other arithmetic  12.9 us (5%)
  blocking collectives  6.25 us (2%)
  local copies, waits for them, and re-layouts  2.85 us (1%)
    pallas_call x4, Pallas kernels, make_spectra(): pl.pallas_call(functools.partial(spectra_kernel, per_step=per_step), grid...  68.3 us
    pallas_call x8, Pallas kernels, class_sums_of(): pl.pallas_call(functools.partial(sums_kernel, classes=classes), grid_spec...  40.4 us
    ppermute x10, waiting for transfers between devices, along(): lax.ppermute(piece, 'dp', [(2 * a + x, 2 * b + x) for a, b in pairs for x...  33.4 us
    pallas_call x2, Pallas kernels, correlate(): pl.pallas_call(functools.partial(correlate_kernel, slots=slots, classes=c...  29.1 us
    ppermute x10, starting transfers between devices, along(): lax.ppermute(piece, 'dp', [(2 * a + x, 2 * b + x) for a, b in pairs for x...  20.1 us
    ppermute x8, waiting for transfers between devices, across(): return lax.ppermute(piece, 'dp', [(d, d ^ 1) for d in range(8)])  11 us
    ppermute x8, starting transfers between devices, across(): return lax.ppermute(piece, 'dp', [(d, d ^ 1) for d in range(8)])  10.2 us
    pallas_call x1, Pallas kernels, make_base(): pl.pallas_call(base_kernel, grid=(count,), in_specs=[pl.BlockSpec(memory_...  6.79 us
  transfers between devices with their start and end apart: 18, of which 8 were waited for; matrix products, arithmetic and copies ran while one was open for 5% of the time, Pallas kernels for 49%

profile of v3, /device:TPU:8, one launch (start us, length us, event | category | flops | bytes accessed | tf_op | source)
XLA Modules:
  0.0 251.4 jit_solution(18143410571448659325)
XLA Ops:
  0.7 3.0 %turn_references.1 = (bf16[3600,128]{1,0:T(8,128)(2,1)}, f32[56,128]{1,0:T(8,128)}) custom-call(s32[1]{0:T(128)} %bitcast.6.first_ref, s32[50]{0:T(128)} %offset_ref.1, bf16[3600,128]{1,0:T(8,128)(2,1)} %bitcast.44), custom_call_target="tpu_custom_call" | custom-call | tf_op jit(solution)/shard_map/turn_references/pallas_call | solution.py:241
  5.1 3.5 %collective-permute-start.1 = (bf16[3600,128]{1,0:T(8,128)(2,1)}, bf16[3600,128]{1,0:T(8,128)(2,1)S(1)}, u32[]{:S(2)}, u32[]{:S(2)}) collective-permute-start(bf16[3600,128]{1,0:T(8,128)(2,1)} %get-tuple-element.36.refs_9_), channel_id=1, source_target_pairs={{8,16},{12,20},{16,8},{20,12},{9,17},{13,21},{17,9},{21,13},{10,18... | collective-permute-start | bytes 2764808 | tf_op jit(solution)/shard_map/ppermute | solution.py:531
  8.7 6.8 %centre.1.base_ref = f32[8,2,288,128]{3,2,1,0:T(8,128)} custom-call(s32[2,8]{1,0:T(2,128)} %bitcast.45, bf16[8,2,288,128]{3,2,1,0:T(8,128)(2,1)} %part_ref.1, f32[2,288,128]{2,1,0:T(8,128)} %constant.49.clone.turns_ref), custom_call_target="tpu_custom_call" | custom-call | tf_op jit(solution)/shard_map/centre/pallas_call | solution.py:83
  16.3 16.0 %spectra.4.refs_4_ = bf16[288,208,256]{2,1,0:T(8,128)(2,1)} custom-call(f32[8,2,288,128]{3,2,1,0:T(8,128)} %centre.1.base_ref, f32[8,128]{1,0:T(8,128)} %fusion.1.ctf_ref.refs_15_, bf16[576,576]{1,0:T(8,128)(2,1)} %constant.50.clone.table_ref, f32[2,5,2,288,128]{4,3,2,1,0:T(8,128)} %constant.51.clone.refs_0_.refs_1_.refs_2_.refs_3_, ...), custom_call_target="tpu_custom_call" | custom-call | tf_op jit(solution)/shard_map/spectra/pallas_call | solution.py:162
  32.3 4.0 %collective-permute-start.4 = (bf16[3600,128]{1,0:T(8,128)(2,1)S(1)}, bf16[3600,128]{1,0:T(8,128)(2,1)S(1)}, u32[]{:S(2)}, u32[]{:S(2)}) collective-permute-start(bf16[3600,128]{1,0:T(8,128)(2,1)S(1)} %collective-permute-done.1), channel_id=1, source_target_pairs={{8,0},{12,4},{16,24},{20,28},{9,1},{13,5},{17,25},{21,29},{10,2},{... | collective-permute-start | bytes 2764808 | tf_op jit(solution)/shard_map/ppermute | solution.py:531
  39.2 20.2 %spectra.5.refs_4_ = bf16[288,208,256]{2,1,0:T(8,128)(2,1)} custom-call(f32[8,2,288,128]{3,2,1,0:T(8,128)} %centre.1.base_ref, f32[8,128]{1,0:T(8,128)} %fusion.1.ctf_ref.refs_15_, bf16[576,576]{1,0:T(8,128)(2,1)} %constant.50.clone.table_ref, f32[2,5,2,288,128]{4,3,2,1,0:T(8,128)} %constant.51.clone.refs_0_.refs_1_.refs_2_.refs_3_, ...), custom_call_target="tpu_custom_call", output_to_operand_aliasing={{}: (7, {})} | custom-call | tf_op jit(solution)/shard_map/spectra/pallas_call | solution.py:162
  62.9 20.1 %spectra.6.refs_4_ = bf16[288,208,256]{2,1,0:T(8,128)(2,1)} custom-call(f32[8,2,288,128]{3,2,1,0:T(8,128)} %centre.1.base_ref, f32[8,128]{1,0:T(8,128)} %fusion.1.ctf_ref.refs_15_, bf16[576,576]{1,0:T(8,128)(2,1)} %constant.50.clone.table_ref, f32[2,5,2,288,128]{4,3,2,1,0:T(8,128)} %constant.51.clone.refs_0_.refs_1_.refs_2_.refs_3_, ...), custom_call_target="tpu_custom_call", output_to_operand_aliasing={{}: (7, {})} | custom-call | tf_op jit(solution)/shard_map/spectra/pallas_call | solution.py:162
  83.9 11.9 %spectra.7 = bf16[288,208,256]{2,1,0:T(8,128)(2,1)} custom-call(f32[8,2,288,128]{3,2,1,0:T(8,128)} %centre.1.base_ref, f32[8,128]{1,0:T(8,128)} %fusion.1.ctf_ref.refs_15_, bf16[576,576]{1,0:T(8,128)(2,1)} %constant.50.clone.table_ref, f32[2,5,2,288,128]{4,3,2,1,0:T(8,128)} %constant.51.clone.refs_0_.refs_1_.refs_2_.refs_3_, ...), custom_call_target="tpu_custom_call", output_to_operand_aliasing={{}: (7, {})} | custom-call | tf_op jit(solution)/shard_map/spectra/pallas_call | solution.py:162
  95.9 11.6 %correlate.1 = (f32[36,112,256]{2,1,0:T(8,128)}, f32[56,128]{1,0:T(8,128)}) custom-call(s32[1]{0:T(128)} %bitcast.10.refs_0_.slot_ref, s32[1]{0:T(128)} %bitcast.11.refs_1_, s32[1]{0:T(128)} %bitcast.12.refs_2_.slot_ref, s32[1]{0:T(128)} %bitcast.13.refs_3_, s32[1]{0:T(128)} %bitcast.4.refs_4_, bf16[8,36,208,256]{3,2,1,0:T(8,128)(2,1)} %bitcast.27, ...), custom_call_target="tpu_custom_call" | custom-call | tf_op jit(solution)/shard_map/correlate/pallas_call | solution.py:407
  108.4 17.6 %scores.1 = (f32[36,56,256]{2,1,0:T(8,128)}, f32[64,128]{1,0:T(8,128)}, f32[4,2,128]{2,1,0:T(2,128)}) custom-call(s32[1]{0:T(128)} %bitcast.refs_0_.slot_ref, s32[1]{0:T(128)} %bitcast.1.refs_1_, s32[1]{0:T(128)} %bitcast.2.refs_2_.slot_ref, s32[1]{0:T(128)} %bitcast.3.refs_3_, s32[1]{0:T(128)} %bitcast.4.refs_4_, bf16[8,36,208,256]{3,2,1,0:T(8,128)(2,1)} %bitcast.31, ...), custom_call_target="tpu_custom_call" | custom-call | tf_op jit(solution)/shard_map/scores/pallas_call | solution.py:407
  125.9 6.3 %psum.7.share_ref = f32[4,2,128]{2,1,0:T(2,128)} all-reduce(f32[4,2,128]{2,1,0:T(2,128)} %get-tuple-element.52), channel_id=1, replica_groups=mesh['dp'=8,'cls'=4] {'cls'}, use_global_device_ids=true, to_apply=%region_0.1 | all-reduce | flops 1024 | bytes 8192 | tf_op jit(solution)/shard_map/psum | solution.py:631
  132.2 5.4 %back.1 = (bf16[36,112,208]{2,1,0:T(8,128)(2,1)}, f32[8,128]{1,0:T(8,128)}, f32[56,128]{1,0:T(8,128)}) custom-call(f32[36,56,256]{2,1,0:T(8,128)} %get-tuple-element.50.weight_ref, f32[64,128]{1,0:T(8,128)} %get-tuple-element.51.stat_ref, f32[4,2,128]{2,1,0:T(2,128)} %psum.7.share_ref, f32[56,128]{1,0:T(8,128)} %get-tuple-element.53.offset_ref), custom_call_target="tpu_custom_call" | custom-call | tf_op jit(solution)/shard_map/back/pallas_call | solution.py:473
  137.6 4.8 %class_sums.8 = bf16[3600,128]{1,0:T(8,128)(2,1)} custom-call(s32[1]{0:T(128)} %bitcast.16.slot_ref, bf16[36,112,208]{2,1,0:T(8,128)(2,1)} %get-tuple-element.56.back_ref, bf16[8,36,208,256]{3,2,1,0:T(8,128)(2,1)} %bitcast.35, f32[56,128]{1,0:T(8,128)} %get-tuple-element.53.offset_ref), custom_call_target="tpu_custom_call" | custom-call | tf_op jit(solution)/shard_map/class_sums/pallas_call | solution.py:507
  144.0 5.2 %class_sums.11 = f32[3600,128]{1,0:T(8,128)} custom-call(s32[1]{0:T(128)} %bitcast.2.refs_2_.slot_ref, bf16[36,112,208]{2,1,0:T(8,128)(2,1)} %get-tuple-element.56.back_ref, bf16[8,36,208,256]{3,2,1,0:T(8,128)(2,1)} %bitcast.36, f32[56,128]{1,0:T(8,128)} %get-tuple-element.53.offset_ref), custom_call_target="tpu_custom_call" | custom-call | tf_op jit(solution)/shard_map/class_sums/pallas_call | solution.py:507
  149.1 4.8 %class_sums.10 = bf16[3600,128]{1,0:T(8,128)(2,1)} custom-call(s32[1]{0:T(128)} %bitcast.18.slot_ref, bf16[36,112,208]{2,1,0:T(8,128)(2,1)} %get-tuple-element.56.back_ref, bf16[8,36,208,256]{3,2,1,0:T(8,128)(2,1)} %bitcast.37, f32[56,128]{1,0:T(8,128)} %get-tuple-element.53.offset_ref), custom_call_target="tpu_custom_call" | custom-call | tf_op jit(solution)/shard_map/class_sums/pallas_call | solution.py:507
  154.0 5.0 %class_sums.9 = bf16[3600,128]{1,0:T(8,128)(2,1)} custom-call(s32[1]{0:T(128)} %bitcast.17.slot_ref, bf16[36,112,208]{2,1,0:T(8,128)(2,1)} %get-tuple-element.56.back_ref, bf16[8,36,208,256]{3,2,1,0:T(8,128)(2,1)} %bitcast.38, f32[56,128]{1,0:T(8,128)} %get-tuple-element.53.offset_ref), custom_call_target="tpu_custom_call" | custom-call | tf_op jit(solution)/shard_map/class_sums/pallas_call | solution.py:507
  159.0 5.9 %collective-permute-done.9 = bf16[3600,128]{1,0:T(8,128)(2,1)S(1)} collective-permute-done((bf16[3600,128]{1,0:T(8,128)(2,1)}, bf16[3600,128]{1,0:T(8,128)(2,1)S(1)}, u32[]{:S(2)}, u32[]{:S(2)}) %collective-permute-start.9) | collective-permute-done | bytes 921632 | tf_op jit(solution)/shard_map/ppermute | solution.py:527
  169.1 5.2 %class_sums.14 = f32[3600,128]{1,0:T(8,128)} custom-call(s32[1]{0:T(128)} %bitcast.12.refs_2_.slot_ref, bf16[36,112,208]{2,1,0:T(8,128)(2,1)} %get-tuple-element.56.back_ref, bf16[8,36,208,256]{3,2,1,0:T(8,128)(2,1)} %bitcast.39, f32[56,128]{1,0:T(8,128)} %get-tuple-element.53.offset_ref), custom_call_target="tpu_custom_call" | custom-call | tf_op jit(solution)/shard_map/class_sums/pallas_call | solution.py:507
  174.3 5.2 %class_sums.13 = f32[3600,128]{1,0:T(8,128)} custom-call(s32[1]{0:T(128)} %bitcast.refs_0_.slot_ref, bf16[36,112,208]{2,1,0:T(8,128)(2,1)} %get-tuple-element.56.back_ref, bf16[8,36,208,256]{3,2,1,0:T(8,128)(2,1)} %bitcast.40, f32[56,128]{1,0:T(8,128)} %get-tuple-element.53.offset_ref), custom_call_target="tpu_custom_call" | custom-call | tf_op jit(solution)/shard_map/class_sums/pallas_call | solution.py:507
  179.5 5.0 %class_sums.12 = bf16[3600,128]{1,0:T(8,128)(2,1)} custom-call(s32[1]{0:T(128)} %bitcast.19.slot_ref, bf16[36,112,208]{2,1,0:T(8,128)(2,1)} %get-tuple-element.56.back_ref, bf16[8,36,208,256]{3,2,1,0:T(8,128)(2,1)} %bitcast.41, f32[56,128]{1,0:T(8,128)} %get-tuple-element.53.offset_ref), custom_call_target="tpu_custom_call" | custom-call | tf_op jit(solution)/shard_map/class_sums/pallas_call | solution.py:507
  188.0 2.8 %collective-permute-done.13 = bf16[3600,128]{1,0:T(8,128)(2,1)} collective-permute-done((bf16[3600,128]{1,0:T(8,128)(2,1)}, bf16[3600,128]{1,0:T(8,128)(2,1)}, u32[]{:S(2)}, u32[]{:S(2)}) %collective-permute-start.13) | collective-permute-done | bytes 921632 | tf_op jit(solution)/shard_map/ppermute | solution.py:531
  190.9 3.1 %add_convert_fusion.2 = bf16[3600,128]{1,0:T(8,128)(2,1)} fusion(bf16[3600,128]{1,0:T(8,128)(2,1)} %collective-permute-done.13, f32[3600,128]{1,0:T(8,128)S(1)} %copy-done.3, bf16[3600,128]{1,0:T(8,128)(2,1)} %collective-permute-done.10, f32[3600,128]{1,0:T(8,128)S(1)} %copy-done.2, bf16[3600,128]{1,0:T(8,128)(2,1)S(1)} %collective-permute-done.9, pred[]{:T(512)S(6)} %or.3), kind=kLoop, calls=%fused_computation.3 | loop fusion | flops 3686400 | bytes 7372801 | tf_op jit(solution)/shard_map/convert_element_type | solution.py:587
  194.0 3.6 %collective-permute-start.16 = (bf16[3600,128]{1,0:T(8,128)(2,1)}, bf16[3600,128]{1,0:T(8,128)(2,1)S(1)}, u32[]{:S(2)}, u32[]{:S(2)}) collective-permute-start(bf16[3600,128]{1,0:T(8,128)(2,1)} %add_convert_fusion.2), channel_id=1, source_target_pairs={{8,16},{12,20},{16,8},{20,12},{9,17},{13,21},{17,9},{21,13},{10,18... | collective-permute-start | bytes 2764808 | tf_op jit(solution)/shard_map/ppermute | solution.py:531
  197.6 5.2 %class_sums.15 = f32[3600,128]{1,0:T(8,128)} custom-call(s32[1]{0:T(128)} %bitcast.10.refs_0_.slot_ref, bf16[36,112,208]{2,1,0:T(8,128)(2,1)} %get-tuple-element.56.back_ref, bf16[8,36,208,256]{3,2,1,0:T(8,128)(2,1)} %bitcast.42, f32[56,128]{1,0:T(8,128)} %get-tuple-element.53.offset_ref), custom_call_target="tpu_custom_call" | custom-call | tf_op jit(solution)/shard_map/class_sums/pallas_call | solution.py:507
  204.0 3.0 %collective-permute-done.11 = bf16[3600,128]{1,0:T(8,128)(2,1)} collective-permute-done((bf16[3600,128]{1,0:T(8,128)(2,1)S(1)}, bf16[3600,128]{1,0:T(8,128)(2,1)}, u32[]{:S(2)}, u32[]{:S(2)}) %collective-permute-start.11) | collective-permute-done | bytes 921632 | tf_op jit(solution)/shard_map/ppermute | solution.py:527
  208.6 7.8 %collective-permute-done.16 = bf16[3600,128]{1,0:T(8,128)(2,1)S(1)} collective-permute-done((bf16[3600,128]{1,0:T(8,128)(2,1)}, bf16[3600,128]{1,0:T(8,128)(2,1)S(1)}, u32[]{:S(2)}, u32[]{:S(2)}) %collective-permute-start.16) | collective-permute-done | bytes 921632 | tf_op jit(solution)/shard_map/ppermute | solution.py:531
  216.3 2.5 add_convert_fusion
  218.8 9.4 %collective-permute-done.14 = bf16[3600,128]{1,0:T(8,128)(2,1)S(1)} collective-permute-done((bf16[3600,128]{1,0:T(8,128)(2,1)}, bf16[3600,128]{1,0:T(8,128)(2,1)S(1)}, u32[]{:S(2)}, u32[]{:S(2)}) %collective-permute-start.14) | collective-permute-done | bytes 921632 | tf_op jit(solution)/shard_map/ppermute | solution.py:531
  228.2 2.5 add_convert_fusion.1
  234.9 9.6 %collective-permute-done.17 = bf16[3600,128]{1,0:T(8,128)(2,1)} collective-permute-done((bf16[3600,128]{1,0:T(8,128)(2,1)}, bf16[3600,128]{1,0:T(8,128)(2,1)}, u32[]{:S(2)}, u32[]{:S(2)}) %collective-permute-start.17) | collective-permute-done | bytes 921632 | tf_op jit(solution)/shard_map/ppermute | solution.py:531
  244.6 3.7 %collective-permute-done.15 = bf16[3600,128]{1,0:T(8,128)(2,1)} collective-permute-done((bf16[3600,128]{1,0:T(8,128)(2,1)}, bf16[3600,128]{1,0:T(8,128)(2,1)}, u32[]{:S(2)}, u32[]{:S(2)}) %collective-permute-start.15) | collective-permute-done | bytes 921632 | tf_op jit(solution)/shard_map/ppermute | solution.py:531
  248.3 3.1 %convert_add_fusion = f32[3600,128]{1,0:T(8,128)} fusion(bf16[3600,128]{1,0:T(8,128)(2,1)} %collective-permute-done.17, bf16[3600,128]{1,0:T(8,128)(2,1)} %collective-permute-done.15, f32[3600,128]{1,0:T(8,128)S(1)} %copy-done.4, bf16[3600,128]{1,0:T(8,128)(2,1)S(1)} %collective-permute-done.12), kind=kLoop, calls=%fused_computation | loop fusion | flops 2764800 | bytes 6451200 | tf_op jit(solution)/shard_map/add | solution.py:596
  (65 shorter events, 26.7 us)
Async XLA Ops:
  0.6 14.9 %copy-start = (f32[16,128]{1,0:T(8,128)S(1)}, f32[16,128]{1,0:T(8,128)}, u32[]{:S(2)}) copy-start(f32[16,128]{1,0:T(8,128)} %param.17) | copy-start | bytes 24580
  3.6 28.7 %collective-permute-start.2 = (bf16[3600,128]{1,0:T(8,128)(2,1)}, bf16[3600,128]{1,0:T(8,128)(2,1)S(1)}, u32[]{:S(2)}, u32[]{:S(2)}) collective-permute-start(bf16[3600,128]{1,0:T(8,128)(2,1)} %get-tuple-element.36.refs_9_), channel_id=1, source_target_pairs={{0,4},{4,0},{8,12},{12,8},{16,20},{20,16},{24,28},{28,24},{1,5},{5... | collective-permute-start | bytes 2764808 | tf_op jit(solution)/shard_map/ppermute | solution.py:527
  5.1 27.2 %collective-permute-start.1 = (bf16[3600,128]{1,0:T(8,128)(2,1)}, bf16[3600,128]{1,0:T(8,128)(2,1)S(1)}, u32[]{:S(2)}, u32[]{:S(2)}) collective-permute-start(bf16[3600,128]{1,0:T(8,128)(2,1)} %get-tuple-element.36.refs_9_), channel_id=1, source_target_pairs={{8,16},{12,20},{16,8},{20,12},{9,17},{13,21},{17,9},{21,13},{10,18... | collective-permute-start | bytes 2764808 | tf_op jit(solution)/shard_map/ppermute | solution.py:531
  8.6 23.7 %collective-permute-start = (bf16[3600,128]{1,0:T(8,128)(2,1)}, bf16[3600,128]{1,0:T(8,128)(2,1)S(1)}, u32[]{:S(2)}, u32[]{:S(2)}) collective-permute-start(bf16[3600,128]{1,0:T(8,128)(2,1)} %get-tuple-element.36.refs_9_), channel_id=1, source_target_pairs={{0,8},{4,12},{8,0},{12,4},{16,24},{20,28},{24,16},{28,20},{1,9},{5... | collective-permute-start | bytes 2764808 | tf_op jit(solution)/shard_map/ppermute | solution.py:531
  32.3 27.2 %copy-start.8 = (bf16[3600,128]{1,0:T(8,128)(2,1)}, bf16[3600,128]{1,0:T(8,128)(2,1)S(1)}, u32[]{:S(2)}) copy-start(bf16[3600,128]{1,0:T(8,128)(2,1)S(1)} %collective-permute-done.2.refs_10_) | copy-start | bytes 2764804
  32.3 27.2 %copy-start.9 = (bf16[3600,128]{1,0:T(8,128)(2,1)}, bf16[3600,128]{1,0:T(8,128)(2,1)S(1)}, u32[]{:S(2)}) copy-start(bf16[3600,128]{1,0:T(8,128)(2,1)S(1)} %collective-permute-done.refs_11_) | copy-start | bytes 2764804
  32.3 27.2 %collective-permute-start.4 = (bf16[3600,128]{1,0:T(8,128)(2,1)S(1)}, bf16[3600,128]{1,0:T(8,128)(2,1)S(1)}, u32[]{:S(2)}, u32[]{:S(2)}) collective-permute-start(bf16[3600,128]{1,0:T(8,128)(2,1)S(1)} %collective-permute-done.1), channel_id=1, source_target_pairs={{8,0},{12,4},{16,24},{20,28},{9,1},{13,5},{17,25},{21,29},{10,2},{... | collective-permute-start | bytes 2764808 | tf_op jit(solution)/shard_map/ppermute | solution.py:531
  36.3 23.2 %collective-permute-start.5 = (bf16[3600,128]{1,0:T(8,128)(2,1)S(1)}, bf16[3600,128]{1,0:T(8,128)(2,1)S(1)}, u32[]{:S(2)}, u32[]{:S(2)}) collective-permute-start(bf16[3600,128]{1,0:T(8,128)(2,1)S(1)} %collective-permute-done.refs_11_), channel_id=1, source_target_pairs={{0,4},{4,0},{8,12},{12,8},{16,20},{20,16},{24,28},{28,24},{1,5},{5... | collective-permute-start | bytes 2764808 | tf_op jit(solution)/shard_map/ppermute | solution.py:527
  36.9 22.7 %collective-permute-start.3 = (bf16[3600,128]{1,0:T(8,128)(2,1)S(1)}, bf16[3600,128]{1,0:T(8,128)(2,1)S(1)}, u32[]{:S(2)}, u32[]{:S(2)}) collective-permute-start(bf16[3600,128]{1,0:T(8,128)(2,1)S(1)} %collective-permute-done.refs_11_), channel_id=1, source_target_pairs={{8,16},{12,20},{16,8},{20,12},{9,17},{13,21},{17,9},{21,13},{10,18... | collective-permute-start | bytes 2764808 | tf_op jit(solution)/shard_map/ppermute | solution.py:531
  59.5 23.5 %copy-start.10 = (bf16[3600,128]{1,0:T(8,128)(2,1)}, bf16[3600,128]{1,0:T(8,128)(2,1)S(1)}, u32[]{:S(2)}) copy-start(bf16[3600,128]{1,0:T(8,128)(2,1)S(1)} %collective-permute-done.5.refs_12_) | copy-start | bytes 2764804
  59.8 23.2 %copy-start.6 = (bf16[3600,128]{1,0:T(8,128)(2,1)}, bf16[3600,128]{1,0:T(8,128)(2,1)S(1)}, u32[]{:S(2)}) copy-start(bf16[3600,128]{1,0:T(8,128)(2,1)S(1)} %add.86.refs_9_) | copy-start | bytes 2764804
  59.8 23.2 %collective-permute-start.7 = (bf16[3600,128]{1,0:T(8,128)(2,1)S(1)}, bf16[3600,128]{1,0:T(8,128)(2,1)S(1)}, u32[]{:S(2)}, u32[]{:S(2)}) collective-permute-start(bf16[3600,128]{1,0:T(8,128)(2,1)S(1)} %add.86.refs_9_), channel_id=1, source_target_pairs={{0,4},{4,0},{8,12},{12,8},{16,20},{20,16},{24,28},{28,24},{1,5},{5... | collective-permute-start | bytes 2764808 | tf_op jit(solution)/shard_map/ppermute | solution.py:527
  61.4 21.7 %collective-permute-start.6 = (bf16[3600,128]{1,0:T(8,128)(2,1)S(1)}, bf16[3600,128]{1,0:T(8,128)(2,1)S(1)}, u32[]{:S(2)}, u32[]{:S(2)}) collective-permute-start(bf16[3600,128]{1,0:T(8,128)(2,1)S(1)} %collective-permute-done.3), channel_id=1, source_target_pairs={{8,0},{12,4},{16,24},{20,28},{9,1},{13,5},{17,25},{21,29},{10,2},{... | collective-permute-start | bytes 2764808 | tf_op jit(solution)/shard_map/ppermute | solution.py:531
  83.0 12.8 %copy-start.11 = (bf16[3600,128]{1,0:T(8,128)(2,1)}, bf16[3600,128]{1,0:T(8,128)(2,1)S(1)}, u32[]{:S(2)}) copy-start(bf16[3600,128]{1,0:T(8,128)(2,1)S(1)} %collective-permute-done.7.refs_10_) | copy-start | bytes 2764804
  83.3 12.5 %copy-start.7 = (bf16[3600,128]{1,0:T(8,128)(2,1)}, bf16[3600,128]{1,0:T(8,128)(2,1)S(1)}, u32[]{:S(2)}) copy-start(bf16[3600,128]{1,0:T(8,128)(2,1)S(1)} %add.87.refs_11_) | copy-start | bytes 2764804
  83.3 24.1 %collective-permute-start.8 = (bf16[3600,128]{1,0:T(8,128)(2,1)S(1)}, bf16[3600,128]{1,0:T(8,128)(2,1)S(1)}, u32[]{:S(2)}, u32[]{:S(2)}) collective-permute-start(bf16[3600,128]{1,0:T(8,128)(2,1)S(1)} %add.87.refs_11_), channel_id=1, source_target_pairs={{0,4},{4,0},{8,12},{12,8},{16,20},{20,16},{24,28},{28,24},{1,5},{5... | collective-permute-start | bytes 2764808 | tf_op jit(solution)/shard_map/ppermute | solution.py:527
  142.5 22.4 %collective-permute-start.9 = (bf16[3600,128]{1,0:T(8,128)(2,1)}, bf16[3600,128]{1,0:T(8,128)(2,1)S(1)}, u32[]{:S(2)}, u32[]{:S(2)}) collective-permute-start(bf16[3600,128]{1,0:T(8,128)(2,1)} %class_sums.8), channel_id=1, source_target_pairs={{0,4},{4,0},{8,12},{12,8},{16,20},{20,16},{24,28},{28,24},{1,5},{5... | collective-permute-start | bytes 2764808 | tf_op jit(solution)/shard_map/ppermute | solution.py:527
  154.0 12.4 %copy-start.2 = (f32[3600,128]{1,0:T(8,128)S(1)}, f32[3600,128]{1,0:T(8,128)}, u32[]{:S(2)}) copy-start(f32[3600,128]{1,0:T(8,128)} %class_sums.11) | copy-start | bytes 5529604
  164.9 21.7 %collective-permute-start.10 = (bf16[3600,128]{1,0:T(8,128)(2,1)}, bf16[3600,128]{1,0:T(8,128)(2,1)}, u32[]{:S(2)}, u32[]{:S(2)}) collective-permute-start(bf16[3600,128]{1,0:T(8,128)(2,1)} %class_sums.9), channel_id=1, source_target_pairs={{0,4},{4,0},{8,12},{12,8},{16,20},{20,16},{24,28},{28,24},{1,5},{5... | collective-permute-start | bytes 2764808 | tf_op jit(solution)/shard_map/ppermute | solution.py:527
  167.6 23.3 %collective-permute-start.13 = (bf16[3600,128]{1,0:T(8,128)(2,1)}, bf16[3600,128]{1,0:T(8,128)(2,1)}, u32[]{:S(2)}, u32[]{:S(2)}) collective-permute-start(bf16[3600,128]{1,0:T(8,128)(2,1)} %fusion), channel_id=1, source_target_pairs={{0,8},{4,12},{24,16},{28,20},{1,9},{5,13},{25,17},{29,21},{2,10},{... | collective-permute-start | bytes 2764808 | tf_op jit(solution)/shard_map/ppermute | solution.py:531
  179.5 7.1 %copy-start.13 = (bf16[3600,128]{1,0:T(8,128)(2,1)S(1)}, bf16[3600,128]{1,0:T(8,128)(2,1)}, u32[]{:S(2)}) copy-start(bf16[3600,128]{1,0:T(8,128)(2,1)} %class_sums.10) | copy-start | bytes 2764804
  179.5 11.4 %copy-start.3 = (f32[3600,128]{1,0:T(8,128)S(1)}, f32[3600,128]{1,0:T(8,128)}, u32[]{:S(2)}) copy-start(f32[3600,128]{1,0:T(8,128)} %class_sums.13) | copy-start | bytes 5529604
  186.5 20.5 %collective-permute-start.11 = (bf16[3600,128]{1,0:T(8,128)(2,1)S(1)}, bf16[3600,128]{1,0:T(8,128)(2,1)}, u32[]{:S(2)}, u32[]{:S(2)}) collective-permute-start(bf16[3600,128]{1,0:T(8,128)(2,1)S(1)} %copy-done.13), channel_id=1, source_target_pairs={{0,4},{4,0},{8,12},{12,8},{16,20},{20,16},{24,28},{28,24},{1,5},{5... | collective-permute-start | bytes 2764808 | tf_op jit(solution)/shard_map/ppermute | solution.py:527
  194.0 22.4 %copy-start.5 = (f32[3600,128]{1,0:T(8,128)S(1)}, f32[3600,128]{1,0:T(8,128)}, u32[]{:S(2)}) copy-start(f32[3600,128]{1,0:T(8,128)} %class_sums.14) | copy-start | bytes 5529604
  194.0 22.4 %collective-permute-start.16 = (bf16[3600,128]{1,0:T(8,128)(2,1)}, bf16[3600,128]{1,0:T(8,128)(2,1)S(1)}, u32[]{:S(2)}, u32[]{:S(2)}) collective-permute-start(bf16[3600,128]{1,0:T(8,128)(2,1)} %add_convert_fusion.2), channel_id=1, source_target_pairs={{8,16},{12,20},{16,8},{20,12},{9,17},{13,21},{17,9},{21,13},{10,18... | collective-permute-start | bytes 2764808 | tf_op jit(solution)/shard_map/ppermute | solution.py:531
  202.8 25.5 %collective-permute-start.14 = (bf16[3600,128]{1,0:T(8,128)(2,1)}, bf16[3600,128]{1,0:T(8,128)(2,1)S(1)}, u32[]{:S(2)}, u32[]{:S(2)}) collective-permute-start(bf16[3600,128]{1,0:T(8,128)(2,1)} %add_convert_fusion.2), channel_id=1, source_target_pairs={{0,8},{4,12},{24,16},{28,20},{1,9},{5,13},{25,17},{29,21},{2,10},{... | collective-permute-start | bytes 2764808 | tf_op jit(solution)/shard_map/ppermute | solution.py:531
  207.1 27.9 %collective-permute-start.12 = (bf16[3600,128]{1,0:T(8,128)(2,1)}, bf16[3600,128]{1,0:T(8,128)(2,1)S(1)}, u32[]{:S(2)}, u32[]{:S(2)}) collective-permute-start(bf16[3600,128]{1,0:T(8,128)(2,1)} %class_sums.12), channel_id=1, source_target_pairs={{0,4},{4,0},{8,12},{12,8},{16,20},{20,16},{24,28},{28,24},{1,5},{5... | collective-permute-start | bytes 2764808 | tf_op jit(solution)/shard_map/ppermute | solution.py:527
  218.8 14.2 %copy-start.14 = (f32[56,128]{1,0:T(8,128)S(1)}, f32[56,128]{1,0:T(8,128)}, u32[]{:S(2)}) copy-start(f32[56,128]{1,0:T(8,128)} %get-tuple-element.55) | copy-start | bytes 86020
  218.8 29.5 %copy-start.4 = (f32[3600,128]{1,0:T(8,128)S(1)}, f32[3600,128]{1,0:T(8,128)}, u32[]{:S(2)}) copy-start(f32[3600,128]{1,0:T(8,128)} %class_sums.15) | copy-start | bytes 5529604
  218.8 25.7 %collective-permute-start.17 = (bf16[3600,128]{1,0:T(8,128)(2,1)}, bf16[3600,128]{1,0:T(8,128)(2,1)}, u32[]{:S(2)}, u32[]{:S(2)}) collective-permute-start(bf16[3600,128]{1,0:T(8,128)(2,1)} %add_convert_fusion), channel_id=1, source_target_pairs={{0,8},{4,12},{8,0},{12,4},{16,24},{20,28},{24,16},{28,20},{1,9},{5... | collective-permute-start | bytes 2764808 | tf_op jit(solution)/shard_map/ppermute | solution.py:531
  230.7 17.6 %collective-permute-start.15 = (bf16[3600,128]{1,0:T(8,128)(2,1)}, bf16[3600,128]{1,0:T(8,128)(2,1)}, u32[]{:S(2)}, u32[]{:S(2)}) collective-permute-start(bf16[3600,128]{1,0:T(8,128)(2,1)} %add_convert_fusion.1), channel_id=1, source_target_pairs={{8,16},{12,20},{16,8},{20,12},{9,17},{13,21},{17,9},{21,13},{10,18... | collective-permute-start | bytes 2764808 | tf_op jit(solution)/shard_map/ppermute | solution.py:531
  233.7 17.7 %copy-start.1 = (f32[16,128]{1,0:T(8,128)S(1)}, f32[16,128]{1,0:T(8,128)}, u32[]{:S(2)}) copy-start(f32[16,128]{1,0:T(8,128)} %param.17) | copy-start | bytes 24580
  (2 other events, 7.7 us)

commit v4 on v3

--- a/solution.py
+++ b/solution.py
@@ -17,6 +17,7 @@
 LANES = 128
 GROUP = 12
 ROWS = 16
+APART = 17
 FOLD = ROTS // 2 + 1
 
 two_pi = 2.0 * math.pi
@@ -128,10 +129,11 @@
             row = 2 * n + j
             ctf_row = ctf_ref[row % count, :][None, :]
             part = spectrum[:, j * cycles : (j + 1) * cycles] * ctf_row
-            re_ref[pl.ds(row, angles, stride=ROWS), :] = part[:angles]
-            im_ref[pl.ds(row, angles, stride=ROWS), :] = part[angles:]
-    out_ref[:, :, :cycles] = re_ref[...].reshape(angles, ROWS, cycles).astype(bf16)
-    out_ref[:, :, cycles:] = im_ref[...].reshape(angles, ROWS, cycles).astype(bf16)
+            re_ref[pl.ds(row, angles, stride=APART), :] = part[:angles]
+            im_ref[pl.ds(row, angles, stride=APART), :] = part[angles:]
+    for m in range(angles):
+        out_ref[m, :, :cycles] = re_ref[m * APART : m * APART + ROWS, :].astype(bf16)
+        out_ref[m, :, cycles:] = im_ref[m * APART : m * APART + ROWS, :].astype(bf16)
 
 
 def spectra_steps(count):
@@ -167,8 +169,8 @@
         out_shape=jax.ShapeDtypeStruct((angles, steps * ROWS, 2 * cycles), bf16),
         scratch_shapes=[
             pltpu.VMEM((2 * angles, ROWS * cycles), bf16),
-            pltpu.VMEM((angles * ROWS, cycles), f32),
-            pltpu.VMEM((angles * ROWS, cycles), f32),
+            pltpu.VMEM((angles * APART, cycles), f32),
+            pltpu.VMEM((angles * APART, cycles), f32),
         ],
         input_output_aliases={} if before is None else {3 + 2 * per_step: 0},
         compiler_params=pltpu.CompilerParams(vmem_limit_bytes=VMEM_LIMIT),
@@ -573,21 +575,21 @@
     at_end = (line == 0) | (line == 3)
 
     crossed = [across(theirs[0])]
-    crossed[0], theirs[1], theirs[2], ours[0] = lax.optimization_barrier(
-        (crossed[0], theirs[1], theirs[2], ours[0])
+    crossed[0], theirs[1], theirs[2], ours[0], ours[1] = lax.optimization_barrier(
+        (crossed[0], theirs[1], theirs[2], ours[0], ours[1])
     )
     crossed.append(across(theirs[1]))
     farthest = ours[0] + crossed[0].astype(f32)
     first = along(farthest.astype(bf16), ((0, 1), (3, 2)))
-    crossed[1], theirs[2], theirs[3], ours[1], ours[2] = lax.optimization_barrier(
-        (crossed[1], theirs[2], theirs[3], ours[1], ours[2])
+    crossed[1], theirs[2], theirs[3], ours[2], ours[3] = lax.optimization_barrier(
+        (crossed[1], theirs[2], theirs[3], ours[2], ours[3])
     )
     crossed.append(across(theirs[2]))
     next_farthest = ours[1] + crossed[1].astype(f32)
     second = (jnp.where(at_end, next_farthest, farthest) + first.astype(f32)).astype(bf16)
     from_ends = along(second, ((0, 1), (3, 2)))
     from_middle = along(second, ((1, 2), (2, 1)))
-    crossed[2], theirs[3], ours[3] = lax.optimization_barrier((crossed[2], theirs[3], ours[3]))
+    crossed[2], theirs[3] = lax.optimization_barrier((crossed[2], theirs[3]))
     crossed.append(across(theirs[3]))
     third = (next_farthest + from_ends.astype(f32)).astype(bf16)
     third = along(third, ((1, 2), (2, 1)))

time: 252 us -> 238 us (0.944)
  Pallas kernels: 153 us -> 142 us
  starting transfers between devices: 30.3 us -> 26.7 us
  waiting for transfers between devices: 44.4 us -> 47.1 us
    pallas_call x4, Pallas kernels: 68.3 us -> 56.8 us  [make_spectra(): pl.pallas_call(functools.partial(spectra_kernel, per_step=per_step), grid...]
    ppermute x8, waiting for transfers between devices: 11 us -> 19.9 us  [across(): return lax.ppermute(piece, 'dp', [(d, d ^ 1) for d in range(8)])]
    ppermute x10, waiting for transfers between devices: 33.4 us -> 27.1 us  [along(): lax.ppermute(piece, 'dp', [(2 * a + x, 2 * b + x) for a, b in pairs for x...]
    ppermute x8, starting transfers between devices: 10.2 us -> 6.71 us  [across(): return lax.ppermute(piece, 'dp', [(d, d ^ 1) for d in range(8)])]
  transfers between devices with their start and end apart: 18 -> 18, of which waited for: 8 -> 14; matrix products, arithmetic and copies ran while one was open for 5% -> 4% of each run, Pallas kernels for 49% -> 47%
where the time goes in v4:
time: 238 us; the launch traced here: 237 us
  Pallas kernels  142 us (60%)
  waiting for transfers between devices  47.1 us (20%)
  starting transfers between devices  26.7 us (11%)
  other arithmetic  10.5 us (4%)
  blocking collectives  6.43 us (3%)
  local copies, waits for them, and re-layouts  2.85 us (1%)
    pallas_call x4, Pallas kernels, make_spectra(): pl.pallas_call(functools.partial(spectra_kernel, per_step=per_step), grid...  56.8 us
    pallas_call x8, Pallas kernels, class_sums_of(): pl.pallas_call(functools.partial(sums_kernel, classes=classes), grid_spec...  40.3 us
    pallas_call x2, Pallas kernels, correlate(): pl.pallas_call(functools.partial(correlate_kernel, slots=slots, classes=c...  29.2 us
    ppermute x10, waiting for transfers between devices, along(): lax.ppermute(piece, 'dp', [(2 * a + x, 2 * b + x) for a, b in pairs for x...  27.1 us
    ppermute x10, starting transfers between devices, along(): lax.ppermute(piece, 'dp', [(2 * a + x, 2 * b + x) for a, b in pairs for x...  20 us
    ppermute x8, waiting for transfers between devices, across(): return lax.ppermute(piece, 'dp', [(d, d ^ 1) for d in range(8)])  19.9 us
    pallas_call x1, Pallas kernels, make_base(): pl.pallas_call(base_kernel, grid=(count,), in_specs=[pl.BlockSpec(memory_...  6.79 us
    ppermute x8, starting transfers between devices, across(): return lax.ppermute(piece, 'dp', [(d, d ^ 1) for d in range(8)])  6.71 us
  transfers between devices with their start and end apart: 18, of which 14 were waited for; matrix products, arithmetic and copies ran while one was open for 4% of the time, Pallas kernels for 47%

profile of v4, /device:TPU:8, one launch (start us, length us, event | category | flops | bytes accessed | tf_op | source)
XLA Modules:
  0.0 236.8 jit_solution(8340044213249112636)
XLA Ops:
  0.7 3.0 %turn_references.1 = (bf16[3600,128]{1,0:T(8,128)(2,1)}, f32[56,128]{1,0:T(8,128)}) custom-call(s32[1]{0:T(128)} %bitcast.6.first_ref, s32[50]{0:T(128)} %offset_ref.1, bf16[3600,128]{1,0:T(8,128)(2,1)} %bitcast.44), custom_call_target="tpu_custom_call" | custom-call | tf_op jit(solution)/shard_map/turn_references/pallas_call | solution.py:243
  5.1 3.5 %collective-permute-start.1 = (bf16[3600,128]{1,0:T(8,128)(2,1)}, bf16[3600,128]{1,0:T(8,128)(2,1)S(1)}, u32[]{:S(2)}, u32[]{:S(2)}) collective-permute-start(bf16[3600,128]{1,0:T(8,128)(2,1)} %get-tuple-element.36.refs_9_), channel_id=1, source_target_pairs={{8,16},{12,20},{16,8},{20,12},{9,17},{13,21},{17,9},{21,13},{10,18... | collective-permute-start | bytes 2764808 | tf_op jit(solution)/shard_map/ppermute | solution.py:533
  8.7 6.8 %centre.1.base_ref = f32[8,2,288,128]{3,2,1,0:T(8,128)} custom-call(s32[2,8]{1,0:T(2,128)} %bitcast.45, bf16[8,2,288,128]{3,2,1,0:T(8,128)(2,1)} %part_ref.1, f32[2,288,128]{2,1,0:T(8,128)} %constant.49.clone.turns_ref), custom_call_target="tpu_custom_call" | custom-call | tf_op jit(solution)/shard_map/centre/pallas_call | solution.py:84
  16.3 13.4 %spectra.4.refs_4_ = bf16[288,208,256]{2,1,0:T(8,128)(2,1)} custom-call(f32[8,2,288,128]{3,2,1,0:T(8,128)} %centre.1.base_ref, f32[8,128]{1,0:T(8,128)} %fusion.1.ctf_ref.refs_15_, bf16[576,576]{1,0:T(8,128)(2,1)} %constant.50.clone.table_ref, f32[2,5,2,288,128]{4,3,2,1,0:T(8,128)} %constant.51.clone.refs_0_.refs_1_.refs_2_.refs_3_, ...), custom_call_target="tpu_custom_call" | custom-call | tf_op jit(solution)/shard_map/spectra/pallas_call | solution.py:164
  30.5 3.1 %collective-permute-start.4 = (bf16[3600,128]{1,0:T(8,128)(2,1)S(1)}, bf16[3600,128]{1,0:T(8,128)(2,1)S(1)}, u32[]{:S(2)}, u32[]{:S(2)}) collective-permute-start(bf16[3600,128]{1,0:T(8,128)(2,1)S(1)} %collective-permute-done.1), channel_id=1, source_target_pairs={{8,0},{12,4},{16,24},{20,28},{9,1},{13,5},{17,25},{21,29},{10,2},{... | collective-permute-start | bytes 2764808 | tf_op jit(solution)/shard_map/ppermute | solution.py:533
  34.2 2.3 collective-permute-start.3
  36.6 16.7 %spectra.5.refs_4_ = bf16[288,208,256]{2,1,0:T(8,128)(2,1)} custom-call(f32[8,2,288,128]{3,2,1,0:T(8,128)} %centre.1.base_ref, f32[8,128]{1,0:T(8,128)} %fusion.1.ctf_ref.refs_15_, bf16[576,576]{1,0:T(8,128)(2,1)} %constant.50.clone.table_ref, f32[2,5,2,288,128]{4,3,2,1,0:T(8,128)} %constant.51.clone.refs_0_.refs_1_.refs_2_.refs_3_, ...), custom_call_target="tpu_custom_call", output_to_operand_aliasing={{}: (7, {})} | custom-call | tf_op jit(solution)/shard_map/spectra/pallas_call | solution.py:164
  54.8 2.1 collective-permute-done.3
  60.1 16.6 %spectra.6.refs_4_ = bf16[288,208,256]{2,1,0:T(8,128)(2,1)} custom-call(f32[8,2,288,128]{3,2,1,0:T(8,128)} %centre.1.base_ref, f32[8,128]{1,0:T(8,128)} %fusion.1.ctf_ref.refs_15_, bf16[576,576]{1,0:T(8,128)(2,1)} %constant.50.clone.table_ref, f32[2,5,2,288,128]{4,3,2,1,0:T(8,128)} %constant.51.clone.refs_0_.refs_1_.refs_2_.refs_3_, ...), custom_call_target="tpu_custom_call", output_to_operand_aliasing={{}: (7, {})} | custom-call | tf_op jit(solution)/shard_map/spectra/pallas_call | solution.py:164
  79.3 10.1 %spectra.7 = bf16[288,208,256]{2,1,0:T(8,128)(2,1)} custom-call(f32[8,2,288,128]{3,2,1,0:T(8,128)} %centre.1.base_ref, f32[8,128]{1,0:T(8,128)} %fusion.1.ctf_ref.refs_15_, bf16[576,576]{1,0:T(8,128)(2,1)} %constant.50.clone.table_ref, f32[2,5,2,288,128]{4,3,2,1,0:T(8,128)} %constant.51.clone.refs_0_.refs_1_.refs_2_.refs_3_, ...), custom_call_target="tpu_custom_call", output_to_operand_aliasing={{}: (7, {})} | custom-call | tf_op jit(solution)/shard_map/spectra/pallas_call | solution.py:164
  89.5 11.6 %correlate.1 = (f32[36,112,256]{2,1,0:T(8,128)}, f32[56,128]{1,0:T(8,128)}) custom-call(s32[1]{0:T(128)} %bitcast.10.refs_0_.slot_ref, s32[1]{0:T(128)} %bitcast.11.refs_1_, s32[1]{0:T(128)} %bitcast.12.refs_2_.slot_ref, s32[1]{0:T(128)} %bitcast.13.refs_3_, s32[1]{0:T(128)} %bitcast.4.refs_4_, bf16[8,36,208,256]{3,2,1,0:T(8,128)(2,1)} %bitcast.27, ...), custom_call_target="tpu_custom_call" | custom-call | tf_op jit(solution)/shard_map/correlate/pallas_call | solution.py:409
  102.0 17.6 %scores.1 = (f32[36,56,256]{2,1,0:T(8,128)}, f32[64,128]{1,0:T(8,128)}, f32[4,2,128]{2,1,0:T(2,128)}) custom-call(s32[1]{0:T(128)} %bitcast.refs_0_.slot_ref, s32[1]{0:T(128)} %bitcast.1.refs_1_, s32[1]{0:T(128)} %bitcast.2.refs_2_.slot_ref, s32[1]{0:T(128)} %bitcast.3.refs_3_, s32[1]{0:T(128)} %bitcast.4.refs_4_, bf16[8,36,208,256]{3,2,1,0:T(8,128)(2,1)} %bitcast.31, ...), custom_call_target="tpu_custom_call" | custom-call | tf_op jit(solution)/shard_map/scores/pallas_call | solution.py:409
  119.6 6.4 %psum.7.share_ref = f32[4,2,128]{2,1,0:T(2,128)} all-reduce(f32[4,2,128]{2,1,0:T(2,128)} %get-tuple-element.52), channel_id=1, replica_groups=mesh['dp'=8,'cls'=4] {'cls'}, use_global_device_ids=true, to_apply=%region_0.1 | all-reduce | flops 1024 | bytes 8192 | tf_op jit(solution)/shard_map/psum | solution.py:633
  126.0 5.4 %back.1 = (bf16[36,112,208]{2,1,0:T(8,128)(2,1)}, f32[8,128]{1,0:T(8,128)}, f32[56,128]{1,0:T(8,128)}) custom-call(f32[36,56,256]{2,1,0:T(8,128)} %get-tuple-element.50.weight_ref, f32[64,128]{1,0:T(8,128)} %get-tuple-element.51.stat_ref, f32[4,2,128]{2,1,0:T(2,128)} %psum.7.share_ref, f32[56,128]{1,0:T(8,128)} %get-tuple-element.53.offset_ref), custom_call_target="tpu_custom_call" | custom-call | tf_op jit(solution)/shard_map/back/pallas_call | solution.py:475
  131.5 4.8 %class_sums.8 = bf16[3600,128]{1,0:T(8,128)(2,1)} custom-call(s32[1]{0:T(128)} %bitcast.16.slot_ref, bf16[36,112,208]{2,1,0:T(8,128)(2,1)} %get-tuple-element.56.back_ref, bf16[8,36,208,256]{3,2,1,0:T(8,128)(2,1)} %bitcast.35, f32[56,128]{1,0:T(8,128)} %get-tuple-element.53.offset_ref), custom_call_target="tpu_custom_call" | custom-call | tf_op jit(solution)/shard_map/class_sums/pallas_call | solution.py:509
  136.6 5.2 %class_sums.12 = f32[3600,128]{1,0:T(8,128)} custom-call(s32[1]{0:T(128)} %bitcast.refs_0_.slot_ref, bf16[36,112,208]{2,1,0:T(8,128)(2,1)} %get-tuple-element.56.back_ref, bf16[8,36,208,256]{3,2,1,0:T(8,128)(2,1)} %bitcast.36, f32[56,128]{1,0:T(8,128)} %get-tuple-element.53.offset_ref), custom_call_target="tpu_custom_call" | custom-call | tf_op jit(solution)/shard_map/class_sums/pallas_call | solution.py:509
  141.8 5.2 %class_sums.11 = f32[3600,128]{1,0:T(8,128)} custom-call(s32[1]{0:T(128)} %bitcast.2.refs_2_.slot_ref, bf16[36,112,208]{2,1,0:T(8,128)(2,1)} %get-tuple-element.56.back_ref, bf16[8,36,208,256]{3,2,1,0:T(8,128)(2,1)} %bitcast.37, f32[56,128]{1,0:T(8,128)} %get-tuple-element.53.offset_ref), custom_call_target="tpu_custom_call" | custom-call | tf_op jit(solution)/shard_map/class_sums/pallas_call | solution.py:509
  146.9 4.8 %class_sums.10 = bf16[3600,128]{1,0:T(8,128)(2,1)} custom-call(s32[1]{0:T(128)} %bitcast.18.slot_ref, bf16[36,112,208]{2,1,0:T(8,128)(2,1)} %get-tuple-element.56.back_ref, bf16[8,36,208,256]{3,2,1,0:T(8,128)(2,1)} %bitcast.38, f32[56,128]{1,0:T(8,128)} %get-tuple-element.53.offset_ref), custom_call_target="tpu_custom_call" | custom-call | tf_op jit(solution)/shard_map/class_sums/pallas_call | solution.py:509
  151.8 5.0 %class_sums.9 = bf16[3600,128]{1,0:T(8,128)(2,1)} custom-call(s32[1]{0:T(128)} %bitcast.17.slot_ref, bf16[36,112,208]{2,1,0:T(8,128)(2,1)} %get-tuple-element.56.back_ref, bf16[8,36,208,256]{3,2,1,0:T(8,128)(2,1)} %bitcast.39, f32[56,128]{1,0:T(8,128)} %get-tuple-element.53.offset_ref), custom_call_target="tpu_custom_call" | custom-call | tf_op jit(solution)/shard_map/class_sums/pallas_call | solution.py:509
  161.5 5.2 %class_sums.15 = f32[3600,128]{1,0:T(8,128)} custom-call(s32[1]{0:T(128)} %bitcast.10.refs_0_.slot_ref, bf16[36,112,208]{2,1,0:T(8,128)(2,1)} %get-tuple-element.56.back_ref, bf16[8,36,208,256]{3,2,1,0:T(8,128)(2,1)} %bitcast.40, f32[56,128]{1,0:T(8,128)} %get-tuple-element.53.offset_ref), custom_call_target="tpu_custom_call" | custom-call | tf_op jit(solution)/shard_map/class_sums/pallas_call | solution.py:509
  166.7 5.2 %class_sums.14 = f32[3600,128]{1,0:T(8,128)} custom-call(s32[1]{0:T(128)} %bitcast.12.refs_2_.slot_ref, bf16[36,112,208]{2,1,0:T(8,128)(2,1)} %get-tuple-element.56.back_ref, bf16[8,36,208,256]{3,2,1,0:T(8,128)(2,1)} %bitcast.41, f32[56,128]{1,0:T(8,128)} %get-tuple-element.53.offset_ref), custom_call_target="tpu_custom_call" | custom-call | tf_op jit(solution)/shard_map/class_sums/pallas_call | solution.py:509
  171.9 5.0 %class_sums.13 = bf16[3600,128]{1,0:T(8,128)(2,1)} custom-call(s32[1]{0:T(128)} %bitcast.19.slot_ref, bf16[36,112,208]{2,1,0:T(8,128)(2,1)} %get-tuple-element.56.back_ref, bf16[8,36,208,256]{3,2,1,0:T(8,128)(2,1)} %bitcast.42, f32[56,128]{1,0:T(8,128)} %get-tuple-element.53.offset_ref), custom_call_target="tpu_custom_call" | custom-call | tf_op jit(solution)/shard_map/class_sums/pallas_call | solution.py:509
  176.8 3.5 %collective-permute-done.10 = bf16[3600,128]{1,0:T(8,128)(2,1)} collective-permute-done((bf16[3600,128]{1,0:T(8,128)(2,1)}, bf16[3600,128]{1,0:T(8,128)(2,1)}, u32[]{:S(2)}, u32[]{:S(2)}) %collective-permute-start.10) | collective-permute-done | bytes 921632 | tf_op jit(solution)/shard_map/ppermute | solution.py:529
  180.7 2.9 %collective-permute-done.13 = bf16[3600,128]{1,0:T(8,128)(2,1)} collective-permute-done((bf16[3600,128]{1,0:T(8,128)(2,1)}, bf16[3600,128]{1,0:T(8,128)(2,1)}, u32[]{:S(2)}, u32[]{:S(2)}) %collective-permute-start.13) | collective-permute-done | bytes 921632 | tf_op jit(solution)/shard_map/ppermute | solution.py:533
  185.6 2.3 collective-permute-start.16
  189.2 11.6 %collective-permute-done.11 = bf16[3600,128]{1,0:T(8,128)(2,1)S(1)} collective-permute-done((bf16[3600,128]{1,0:T(8,128)(2,1)S(1)}, bf16[3600,128]{1,0:T(8,128)(2,1)S(1)}, u32[]{:S(2)}, u32[]{:S(2)}) %collective-permute-start.11) | collective-permute-done | bytes 921632 | tf_op jit(solution)/shard_map/ppermute | solution.py:529
  201.2 6.6 %collective-permute-done.16 = bf16[3600,128]{1,0:T(8,128)(2,1)S(1)} collective-permute-done((bf16[3600,128]{1,0:T(8,128)(2,1)S(1)}, bf16[3600,128]{1,0:T(8,128)(2,1)S(1)}, u32[]{:S(2)}, u32[]{:S(2)}) %collective-permute-start.16) | collective-permute-done | bytes 921632 | tf_op jit(solution)/shard_map/ppermute | solution.py:533
  210.6 2.4 %add_convert_fusion.1 = bf16[3600,128]{1,0:T(8,128)(2,1)} fusion(bf16[3600,128]{1,0:T(8,128)(2,1)S(1)} %collective-permute-done.14, f32[3600,128]{1,0:T(8,128)S(1)} %copy-done.3, bf16[3600,128]{1,0:T(8,128)(2,1)} %collective-permute-done.10), kind=kLoop, calls=%fused_computation.2 | loop fusion | flops 2304000 | bytes 4608000 | tf_op jit(solution)/shard_map/convert_element_type | solution.py:594
  213.0 4.8 %collective-permute-start.15 = (bf16[3600,128]{1,0:T(8,128)(2,1)}, bf16[3600,128]{1,0:T(8,128)(2,1)}, u32[]{:S(2)}, u32[]{:S(2)}) collective-permute-start(bf16[3600,128]{1,0:T(8,128)(2,1)} %add_convert_fusion.1), channel_id=1, source_target_pairs={{8,16},{12,20},{16,8},{20,12},{9,17},{13,21},{17,9},{21,13},{10,18... | collective-permute-start | bytes 2764808 | tf_op jit(solution)/shard_map/ppermute | solution.py:533
  220.6 9.1 %collective-permute-done.17 = bf16[3600,128]{1,0:T(8,128)(2,1)} collective-permute-done((bf16[3600,128]{1,0:T(8,128)(2,1)}, bf16[3600,128]{1,0:T(8,128)(2,1)}, u32[]{:S(2)}, u32[]{:S(2)}) %collective-permute-start.17) | collective-permute-done | bytes 921632 | tf_op jit(solution)/shard_map/ppermute | solution.py:533
  229.6 4.0 %collective-permute-done.15 = bf16[3600,128]{1,0:T(8,128)(2,1)} collective-permute-done((bf16[3600,128]{1,0:T(8,128)(2,1)}, bf16[3600,128]{1,0:T(8,128)(2,1)}, u32[]{:S(2)}, u32[]{:S(2)}) %collective-permute-start.15) | collective-permute-done | bytes 921632 | tf_op jit(solution)/shard_map/ppermute | solution.py:533
  233.6 3.2 %convert_add_fusion = f32[3600,128]{1,0:T(8,128)} fusion(bf16[3600,128]{1,0:T(8,128)(2,1)} %collective-permute-done.17, bf16[3600,128]{1,0:T(8,128)(2,1)} %collective-permute-done.15, f32[3600,128]{1,0:T(8,128)S(1)} %copy-done.4, bf16[3600,128]{1,0:T(8,128)(2,1)S(1)} %collective-permute-done.12), kind=kLoop, calls=%fused_computation | loop fusion | flops 2764800 | bytes 6451200 | tf_op jit(solution)/shard_map/add | solution.py:598
  (65 shorter events, 26.6 us)
Async XLA Ops:
  0.6 14.9 %copy-start = (f32[16,128]{1,0:T(8,128)S(1)}, f32[16,128]{1,0:T(8,128)}, u32[]{:S(2)}) copy-start(f32[16,128]{1,0:T(8,128)} %param.17) | copy-start | bytes 24580
  3.6 26.0 %collective-permute-start.2 = (bf16[3600,128]{1,0:T(8,128)(2,1)}, bf16[3600,128]{1,0:T(8,128)(2,1)S(1)}, u32[]{:S(2)}, u32[]{:S(2)}) collective-permute-start(bf16[3600,128]{1,0:T(8,128)(2,1)} %get-tuple-element.36.refs_9_), channel_id=1, source_target_pairs={{0,4},{4,0},{8,12},{12,8},{16,20},{20,16},{24,28},{28,24},{1,5},{5... | collective-permute-start | bytes 2764808 | tf_op jit(solution)/shard_map/ppermute | solution.py:529
  5.1 24.5 %collective-permute-start.1 = (bf16[3600,128]{1,0:T(8,128)(2,1)}, bf16[3600,128]{1,0:T(8,128)(2,1)S(1)}, u32[]{:S(2)}, u32[]{:S(2)}) collective-permute-start(bf16[3600,128]{1,0:T(8,128)(2,1)} %get-tuple-element.36.refs_9_), channel_id=1, source_target_pairs={{8,16},{12,20},{16,8},{20,12},{9,17},{13,21},{17,9},{21,13},{10,18... | collective-permute-start | bytes 2764808 | tf_op jit(solution)/shard_map/ppermute | solution.py:533
  8.6 21.9 %collective-permute-start = (bf16[3600,128]{1,0:T(8,128)(2,1)}, bf16[3600,128]{1,0:T(8,128)(2,1)S(1)}, u32[]{:S(2)}, u32[]{:S(2)}) collective-permute-start(bf16[3600,128]{1,0:T(8,128)(2,1)} %get-tuple-element.36.refs_9_), channel_id=1, source_target_pairs={{0,8},{4,12},{8,0},{12,4},{16,24},{20,28},{24,16},{28,20},{1,9},{5... | collective-permute-start | bytes 2764808 | tf_op jit(solution)/shard_map/ppermute | solution.py:533
  29.6 23.7 %copy-start.8 = (bf16[3600,128]{1,0:T(8,128)(2,1)}, bf16[3600,128]{1,0:T(8,128)(2,1)S(1)}, u32[]{:S(2)}) copy-start(bf16[3600,128]{1,0:T(8,128)(2,1)S(1)} %collective-permute-done.2.refs_10_) | copy-start | bytes 2764804
  30.5 22.8 %copy-start.9 = (bf16[3600,128]{1,0:T(8,128)(2,1)}, bf16[3600,128]{1,0:T(8,128)(2,1)S(1)}, u32[]{:S(2)}) copy-start(bf16[3600,128]{1,0:T(8,128)(2,1)S(1)} %collective-permute-done.refs_11_) | copy-start | bytes 2764804
  30.5 22.8 %collective-permute-start.4 = (bf16[3600,128]{1,0:T(8,128)(2,1)S(1)}, bf16[3600,128]{1,0:T(8,128)(2,1)S(1)}, u32[]{:S(2)}, u32[]{:S(2)}) collective-permute-start(bf16[3600,128]{1,0:T(8,128)(2,1)S(1)} %collective-permute-done.1), channel_id=1, source_target_pairs={{8,0},{12,4},{16,24},{20,28},{9,1},{13,5},{17,25},{21,29},{10,2},{... | collective-permute-start | bytes 2764808 | tf_op jit(solution)/shard_map/ppermute | solution.py:533
  33.6 21.1 %collective-permute-start.5 = (bf16[3600,128]{1,0:T(8,128)(2,1)S(1)}, bf16[3600,128]{1,0:T(8,128)(2,1)S(1)}, u32[]{:S(2)}, u32[]{:S(2)}) collective-permute-start(bf16[3600,128]{1,0:T(8,128)(2,1)S(1)} %collective-permute-done.refs_11_), channel_id=1, source_target_pairs={{0,4},{4,0},{8,12},{12,8},{16,20},{20,16},{24,28},{28,24},{1,5},{5... | collective-permute-start | bytes 2764808 | tf_op jit(solution)/shard_map/ppermute | solution.py:529
  34.2 22.7 %collective-permute-start.3 = (bf16[3600,128]{1,0:T(8,128)(2,1)S(1)}, bf16[3600,128]{1,0:T(8,128)(2,1)S(1)}, u32[]{:S(2)}, u32[]{:S(2)}) collective-permute-start(bf16[3600,128]{1,0:T(8,128)(2,1)S(1)} %collective-permute-done.refs_11_), channel_id=1, source_target_pairs={{8,16},{12,20},{16,8},{20,12},{9,17},{13,21},{17,9},{21,13},{10,18... | collective-permute-start | bytes 2764808 | tf_op jit(solution)/shard_map/ppermute | solution.py:533
  54.8 21.9 %copy-start.10 = (bf16[3600,128]{1,0:T(8,128)(2,1)}, bf16[3600,128]{1,0:T(8,128)(2,1)S(1)}, u32[]{:S(2)}) copy-start(bf16[3600,128]{1,0:T(8,128)(2,1)S(1)} %collective-permute-done.5.refs_12_) | copy-start | bytes 2764804
  57.1 19.5 %copy-start.6 = (bf16[3600,128]{1,0:T(8,128)(2,1)}, bf16[3600,128]{1,0:T(8,128)(2,1)S(1)}, u32[]{:S(2)}) copy-start(bf16[3600,128]{1,0:T(8,128)(2,1)S(1)} %add.86.refs_9_) | copy-start | bytes 2764804
  57.2 20.1 %collective-permute-start.7 = (bf16[3600,128]{1,0:T(8,128)(2,1)S(1)}, bf16[3600,128]{1,0:T(8,128)(2,1)S(1)}, u32[]{:S(2)}, u32[]{:S(2)}) collective-permute-start(bf16[3600,128]{1,0:T(8,128)(2,1)S(1)} %add.86.refs_9_), channel_id=1, source_target_pairs={{0,4},{4,0},{8,12},{12,8},{16,20},{20,16},{24,28},{28,24},{1,5},{5... | collective-permute-start | bytes 2764808 | tf_op jit(solution)/shard_map/ppermute | solution.py:529
  58.7 18.6 %collective-permute-start.6 = (bf16[3600,128]{1,0:T(8,128)(2,1)S(1)}, bf16[3600,128]{1,0:T(8,128)(2,1)S(1)}, u32[]{:S(2)}, u32[]{:S(2)}) collective-permute-start(bf16[3600,128]{1,0:T(8,128)(2,1)S(1)} %collective-permute-done.3), channel_id=1, source_target_pairs={{8,0},{12,4},{16,24},{20,28},{9,1},{13,5},{17,25},{21,29},{10,2},{... | collective-permute-start | bytes 2764808 | tf_op jit(solution)/shard_map/ppermute | solution.py:533
  77.2 12.3 %copy-start.11 = (bf16[3600,128]{1,0:T(8,128)(2,1)}, bf16[3600,128]{1,0:T(8,128)(2,1)S(1)}, u32[]{:S(2)}) copy-start(bf16[3600,128]{1,0:T(8,128)(2,1)S(1)} %collective-permute-done.7.refs_10_) | copy-start | bytes 2764804
  77.6 11.9 %copy-start.7 = (bf16[3600,128]{1,0:T(8,128)(2,1)}, bf16[3600,128]{1,0:T(8,128)(2,1)S(1)}, u32[]{:S(2)}) copy-start(bf16[3600,128]{1,0:T(8,128)(2,1)S(1)} %add.87.refs_11_) | copy-start | bytes 2764804
  77.6 23.4 %collective-permute-start.8 = (bf16[3600,128]{1,0:T(8,128)(2,1)S(1)}, bf16[3600,128]{1,0:T(8,128)(2,1)S(1)}, u32[]{:S(2)}, u32[]{:S(2)}) collective-permute-start(bf16[3600,128]{1,0:T(8,128)(2,1)S(1)} %add.87.refs_11_), channel_id=1, source_target_pairs={{0,4},{4,0},{8,12},{12,8},{16,20},{20,16},{24,28},{28,24},{1,5},{5... | collective-permute-start | bytes 2764808 | tf_op jit(solution)/shard_map/ppermute | solution.py:529
  136.3 22.4 %collective-permute-start.9 = (bf16[3600,128]{1,0:T(8,128)(2,1)}, bf16[3600,128]{1,0:T(8,128)(2,1)S(1)}, u32[]{:S(2)}, u32[]{:S(2)}) collective-permute-start(bf16[3600,128]{1,0:T(8,128)(2,1)} %class_sums.8), channel_id=1, source_target_pairs={{0,4},{4,0},{8,12},{12,8},{16,20},{20,16},{24,28},{28,24},{1,5},{5... | collective-permute-start | bytes 2764808 | tf_op jit(solution)/shard_map/ppermute | solution.py:529
  151.8 7.3 %copy-start.2 = (f32[3600,128]{1,0:T(8,128)S(1)}, f32[3600,128]{1,0:T(8,128)}, u32[]{:S(2)}) copy-start(f32[3600,128]{1,0:T(8,128)} %class_sums.11) | copy-start | bytes 5529604
  158.7 21.7 %collective-permute-start.10 = (bf16[3600,128]{1,0:T(8,128)(2,1)}, bf16[3600,128]{1,0:T(8,128)(2,1)}, u32[]{:S(2)}, u32[]{:S(2)}) collective-permute-start(bf16[3600,128]{1,0:T(8,128)(2,1)} %class_sums.9), channel_id=1, source_target_pairs={{0,4},{4,0},{8,12},{12,8},{16,20},{20,16},{24,28},{28,24},{1,5},{5... | collective-permute-start | bytes 2764808 | tf_op jit(solution)/shard_map/ppermute | solution.py:529
  160.2 23.4 %collective-permute-start.13 = (bf16[3600,128]{1,0:T(8,128)(2,1)}, bf16[3600,128]{1,0:T(8,128)(2,1)}, u32[]{:S(2)}, u32[]{:S(2)}) collective-permute-start(bf16[3600,128]{1,0:T(8,128)(2,1)} %fusion), channel_id=1, source_target_pairs={{0,8},{4,12},{24,16},{28,20},{1,9},{5,13},{25,17},{29,21},{2,10},{... | collective-permute-start | bytes 2764808 | tf_op jit(solution)/shard_map/ppermute | solution.py:533
  171.9 8.5 %copy-start.13 = (bf16[3600,128]{1,0:T(8,128)(2,1)S(1)}, bf16[3600,128]{1,0:T(8,128)(2,1)}, u32[]{:S(2)}) copy-start(bf16[3600,128]{1,0:T(8,128)(2,1)} %class_sums.10) | copy-start | bytes 2764804
  171.9 11.7 %copy-start.3 = (f32[3600,128]{1,0:T(8,128)S(1)}, f32[3600,128]{1,0:T(8,128)}, u32[]{:S(2)}) copy-start(f32[3600,128]{1,0:T(8,128)} %class_sums.12) | copy-start | bytes 5529604
  176.8 30.9 %copy-start.5 = (f32[3600,128]{1,0:T(8,128)S(1)}, f32[3600,128]{1,0:T(8,128)}, u32[]{:S(2)}) copy-start(f32[3600,128]{1,0:T(8,128)} %class_sums.14) | copy-start | bytes 5529604
  180.4 20.4 %collective-permute-start.11 = (bf16[3600,128]{1,0:T(8,128)(2,1)S(1)}, bf16[3600,128]{1,0:T(8,128)(2,1)S(1)}, u32[]{:S(2)}, u32[]{:S(2)}) collective-permute-start(bf16[3600,128]{1,0:T(8,128)(2,1)S(1)} %copy-done.13), channel_id=1, source_target_pairs={{0,4},{4,0},{8,12},{12,8},{16,20},{20,16},{24,28},{28,24},{1,5},{5... | collective-permute-start | bytes 2764808 | tf_op jit(solution)/shard_map/ppermute | solution.py:529
  185.6 22.2 %collective-permute-start.16 = (bf16[3600,128]{1,0:T(8,128)(2,1)S(1)}, bf16[3600,128]{1,0:T(8,128)(2,1)S(1)}, u32[]{:S(2)}, u32[]{:S(2)}) collective-permute-start(bf16[3600,128]{1,0:T(8,128)(2,1)S(1)} %add_convert_fusion.2), channel_id=1, source_target_pairs={{8,16},{12,20},{16,8},{20,12},{9,17},{13,21},{17,9},{21,13},{10,18... | collective-permute-start | bytes 2764808 | tf_op jit(solution)/shard_map/ppermute | solution.py:533
  187.9 22.7 %collective-permute-start.14 = (bf16[3600,128]{1,0:T(8,128)(2,1)S(1)}, bf16[3600,128]{1,0:T(8,128)(2,1)S(1)}, u32[]{:S(2)}, u32[]{:S(2)}) collective-permute-start(bf16[3600,128]{1,0:T(8,128)(2,1)S(1)} %add_convert_fusion.2), channel_id=1, source_target_pairs={{0,8},{4,12},{24,16},{28,20},{1,9},{5,13},{25,17},{29,21},{2,10},{... | collective-permute-start | bytes 2764808 | tf_op jit(solution)/shard_map/ppermute | solution.py:533
  200.8 19.7 %collective-permute-start.12 = (bf16[3600,128]{1,0:T(8,128)(2,1)}, bf16[3600,128]{1,0:T(8,128)(2,1)S(1)}, u32[]{:S(2)}, u32[]{:S(2)}) collective-permute-start(bf16[3600,128]{1,0:T(8,128)(2,1)} %class_sums.13), channel_id=1, source_target_pairs={{0,4},{4,0},{8,12},{12,8},{16,20},{20,16},{24,28},{28,24},{1,5},{5... | collective-permute-start | bytes 2764808 | tf_op jit(solution)/shard_map/ppermute | solution.py:529
  209.1 8.7 %copy-start.14 = (f32[56,128]{1,0:T(8,128)S(1)}, f32[56,128]{1,0:T(8,128)}, u32[]{:S(2)}) copy-start(f32[56,128]{1,0:T(8,128)} %get-tuple-element.55) | copy-start | bytes 86020
  209.1 24.5 %copy-start.4 = (f32[3600,128]{1,0:T(8,128)S(1)}, f32[3600,128]{1,0:T(8,128)}, u32[]{:S(2)}) copy-start(f32[3600,128]{1,0:T(8,128)} %class_sums.15) | copy-start | bytes 5529604
  209.1 20.6 %collective-permute-start.17 = (bf16[3600,128]{1,0:T(8,128)(2,1)}, bf16[3600,128]{1,0:T(8,128)(2,1)}, u32[]{:S(2)}, u32[]{:S(2)}) collective-permute-start(bf16[3600,128]{1,0:T(8,128)(2,1)} %add_convert_fusion), channel_id=1, source_target_pairs={{0,8},{4,12},{8,0},{12,4},{16,24},{20,28},{24,16},{28,20},{1,9},{5... | collective-permute-start | bytes 2764808 | tf_op jit(solution)/shard_map/ppermute | solution.py:533
  213.0 20.6 %collective-permute-start.15 = (bf16[3600,128]{1,0:T(8,128)(2,1)}, bf16[3600,128]{1,0:T(8,128)(2,1)}, u32[]{:S(2)}, u32[]{:S(2)}) collective-permute-start(bf16[3600,128]{1,0:T(8,128)(2,1)} %add_convert_fusion.1), channel_id=1, source_target_pairs={{8,16},{12,20},{16,8},{20,12},{9,17},{13,21},{17,9},{21,13},{10,18... | collective-permute-start | bytes 2764808 | tf_op jit(solution)/shard_map/ppermute | solution.py:533
  218.5 18.3 %copy-start.1 = (f32[16,128]{1,0:T(8,128)S(1)}, f32[16,128]{1,0:T(8,128)}, u32[]{:S(2)}) copy-start(f32[16,128]{1,0:T(8,128)} %param.17) | copy-start | bytes 24580
  (2 other events, 7.7 us)

commit v5 on v4

--- a/solution.py
+++ b/solution.py
@@ -60,30 +60,33 @@
 
 
 def base_kernel(shift_ref, part_ref, turns_ref, base_ref):
-    p = pl.program_id(0)
-    sx = shift_ref[0, p].astype(f32)
-    sy = shift_ref[1, p].astype(f32)
+    here, _, angles, _ = part_ref.shape
     chunk = 32
-
-    def turn(n, carry):
-        rows = pl.ds(pl.multiple_of(n * chunk, chunk), chunk)
-        cosine, sine_part = cos_sin_of_turns(sx * turns_ref[0, rows, :] + sy * turns_ref[1, rows, :])
-        re = part_ref[0, 0, rows, :].astype(f32)
-        im = part_ref[0, 1, rows, :].astype(f32)
-        base_ref[0, 0, rows, :] = re * cosine + im * sine_part
-        base_ref[0, 1, rows, :] = im * cosine - re * sine_part
-        return carry
-
-    lax.fori_loop(0, part_ref.shape[2] // chunk, turn, 0)
+    for q in range(here):
+        p = pl.program_id(0) * here + q
+        sx = shift_ref[0, p].astype(f32)
+        sy = shift_ref[1, p].astype(f32)
+
+        def turn(n, carry):
+            rows = pl.ds(pl.multiple_of(n * chunk, chunk), chunk)
+            cosine, sine_part = cos_sin_of_turns(sx * turns_ref[0, rows, :] + sy * turns_ref[1, rows, :])
+            re = part_ref[q, 0, rows, :].astype(f32)
+            im = part_ref[q, 1, rows, :].astype(f32)
+            base_ref[q, 0, rows, :] = re * cosine + im * sine_part
+            base_ref[q, 1, rows, :] = im * cosine - re * sine_part
+            return carry
+
+        lax.fori_loop(0, angles // chunk, turn, 0)
 
 
 def make_base(particles, prior_shift):
     count, _, angles, cycles = particles.shape
     turns, _ = shift_tables(angles, cycles)
-    image = pl.BlockSpec((1, 2, angles, cycles), lambda p: (p, 0, 0, 0))
+    here = count // 2
+    image = pl.BlockSpec((here, 2, angles, cycles), lambda p: (p, 0, 0, 0))
     return pl.pallas_call(
         base_kernel,
-        grid=(count,),
+        grid=(2,),
         in_specs=[
             pl.BlockSpec(memory_space=pltpu.SMEM),
             image,
@@ -98,33 +101,37 @@
 
 def spectra_kernel(base_ref, ctf_ref, table_ref, *refs, per_step):
     factor_refs, refs = refs[: 2 * per_step], refs[2 * per_step :]
-    out_ref, data_ref, re_ref, im_ref = refs[-4:]
+    chunks = ROWS // 2
+    out_ref, turn_ref, re_ref, im_ref = refs[-4 - chunks : -chunks]
+    data_refs = refs[-chunks:]
     count, _, angles, cycles = base_ref.shape
     chunk = 32
 
     for g in range(per_step):
         x_ref, y_ref = factor_refs[2 * g], factor_refs[2 * g + 1]
-
-        def shift(n, carry):
-            rows = pl.ds(pl.multiple_of(n * chunk, chunk), chunk)
-            low = pl.ds(pl.multiple_of(angles + n * chunk, chunk), chunk)
+        for start in range(0, angles, chunk):
+            rows = slice(start, start + chunk)
             xr, xi = x_ref[0, 0, 0, rows, :], x_ref[0, 0, 1, rows, :]
             yr, yi = y_ref[0, 0, 0, rows, :], y_ref[0, 0, 1, rows, :]
-            tr = xr * yr - xi * yi
-            ti = xr * yi + xi * yr
-            for p in range(count):
+            turn_ref[g, 0, rows, :] = xr * yr - xi * yi
+            turn_ref[g, 1, rows, :] = xr * yi + xi * yr
+
+    def shift(n):
+        for j in range(2):
+            g, p = (2 * n + j) // count, (2 * n + j) % count
+            lanes = slice(j * cycles, (j + 1) * cycles)
+            for start in range(0, angles, chunk):
+                rows = slice(start, start + chunk)
+                tr, ti = turn_ref[g, 0, rows, :], turn_ref[g, 1, rows, :]
                 gr, gi = base_ref[p, 0, rows, :], base_ref[p, 1, rows, :]
-                lanes = pl.ds((g * count + p) * cycles, cycles)
-                data_ref[rows, lanes] = (gr * tr - gi * ti).astype(bf16)
-                data_ref[low, lanes] = (gr * ti + gi * tr).astype(bf16)
-            return carry
-
-        lax.fori_loop(0, angles // chunk, shift, 0)
-
-    for n in range(ROWS // 2):
-        spectrum = jnp.dot(
-            table_ref[...], data_ref[:, n * 2 * cycles : (n + 1) * 2 * cycles], preferred_element_type=f32
-        )
+                data_refs[n][rows, lanes] = (gr * tr - gi * ti).astype(bf16)
+                data_refs[n][angles + start : angles + start + chunk, lanes] = (gr * ti + gi * tr).astype(bf16)
+
+    shift(0)
+    for n in range(chunks):
+        if n + 1 < chunks:
+            shift(n + 1)
+        spectrum = jnp.dot(table_ref[...], data_refs[n][...], preferred_element_type=f32)
         for j in range(2):
             row = 2 * n + j
             ctf_row = ctf_ref[row % count, :][None, :]
@@ -168,10 +175,11 @@
         out_specs=pl.BlockSpec((angles, ROWS, 2 * cycles), lambda i: (0, i + first, 0)),
         out_shape=jax.ShapeDtypeStruct((angles, steps * ROWS, 2 * cycles), bf16),
         scratch_shapes=[
-            pltpu.VMEM((2 * angles, ROWS * cycles), bf16),
+            pltpu.VMEM((per_step, 2, angles, cycles), f32),
             pltpu.VMEM((angles * APART, cycles), f32),
             pltpu.VMEM((angles * APART, cycles), f32),
-        ],
+        ]
+        + [pltpu.VMEM((2 * angles, 2 * cycles), bf16)] * (ROWS // 2),
         input_output_aliases={} if before is None else {3 + 2 * per_step: 0},
         compiler_params=pltpu.CompilerParams(vmem_limit_bytes=VMEM_LIMIT),
         name="spectra",
@@ -537,7 +545,7 @@
     index = lax.axis_index("dp")
     line, side = index // 2, index % 2
     _, steps = spectra_steps(base.shape[0])
-    cuts = [0, 3 * steps // 13, 7 * steps // 13, 11 * steps // 13, steps]
+    cuts = [0, 2 * steps // 13, 6 * steps // 13, 10 * steps // 13, steps]
 
     own_crossed = across(piece)
     near = along(piece, ((0, 1), (1, 0), (2, 3), (3, 2)))
@@ -624,11 +632,11 @@
     queries = weighted.shape[1]
     weighted = weighted.reshape(slots, ROTS, queries, 2 * cycles)
 
-    half = slots // 2
+    early = 3 * slots // 4
     part = lax.axis_index("cls")
-    corr, power = correlate(slot_of[:half], weighted, pieces[:half], classes, part)
+    corr, power = correlate(slot_of[:early], weighted, pieces[:early], classes, part)
     weights, stat, share = correlate(
-        slot_of[half:], weighted, pieces[half:], classes, part, corr, power, ctf_rows, lax.axis_size("cls")
+        slot_of[early:], weighted, pieces[early:], classes, part, corr, power, ctf_rows, lax.axis_size("cls")
     )
     shares = lax.psum(share, "cls")
     back, evidence, posterior = make_back(weights, stat, shares, offsets, queries)

time: 238 us -> 241 us (1.013); the launches traced: 237 us -> 237 us
  Pallas kernels: 142 us -> 132 us
  starting transfers between devices: 26.7 us -> 31.7 us
  waiting for transfers between devices: 47.1 us -> 52.1 us
    ppermute x10, waiting for transfers between devices: 27.1 us -> 45.2 us  [along(): lax.ppermute(piece, 'dp', [(2 * a + x, 2 * b + x) for a, b in pairs for x...]
    ppermute x8, waiting for transfers between devices: 19.9 us -> 6.88 us  [across(): return lax.ppermute(piece, 'dp', [(d, d ^ 1) for d in range(8)])]
    pallas_call x4, Pallas kernels: 56.8 us -> 50 us  [make_spectra(): pl.pallas_call(functools.partial(spectra_kernel, per_step=per_step), grid...]
    ppermute x8, starting transfers between devices: 6.71 us -> 10 us  [across(): return lax.ppermute(piece, 'dp', [(d, d ^ 1) for d in range(8)])]
  transfers between devices with their start and end apart: 18 -> 18, of which waited for: 14 -> 14; matrix products, arithmetic and copies ran while one was open for 4% -> 3% of each run, Pallas kernels for 47% -> 44%
where the time goes in v5:
time: 241 us; the launch traced here: 237 us
  Pallas kernels  132 us (55%)
  waiting for transfers between devices  52.1 us (22%)
  starting transfers between devices  31.7 us (13%)
  other arithmetic  10.6 us (4%)
  blocking collectives  6.23 us (3%)
  local copies, waits for them, and re-layouts  2.85 us (1%)
    pallas_call x4, Pallas kernels, make_spectra(): pl.pallas_call(functools.partial(spectra_kernel, per_step=per_step), grid...  50 us
    ppermute x10, waiting for transfers between devices, along(): lax.ppermute(piece, 'dp', [(2 * a + x, 2 * b + x) for a, b in pairs for x...  45.2 us
    pallas_call x8, Pallas kernels, class_sums_of(): pl.pallas_call(functools.partial(sums_kernel, classes=classes), grid_spec...  40.3 us
    pallas_call x2, Pallas kernels, correlate(): pl.pallas_call(functools.partial(correlate_kernel, slots=slots, classes=c...  28.6 us
    ppermute x10, starting transfers between devices, along(): lax.ppermute(piece, 'dp', [(2 * a + x, 2 * b + x) for a, b in pairs for x...  21.6 us
    ppermute x8, starting transfers between devices, across(): return lax.ppermute(piece, 'dp', [(d, d ^ 1) for d in range(8)])  10 us
    ppermute x8, waiting for transfers between devices, across(): return lax.ppermute(piece, 'dp', [(d, d ^ 1) for d in range(8)])  6.88 us
    psum x1, blocking collectives, local(): shares = lax.psum(share, 'cls')  6.23 us
  transfers between devices with their start and end apart: 18, of which 14 were waited for; matrix products, arithmetic and copies ran while one was open for 3% of the time, Pallas kernels for 44%

profile of v5, /device:TPU:8, one launch (start us, length us, event | category | flops | bytes accessed | tf_op | source)
XLA Modules:
  0.0 237.0 jit_solution(6379582604398734115)
XLA Ops:
  0.7 3.0 %turn_references.1 = (bf16[3600,128]{1,0:T(8,128)(2,1)}, f32[56,128]{1,0:T(8,128)}) custom-call(s32[1]{0:T(128)} %bitcast.4.first_ref, s32[50]{0:T(128)} %offset_ref.1, bf16[3600,128]{1,0:T(8,128)(2,1)} %bitcast.44), custom_call_target="tpu_custom_call" | custom-call | tf_op jit(solution)/shard_map/turn_references/pallas_call | solution.py:251
  3.6 5.0 %collective-permute-start.1 = (bf16[3600,128]{1,0:T(8,128)(2,1)}, bf16[3600,128]{1,0:T(8,128)(2,1)S(1)}, u32[]{:S(2)}, u32[]{:S(2)}) collective-permute-start(bf16[3600,128]{1,0:T(8,128)(2,1)} %get-tuple-element.36.refs_13_), channel_id=1, source_target_pairs={{8,16},{12,20},{16,8},{20,12},{9,17},{13,21},{17,9},{21,13},{10,18... | collective-permute-start | bytes 2764808 | tf_op jit(solution)/shard_map/ppermute | solution.py:541
  10.2 4.7 %centre.1.base_ref = f32[8,2,288,128]{3,2,1,0:T(8,128)} custom-call(s32[2,8]{1,0:T(2,128)} %bitcast.45, bf16[8,2,288,128]{3,2,1,0:T(8,128)(2,1)} %part_ref.1, f32[2,288,128]{2,1,0:T(8,128)} %constant.49.clone.turns_ref), custom_call_target="tpu_custom_call" | custom-call | tf_op jit(solution)/shard_map/centre/pallas_call | solution.py:87
  15.7 9.2 %spectra.4.refs_4_ = bf16[288,208,256]{2,1,0:T(8,128)(2,1)} custom-call(f32[8,2,288,128]{3,2,1,0:T(8,128)} %centre.1.base_ref, f32[8,128]{1,0:T(8,128)} %fusion.1.ctf_ref.refs_9_, bf16[576,576]{1,0:T(8,128)(2,1)} %constant.50.clone.table_ref, f32[2,5,2,288,128]{4,3,2,1,0:T(8,128)} %constant.51.clone.refs_0_.refs_1_.refs_2_.refs_3_, ...), custom_call_target="tpu_custom_call" | custom-call | tf_op jit(solution)/shard_map/spectra/pallas_call | solution.py:171
  26.0 3.0 %collective-permute-done.1 = bf16[3600,128]{1,0:T(8,128)(2,1)S(1)} collective-permute-done((bf16[3600,128]{1,0:T(8,128)(2,1)}, bf16[3600,128]{1,0:T(8,128)(2,1)S(1)}, u32[]{:S(2)}, u32[]{:S(2)}) %collective-permute-start.1) | collective-permute-done | bytes 921632 | tf_op jit(solution)/shard_map/ppermute | solution.py:541
  30.6 2.2 collective-permute-start.3
  35.7 14.6 %spectra.5.refs_4_ = bf16[288,208,256]{2,1,0:T(8,128)(2,1)} custom-call(f32[8,2,288,128]{3,2,1,0:T(8,128)} %centre.1.base_ref, f32[8,128]{1,0:T(8,128)} %fusion.1.ctf_ref.refs_9_, bf16[576,576]{1,0:T(8,128)(2,1)} %constant.50.clone.table_ref, f32[2,5,2,288,128]{4,3,2,1,0:T(8,128)} %constant.51.clone.refs_0_.refs_1_.refs_2_.refs_3_, ...), custom_call_target="tpu_custom_call", output_to_operand_aliasing={{}: (7, {})} | custom-call | tf_op jit(solution)/shard_map/spectra/pallas_call | solution.py:171
  50.3 2.9 %collective-permute-done.3 = bf16[3600,128]{1,0:T(8,128)(2,1)S(1)} collective-permute-done((bf16[3600,128]{1,0:T(8,128)(2,1)S(1)}, bf16[3600,128]{1,0:T(8,128)(2,1)S(1)}, u32[]{:S(2)}, u32[]{:S(2)}) %collective-permute-start.3) | collective-permute-done | bytes 921632 | tf_op jit(solution)/shard_map/ppermute | solution.py:541
  55.4 3.9 %collective-permute-start.6 = (bf16[3600,128]{1,0:T(8,128)(2,1)S(1)}, bf16[3600,128]{1,0:T(8,128)(2,1)S(1)}, u32[]{:S(2)}, u32[]{:S(2)}) collective-permute-start(bf16[3600,128]{1,0:T(8,128)(2,1)S(1)} %collective-permute-done.3), channel_id=1, source_target_pairs={{8,0},{12,4},{16,24},{20,28},{9,1},{13,5},{17,25},{21,29},{10,2},{... | collective-permute-start | bytes 2764808 | tf_op jit(solution)/shard_map/ppermute | solution.py:541
  59.3 14.5 %spectra.6.refs_4_ = bf16[288,208,256]{2,1,0:T(8,128)(2,1)} custom-call(f32[8,2,288,128]{3,2,1,0:T(8,128)} %centre.1.base_ref, f32[8,128]{1,0:T(8,128)} %fusion.1.ctf_ref.refs_9_, bf16[576,576]{1,0:T(8,128)(2,1)} %constant.50.clone.table_ref, f32[2,5,2,288,128]{4,3,2,1,0:T(8,128)} %constant.51.clone.refs_0_.refs_1_.refs_2_.refs_3_, ...), custom_call_target="tpu_custom_call", output_to_operand_aliasing={{}: (7, {})} | custom-call | tf_op jit(solution)/shard_map/spectra/pallas_call | solution.py:171
  77.9 11.8 %spectra.7 = bf16[288,208,256]{2,1,0:T(8,128)(2,1)} custom-call(f32[8,2,288,128]{3,2,1,0:T(8,128)} %centre.1.base_ref, f32[8,128]{1,0:T(8,128)} %fusion.1.ctf_ref.refs_9_, bf16[576,576]{1,0:T(8,128)(2,1)} %constant.50.clone.table_ref, f32[2,5,2,288,128]{4,3,2,1,0:T(8,128)} %constant.51.clone.refs_0_.refs_1_.refs_2_.refs_3_, ...), custom_call_target="tpu_custom_call", output_to_operand_aliasing={{}: (7, {})} | custom-call | tf_op jit(solution)/shard_map/spectra/pallas_call | solution.py:171
  89.7 15.2 %correlate.1 = (f32[36,112,256]{2,1,0:T(8,128)}, f32[56,128]{1,0:T(8,128)}) custom-call(s32[1]{0:T(128)} %bitcast.8.refs_0_.slot_ref, s32[1]{0:T(128)} %bitcast.9.refs_1_, s32[1]{0:T(128)} %bitcast.10.refs_2_.slot_ref, s32[1]{0:T(128)} %bitcast.11.refs_3_, s32[1]{0:T(128)} %bitcast.12.refs_4_.slot_ref, s32[1]{0:T(128)} %bitcast.13.refs_5_, ...), custom_call_target="tpu_custom_call" | custom-call | tf_op jit(solution)/shard_map/correlate/pallas_call | solution.py:417
  105.8 13.4 %scores.1 = (f32[36,56,256]{2,1,0:T(8,128)}, f32[64,128]{1,0:T(8,128)}, f32[4,2,128]{2,1,0:T(2,128)}) custom-call(s32[1]{0:T(128)} %bitcast.refs_0_.slot_ref, s32[1]{0:T(128)} %bitcast.1.refs_1_, s32[1]{0:T(128)} %bitcast.2.refs_6_.refs_2_, bf16[8,36,208,256]{3,2,1,0:T(8,128)(2,1)} %bitcast.33, bf16[8,36,208,256]{3,2,1,0:T(8,128)(2,1)} %bitcast.34, ...), custom_call_target="tpu_custom_call" | custom-call | tf_op jit(solution)/shard_map/scores/pallas_call | solution.py:417
  119.2 6.2 %psum.7.share_ref = f32[4,2,128]{2,1,0:T(2,128)} all-reduce(f32[4,2,128]{2,1,0:T(2,128)} %get-tuple-element.52), channel_id=1, replica_groups=mesh['dp'=8,'cls'=4] {'cls'}, use_global_device_ids=true, to_apply=%region_0.1 | all-reduce | flops 1024 | bytes 8192 | tf_op jit(solution)/shard_map/psum | solution.py:641
  125.4 5.4 %back.1 = (bf16[36,112,208]{2,1,0:T(8,128)(2,1)}, f32[8,128]{1,0:T(8,128)}, f32[56,128]{1,0:T(8,128)}) custom-call(f32[36,56,256]{2,1,0:T(8,128)} %get-tuple-element.50.weight_ref, f32[64,128]{1,0:T(8,128)} %get-tuple-element.51.stat_ref, f32[4,2,128]{2,1,0:T(2,128)} %psum.7.share_ref, f32[56,128]{1,0:T(8,128)} %get-tuple-element.53.offset_ref), custom_call_target="tpu_custom_call" | custom-call | tf_op jit(solution)/shard_map/back/pallas_call | solution.py:483
  130.9 4.8 %class_sums.8 = bf16[3600,128]{1,0:T(8,128)(2,1)} custom-call(s32[1]{0:T(128)} %bitcast.16.slot_ref, bf16[36,112,208]{2,1,0:T(8,128)(2,1)} %get-tuple-element.56.back_ref, bf16[8,36,208,256]{3,2,1,0:T(8,128)(2,1)} %bitcast.35, f32[56,128]{1,0:T(8,128)} %get-tuple-element.53.offset_ref), custom_call_target="tpu_custom_call" | custom-call | tf_op jit(solution)/shard_map/class_sums/pallas_call | solution.py:517
  136.2 5.2 %class_sums.12 = f32[3600,128]{1,0:T(8,128)} custom-call(s32[1]{0:T(128)} %bitcast.12.refs_4_.slot_ref, bf16[36,112,208]{2,1,0:T(8,128)(2,1)} %get-tuple-element.56.back_ref, bf16[8,36,208,256]{3,2,1,0:T(8,128)(2,1)} %bitcast.36, f32[56,128]{1,0:T(8,128)} %get-tuple-element.53.offset_ref), custom_call_target="tpu_custom_call" | custom-call | tf_op jit(solution)/shard_map/class_sums/pallas_call | solution.py:517
  141.4 5.2 %class_sums.11 = f32[3600,128]{1,0:T(8,128)} custom-call(s32[1]{0:T(128)} %bitcast.refs_0_.slot_ref, bf16[36,112,208]{2,1,0:T(8,128)(2,1)} %get-tuple-element.56.back_ref, bf16[8,36,208,256]{3,2,1,0:T(8,128)(2,1)} %bitcast.37, f32[56,128]{1,0:T(8,128)} %get-tuple-element.53.offset_ref), custom_call_target="tpu_custom_call" | custom-call | tf_op jit(solution)/shard_map/class_sums/pallas_call | solution.py:517
  146.6 4.8 %class_sums.10 = bf16[3600,128]{1,0:T(8,128)(2,1)} custom-call(s32[1]{0:T(128)} %bitcast.18.slot_ref, bf16[36,112,208]{2,1,0:T(8,128)(2,1)} %get-tuple-element.56.back_ref, bf16[8,36,208,256]{3,2,1,0:T(8,128)(2,1)} %bitcast.38, f32[56,128]{1,0:T(8,128)} %get-tuple-element.53.offset_ref), custom_call_target="tpu_custom_call" | custom-call | tf_op jit(solution)/shard_map/class_sums/pallas_call | solution.py:517
  151.4 5.0 %class_sums.9 = bf16[3600,128]{1,0:T(8,128)(2,1)} custom-call(s32[1]{0:T(128)} %bitcast.17.slot_ref, bf16[36,112,208]{2,1,0:T(8,128)(2,1)} %get-tuple-element.56.back_ref, bf16[8,36,208,256]{3,2,1,0:T(8,128)(2,1)} %bitcast.39, f32[56,128]{1,0:T(8,128)} %get-tuple-element.53.offset_ref), custom_call_target="tpu_custom_call" | custom-call | tf_op jit(solution)/shard_map/class_sums/pallas_call | solution.py:517
  161.4 5.2 %class_sums.15 = f32[3600,128]{1,0:T(8,128)} custom-call(s32[1]{0:T(128)} %bitcast.8.refs_0_.slot_ref, bf16[36,112,208]{2,1,0:T(8,128)(2,1)} %get-tuple-element.56.back_ref, bf16[8,36,208,256]{3,2,1,0:T(8,128)(2,1)} %bitcast.40, f32[56,128]{1,0:T(8,128)} %get-tuple-element.53.offset_ref), custom_call_target="tpu_custom_call" | custom-call | tf_op jit(solution)/shard_map/class_sums/pallas_call | solution.py:517
  166.6 5.2 %class_sums.14 = f32[3600,128]{1,0:T(8,128)} custom-call(s32[1]{0:T(128)} %bitcast.10.refs_2_.slot_ref, bf16[36,112,208]{2,1,0:T(8,128)(2,1)} %get-tuple-element.56.back_ref, bf16[8,36,208,256]{3,2,1,0:T(8,128)(2,1)} %bitcast.41, f32[56,128]{1,0:T(8,128)} %get-tuple-element.53.offset_ref), custom_call_target="tpu_custom_call" | custom-call | tf_op jit(solution)/shard_map/class_sums/pallas_call | solution.py:517
  171.8 5.0 %class_sums.13 = bf16[3600,128]{1,0:T(8,128)(2,1)} custom-call(s32[1]{0:T(128)} %bitcast.19.slot_ref, bf16[36,112,208]{2,1,0:T(8,128)(2,1)} %get-tuple-element.56.back_ref, bf16[8,36,208,256]{3,2,1,0:T(8,128)(2,1)} %bitcast.42, f32[56,128]{1,0:T(8,128)} %get-tuple-element.53.offset_ref), custom_call_target="tpu_custom_call" | custom-call | tf_op jit(solution)/shard_map/class_sums/pallas_call | solution.py:517
  176.7 3.1 %collective-permute-done.10 = bf16[3600,128]{1,0:T(8,128)(2,1)} collective-permute-done((bf16[3600,128]{1,0:T(8,128)(2,1)}, bf16[3600,128]{1,0:T(8,128)(2,1)}, u32[]{:S(2)}, u32[]{:S(2)}) %collective-permute-start.10) | collective-permute-done | bytes 921632 | tf_op jit(solution)/shard_map/ppermute | solution.py:537
  179.8 3.5 %collective-permute-done.13 = bf16[3600,128]{1,0:T(8,128)(2,1)} collective-permute-done((bf16[3600,128]{1,0:T(8,128)(2,1)}, bf16[3600,128]{1,0:T(8,128)(2,1)}, u32[]{:S(2)}, u32[]{:S(2)}) %collective-permute-start.13) | collective-permute-done | bytes 921632 | tf_op jit(solution)/shard_map/ppermute | solution.py:541
  186.8 3.0 %collective-permute-start.16 = (bf16[3600,128]{1,0:T(8,128)(2,1)S(1)}, bf16[3600,128]{1,0:T(8,128)(2,1)S(1)}, u32[]{:S(2)}, u32[]{:S(2)}) collective-permute-start(bf16[3600,128]{1,0:T(8,128)(2,1)S(1)} %add_convert_fusion.2), channel_id=1, source_target_pairs={{8,16},{12,20},{16,8},{20,12},{9,17},{13,21},{17,9},{21,13},{10,18... | collective-permute-start | bytes 2764808 | tf_op jit(solution)/shard_map/ppermute | solution.py:541
  191.4 16.2 %collective-permute-done.14 = bf16[3600,128]{1,0:T(8,128)(2,1)S(1)} collective-permute-done((bf16[3600,128]{1,0:T(8,128)(2,1)S(1)}, bf16[3600,128]{1,0:T(8,128)(2,1)S(1)}, u32[]{:S(2)}, u32[]{:S(2)}) %collective-permute-start.14) | collective-permute-done | bytes 921632 | tf_op jit(solution)/shard_map/ppermute | solution.py:541
  207.7 2.4 %add_convert_fusion.1 = bf16[3600,128]{1,0:T(8,128)(2,1)} fusion(bf16[3600,128]{1,0:T(8,128)(2,1)S(1)} %collective-permute-done.14, f32[3600,128]{1,0:T(8,128)S(1)} %copy-done.3, bf16[3600,128]{1,0:T(8,128)(2,1)} %collective-permute-done.10), kind=kLoop, calls=%fused_computation.2 | loop fusion | flops 2304000 | bytes 4608000 | tf_op jit(solution)/shard_map/convert_element_type | solution.py:602
  210.1 3.2 %collective-permute-start.15 = (bf16[3600,128]{1,0:T(8,128)(2,1)}, bf16[3600,128]{1,0:T(8,128)(2,1)S(1)}, u32[]{:S(2)}, u32[]{:S(2)}) collective-permute-start(bf16[3600,128]{1,0:T(8,128)(2,1)} %add_convert_fusion.1), channel_id=1, source_target_pairs={{8,16},{12,20},{16,8},{20,12},{9,17},{13,21},{17,9},{21,13},{10,18... | collective-permute-start | bytes 2764808 | tf_op jit(solution)/shard_map/ppermute | solution.py:541
  217.9 13.7 %collective-permute-done.15 = bf16[3600,128]{1,0:T(8,128)(2,1)S(1)} collective-permute-done((bf16[3600,128]{1,0:T(8,128)(2,1)}, bf16[3600,128]{1,0:T(8,128)(2,1)S(1)}, u32[]{:S(2)}, u32[]{:S(2)}) %collective-permute-start.15) | collective-permute-done | bytes 921632 | tf_op jit(solution)/shard_map/ppermute | solution.py:541
  231.7 2.3 collective-permute-done.17
  233.9 3.1 %convert_add_fusion = f32[3600,128]{1,0:T(8,128)} fusion(bf16[3600,128]{1,0:T(8,128)(2,1)} %collective-permute-done.17, bf16[3600,128]{1,0:T(8,128)(2,1)S(1)} %collective-permute-done.15, f32[3600,128]{1,0:T(8,128)S(1)} %copy-done.4, bf16[3600,128]{1,0:T(8,128)(2,1)} %collective-permute-done.12), kind=kLoop, calls=%fused_computation | loop fusion | flops 2764800 | bytes 6451200 | tf_op jit(solution)/shard_map/add | solution.py:606
  (65 shorter events, 30.4 us)
Async XLA Ops:
  0.6 14.3 %copy-start = (f32[16,128]{1,0:T(8,128)S(1)}, f32[16,128]{1,0:T(8,128)}, u32[]{:S(2)}) copy-start(f32[16,128]{1,0:T(8,128)} %param.17) | copy-start | bytes 24580
  3.6 22.4 %collective-permute-start = (bf16[3600,128]{1,0:T(8,128)(2,1)}, bf16[3600,128]{1,0:T(8,128)(2,1)S(1)}, u32[]{:S(2)}, u32[]{:S(2)}) collective-permute-start(bf16[3600,128]{1,0:T(8,128)(2,1)} %get-tuple-element.36.refs_13_), channel_id=1, source_target_pairs={{0,8},{4,12},{8,0},{12,4},{16,24},{20,28},{24,16},{28,20},{1,9},{5... | collective-permute-start | bytes 2764808 | tf_op jit(solution)/shard_map/ppermute | solution.py:541
  3.6 25.4 %collective-permute-start.1 = (bf16[3600,128]{1,0:T(8,128)(2,1)}, bf16[3600,128]{1,0:T(8,128)(2,1)S(1)}, u32[]{:S(2)}, u32[]{:S(2)}) collective-permute-start(bf16[3600,128]{1,0:T(8,128)(2,1)} %get-tuple-element.36.refs_13_), channel_id=1, source_target_pairs={{8,16},{12,20},{16,8},{20,12},{9,17},{13,21},{17,9},{21,13},{10,18... | collective-permute-start | bytes 2764808 | tf_op jit(solution)/shard_map/ppermute | solution.py:541
  8.7 21.9 %collective-permute-start.2 = (bf16[3600,128]{1,0:T(8,128)(2,1)}, bf16[3600,128]{1,0:T(8,128)(2,1)S(1)}, u32[]{:S(2)}, u32[]{:S(2)}) collective-permute-start(bf16[3600,128]{1,0:T(8,128)(2,1)} %get-tuple-element.36.refs_13_), channel_id=1, source_target_pairs={{0,4},{4,0},{8,12},{12,8},{16,20},{20,16},{24,28},{28,24},{1,5},{5... | collective-permute-start | bytes 2764808 | tf_op jit(solution)/shard_map/ppermute | solution.py:537
  26.0 24.2 %copy-start.8 = (bf16[3600,128]{1,0:T(8,128)(2,1)}, bf16[3600,128]{1,0:T(8,128)(2,1)S(1)}, u32[]{:S(2)}) copy-start(bf16[3600,128]{1,0:T(8,128)(2,1)S(1)} %collective-permute-done.refs_15_) | copy-start | bytes 2764804
  30.6 19.7 %copy-start.9 = (bf16[3600,128]{1,0:T(8,128)(2,1)}, bf16[3600,128]{1,0:T(8,128)(2,1)S(1)}, u32[]{:S(2)}) copy-start(bf16[3600,128]{1,0:T(8,128)(2,1)S(1)} %collective-permute-done.2.refs_14_) | copy-start | bytes 2764804
  30.6 22.6 %collective-permute-start.3 = (bf16[3600,128]{1,0:T(8,128)(2,1)S(1)}, bf16[3600,128]{1,0:T(8,128)(2,1)S(1)}, u32[]{:S(2)}, u32[]{:S(2)}) collective-permute-start(bf16[3600,128]{1,0:T(8,128)(2,1)S(1)} %collective-permute-done.refs_15_), channel_id=1, source_target_pairs={{8,16},{12,20},{16,8},{20,12},{9,17},{13,21},{17,9},{21,13},{10,18... | collective-permute-start | bytes 2764808 | tf_op jit(solution)/shard_map/ppermute | solution.py:541
  32.8 20.8 %collective-permute-start.5 = (bf16[3600,128]{1,0:T(8,128)(2,1)S(1)}, bf16[3600,128]{1,0:T(8,128)(2,1)S(1)}, u32[]{:S(2)}, u32[]{:S(2)}) collective-permute-start(bf16[3600,128]{1,0:T(8,128)(2,1)S(1)} %collective-permute-done.refs_15_), channel_id=1, source_target_pairs={{0,4},{4,0},{8,12},{12,8},{16,20},{20,16},{24,28},{28,24},{1,5},{5... | collective-permute-start | bytes 2764808 | tf_op jit(solution)/shard_map/ppermute | solution.py:537
  34.3 19.5 %collective-permute-start.4 = (bf16[3600,128]{1,0:T(8,128)(2,1)S(1)}, bf16[3600,128]{1,0:T(8,128)(2,1)S(1)}, u32[]{:S(2)}, u32[]{:S(2)}) collective-permute-start(bf16[3600,128]{1,0:T(8,128)(2,1)S(1)} %collective-permute-done.1), channel_id=1, source_target_pairs={{8,0},{12,4},{16,24},{20,28},{9,1},{13,5},{17,25},{21,29},{10,2},{... | collective-permute-start | bytes 2764808 | tf_op jit(solution)/shard_map/ppermute | solution.py:541
  53.6 20.3 %copy-start.10 = (bf16[3600,128]{1,0:T(8,128)(2,1)}, bf16[3600,128]{1,0:T(8,128)(2,1)S(1)}, u32[]{:S(2)}) copy-start(bf16[3600,128]{1,0:T(8,128)(2,1)S(1)} %collective-permute-done.5.refs_16_) | copy-start | bytes 2764804
  54.1 19.8 %copy-start.6 = (bf16[3600,128]{1,0:T(8,128)(2,1)}, bf16[3600,128]{1,0:T(8,128)(2,1)S(1)}, u32[]{:S(2)}) copy-start(bf16[3600,128]{1,0:T(8,128)(2,1)S(1)} %add.84.refs_17_) | copy-start | bytes 2764804
  54.1 19.9 %collective-permute-start.7 = (bf16[3600,128]{1,0:T(8,128)(2,1)S(1)}, bf16[3600,128]{1,0:T(8,128)(2,1)S(1)}, u32[]{:S(2)}, u32[]{:S(2)}) collective-permute-start(bf16[3600,128]{1,0:T(8,128)(2,1)S(1)} %add.84.refs_17_), channel_id=1, source_target_pairs={{0,4},{4,0},{8,12},{12,8},{16,20},{20,16},{24,28},{28,24},{1,5},{5... | collective-permute-start | bytes 2764808 | tf_op jit(solution)/shard_map/ppermute | solution.py:537
  55.4 20.7 %collective-permute-start.6 = (bf16[3600,128]{1,0:T(8,128)(2,1)S(1)}, bf16[3600,128]{1,0:T(8,128)(2,1)S(1)}, u32[]{:S(2)}, u32[]{:S(2)}) collective-permute-start(bf16[3600,128]{1,0:T(8,128)(2,1)S(1)} %collective-permute-done.3), channel_id=1, source_target_pairs={{8,0},{12,4},{16,24},{20,28},{9,1},{13,5},{17,25},{21,29},{10,2},{... | collective-permute-start | bytes 2764808 | tf_op jit(solution)/shard_map/ppermute | solution.py:541
  73.9 15.7 %copy-start.11 = (bf16[3600,128]{1,0:T(8,128)(2,1)}, bf16[3600,128]{1,0:T(8,128)(2,1)S(1)}, u32[]{:S(2)}) copy-start(bf16[3600,128]{1,0:T(8,128)(2,1)S(1)} %collective-permute-done.7.refs_18_) | copy-start | bytes 2764804
  76.3 13.3 %copy-start.7 = (bf16[3600,128]{1,0:T(8,128)(2,1)}, bf16[3600,128]{1,0:T(8,128)(2,1)S(1)}, u32[]{:S(2)}) copy-start(bf16[3600,128]{1,0:T(8,128)(2,1)S(1)} %add.85.refs_5_) | copy-start | bytes 2764804
  76.3 28.6 %collective-permute-start.8 = (bf16[3600,128]{1,0:T(8,128)(2,1)S(1)}, bf16[3600,128]{1,0:T(8,128)(2,1)S(1)}, u32[]{:S(2)}, u32[]{:S(2)}) collective-permute-start(bf16[3600,128]{1,0:T(8,128)(2,1)S(1)} %add.85.refs_5_), channel_id=1, source_target_pairs={{0,4},{4,0},{8,12},{12,8},{16,20},{20,16},{24,28},{28,24},{1,5},{5... | collective-permute-start | bytes 2764808 | tf_op jit(solution)/shard_map/ppermute | solution.py:537
  135.7 22.4 %collective-permute-start.9 = (bf16[3600,128]{1,0:T(8,128)(2,1)}, bf16[3600,128]{1,0:T(8,128)(2,1)S(1)}, u32[]{:S(2)}, u32[]{:S(2)}) collective-permute-start(bf16[3600,128]{1,0:T(8,128)(2,1)} %class_sums.8), channel_id=1, source_target_pairs={{0,4},{4,0},{8,12},{12,8},{16,20},{20,16},{24,28},{28,24},{1,5},{5... | collective-permute-start | bytes 2764808 | tf_op jit(solution)/shard_map/ppermute | solution.py:537
  151.4 7.3 %copy-start.2 = (f32[3600,128]{1,0:T(8,128)S(1)}, f32[3600,128]{1,0:T(8,128)}, u32[]{:S(2)}) copy-start(f32[3600,128]{1,0:T(8,128)} %class_sums.11) | copy-start | bytes 5529604
  158.1 21.6 %collective-permute-start.10 = (bf16[3600,128]{1,0:T(8,128)(2,1)}, bf16[3600,128]{1,0:T(8,128)(2,1)}, u32[]{:S(2)}, u32[]{:S(2)}) collective-permute-start(bf16[3600,128]{1,0:T(8,128)(2,1)} %class_sums.9), channel_id=1, source_target_pairs={{0,4},{4,0},{8,12},{12,8},{16,20},{20,16},{24,28},{28,24},{1,5},{5... | collective-permute-start | bytes 2764808 | tf_op jit(solution)/shard_map/ppermute | solution.py:537
  159.9 23.4 %collective-permute-start.13 = (bf16[3600,128]{1,0:T(8,128)(2,1)}, bf16[3600,128]{1,0:T(8,128)(2,1)}, u32[]{:S(2)}, u32[]{:S(2)}) collective-permute-start(bf16[3600,128]{1,0:T(8,128)(2,1)} %fusion), channel_id=1, source_target_pairs={{0,8},{4,12},{24,16},{28,20},{1,9},{5,13},{25,17},{29,21},{2,10},{... | collective-permute-start | bytes 2764808 | tf_op jit(solution)/shard_map/ppermute | solution.py:541
  171.8 11.5 %copy-start.3 = (f32[3600,128]{1,0:T(8,128)S(1)}, f32[3600,128]{1,0:T(8,128)}, u32[]{:S(2)}) copy-start(f32[3600,128]{1,0:T(8,128)} %class_sums.12) | copy-start | bytes 5529604
  176.7 13.2 %copy-start.13 = (bf16[3600,128]{1,0:T(8,128)(2,1)S(1)}, bf16[3600,128]{1,0:T(8,128)(2,1)}, u32[]{:S(2)}) copy-start(bf16[3600,128]{1,0:T(8,128)(2,1)} %class_sums.10) | copy-start | bytes 2764804
  185.4 27.9 %copy-start.5 = (f32[3600,128]{1,0:T(8,128)S(1)}, f32[3600,128]{1,0:T(8,128)}, u32[]{:S(2)}) copy-start(f32[3600,128]{1,0:T(8,128)} %class_sums.14) | copy-start | bytes 5529604
  185.4 22.3 %collective-permute-start.14 = (bf16[3600,128]{1,0:T(8,128)(2,1)S(1)}, bf16[3600,128]{1,0:T(8,128)(2,1)S(1)}, u32[]{:S(2)}, u32[]{:S(2)}) collective-permute-start(bf16[3600,128]{1,0:T(8,128)(2,1)S(1)} %add_convert_fusion.2), channel_id=1, source_target_pairs={{0,8},{4,12},{24,16},{28,20},{1,9},{5,13},{25,17},{29,21},{2,10},{... | collective-permute-start | bytes 2764808 | tf_op jit(solution)/shard_map/ppermute | solution.py:541
  186.8 26.5 %collective-permute-start.16 = (bf16[3600,128]{1,0:T(8,128)(2,1)S(1)}, bf16[3600,128]{1,0:T(8,128)(2,1)S(1)}, u32[]{:S(2)}, u32[]{:S(2)}) collective-permute-start(bf16[3600,128]{1,0:T(8,128)(2,1)S(1)} %add_convert_fusion.2), channel_id=1, source_target_pairs={{8,16},{12,20},{16,8},{20,12},{9,17},{13,21},{17,9},{21,13},{10,18... | collective-permute-start | bytes 2764808 | tf_op jit(solution)/shard_map/ppermute | solution.py:541
  189.9 23.4 %collective-permute-start.11 = (bf16[3600,128]{1,0:T(8,128)(2,1)S(1)}, bf16[3600,128]{1,0:T(8,128)(2,1)S(1)}, u32[]{:S(2)}, u32[]{:S(2)}) collective-permute-start(bf16[3600,128]{1,0:T(8,128)(2,1)S(1)} %copy-done.13), channel_id=1, source_target_pairs={{0,4},{4,0},{8,12},{12,8},{16,20},{20,16},{24,28},{28,24},{1,5},{5... | collective-permute-start | bytes 2764808 | tf_op jit(solution)/shard_map/ppermute | solution.py:537
  210.1 5.9 %copy-start.14 = (f32[56,128]{1,0:T(8,128)S(1)}, f32[56,128]{1,0:T(8,128)}, u32[]{:S(2)}) copy-start(f32[56,128]{1,0:T(8,128)} %get-tuple-element.55) | copy-start | bytes 86020
  210.1 23.8 %copy-start.4 = (f32[3600,128]{1,0:T(8,128)S(1)}, f32[3600,128]{1,0:T(8,128)}, u32[]{:S(2)}) copy-start(f32[3600,128]{1,0:T(8,128)} %class_sums.15) | copy-start | bytes 5529604
  210.1 21.6 %collective-permute-start.15 = (bf16[3600,128]{1,0:T(8,128)(2,1)}, bf16[3600,128]{1,0:T(8,128)(2,1)S(1)}, u32[]{:S(2)}, u32[]{:S(2)}) collective-permute-start(bf16[3600,128]{1,0:T(8,128)(2,1)} %add_convert_fusion.1), channel_id=1, source_target_pairs={{8,16},{12,20},{16,8},{20,12},{9,17},{13,21},{17,9},{21,13},{10,18... | collective-permute-start | bytes 2764808 | tf_op jit(solution)/shard_map/ppermute | solution.py:541
  214.6 19.4 %collective-permute-start.17 = (bf16[3600,128]{1,0:T(8,128)(2,1)}, bf16[3600,128]{1,0:T(8,128)(2,1)}, u32[]{:S(2)}, u32[]{:S(2)}) collective-permute-start(bf16[3600,128]{1,0:T(8,128)(2,1)} %add_convert_fusion), channel_id=1, source_target_pairs={{0,8},{4,12},{8,0},{12,4},{16,24},{20,28},{24,16},{28,20},{1,9},{5... | collective-permute-start | bytes 2764808 | tf_op jit(solution)/shard_map/ppermute | solution.py:541
  214.6 19.4 %collective-permute-start.12 = (bf16[3600,128]{1,0:T(8,128)(2,1)}, bf16[3600,128]{1,0:T(8,128)(2,1)}, u32[]{:S(2)}, u32[]{:S(2)}) collective-permute-start(bf16[3600,128]{1,0:T(8,128)(2,1)} %class_sums.13), channel_id=1, source_target_pairs={{0,4},{4,0},{8,12},{12,8},{16,20},{20,16},{24,28},{28,24},{1,5},{5... | collective-permute-start | bytes 2764808 | tf_op jit(solution)/shard_map/ppermute | solution.py:537
  216.7 20.3 %copy-start.1 = (f32[16,128]{1,0:T(8,128)S(1)}, f32[16,128]{1,0:T(8,128)}, u32[]{:S(2)}) copy-start(f32[16,128]{1,0:T(8,128)} %param.17) | copy-start | bytes 24580
  (2 other events, 5.6 us)

commit v6 on v5

--- a/solution.py
+++ b/solution.py
@@ -508,7 +508,8 @@
     out_ref[...] = wide_ref[...].astype(out_ref.dtype)
 
 
-def class_sums_of(slot, back, weighted, offsets, classes, dtype):
+def class_sums_of(slot, back, weighted, offsets, classes, dtype, groups=(0, ROTS // GROUP)):
+    begin, end = groups
     _, _, queries, double = weighted.shape
     cycles = double // 2
     rows = back.shape[1]
@@ -518,16 +519,16 @@
         functools.partial(sums_kernel, classes=classes),
         grid_spec=pltpu.PrefetchScalarGridSpec(
             num_scalar_prefetch=1,
-            grid=(ROTS // GROUP,),
+            grid=(end - begin,),
             in_specs=[
-                pl.BlockSpec((GROUP, rows, queries), lambda g, u: (g, 0, 0)),
-                pl.BlockSpec((1, GROUP, queries, double), lambda g, u: (u[0], g, 0, 0)),
+                pl.BlockSpec((GROUP, rows, queries), lambda g, u: (g + begin, 0, 0)),
+                pl.BlockSpec((1, GROUP, queries, double), lambda g, u: (u[0], g + begin, 0, 0)),
                 pl.BlockSpec(offsets.shape, lambda g, u: (0, 0)),
             ],
             out_specs=piece,
             scratch_shapes=[pltpu.VMEM((block, cycles), f32)],
         ),
-        out_shape=jax.ShapeDtypeStruct((ROTS * 2 * classes, cycles), dtype),
+        out_shape=jax.ShapeDtypeStruct(((end - begin) * block, cycles), dtype),
         compiler_params=pltpu.CompilerParams(vmem_limit_bytes=VMEM_LIMIT),
         name="class_sums",
     )(jnp.reshape(slot, (1,)).astype(jnp.int32), back, weighted, offsets)
@@ -545,7 +546,7 @@
     index = lax.axis_index("dp")
     line, side = index // 2, index % 2
     _, steps = spectra_steps(base.shape[0])
-    cuts = [0, 2 * steps // 13, 6 * steps // 13, 10 * steps // 13, steps]
+    cuts = [0, 3 * steps // 13, 8 * steps // 13, steps]
 
     own_crossed = across(piece)
     near = along(piece, ((0, 1), (1, 0), (2, 3), (3, 2)))
@@ -566,7 +567,6 @@
     weighted, far_end, third_crossed = lax.optimization_barrier((weighted, far_end, third_crossed))
     fourth = far_middle + far_end
     fourth_crossed = across(fourth)
-    weighted = make_spectra(base, ctf_rows, cuts[3], cuts[4], weighted)
 
     pieces = [piece, own_crossed, near, near_crossed, third, third_crossed, fourth, fourth_crossed]
     places = [line, line ^ 1, jnp.where(line < 2, 2, 1), jnp.where(line < 2, 3, 0)]
@@ -574,36 +574,98 @@
     return weighted, pieces, slot_of
 
 
+def add_kernel(own_ref, *refs):
+    first = pl.program_id(0) == 0
+    whole_ref, pairs, out_ref = refs[0], refs[1:-1], refs[-1]
+    total = own_ref[...] + whole_ref[...].astype(f32)
+    for n in range(0, len(pairs), 2):
+        total = total + jnp.where(first, pairs[n][...], pairs[n + 1][...]).astype(f32)
+    out_ref[...] = total
+
+
+def add_pieces(own, whole, pairs, block):
+    rows, cycles = own.shape
+    spec = pl.BlockSpec((block, cycles), lambda g: (g, 0))
+    head = pl.BlockSpec((block, cycles), lambda g: (0, 0))
+    rest = pl.BlockSpec((block, cycles), lambda g: (jnp.maximum(g - 1, 0), 0))
+    return pl.pallas_call(
+        add_kernel,
+        grid=(rows // block,),
+        in_specs=[spec, spec] + [head, rest] * len(pairs),
+        out_specs=spec,
+        out_shape=jax.ShapeDtypeStruct(own.shape, f32),
+        name="add_pieces",
+    )(own, whole, *[part for pair in pairs for part in pair])
+
+
 def reduce_on_line(back, weighted, offsets, classes):
     index = lax.axis_index("dp")
     line, side = index // 2, index % 2
     order = [jnp.where(line < 2, 3, 0), jnp.where(line < 2, 2, 1), line ^ 1, line]
-    theirs = [class_sums_of(2 * z + 1 - side, back, weighted, offsets, classes, bf16) for z in order]
-    ours = [class_sums_of(2 * z + side, back, weighted, offsets, classes, f32) for z in order]
+    groups = ((0, 1), (1, ROTS // GROUP))
+    block = 2 * GROUP * classes
+    rows = [slice(a * block, b * block) for a, b in groups]
+
+    def theirs(n, back, some=(0, ROTS // GROUP)):
+        return class_sums_of(2 * order[n] + 1 - side, back, weighted, offsets, classes, bf16, some)
+
+    def ours(n, back):
+        return class_sums_of(2 * order[n] + side, back, weighted, offsets, classes, f32)
+
+    def wide(piece):
+        return piece.astype(f32)
+
+    def then(back, *done):
+        return lax.optimization_barrier((back, *done))[0]
+
     at_end = (line == 0) | (line == 3)
-
-    crossed = [across(theirs[0])]
-    crossed[0], theirs[1], theirs[2], ours[0], ours[1] = lax.optimization_barrier(
-        (crossed[0], theirs[1], theirs[2], ours[0], ours[1])
-    )
-    crossed.append(across(theirs[1]))
-    farthest = ours[0] + crossed[0].astype(f32)
-    first = along(farthest.astype(bf16), ((0, 1), (3, 2)))
-    crossed[1], theirs[2], theirs[3], ours[2], ours[3] = lax.optimization_barrier(
-        (crossed[1], theirs[2], theirs[3], ours[2], ours[3])
-    )
-    crossed.append(across(theirs[2]))
-    next_farthest = ours[1] + crossed[1].astype(f32)
-    second = (jnp.where(at_end, next_farthest, farthest) + first.astype(f32)).astype(bf16)
-    from_ends = along(second, ((0, 1), (3, 2)))
-    from_middle = along(second, ((1, 2), (2, 1)))
-    crossed[2], theirs[3] = lax.optimization_barrier((crossed[2], theirs[3]))
-    crossed.append(across(theirs[3]))
-    third = (next_farthest + from_ends.astype(f32)).astype(bf16)
-    third = along(third, ((1, 2), (2, 1)))
-    fourth = (ours[2] + crossed[2].astype(f32) + from_middle.astype(f32)).astype(bf16)
-    fourth = along(fourth, ((0, 1), (1, 0), (2, 3), (3, 2)))
-    return ours[3] + crossed[3].astype(f32) + third.astype(f32) + fourth.astype(f32)
+    away = [theirs(0, back, groups[0])]
+    crossed = [across(away[0])]
+    back = then(back, away[0])
+    away.append(theirs(0, back, groups[1]))
+    crossed.append(across(away[1]))
+    back = then(back, away[1])
+    own = [ours(0, back)]
+    crossed[0], own[0] = lax.optimization_barrier((crossed[0], own[0]))
+    farthest = [own[0][rows[0]] + wide(crossed[0])]
+    message = farthest[0].astype(bf16)
+    first = [along(message, ((0, 1), (3, 2)))]
+    back = then(back, message)
+    away.append(theirs(1, back))
+    crossed.append(across(away[2]))
+    back = then(back, away[2])
+    own.append(ours(1, back))
+    crossed[1], own[1] = lax.optimization_barrier((crossed[1], own[1]))
+    farthest.append(own[0][rows[1]] + wide(crossed[1]))
+    message = farthest[1].astype(bf16)
+    first.append(along(message, ((0, 1), (3, 2))))
+    back = then(back, message)
+    away.append(theirs(2, back))
+    crossed.append(across(away[3]))
+    back = then(back, away[3])
+    own.append(ours(2, back))
+    back = then(back, own[2])
+    away.append(theirs(3, back))
+    crossed.append(across(away[4]))
+    crossed[2], away[4] = lax.optimization_barrier((crossed[2], away[4]))
+    next_farthest = [own[1][r] + wide(crossed[2][r]) for r in rows]
+    second = [
+        (jnp.where(at_end, b, a) + wide(c)).astype(bf16) for a, b, c in zip(farthest, next_farthest, first)
+    ]
+    from_ends = [along(piece, ((0, 1), (3, 2))) for piece in second]
+    from_middle = [along(piece, ((1, 2), (2, 1))) for piece in second]
+    back = then(back, *second)
+    own.append(ours(3, back))
+    message = (next_farthest[0] + wide(from_ends[0])).astype(bf16)
+    third = [along(message, ((1, 2), (2, 1)))]
+    crossed[3], from_middle[0], message = lax.optimization_barrier((crossed[3], from_middle[0], message))
+    message = (own[2][rows[0]] + wide(crossed[3][rows[0]]) + wide(from_middle[0])).astype(bf16)
+    fourth = [along(message, ((0, 1), (1, 0), (2, 3), (3, 2)))]
+    message = (own[2][rows[1]] + wide(crossed[3][rows[1]]) + wide(from_middle[1])).astype(bf16)
+    fourth.append(along(message, ((0, 1), (1, 0), (2, 3), (3, 2))))
+    message = (next_farthest[1] + wide(from_ends[1])).astype(bf16)
+    third.append(along(message, ((1, 2), (2, 1))))
+    return add_pieces(own[3], crossed[4], (third, fourth), block)
 
 
 def local(particles, references, ctf_table, rot_offset, prior_shift, defocus_group):
@@ -632,7 +694,7 @@
     queries = weighted.shape[1]
     weighted = weighted.reshape(slots, ROTS, queries, 2 * cycles)
 
-    early = 3 * slots // 4
+    early = slots - 1
     part = lax.axis_index("cls")
     corr, power = correlate(slot_of[:early], weighted, pieces[:early], classes, part)
     weights, stat, share = correlate(

time: 241 us -> 224 us (0.929)
  waiting for transfers between devices: 52.1 us -> 28.5 us
  starting transfers between devices: 31.7 us -> 41.1 us
  other arithmetic: 10.6 us -> 6.87 us
    ppermute x10 -> x15, waiting for transfers between devices: 45.2 us -> 25.8 us  [along(): lax.ppermute(piece, 'dp', [(2 * a + x, 2 * b + x) for a, b in pairs for x...]
    ppermute x10 -> x15, starting transfers between devices: 21.6 us -> 29.4 us  [along(): lax.ppermute(piece, 'dp', [(2 * a + x, 2 * b + x) for a, b in pairs for x...]
    pallas_call x0 -> x1, Pallas kernels: none -> 4.62 us  [add_pieces(): pl.pallas_call(add_kernel, grid=(rows // block,), in_specs=[spec, spec] +...]
    ppermute x8 -> x9, waiting for transfers between devices: 6.88 us -> 2.67 us  [across(): return lax.ppermute(piece, 'dp', [(d, d ^ 1) for d in range(8)])]
    pallas_call x4 -> x3, Pallas kernels: 50 us -> 46.2 us  [make_spectra(): pl.pallas_call(functools.partial(spectra_kernel, per_step=per_step), grid...]
    add x1 -> x0, other arithmetic: 3.11 us -> none  [reduce_on_line(): ours[3] + crossed[3].astype(f32) + third.astype(f32) + fourth.astype(f32)]
    ppermute x8 -> x9, starting transfers between devices: 10 us -> 11.7 us  [across(): return lax.ppermute(piece, 'dp', [(d, d ^ 1) for d in range(8)])]
    pallas_call x8 -> x9, Pallas kernels: 40.3 us -> 41.3 us  [class_sums_of(): pl.pallas_call(functools.partial(sums_kernel, classes=classes), grid_spec...]
  transfers between devices with their start and end apart: 18 -> 24, of which waited for: 14 -> 10; matrix products, arithmetic and copies ran while one was open for 3% -> 4% of each run, Pallas kernels for 44% -> 48%
where the time goes in v6:
time: 224 us; the launch traced here: 222 us
  Pallas kernels  134 us (60%)
  starting transfers between devices  41.1 us (18%)
  waiting for transfers between devices  28.5 us (13%)
  other arithmetic  6.87 us (3%)
  blocking collectives  6.23 us (3%)
  local copies, waits for them, and re-layouts  3.65 us (2%)
    pallas_call x3, Pallas kernels, make_spectra(): pl.pallas_call(functools.partial(spectra_kernel, per_step=per_step), grid...  46.2 us
    pallas_call x9, Pallas kernels, class_sums_of(): pl.pallas_call(functools.partial(sums_kernel, classes=classes), grid_spec...  41.3 us
    ppermute x15, starting transfers between devices, along(): lax.ppermute(piece, 'dp', [(2 * a + x, 2 * b + x) for a, b in pairs for x...  29.4 us
    pallas_call x2, Pallas kernels, correlate(): pl.pallas_call(functools.partial(correlate_kernel, slots=slots, classes=c...  28.4 us
    ppermute x15, waiting for transfers between devices, along(): lax.ppermute(piece, 'dp', [(2 * a + x, 2 * b + x) for a, b in pairs for x...  25.8 us
    ppermute x9, starting transfers between devices, across(): return lax.ppermute(piece, 'dp', [(d, d ^ 1) for d in range(8)])  11.7 us
    psum x1, blocking collectives, local(): shares = lax.psum(share, 'cls')  6.23 us
    pallas_call x1, Pallas kernels, make_back(): pl.pallas_call(back_kernel, out_shape=[jax.ShapeDtypeStruct((ROTS, 2 * pa...  5.45 us
  transfers between devices with their start and end apart: 24, of which 10 were waited for; matrix products, arithmetic and copies ran while one was open for 4% of the time, Pallas kernels for 48%

profile of v6, /device:TPU:8, one launch (start us, length us, event | category | flops | bytes accessed | tf_op | source)
XLA Modules:
  0.0 221.7 jit_solution(11156017251788189846)
XLA Ops:
  0.7 3.0 %turn_references.1 = (bf16[3600,128]{1,0:T(8,128)(2,1)}, f32[56,128]{1,0:T(8,128)}) custom-call(s32[1]{0:T(128)} %bitcast.3.first_ref, s32[50]{0:T(128)} %offset_ref.1, bf16[3600,128]{1,0:T(8,128)(2,1)} %bitcast.45), custom_call_target="tpu_custom_call" | custom-call | tf_op jit(solution)/shard_map/turn_references/pallas_call | solution.py:251
  3.6 5.0 %collective-permute-start.1 = (bf16[3600,128]{1,0:T(8,128)(2,1)}, bf16[3600,128]{1,0:T(8,128)(2,1)S(1)}, u32[]{:S(2)}, u32[]{:S(2)}) collective-permute-start(bf16[3600,128]{1,0:T(8,128)(2,1)} %get-tuple-element.39.refs_15_), channel_id=1, source_target_pairs={{8,16},{12,20},{16,8},{20,12},{9,17},{13,21},{17,9},{21,13},{10,18... | collective-permute-start | bytes 2764808 | tf_op jit(solution)/shard_map/ppermute | solution.py:542
  10.2 4.6 %centre.1.base_ref = f32[8,2,288,128]{3,2,1,0:T(8,128)} custom-call(s32[2,8]{1,0:T(2,128)} %bitcast.46, bf16[8,2,288,128]{3,2,1,0:T(8,128)(2,1)} %part_ref.1, f32[2,288,128]{2,1,0:T(8,128)} %constant.49.clone.turns_ref), custom_call_target="tpu_custom_call" | custom-call | tf_op jit(solution)/shard_map/centre/pallas_call | solution.py:87
  15.7 11.8 %spectra.3.refs_4_ = bf16[288,208,256]{2,1,0:T(8,128)(2,1)} custom-call(f32[8,2,288,128]{3,2,1,0:T(8,128)} %centre.1.base_ref, f32[8,128]{1,0:T(8,128)} %fusion.6.ctf_ref.refs_6_, bf16[576,576]{1,0:T(8,128)(2,1)} %constant.50.clone.table_ref, f32[2,5,2,288,128]{4,3,2,1,0:T(8,128)} %constant.51.clone.refs_0_.refs_1_.refs_2_.refs_3_, ...), custom_call_target="tpu_custom_call" | custom-call | tf_op jit(solution)/shard_map/spectra/pallas_call | solution.py:171
  30.6 2.2 collective-permute-start.3
  35.7 17.2 %spectra.4.refs_4_ = bf16[288,208,256]{2,1,0:T(8,128)(2,1)} custom-call(f32[8,2,288,128]{3,2,1,0:T(8,128)} %centre.1.base_ref, f32[8,128]{1,0:T(8,128)} %fusion.6.ctf_ref.refs_6_, bf16[576,576]{1,0:T(8,128)(2,1)} %constant.50.clone.table_ref, f32[2,5,2,288,128]{4,3,2,1,0:T(8,128)} %constant.51.clone.refs_0_.refs_1_.refs_2_.refs_3_, ...), custom_call_target="tpu_custom_call", output_to_operand_aliasing={{}: (7, {})} | custom-call | tf_op jit(solution)/shard_map/spectra/pallas_call | solution.py:171
  55.4 3.9 %collective-permute-start.6 = (bf16[3600,128]{1,0:T(8,128)(2,1)S(1)}, bf16[3600,128]{1,0:T(8,128)(2,1)S(1)}, u32[]{:S(2)}, u32[]{:S(2)}) collective-permute-start(bf16[3600,128]{1,0:T(8,128)(2,1)S(1)} %collective-permute-done.3), channel_id=1, source_target_pairs={{8,0},{12,4},{16,24},{20,28},{9,1},{13,5},{17,25},{21,29},{10,2},{... | collective-permute-start | bytes 2764808 | tf_op jit(solution)/shard_map/ppermute | solution.py:542
  59.3 17.2 %spectra.5 = bf16[288,208,256]{2,1,0:T(8,128)(2,1)} custom-call(f32[8,2,288,128]{3,2,1,0:T(8,128)} %centre.1.base_ref, f32[8,128]{1,0:T(8,128)} %fusion.6.ctf_ref.refs_6_, bf16[576,576]{1,0:T(8,128)(2,1)} %constant.50.clone.table_ref, f32[2,5,2,288,128]{4,3,2,1,0:T(8,128)} %constant.51.clone.refs_0_.refs_1_.refs_2_.refs_3_, ...), custom_call_target="tpu_custom_call", output_to_operand_aliasing={{}: (7, {})} | custom-call | tf_op jit(solution)/shard_map/spectra/pallas_call | solution.py:171
  76.8 1.6 collective-permute-start.8
  78.4 17.1 %correlate.1 = (f32[36,112,256]{2,1,0:T(8,128)}, f32[56,128]{1,0:T(8,128)}) custom-call(s32[1]{0:T(128)} %bitcast.7.refs_0_.slot_ref, s32[1]{0:T(128)} %bitcast.8.refs_1_, s32[1]{0:T(128)} %bitcast.9.refs_2_.slot_ref, s32[1]{0:T(128)} %bitcast.10.refs_3_, s32[1]{0:T(128)} %bitcast.11.refs_4_.slot_ref, s32[1]{0:T(128)} %bitcast.12.refs_5_, ...), custom_call_target="tpu_custom_call" | custom-call | tf_op jit(solution)/shard_map/correlate/pallas_call | solution.py:417
  97.0 11.3 %scores.1 = (f32[36,56,256]{2,1,0:T(8,128)}, f32[64,128]{1,0:T(8,128)}, f32[4,2,128]{2,1,0:T(2,128)}) custom-call(s32[1]{0:T(128)} %bitcast.refs_0_, s32[1]{0:T(128)} %bitcast.1.refs_7_.refs_1_, bf16[8,36,208,256]{3,2,1,0:T(8,128)(2,1)} %bitcast.34, bf16[3600,128]{1,0:T(8,128)(2,1)} %copy-done.14, f32[36,112,256]{2,1,0:T(8,128)} %get-tuple-element.51.refs_4_, ...), custom_call_target="tpu_custom_call" | custom-call | tf_op jit(solution)/shard_map/scores/pallas_call | solution.py:417
  108.3 6.2 %psum.7.share_ref = f32[4,2,128]{2,1,0:T(2,128)} all-reduce(f32[4,2,128]{2,1,0:T(2,128)} %get-tuple-element.55), channel_id=1, replica_groups=mesh['dp'=8,'cls'=4] {'cls'}, use_global_device_ids=true, to_apply=%region_0.1 | all-reduce | flops 1024 | bytes 8192 | tf_op jit(solution)/shard_map/psum | solution.py:703
  114.6 5.4 %back.1 = (bf16[36,112,208]{2,1,0:T(8,128)(2,1)}, f32[8,128]{1,0:T(8,128)}, f32[56,128]{1,0:T(8,128)}) custom-call(f32[36,56,256]{2,1,0:T(8,128)} %get-tuple-element.53.weight_ref, f32[64,128]{1,0:T(8,128)} %get-tuple-element.54.stat_ref, f32[4,2,128]{2,1,0:T(2,128)} %psum.7.share_ref, f32[56,128]{1,0:T(8,128)} %get-tuple-element.56.offset_ref), custom_call_target="tpu_custom_call" | custom-call | tf_op jit(solution)/shard_map/back/pallas_call | solution.py:483
  120.0 2.6 %class_sums.9 = bf16[1200,128]{1,0:T(8,128)(2,1)} custom-call(s32[1]{0:T(128)} %bitcast.16.slot_ref, bf16[36,112,208]{2,1,0:T(8,128)(2,1)} %get-tuple-element.72.back_ref, bf16[8,36,208,256]{3,2,1,0:T(8,128)(2,1)} %bitcast.35, f32[56,128]{1,0:T(8,128)} %get-tuple-element.56.offset_ref), custom_call_target="tpu_custom_call" | custom-call | tf_op jit(solution)/shard_map/class_sums/pallas_call | solution.py:518
  124.1 3.2 %class_sums.10 = bf16[2400,128]{1,0:T(8,128)(2,1)} custom-call(s32[1]{0:T(128)} %bitcast.16.slot_ref, bf16[36,112,208]{2,1,0:T(8,128)(2,1)} %get-tuple-element.72.back_ref, bf16[8,36,208,256]{3,2,1,0:T(8,128)(2,1)} %bitcast.36, f32[56,128]{1,0:T(8,128)} %get-tuple-element.56.offset_ref), custom_call_target="tpu_custom_call" | custom-call | tf_op jit(solution)/shard_map/class_sums/pallas_call | solution.py:518
  127.9 5.2 %class_sums.11 = f32[3600,128]{1,0:T(8,128)} custom-call(s32[1]{0:T(128)} %bitcast.13.refs_6_.slot_ref, bf16[36,112,208]{2,1,0:T(8,128)(2,1)} %get-tuple-element.72.back_ref, bf16[8,36,208,256]{3,2,1,0:T(8,128)(2,1)} %bitcast.37, f32[56,128]{1,0:T(8,128)} %get-tuple-element.56.offset_ref), custom_call_target="tpu_custom_call" | custom-call | tf_op jit(solution)/shard_map/class_sums/pallas_call | solution.py:518
  133.0 2.0 fusion.5
  135.0 4.8 %class_sums.12 = bf16[3600,128]{1,0:T(8,128)(2,1)} custom-call(s32[1]{0:T(128)} %bitcast.17.slot_ref, bf16[36,112,208]{2,1,0:T(8,128)(2,1)} %get-tuple-element.72.back_ref, bf16[8,36,208,256]{3,2,1,0:T(8,128)(2,1)} %bitcast.38, f32[56,128]{1,0:T(8,128)} %get-tuple-element.56.offset_ref), custom_call_target="tpu_custom_call" | custom-call | tf_op jit(solution)/shard_map/class_sums/pallas_call | solution.py:518
  142.7 5.2 %class_sums.13 = f32[3600,128]{1,0:T(8,128)} custom-call(s32[1]{0:T(128)} %bitcast.11.refs_4_.slot_ref, bf16[36,112,208]{2,1,0:T(8,128)(2,1)} %get-tuple-element.72.back_ref, bf16[8,36,208,256]{3,2,1,0:T(8,128)(2,1)} %bitcast.39, f32[56,128]{1,0:T(8,128)} %get-tuple-element.56.offset_ref), custom_call_target="tpu_custom_call" | custom-call | tf_op jit(solution)/shard_map/class_sums/pallas_call | solution.py:518
  150.2 4.9 %class_sums.14 = bf16[3600,128]{1,0:T(8,128)(2,1)} custom-call(s32[1]{0:T(128)} %bitcast.18.slot_ref, bf16[36,112,208]{2,1,0:T(8,128)(2,1)} %get-tuple-element.72.back_ref, bf16[8,36,208,256]{3,2,1,0:T(8,128)(2,1)} %bitcast.40, f32[56,128]{1,0:T(8,128)} %get-tuple-element.56.offset_ref), custom_call_target="tpu_custom_call" | custom-call | tf_op jit(solution)/shard_map/class_sums/pallas_call | solution.py:518
  155.7 5.2 %class_sums.15 = f32[3600,128]{1,0:T(8,128)} custom-call(s32[1]{0:T(128)} %bitcast.9.refs_2_.slot_ref, bf16[36,112,208]{2,1,0:T(8,128)(2,1)} %get-tuple-element.72.back_ref, bf16[8,36,208,256]{3,2,1,0:T(8,128)(2,1)} %bitcast.41, f32[56,128]{1,0:T(8,128)} %get-tuple-element.56.offset_ref), custom_call_target="tpu_custom_call" | custom-call | tf_op jit(solution)/shard_map/class_sums/pallas_call | solution.py:518
  160.9 5.0 %class_sums.16 = bf16[3600,128]{1,0:T(8,128)(2,1)} custom-call(s32[1]{0:T(128)} %bitcast.19.slot_ref, bf16[36,112,208]{2,1,0:T(8,128)(2,1)} %get-tuple-element.72.back_ref, bf16[8,36,208,256]{3,2,1,0:T(8,128)(2,1)} %bitcast.42, f32[56,128]{1,0:T(8,128)} %get-tuple-element.56.offset_ref), custom_call_target="tpu_custom_call" | custom-call | tf_op jit(solution)/shard_map/class_sums/pallas_call | solution.py:518
  168.4 1.6 add_convert_fusion.1
  170.0 3.0 %collective-permute-start.22 = (bf16[2400,128]{1,0:T(8,128)(2,1)S(1)}, bf16[2400,128]{1,0:T(8,128)(2,1)S(1)}, u32[]{:S(2)}, u32[]{:S(2)}) collective-permute-start(bf16[2400,128]{1,0:T(8,128)(2,1)S(1)} %add_convert_fusion.1), channel_id=1, source_target_pairs={{8,16},{12,20},{16,8},{20,12},{9,17},{13,21},{17,9},{21,13},{10,18... | collective-permute-start | bytes 1843208 | tf_op jit(solution)/shard_map/ppermute | solution.py:542
  173.1 1.6 collective-permute-start.14
  174.6 2.8 %collective-permute-start.20 = (bf16[1200,128]{1,0:T(8,128)(2,1)S(1)}, bf16[1200,128]{1,0:T(8,128)(2,1)S(1)}, u32[]{:S(2)}, u32[]{:S(2)}) collective-permute-start(bf16[1200,128]{1,0:T(8,128)(2,1)S(1)} %add_convert_fusion.3), channel_id=1, source_target_pairs={{8,16},{12,20},{16,8},{20,12},{9,17},{13,21},{17,9},{21,13},{10,18... | collective-permute-start | bytes 921608 | tf_op jit(solution)/shard_map/ppermute | solution.py:542
  179.8 13.2 %collective-permute-done.20 = bf16[1200,128]{1,0:T(8,128)(2,1)S(1)} collective-permute-done((bf16[1200,128]{1,0:T(8,128)(2,1)S(1)}, bf16[1200,128]{1,0:T(8,128)(2,1)S(1)}, u32[]{:S(2)}, u32[]{:S(2)}) %collective-permute-start.20) | collective-permute-done | bytes 307232 | tf_op jit(solution)/shard_map/ppermute | solution.py:542
  193.0 3.0 %collective-permute-start.16 = (bf16[1200,128]{1,0:T(8,128)(2,1)S(1)}, bf16[1200,128]{1,0:T(8,128)(2,1)}, u32[]{:S(2)}, u32[]{:S(2)}) collective-permute-start(bf16[1200,128]{1,0:T(8,128)(2,1)S(1)} %add_convert_fusion.2), channel_id=1, source_target_pairs={{8,16},{12,20},{16,8},{20,12},{9,17},{13,21},{17,9},{21,13},{10,18... | collective-permute-start | bytes 921608 | tf_op jit(solution)/shard_map/ppermute | solution.py:542
  196.6 2.8 %collective-permute-start.18 = (bf16[2400,128]{1,0:T(8,128)(2,1)S(1)}, bf16[2400,128]{1,0:T(8,128)(2,1)S(1)}, u32[]{:S(2)}, u32[]{:S(2)}) collective-permute-start(bf16[2400,128]{1,0:T(8,128)(2,1)S(1)} %add_convert_fusion), channel_id=1, source_target_pairs={{8,16},{12,20},{16,8},{20,12},{9,17},{13,21},{17,9},{21,13},{10,18... | collective-permute-start | bytes 1843208 | tf_op jit(solution)/shard_map/ppermute | solution.py:542
  201.4 5.2 %class_sums.17.own_ref = f32[3600,128]{1,0:T(8,128)} custom-call(s32[1]{0:T(128)} %bitcast.7.refs_0_.slot_ref, bf16[36,112,208]{2,1,0:T(8,128)(2,1)} %get-tuple-element.72.back_ref, bf16[8,36,208,256]{3,2,1,0:T(8,128)(2,1)} %bitcast.43, f32[56,128]{1,0:T(8,128)} %get-tuple-element.56.offset_ref), custom_call_target="tpu_custom_call" | custom-call | tf_op jit(solution)/shard_map/class_sums/pallas_call | solution.py:518
  206.7 9.6 %collective-permute-done.21.refs_3_ = bf16[1200,128]{1,0:T(8,128)(2,1)} collective-permute-done((bf16[1200,128]{1,0:T(8,128)(2,1)S(1)}, bf16[1200,128]{1,0:T(8,128)(2,1)}, u32[]{:S(2)}, u32[]{:S(2)}) %collective-permute-start.21) | collective-permute-done | bytes 307232 | tf_op jit(solution)/shard_map/ppermute | solution.py:542
  217.1 4.6 %add_pieces.1 = f32[3600,128]{1,0:T(8,128)} custom-call(f32[3600,128]{1,0:T(8,128)} %class_sums.17.own_ref, bf16[3600,128]{1,0:T(8,128)(2,1)} %copy-done.13, bf16[1200,128]{1,0:T(8,128)(2,1)} %collective-permute-done.16.refs_1_, bf16[2400,128]{1,0:T(8,128)(2,1)} %copy-done.15, bf16[1200,128]{1,0:T(8,128)(2,1)} %collective-permute-done.21.refs_3_, ...), custom_call_target="tpu_custom_call" | custom-call | tf_op jit(solution)/shard_map/add_pieces/pallas_call | solution.py:591
  (85 shorter events, 28.6 us)
Async XLA Ops:
  0.6 14.3 %copy-start = (f32[16,128]{1,0:T(8,128)S(1)}, f32[16,128]{1,0:T(8,128)}, u32[]{:S(2)}) copy-start(f32[16,128]{1,0:T(8,128)} %param.15) | copy-start | bytes 24580
  3.6 23.9 %collective-permute-start = (bf16[3600,128]{1,0:T(8,128)(2,1)}, bf16[3600,128]{1,0:T(8,128)(2,1)S(1)}, u32[]{:S(2)}, u32[]{:S(2)}) collective-permute-start(bf16[3600,128]{1,0:T(8,128)(2,1)} %get-tuple-element.39.refs_15_), channel_id=1, source_target_pairs={{0,8},{4,12},{8,0},{12,4},{16,24},{20,28},{24,16},{28,20},{1,9},{5... | collective-permute-start | bytes 2764808 | tf_op jit(solution)/shard_map/ppermute | solution.py:542
  3.6 25.4 %collective-permute-start.1 = (bf16[3600,128]{1,0:T(8,128)(2,1)}, bf16[3600,128]{1,0:T(8,128)(2,1)S(1)}, u32[]{:S(2)}, u32[]{:S(2)}) collective-permute-start(bf16[3600,128]{1,0:T(8,128)(2,1)} %get-tuple-element.39.refs_15_), channel_id=1, source_target_pairs={{8,16},{12,20},{16,8},{20,12},{9,17},{13,21},{17,9},{21,13},{10,18... | collective-permute-start | bytes 2764808 | tf_op jit(solution)/shard_map/ppermute | solution.py:542
  8.7 21.9 %collective-permute-start.2 = (bf16[3600,128]{1,0:T(8,128)(2,1)}, bf16[3600,128]{1,0:T(8,128)(2,1)S(1)}, u32[]{:S(2)}, u32[]{:S(2)}) collective-permute-start(bf16[3600,128]{1,0:T(8,128)(2,1)} %get-tuple-element.39.refs_15_), channel_id=1, source_target_pairs={{0,4},{4,0},{8,12},{12,8},{16,20},{20,16},{24,28},{28,24},{1,5},{5... | collective-permute-start | bytes 2764808 | tf_op jit(solution)/shard_map/ppermute | solution.py:538
  27.5 25.3 %copy-start.9 = (bf16[3600,128]{1,0:T(8,128)(2,1)}, bf16[3600,128]{1,0:T(8,128)(2,1)S(1)}, u32[]{:S(2)}) copy-start(bf16[3600,128]{1,0:T(8,128)(2,1)S(1)} %collective-permute-done.refs_17_) | copy-start | bytes 2764804
  30.6 22.3 %copy-start.10 = (bf16[3600,128]{1,0:T(8,128)(2,1)}, bf16[3600,128]{1,0:T(8,128)(2,1)S(1)}, u32[]{:S(2)}) copy-start(bf16[3600,128]{1,0:T(8,128)(2,1)S(1)} %collective-permute-done.2.refs_16_) | copy-start | bytes 2764804
  30.6 22.6 %collective-permute-start.3 = (bf16[3600,128]{1,0:T(8,128)(2,1)S(1)}, bf16[3600,128]{1,0:T(8,128)(2,1)S(1)}, u32[]{:S(2)}, u32[]{:S(2)}) collective-permute-start(bf16[3600,128]{1,0:T(8,128)(2,1)S(1)} %collective-permute-done.refs_17_), channel_id=1, source_target_pairs={{8,16},{12,20},{16,8},{20,12},{9,17},{13,21},{17,9},{21,13},{10,18... | collective-permute-start | bytes 2764808 | tf_op jit(solution)/shard_map/ppermute | solution.py:542
  32.8 20.8 %collective-permute-start.5 = (bf16[3600,128]{1,0:T(8,128)(2,1)S(1)}, bf16[3600,128]{1,0:T(8,128)(2,1)S(1)}, u32[]{:S(2)}, u32[]{:S(2)}) collective-permute-start(bf16[3600,128]{1,0:T(8,128)(2,1)S(1)} %collective-permute-done.refs_17_), channel_id=1, source_target_pairs={{0,4},{4,0},{8,12},{12,8},{16,20},{20,16},{24,28},{28,24},{1,5},{5... | collective-permute-start | bytes 2764808 | tf_op jit(solution)/shard_map/ppermute | solution.py:538
  34.3 19.5 %collective-permute-start.4 = (bf16[3600,128]{1,0:T(8,128)(2,1)S(1)}, bf16[3600,128]{1,0:T(8,128)(2,1)S(1)}, u32[]{:S(2)}, u32[]{:S(2)}) collective-permute-start(bf16[3600,128]{1,0:T(8,128)(2,1)S(1)} %collective-permute-done.1), channel_id=1, source_target_pairs={{8,0},{12,4},{16,24},{20,28},{9,1},{13,5},{17,25},{21,29},{10,2},{... | collective-permute-start | bytes 2764808 | tf_op jit(solution)/shard_map/ppermute | solution.py:542
  53.6 23.0 %copy-start.11 = (bf16[3600,128]{1,0:T(8,128)(2,1)}, bf16[3600,128]{1,0:T(8,128)(2,1)S(1)}, u32[]{:S(2)}) copy-start(bf16[3600,128]{1,0:T(8,128)(2,1)S(1)} %collective-permute-done.5.refs_18_) | copy-start | bytes 2764804
  54.1 22.4 %copy-start.5 = (bf16[3600,128]{1,0:T(8,128)(2,1)}, bf16[3600,128]{1,0:T(8,128)(2,1)S(1)}, u32[]{:S(2)}) copy-start(bf16[3600,128]{1,0:T(8,128)(2,1)S(1)} %add.93.refs_19_) | copy-start | bytes 2764804
  54.1 22.4 %collective-permute-start.7 = (bf16[3600,128]{1,0:T(8,128)(2,1)S(1)}, bf16[3600,128]{1,0:T(8,128)(2,1)S(1)}, u32[]{:S(2)}, u32[]{:S(2)}) collective-permute-start(bf16[3600,128]{1,0:T(8,128)(2,1)S(1)} %add.93.refs_19_), channel_id=1, source_target_pairs={{0,4},{4,0},{8,12},{12,8},{16,20},{20,16},{24,28},{28,24},{1,5},{5... | collective-permute-start | bytes 2764808 | tf_op jit(solution)/shard_map/ppermute | solution.py:538
  55.4 21.2 %collective-permute-start.6 = (bf16[3600,128]{1,0:T(8,128)(2,1)S(1)}, bf16[3600,128]{1,0:T(8,128)(2,1)S(1)}, u32[]{:S(2)}, u32[]{:S(2)}) collective-permute-start(bf16[3600,128]{1,0:T(8,128)(2,1)S(1)} %collective-permute-done.3), channel_id=1, source_target_pairs={{8,0},{12,4},{16,24},{20,28},{9,1},{13,5},{17,25},{21,29},{10,2},{... | collective-permute-start | bytes 2764808 | tf_op jit(solution)/shard_map/ppermute | solution.py:542
  76.8 19.3 %collective-permute-start.8 = (bf16[3600,128]{1,0:T(8,128)(2,1)S(1)}, bf16[3600,128]{1,0:T(8,128)(2,1)S(1)}, u32[]{:S(2)}, u32[]{:S(2)}) collective-permute-start(bf16[3600,128]{1,0:T(8,128)(2,1)S(1)} %add.94.refs_21_), channel_id=1, source_target_pairs={{0,4},{4,0},{8,12},{12,8},{16,20},{20,16},{24,28},{28,24},{1,5},{5... | collective-permute-start | bytes 2764808 | tf_op jit(solution)/shard_map/ppermute | solution.py:538
  122.6 10.4 %collective-permute-start.9 = (bf16[1200,128]{1,0:T(8,128)(2,1)}, bf16[1200,128]{1,0:T(8,128)(2,1)S(1)}, u32[]{:S(2)}, u32[]{:S(2)}) collective-permute-start(bf16[1200,128]{1,0:T(8,128)(2,1)} %class_sums.9), channel_id=1, source_target_pairs={{0,4},{4,0},{8,12},{12,8},{16,20},{20,16},{24,28},{28,24},{1,5},{5... | collective-permute-start | bytes 921608 | tf_op jit(solution)/shard_map/ppermute | solution.py:538
  127.3 20.5 %collective-permute-start.10 = (bf16[2400,128]{1,0:T(8,128)(2,1)}, bf16[2400,128]{1,0:T(8,128)(2,1)S(1)}, u32[]{:S(2)}, u32[]{:S(2)}) collective-permute-start(bf16[2400,128]{1,0:T(8,128)(2,1)} %class_sums.10), channel_id=1, source_target_pairs={{0,4},{4,0},{8,12},{12,8},{16,20},{20,16},{24,28},{28,24},{1,5},{5... | collective-permute-start | bytes 1843208 | tf_op jit(solution)/shard_map/ppermute | solution.py:538
  139.9 26.0 %collective-permute-start.11 = (bf16[3600,128]{1,0:T(8,128)(2,1)}, bf16[3600,128]{1,0:T(8,128)(2,1)S(1)}, u32[]{:S(2)}, u32[]{:S(2)}) collective-permute-start(bf16[3600,128]{1,0:T(8,128)(2,1)} %class_sums.12), channel_id=1, source_target_pairs={{0,4},{4,0},{8,12},{12,8},{16,20},{20,16},{24,28},{28,24},{1,5},{5... | collective-permute-start | bytes 2764808 | tf_op jit(solution)/shard_map/ppermute | solution.py:538
  141.4 24.5 %collective-permute-start.12 = (bf16[1200,128]{1,0:T(8,128)(2,1)}, bf16[1200,128]{1,0:T(8,128)(2,1)}, u32[]{:S(2)}, u32[]{:S(2)}) collective-permute-start(bf16[1200,128]{1,0:T(8,128)(2,1)} %fusion.5), channel_id=1, source_target_pairs={{0,8},{4,12},{24,16},{28,20},{1,9},{5,13},{25,17},{29,21},{2,10},{... | collective-permute-start | bytes 921608 | tf_op jit(solution)/shard_map/ppermute | solution.py:542
  148.9 19.5 %collective-permute-start.13 = (bf16[2400,128]{1,0:T(8,128)(2,1)}, bf16[2400,128]{1,0:T(8,128)(2,1)}, u32[]{:S(2)}, u32[]{:S(2)}) collective-permute-start(bf16[2400,128]{1,0:T(8,128)(2,1)} %fusion.2), channel_id=1, source_target_pairs={{0,8},{4,12},{24,16},{28,20},{1,9},{5,13},{25,17},{29,21},{2,10},{... | collective-permute-start | bytes 1843208 | tf_op jit(solution)/shard_map/ppermute | solution.py:542
  155.0 41.0 %collective-permute-start.19 = (bf16[3600,128]{1,0:T(8,128)(2,1)}, bf16[3600,128]{1,0:T(8,128)(2,1)S(1)}, u32[]{:S(2)}, u32[]{:S(2)}) collective-permute-start(bf16[3600,128]{1,0:T(8,128)(2,1)} %class_sums.14), channel_id=1, source_target_pairs={{0,4},{4,0},{8,12},{12,8},{16,20},{20,16},{24,28},{28,24},{1,5},{5... | collective-permute-start | bytes 2764808 | tf_op jit(solution)/shard_map/ppermute | solution.py:538
  167.1 11.2 %collective-permute-start.15 = (bf16[1200,128]{1,0:T(8,128)(2,1)S(1)}, bf16[1200,128]{1,0:T(8,128)(2,1)S(1)}, u32[]{:S(2)}, u32[]{:S(2)}) collective-permute-start(bf16[1200,128]{1,0:T(8,128)(2,1)S(1)} %add_convert_fusion.3), channel_id=1, source_target_pairs={{0,8},{4,12},{24,16},{28,20},{1,9},{5,13},{25,17},{29,21},{2,10},{... | collective-permute-start | bytes 921608 | tf_op jit(solution)/shard_map/ppermute | solution.py:542
  168.4 27.6 %copy-start.4 = (f32[3600,128]{1,0:T(8,128)S(1)}, f32[3600,128]{1,0:T(8,128)}, u32[]{:S(2)}) copy-start(f32[3600,128]{1,0:T(8,128)} %class_sums.15) | copy-start | bytes 5529604
  170.0 26.0 %collective-permute-start.22 = (bf16[2400,128]{1,0:T(8,128)(2,1)S(1)}, bf16[2400,128]{1,0:T(8,128)(2,1)S(1)}, u32[]{:S(2)}, u32[]{:S(2)}) collective-permute-start(bf16[2400,128]{1,0:T(8,128)(2,1)S(1)} %add_convert_fusion.1), channel_id=1, source_target_pairs={{8,16},{12,20},{16,8},{20,12},{9,17},{13,21},{17,9},{21,13},{10,18... | collective-permute-start | bytes 1843208 | tf_op jit(solution)/shard_map/ppermute | solution.py:542
  173.1 33.6 %collective-permute-start.14 = (bf16[3600,128]{1,0:T(8,128)(2,1)}, bf16[3600,128]{1,0:T(8,128)(2,1)S(1)}, u32[]{:S(2)}, u32[]{:S(2)}) collective-permute-start(bf16[3600,128]{1,0:T(8,128)(2,1)} %class_sums.16), channel_id=1, source_target_pairs={{0,4},{4,0},{8,12},{12,8},{16,20},{20,16},{24,28},{28,24},{1,5},{5... | collective-permute-start | bytes 2764808 | tf_op jit(solution)/shard_map/ppermute | solution.py:538
  174.6 18.3 %collective-permute-start.20 = (bf16[1200,128]{1,0:T(8,128)(2,1)S(1)}, bf16[1200,128]{1,0:T(8,128)(2,1)S(1)}, u32[]{:S(2)}, u32[]{:S(2)}) collective-permute-start(bf16[1200,128]{1,0:T(8,128)(2,1)S(1)} %add_convert_fusion.3), channel_id=1, source_target_pairs={{8,16},{12,20},{16,8},{20,12},{9,17},{13,21},{17,9},{21,13},{10,18... | collective-permute-start | bytes 921608 | tf_op jit(solution)/shard_map/ppermute | solution.py:542
  178.3 18.0 %collective-permute-start.17 = (bf16[2400,128]{1,0:T(8,128)(2,1)S(1)}, bf16[2400,128]{1,0:T(8,128)(2,1)S(1)}, u32[]{:S(2)}, u32[]{:S(2)}) collective-permute-start(bf16[2400,128]{1,0:T(8,128)(2,1)S(1)} %add_convert_fusion.1), channel_id=1, source_target_pairs={{0,8},{4,12},{24,16},{28,20},{1,9},{5,13},{25,17},{29,21},{2,10},{... | collective-permute-start | bytes 1843208 | tf_op jit(solution)/shard_map/ppermute | solution.py:542
  193.0 23.3 %collective-permute-start.16 = (bf16[1200,128]{1,0:T(8,128)(2,1)S(1)}, bf16[1200,128]{1,0:T(8,128)(2,1)}, u32[]{:S(2)}, u32[]{:S(2)}) collective-permute-start(bf16[1200,128]{1,0:T(8,128)(2,1)S(1)} %add_convert_fusion.2), channel_id=1, source_target_pairs={{8,16},{12,20},{16,8},{20,12},{9,17},{13,21},{17,9},{21,13},{10,18... | collective-permute-start | bytes 921608 | tf_op jit(solution)/shard_map/ppermute | solution.py:542
  196.2 20.0 %collective-permute-start.23 = (bf16[2400,128]{1,0:T(8,128)(2,1)S(1)}, bf16[2400,128]{1,0:T(8,128)(2,1)}, u32[]{:S(2)}, u32[]{:S(2)}) collective-permute-start(bf16[2400,128]{1,0:T(8,128)(2,1)S(1)} %fusion.1), channel_id=1, source_target_pairs={{0,8},{4,12},{8,0},{12,4},{16,24},{20,28},{24,16},{28,20},{1,9},{5... | collective-permute-start | bytes 1843208 | tf_op jit(solution)/shard_map/ppermute | solution.py:542
  196.6 19.7 %collective-permute-start.18 = (bf16[2400,128]{1,0:T(8,128)(2,1)S(1)}, bf16[2400,128]{1,0:T(8,128)(2,1)S(1)}, u32[]{:S(2)}, u32[]{:S(2)}) collective-permute-start(bf16[2400,128]{1,0:T(8,128)(2,1)S(1)} %add_convert_fusion), channel_id=1, source_target_pairs={{8,16},{12,20},{16,8},{20,12},{9,17},{13,21},{17,9},{21,13},{10,18... | collective-permute-start | bytes 1843208 | tf_op jit(solution)/shard_map/ppermute | solution.py:542
  199.5 16.8 %collective-permute-start.21 = (bf16[1200,128]{1,0:T(8,128)(2,1)S(1)}, bf16[1200,128]{1,0:T(8,128)(2,1)}, u32[]{:S(2)}, u32[]{:S(2)}) collective-permute-start(bf16[1200,128]{1,0:T(8,128)(2,1)S(1)} %fusion.4), channel_id=1, source_target_pairs={{0,8},{4,12},{8,0},{12,4},{16,24},{20,28},{24,16},{28,20},{1,9},{5... | collective-permute-start | bytes 921608 | tf_op jit(solution)/shard_map/ppermute | solution.py:542
  201.4 20.3 %copy-start.1 = (f32[16,128]{1,0:T(8,128)S(1)}, f32[16,128]{1,0:T(8,128)}, u32[]{:S(2)}) copy-start(f32[16,128]{1,0:T(8,128)} %param.15) | copy-start | bytes 24580
  206.7 9.6 %copy-start.13 = (bf16[3600,128]{1,0:T(8,128)(2,1)}, bf16[3600,128]{1,0:T(8,128)(2,1)S(1)}, u32[]{:S(2)}) copy-start(bf16[3600,128]{1,0:T(8,128)(2,1)S(1)} %collective-permute-done.14.refs_0_) | copy-start | bytes 2764804
  (10 other events, 33.3 us)

commit v7 on v5

--- a/solution.py
+++ b/solution.py
@@ -493,44 +493,57 @@
     )(weights, stat, shares, offsets)
 
 
-def sums_kernel(slot_ref, back_ref, weighted_ref, offset_ref, out_ref, wide_ref, *, classes):
+def sums_kernel(*refs, count, classes):
+    slot_refs, (back_ref, *refs) = refs[:count], refs[count:]
+    weighted_refs, (offset_ref, *refs) = refs[:count], refs[count:]
+    out_refs, wide_refs = refs[:count], refs[count:]
     padded = offset_ref.shape[0]
-    cycles = wide_ref.shape[1]
-    turns = offset_ref[...] * (slot_ref[0].astype(f32) * (1.0 / ANG_STEP))
-    cosine, sine_part = cos_sin_of_turns(turns)
+    cycles = wide_refs[0].shape[1]
+    turns = [
+        cos_sin_of_turns(offset_ref[...] * (slot_ref[0].astype(f32) * (1.0 / ANG_STEP)))
+        for slot_ref in slot_refs
+    ]
     for i in range(GROUP):
-        product = jnp.dot(back_ref[i], weighted_ref[0, i], preferred_element_type=f32)
-        re = product[:padded, :cycles] - product[padded:, cycles:]
-        im = product[:padded, cycles:] + product[padded:, :cycles]
-        start = 2 * i * classes
-        wide_ref[pl.ds(start, classes, stride=2), :] = (re * cosine - im * sine_part)[:classes]
-        wide_ref[pl.ds(start + 1, classes, stride=2), :] = (re * sine_part + im * cosine)[:classes]
-    out_ref[...] = wide_ref[...].astype(out_ref.dtype)
-
-
-def class_sums_of(slot, back, weighted, offsets, classes, dtype):
+        for (cosine, sine_part), weighted_ref, wide_ref in zip(turns, weighted_refs, wide_refs):
+            product = jnp.dot(back_ref[i], weighted_ref[0, i], preferred_element_type=f32)
+            re = product[:padded, :cycles] - product[padded:, cycles:]
+            im = product[:padded, cycles:] + product[padded:, :cycles]
+            start = 2 * i * classes
+            wide_ref[pl.ds(start, classes, stride=2), :] = (re * cosine - im * sine_part)[:classes]
+            wide_ref[pl.ds(start + 1, classes, stride=2), :] = (re * sine_part + im * cosine)[:classes]
+    for out_ref, wide_ref in zip(out_refs, wide_refs):
+        out_ref[...] = wide_ref[...].astype(out_ref.dtype)
+
+
+def class_sums_of(slots, back, weighted, offsets, classes, dtypes, groups=(0, ROTS // GROUP)):
+    begin, end = groups
     _, _, queries, double = weighted.shape
     cycles = double // 2
     rows = back.shape[1]
     block = 2 * GROUP * classes
-    piece = pl.BlockSpec((block, cycles), lambda g, u: (g, 0))
+    count = len(slots)
+    scalars = [jnp.reshape(slot, (1,)).astype(jnp.int32) for slot in slots]
     return pl.pallas_call(
-        functools.partial(sums_kernel, classes=classes),
+        functools.partial(sums_kernel, count=count, classes=classes),
         grid_spec=pltpu.PrefetchScalarGridSpec(
-            num_scalar_prefetch=1,
-            grid=(ROTS // GROUP,),
-            in_specs=[
-                pl.BlockSpec((GROUP, rows, queries), lambda g, u: (g, 0, 0)),
-                pl.BlockSpec((1, GROUP, queries, double), lambda g, u: (u[0], g, 0, 0)),
-                pl.BlockSpec(offsets.shape, lambda g, u: (0, 0)),
-            ],
-            out_specs=piece,
-            scratch_shapes=[pltpu.VMEM((block, cycles), f32)],
+            num_scalar_prefetch=count,
+            grid=(end - begin,),
+            in_specs=[pl.BlockSpec((GROUP, rows, queries), lambda g, *u: (g + begin, 0, 0))]
+            + [
+                pl.BlockSpec(
+                    (1, GROUP, queries, double),
+                    functools.partial(lambda j, g, *u: (u[j][0], g + begin, 0, 0), j),
+                )
+                for j in range(count)
+            ]
+            + [pl.BlockSpec(offsets.shape, lambda g, *u: (0, 0))],
+            out_specs=[pl.BlockSpec((block, cycles), lambda g, *u: (g, 0))] * count,
+            scratch_shapes=[pltpu.VMEM((block, cycles), f32)] * count,
         ),
-        out_shape=jax.ShapeDtypeStruct((ROTS * 2 * classes, cycles), dtype),
+        out_shape=[jax.ShapeDtypeStruct(((end - begin) * block, cycles), dtype) for dtype in dtypes],
         compiler_params=pltpu.CompilerParams(vmem_limit_bytes=VMEM_LIMIT),
         name="class_sums",
-    )(jnp.reshape(slot, (1,)).astype(jnp.int32), back, weighted, offsets)
+    )(*scalars, back, *[weighted] * count, offsets)
 
 
 def across(piece):
@@ -545,7 +558,7 @@
     index = lax.axis_index("dp")
     line, side = index // 2, index % 2
     _, steps = spectra_steps(base.shape[0])
-    cuts = [0, 2 * steps // 13, 6 * steps // 13, 10 * steps // 13, steps]
+    cuts = [0, 3 * steps // 13, 8 * steps // 13, steps]
 
     own_crossed = across(piece)
     near = along(piece, ((0, 1), (1, 0), (2, 3), (3, 2)))
@@ -566,7 +579,6 @@
     weighted, far_end, third_crossed = lax.optimization_barrier((weighted, far_end, third_crossed))
     fourth = far_middle + far_end
     fourth_crossed = across(fourth)
-    weighted = make_spectra(base, ctf_rows, cuts[3], cuts[4], weighted)
 
     pieces = [piece, own_crossed, near, near_crossed, third, third_crossed, fourth, fourth_crossed]
     places = [line, line ^ 1, jnp.where(line < 2, 2, 1), jnp.where(line < 2, 3, 0)]
@@ -574,36 +586,88 @@
     return weighted, pieces, slot_of
 
 
+def add_kernel(own_ref, *refs):
+    *whole_refs, head_ref, rest_ref, out_ref = refs
+    total = own_ref[...]
+    for ref in whole_refs:
+        total = total + ref[...].astype(f32)
+    part = jnp.where(pl.program_id(0) == 0, head_ref[...], rest_ref[...])
+    out_ref[...] = total + part.astype(f32)
+
+
+def add_pieces(own, whole, pair, block):
+    rows, cycles = own.shape
+    spec = pl.BlockSpec((block, cycles), lambda g: (g, 0))
+    head = pl.BlockSpec((block, cycles), lambda g: (0, 0))
+    rest = pl.BlockSpec((block, cycles), lambda g: (jnp.maximum(g - 1, 0), 0))
+    return pl.pallas_call(
+        add_kernel,
+        grid=(rows // block,),
+        in_specs=[spec] * (1 + len(whole)) + [head, rest],
+        out_specs=spec,
+        out_shape=jax.ShapeDtypeStruct(own.shape, f32),
+        name="add_pieces",
+    )(own, *whole, *pair)
+
+
 def reduce_on_line(back, weighted, offsets, classes):
     index = lax.axis_index("dp")
     line, side = index // 2, index % 2
     order = [jnp.where(line < 2, 3, 0), jnp.where(line < 2, 2, 1), line ^ 1, line]
-    theirs = [class_sums_of(2 * z + 1 - side, back, weighted, offsets, classes, bf16) for z in order]
-    ours = [class_sums_of(2 * z + side, back, weighted, offsets, classes, f32) for z in order]
-    at_end = (line == 0) | (line == 3)
-
-    crossed = [across(theirs[0])]
-    crossed[0], theirs[1], theirs[2], ours[0], ours[1] = lax.optimization_barrier(
-        (crossed[0], theirs[1], theirs[2], ours[0], ours[1])
+    theirs = [2 * z + 1 - side for z in order]
+    ours = [2 * z + side for z in order]
+    groups = ((0, 1), (1, ROTS // GROUP))
+    block = 2 * GROUP * classes
+    head, rest = [slice(a * block, b * block) for a, b in groups]
+    to_middle, between = ((0, 1), (3, 2)), ((1, 2), (2, 1))
+    neighbours = ((0, 1), (1, 0), (2, 3), (3, 2))
+
+    def sums(slots, dtypes, back, some=(0, ROTS // GROUP)):
+        return class_sums_of(slots, back, weighted, offsets, classes, dtypes, some)
+
+    def wide(piece):
+        return piece.astype(f32)
+
+    def then(back, *done):
+        return lax.optimization_barrier((back, *done))[0]
+
+    (away,) = sums(theirs[:1], [bf16], back, groups[0])
+    crossed_head = across(away)
+    back = then(back, away)
+    (away,) = sums(theirs[:1], [bf16], back, groups[1])
+    crossed_rest = across(away)
+    back = then(back, away)
+    own_0, away = sums([ours[0], theirs[1]], [f32, bf16], back)
+    crossed_1 = across(away)
+    crossed_head, own_0 = lax.optimization_barrier((crossed_head, own_0))
+    message = (own_0[head] + wide(crossed_head)).astype(bf16)
+    first_head = along(message, to_middle)
+    back = then(back, message)
+    own_1, away = sums([ours[1], theirs[2]], [f32, bf16], back)
+    crossed_2 = across(away)
+    crossed_rest, own_1 = lax.optimization_barrier((crossed_rest, own_1))
+    message = (own_0[rest] + wide(crossed_rest)).astype(bf16)
+    first_rest = along(message, to_middle)
+    back = then(back, message)
+    message = (own_0[head] + wide(crossed_head) + wide(first_head)).astype(bf16)
+    middle_head = along(message, between)
+    back = then(back, message)
+    own_2, away = sums([ours[2], theirs[3]], [f32, bf16], back)
+    crossed_3 = across(away)
+    crossed_1, first_rest, middle_head, own_2 = lax.optimization_barrier(
+        (crossed_1, first_rest, middle_head, own_2)
     )
-    crossed.append(across(theirs[1]))
-    farthest = ours[0] + crossed[0].astype(f32)
-    first = along(farthest.astype(bf16), ((0, 1), (3, 2)))
-    crossed[1], theirs[2], theirs[3], ours[2], ours[3] = lax.optimization_barrier(
-        (crossed[1], theirs[2], theirs[3], ours[2], ours[3])
-    )
-    crossed.append(across(theirs[2]))
-    next_farthest = ours[1] + crossed[1].astype(f32)
-    second = (jnp.where(at_end, next_farthest, farthest) + first.astype(f32)).astype(bf16)
-    from_ends = along(second, ((0, 1), (3, 2)))
-    from_middle = along(second, ((1, 2), (2, 1)))
-    crossed[2], theirs[3] = lax.optimization_barrier((crossed[2], theirs[3]))
-    crossed.append(across(theirs[3]))
-    third = (next_farthest + from_ends.astype(f32)).astype(bf16)
-    third = along(third, ((1, 2), (2, 1)))
-    fourth = (ours[2] + crossed[2].astype(f32) + from_middle.astype(f32)).astype(bf16)
-    fourth = along(fourth, ((0, 1), (1, 0), (2, 3), (3, 2)))
-    return ours[3] + crossed[3].astype(f32) + third.astype(f32) + fourth.astype(f32)
+    message = (own_0[rest] + wide(crossed_rest) + wide(first_rest)).astype(bf16)
+    middle_rest = along(message, between)
+    from_end = along((own_1 + wide(crossed_1)).astype(bf16), to_middle)
+    back = then(back, message)
+    (own_3,) = sums(ours[3:], [f32], back)
+    message = (own_2[head] + wide(crossed_2[head]) + wide(middle_head)).astype(bf16)
+    last_head = along(message, neighbours)
+    message = (own_2[rest] + wide(crossed_2[rest]) + wide(middle_rest)).astype(bf16)
+    last_rest = along(message, neighbours)
+    third = along((own_1 + wide(crossed_1) + wide(from_end)).astype(bf16), between)
+    return add_pieces(own_3, (crossed_3, third), (last_head, last_rest), block)
 
 
 def local(particles, references, ctf_table, rot_offset, prior_shift, defocus_group):
@@ -632,7 +696,7 @@
     queries = weighted.shape[1]
     weighted = weighted.reshape(slots, ROTS, queries, 2 * cycles)
 
-    early = 3 * slots // 4
+    early = slots - 1
     part = lax.axis_index("cls")
     corr, power = correlate(slot_of[:early], weighted, pieces[:early], classes, part)
     weights, stat, share = correlate(
@@ -645,7 +709,7 @@
     if on_line:
         class_rows = reduce_on_line(back, weighted, offsets, classes)
     else:
-        sums = [class_sums_of(slot_of[u], back, weighted, offsets, classes, bf16) for u in range(slots)]
+        sums = [class_sums_of([u], back, weighted, offsets, classes, [bf16])[0] for u in slot_of]
         summed = lax.psum_scatter(jnp.concatenate(sums, 0), "dp", scatter_dimension=0, tiled=True)
         class_rows = summed.astype(f32)
     class_sums = jnp.transpose(class_rows.reshape(own_rows, classes, 2, cycles), (0, 2, 1, 3))

time: 241 us -> 221 us (0.917); the launches traced: 237 us -> 221 us
  waiting for transfers between devices: 52.1 us -> 37.3 us
  Pallas kernels: 132 us -> 124 us
  starting transfers between devices: 31.7 us -> 39.4 us
  other arithmetic: 10.6 us -> 7.72 us
    ppermute x10 -> x13, waiting for transfers between devices: 45.2 us -> 17.5 us  [along(): lax.ppermute(piece, 'dp', [(2 * a + x, 2 * b + x) for a, b in pairs for x...]
    ppermute x8 -> x9, waiting for transfers between devices: 6.88 us -> 19.8 us  [across(): return lax.ppermute(piece, 'dp', [(d, d ^ 1) for d in range(8)])]
    ppermute x10 -> x13, starting transfers between devices: 21.6 us -> 26.9 us  [along(): lax.ppermute(piece, 'dp', [(2 * a + x, 2 * b + x) for a, b in pairs for x...]
    pallas_call x4 -> x3, Pallas kernels: 50 us -> 46.3 us  [make_spectra(): pl.pallas_call(functools.partial(spectra_kernel, per_step=per_step), grid...]
    pallas_call x8 -> x7, Pallas kernels: 40.3 us -> 36.7 us  [the longest x6 32.2 us: class_sums_of(): pl.pallas_call(functools.partial(sums_kernel, count=count, classes=classe...]
    add x1 -> x0, other arithmetic: 3.11 us -> none  [reduce_on_line(): ours[3] + crossed[3].astype(f32) + third.astype(f32) + fourth.astype(f32)]
    ppermute x8 -> x9, starting transfers between devices: 10 us -> 12.5 us  [across(): return lax.ppermute(piece, 'dp', [(d, d ^ 1) for d in range(8)])]
    convert_element_type x4 -> x8, other arithmetic: 7 us -> 7.24 us  [the longest x1 1.31 us: reduce_on_line(): (own_1 + wide(crossed_1) + wide(from_end)).astype(bf16)]
  transfers between devices with their start and end apart: 18 -> 22, of which waited for: 14 -> 11; matrix products, arithmetic and copies ran while one was open for 3% -> 4% of each run, Pallas kernels for 44% -> 44%
where the time goes in v7:
time: 221 us
  Pallas kernels  124 us (56%)
  starting transfers between devices  39.4 us (18%)
  waiting for transfers between devices  37.3 us (17%)
  other arithmetic  7.72 us (3%)
  blocking collectives  6.23 us (3%)
  local copies, waits for them, and re-layouts  3.79 us (2%)
    pallas_call x3, Pallas kernels, make_spectra(): pl.pallas_call(functools.partial(spectra_kernel, per_step=per_step), grid...  46.3 us
    pallas_call x6, Pallas kernels, class_sums_of(): pl.pallas_call(functools.partial(sums_kernel, count=count, classes=classe...  32.2 us
    pallas_call x2, Pallas kernels, correlate(): pl.pallas_call(functools.partial(correlate_kernel, slots=slots, classes=c...  28.4 us
    ppermute x13, starting transfers between devices, along(): lax.ppermute(piece, 'dp', [(2 * a + x, 2 * b + x) for a, b in pairs for x...  26.9 us
    ppermute x9, waiting for transfers between devices, across(): return lax.ppermute(piece, 'dp', [(d, d ^ 1) for d in range(8)])  19.8 us
    ppermute x13, waiting for transfers between devices, along(): lax.ppermute(piece, 'dp', [(2 * a + x, 2 * b + x) for a, b in pairs for x...  17.5 us
    ppermute x9, starting transfers between devices, across(): return lax.ppermute(piece, 'dp', [(d, d ^ 1) for d in range(8)])  12.5 us
    psum x1, blocking collectives, local(): shares = lax.psum(share, 'cls')  6.23 us
  transfers between devices with their start and end apart: 22, of which 11 were waited for; matrix products, arithmetic and copies ran while one was open for 4% of the time, Pallas kernels for 44%

profile of v7, /device:TPU:8, one launch (start us, length us, event | category | flops | bytes accessed | tf_op | source)
XLA Modules:
  0.0 220.6 jit_solution(15677586932513968645)
XLA Ops:
  0.7 3.0 %turn_references.1 = (bf16[3600,128]{1,0:T(8,128)(2,1)}, f32[56,128]{1,0:T(8,128)}) custom-call(s32[1]{0:T(128)} %bitcast.3.first_ref, s32[50]{0:T(128)} %offset_ref.1, bf16[3600,128]{1,0:T(8,128)(2,1)} %bitcast.45), custom_call_target="tpu_custom_call" | custom-call | tf_op jit(solution)/shard_map/turn_references/pallas_call | solution.py:251
  3.6 5.0 %collective-permute-start.1 = (bf16[3600,128]{1,0:T(8,128)(2,1)}, bf16[3600,128]{1,0:T(8,128)(2,1)S(1)}, u32[]{:S(2)}, u32[]{:S(2)}) collective-permute-start(bf16[3600,128]{1,0:T(8,128)(2,1)} %get-tuple-element.44.refs_15_), channel_id=1, source_target_pairs={{8,16},{12,20},{16,8},{20,12},{9,17},{13,21},{17,9},{21,13},{10,18... | collective-permute-start | bytes 2764808 | tf_op jit(solution)/shard_map/ppermute | solution.py:554
  8.7 1.6 collective-permute-start.2
  10.2 4.6 %centre.1.base_ref = f32[8,2,288,128]{3,2,1,0:T(8,128)} custom-call(s32[2,8]{1,0:T(2,128)} %bitcast.46, bf16[8,2,288,128]{3,2,1,0:T(8,128)(2,1)} %part_ref.1, f32[2,288,128]{2,1,0:T(8,128)} %constant.49.clone.turns_ref), custom_call_target="tpu_custom_call" | custom-call | tf_op jit(solution)/shard_map/centre/pallas_call | solution.py:87
  15.7 11.8 %spectra.3.refs_4_ = bf16[288,208,256]{2,1,0:T(8,128)(2,1)} custom-call(f32[8,2,288,128]{3,2,1,0:T(8,128)} %centre.1.base_ref, f32[8,128]{1,0:T(8,128)} %fusion.3.ctf_ref.refs_6_, bf16[576,576]{1,0:T(8,128)(2,1)} %constant.50.clone.table_ref, f32[2,5,2,288,128]{4,3,2,1,0:T(8,128)} %constant.51.clone.refs_0_.refs_1_.refs_2_.refs_3_, ...), custom_call_target="tpu_custom_call" | custom-call | tf_op jit(solution)/shard_map/spectra/pallas_call | solution.py:171
  27.4 1.6 collective-permute-done.1
  30.6 2.2 collective-permute-start.3
  32.8 1.6 collective-permute-start.5
  35.7 17.3 %spectra.4.refs_4_ = bf16[288,208,256]{2,1,0:T(8,128)(2,1)} custom-call(f32[8,2,288,128]{3,2,1,0:T(8,128)} %centre.1.base_ref, f32[8,128]{1,0:T(8,128)} %fusion.3.ctf_ref.refs_6_, bf16[576,576]{1,0:T(8,128)(2,1)} %constant.50.clone.table_ref, f32[2,5,2,288,128]{4,3,2,1,0:T(8,128)} %constant.51.clone.refs_0_.refs_1_.refs_2_.refs_3_, ...), custom_call_target="tpu_custom_call", output_to_operand_aliasing={{}: (7, {})} | custom-call | tf_op jit(solution)/shard_map/spectra/pallas_call | solution.py:171
  55.4 3.9 %collective-permute-start.6 = (bf16[3600,128]{1,0:T(8,128)(2,1)S(1)}, bf16[3600,128]{1,0:T(8,128)(2,1)S(1)}, u32[]{:S(2)}, u32[]{:S(2)}) collective-permute-start(bf16[3600,128]{1,0:T(8,128)(2,1)S(1)} %collective-permute-done.3), channel_id=1, source_target_pairs={{8,0},{12,4},{16,24},{20,28},{9,1},{13,5},{17,25},{21,29},{10,2},{... | collective-permute-start | bytes 2764808 | tf_op jit(solution)/shard_map/ppermute | solution.py:554
  59.3 17.2 %spectra.5 = bf16[288,208,256]{2,1,0:T(8,128)(2,1)} custom-call(f32[8,2,288,128]{3,2,1,0:T(8,128)} %centre.1.base_ref, f32[8,128]{1,0:T(8,128)} %fusion.3.ctf_ref.refs_6_, bf16[576,576]{1,0:T(8,128)(2,1)} %constant.50.clone.table_ref, f32[2,5,2,288,128]{4,3,2,1,0:T(8,128)} %constant.51.clone.refs_0_.refs_1_.refs_2_.refs_3_, ...), custom_call_target="tpu_custom_call", output_to_operand_aliasing={{}: (7, {})} | custom-call | tf_op jit(solution)/shard_map/spectra/pallas_call | solution.py:171
  76.9 1.6 collective-permute-start.8
  78.4 17.1 %correlate.1 = (f32[36,112,256]{2,1,0:T(8,128)}, f32[56,128]{1,0:T(8,128)}) custom-call(s32[1]{0:T(128)} %bitcast.7.refs_0_, s32[1]{0:T(128)} %bitcast.8.refs_1_, s32[1]{0:T(128)} %bitcast.9.refs_2_.refs_0_, s32[1]{0:T(128)} %bitcast.10.refs_3_, s32[1]{0:T(128)} %bitcast.11.refs_4_.refs_0_, s32[1]{0:T(128)} %bitcast.12.refs_5_, s32[1]{0:T(128)} %bitcast.13.refs_6_.refs_0_, ...), custom_call_target="tpu_custom_call" | custom-call | tf_op jit(solution)/shard_map/correlate/pallas_call | solution.py:417
  97.1 11.3 %scores.1 = (f32[36,56,256]{2,1,0:T(8,128)}, f32[64,128]{1,0:T(8,128)}, f32[4,2,128]{2,1,0:T(2,128)}) custom-call(s32[1]{0:T(128)} %bitcast.refs_0_, s32[1]{0:T(128)} %bitcast.1.refs_7_.refs_1_, bf16[8,36,208,256]{3,2,1,0:T(8,128)(2,1)} %bitcast.34, bf16[3600,128]{1,0:T(8,128)(2,1)} %copy-done.15, f32[36,112,256]{2,1,0:T(8,128)} %get-tuple-element.56.refs_4_, ...), custom_call_target="tpu_custom_call" | custom-call | tf_op jit(solution)/shard_map/scores/pallas_call | solution.py:417
  108.4 6.2 %psum.7.share_ref = f32[4,2,128]{2,1,0:T(2,128)} all-reduce(f32[4,2,128]{2,1,0:T(2,128)} %get-tuple-element.60), channel_id=1, replica_groups=mesh['dp'=8,'cls'=4] {'cls'}, use_global_device_ids=true, to_apply=%region_0.1 | all-reduce | flops 1024 | bytes 8192 | tf_op jit(solution)/shard_map/psum | solution.py:705
  114.6 5.5 %back.1 = (bf16[36,112,208]{2,1,0:T(8,128)(2,1)}, f32[8,128]{1,0:T(8,128)}, f32[56,128]{1,0:T(8,128)}) custom-call(f32[36,56,256]{2,1,0:T(8,128)} %get-tuple-element.58.weight_ref, f32[64,128]{1,0:T(8,128)} %get-tuple-element.59.stat_ref, f32[4,2,128]{2,1,0:T(2,128)} %psum.7.share_ref, f32[56,128]{1,0:T(8,128)} %get-tuple-element.61.offset_ref.refs_3_.refs_5_), custom_call_target="tpu_custom_call" | custom-call | tf_op jit(solution)/shard_map/back/pallas_call | solution.py:483
  120.1 2.6 %class_sums.6 = bf16[1200,128]{1,0:T(8,128)(2,1)} custom-call(s32[1]{0:T(128)} %bitcast.16.refs_0_, bf16[36,112,208]{2,1,0:T(8,128)(2,1)} %get-tuple-element.78.refs_1_.refs_2_, bf16[8,36,208,256]{3,2,1,0:T(8,128)(2,1)} %bitcast.35, f32[56,128]{1,0:T(8,128)} %get-tuple-element.61.offset_ref.refs_3_.refs_5_), custom_call_target="tpu_custom_call" | custom-call | tf_op jit(solution)/shard_map/class_sums/pallas_call | solution.py:526
  124.2 3.2 %class_sums.7 = bf16[2400,128]{1,0:T(8,128)(2,1)} custom-call(s32[1]{0:T(128)} %bitcast.16.refs_0_, bf16[36,112,208]{2,1,0:T(8,128)(2,1)} %get-tuple-element.78.refs_1_.refs_2_, bf16[8,36,208,256]{3,2,1,0:T(8,128)(2,1)} %bitcast.36, f32[56,128]{1,0:T(8,128)} %get-tuple-element.61.offset_ref.refs_3_.refs_5_), custom_call_target="tpu_custom_call" | custom-call | tf_op jit(solution)/shard_map/class_sums/pallas_call | solution.py:526
  128.0 7.0 %class_sums.8 = (f32[3600,128]{1,0:T(8,128)}, bf16[3600,128]{1,0:T(8,128)(2,1)}) custom-call(s32[1]{0:T(128)} %bitcast.13.refs_6_.refs_0_, s32[1]{0:T(128)} %bitcast.17.refs_1_, bf16[36,112,208]{2,1,0:T(8,128)(2,1)} %get-tuple-element.78.refs_1_.refs_2_, bf16[8,36,208,256]{3,2,1,0:T(8,128)(2,1)} %bitcast.37, bf16[8,36,208,256]{3,2,1,0:T(8,128)(2,1)} %bitcast.38, ...), custom_call_target="tpu_custom_call" | custom-call | tf_op jit(solution)/shard_map/class_sums/pallas_call | solution.py:526
  139.0 7.2 %class_sums.9 = (f32[3600,128]{1,0:T(8,128)}, bf16[3600,128]{1,0:T(8,128)(2,1)}) custom-call(s32[1]{0:T(128)} %bitcast.11.refs_4_.refs_0_, s32[1]{0:T(128)} %bitcast.18.refs_1_, bf16[36,112,208]{2,1,0:T(8,128)(2,1)} %get-tuple-element.78.refs_1_.refs_2_, bf16[8,36,208,256]{3,2,1,0:T(8,128)(2,1)} %bitcast.39, bf16[8,36,208,256]{3,2,1,0:T(8,128)(2,1)} %bitcast.40, ...), custom_call_target="tpu_custom_call" | custom-call | tf_op jit(solution)/shard_map/class_sums/pallas_call | solution.py:526
  149.3 3.1 %collective-permute-start.14 = (bf16[1200,128]{1,0:T(8,128)(2,1)}, bf16[1200,128]{1,0:T(8,128)(2,1)}, u32[]{:S(2)}, u32[]{:S(2)}) collective-permute-start(bf16[1200,128]{1,0:T(8,128)(2,1)} %add_convert_fusion.4), channel_id=1, source_target_pairs={{8,16},{12,20},{16,8},{20,12},{9,17},{13,21},{17,9},{21,13},{10,18... | collective-permute-start | bytes 921608 | tf_op jit(solution)/shard_map/ppermute | solution.py:554
  153.9 7.0 %class_sums.10 = (f32[3600,128]{1,0:T(8,128)}, bf16[3600,128]{1,0:T(8,128)(2,1)}) custom-call(s32[1]{0:T(128)} %bitcast.9.refs_2_.refs_0_, s32[1]{0:T(128)} %bitcast.19.refs_1_, bf16[36,112,208]{2,1,0:T(8,128)(2,1)} %get-tuple-element.78.refs_1_.refs_2_, bf16[8,36,208,256]{3,2,1,0:T(8,128)(2,1)} %bitcast.41, bf16[8,36,208,256]{3,2,1,0:T(8,128)(2,1)} %bitcast.42, ...), custom_call_target="tpu_custom_call" | custom-call | tf_op jit(solution)/shard_map/class_sums/pallas_call | solution.py:526
  160.9 5.0 %collective-permute-done.12 = bf16[3600,128]{1,0:T(8,128)(2,1)S(1)} collective-permute-done((bf16[3600,128]{1,0:T(8,128)(2,1)}, bf16[3600,128]{1,0:T(8,128)(2,1)S(1)}, u32[]{:S(2)}, u32[]{:S(2)}) %collective-permute-start.12) | collective-permute-done | bytes 921632 | tf_op jit(solution)/shard_map/ppermute | solution.py:550
  167.3 3.2 %collective-permute-start.20 = (bf16[2400,128]{1,0:T(8,128)(2,1)S(1)}, bf16[2400,128]{1,0:T(8,128)(2,1)S(1)}, u32[]{:S(2)}, u32[]{:S(2)}) collective-permute-start(bf16[2400,128]{1,0:T(8,128)(2,1)S(1)} %add_convert_fusion.2), channel_id=1, source_target_pairs={{8,16},{12,20},{16,8},{20,12},{9,17},{13,21},{17,9},{21,13},{10,18... | collective-permute-start | bytes 1843208 | tf_op jit(solution)/shard_map/ppermute | solution.py:554
  172.0 1.6 collective-permute-start.15
  173.6 12.1 %collective-permute-done.18 = bf16[3600,128]{1,0:T(8,128)(2,1)S(1)} collective-permute-done((bf16[3600,128]{1,0:T(8,128)(2,1)}, bf16[3600,128]{1,0:T(8,128)(2,1)S(1)}, u32[]{:S(2)}, u32[]{:S(2)}) %collective-permute-start.18) | collective-permute-done | bytes 921632 | tf_op jit(solution)/shard_map/ppermute | solution.py:550
  187.4 8.6 %collective-permute-done.16 = bf16[3600,128]{1,0:T(8,128)(2,1)S(1)} collective-permute-done((bf16[3600,128]{1,0:T(8,128)(2,1)S(1)}, bf16[3600,128]{1,0:T(8,128)(2,1)S(1)}, u32[]{:S(2)}, u32[]{:S(2)}) %collective-permute-start.16) | collective-permute-done | bytes 921632 | tf_op jit(solution)/shard_map/ppermute | solution.py:554
  197.3 2.8 %collective-permute-start.17 = (bf16[3600,128]{1,0:T(8,128)(2,1)}, bf16[3600,128]{1,0:T(8,128)(2,1)S(1)}, u32[]{:S(2)}, u32[]{:S(2)}) collective-permute-start(bf16[3600,128]{1,0:T(8,128)(2,1)} %add_convert_fusion), channel_id=1, source_target_pairs={{8,16},{12,20},{16,8},{20,12},{9,17},{13,21},{17,9},{21,13},{10,18... | collective-permute-start | bytes 2764808 | tf_op jit(solution)/shard_map/ppermute | solution.py:554
  203.1 5.2 %class_sums.11.own_ref = f32[3600,128]{1,0:T(8,128)} custom-call(s32[1]{0:T(128)} %bitcast.7.refs_0_, bf16[36,112,208]{2,1,0:T(8,128)(2,1)} %get-tuple-element.78.refs_1_.refs_2_, bf16[8,36,208,256]{3,2,1,0:T(8,128)(2,1)} %bitcast.43, f32[56,128]{1,0:T(8,128)} %get-tuple-element.61.offset_ref.refs_3_.refs_5_), custom_call_target="tpu_custom_call" | custom-call | tf_op jit(solution)/shard_map/class_sums/pallas_call | solution.py:526
  208.4 4.2 %collective-permute-done.19.refs_2_ = bf16[1200,128]{1,0:T(8,128)(2,1)} collective-permute-done((bf16[1200,128]{1,0:T(8,128)(2,1)S(1)}, bf16[1200,128]{1,0:T(8,128)(2,1)}, u32[]{:S(2)}, u32[]{:S(2)}) %collective-permute-start.19) | collective-permute-done | bytes 307232 | tf_op jit(solution)/shard_map/ppermute | solution.py:554
  212.5 2.7 %collective-permute-done.17.refs_1_ = bf16[3600,128]{1,0:T(8,128)(2,1)S(1)} collective-permute-done((bf16[3600,128]{1,0:T(8,128)(2,1)}, bf16[3600,128]{1,0:T(8,128)(2,1)S(1)}, u32[]{:S(2)}, u32[]{:S(2)}) %collective-permute-start.17) | collective-permute-done | bytes 921632 | tf_op jit(solution)/shard_map/ppermute | solution.py:554
  216.1 4.5 %add_pieces.1 = f32[3600,128]{1,0:T(8,128)} custom-call(f32[3600,128]{1,0:T(8,128)} %class_sums.11.own_ref, bf16[3600,128]{1,0:T(8,128)(2,1)} %copy-done.13, bf16[3600,128]{1,0:T(8,128)(2,1)} %copy-done.14, bf16[1200,128]{1,0:T(8,128)(2,1)} %collective-permute-done.19.refs_2_, bf16[2400,128]{1,0:T(8,128)(2,1)} %copy-done.16), custom_call_target="tpu_custom_call" | custom-call | tf_op jit(solution)/shard_map/add_pieces/pallas_call | solution.py:603
  (80 shorter events, 28.3 us)
Async XLA Ops:
  0.6 14.3 %copy-start = (f32[16,128]{1,0:T(8,128)S(1)}, f32[16,128]{1,0:T(8,128)}, u32[]{:S(2)}) copy-start(f32[16,128]{1,0:T(8,128)} %param.15) | copy-start | bytes 24580
  3.6 23.8 %collective-permute-start = (bf16[3600,128]{1,0:T(8,128)(2,1)}, bf16[3600,128]{1,0:T(8,128)(2,1)S(1)}, u32[]{:S(2)}, u32[]{:S(2)}) collective-permute-start(bf16[3600,128]{1,0:T(8,128)(2,1)} %get-tuple-element.44.refs_15_), channel_id=1, source_target_pairs={{0,8},{4,12},{8,0},{12,4},{16,24},{20,28},{24,16},{28,20},{1,9},{5... | collective-permute-start | bytes 2764808 | tf_op jit(solution)/shard_map/ppermute | solution.py:554
  3.6 25.4 %collective-permute-start.1 = (bf16[3600,128]{1,0:T(8,128)(2,1)}, bf16[3600,128]{1,0:T(8,128)(2,1)S(1)}, u32[]{:S(2)}, u32[]{:S(2)}) collective-permute-start(bf16[3600,128]{1,0:T(8,128)(2,1)} %get-tuple-element.44.refs_15_), channel_id=1, source_target_pairs={{8,16},{12,20},{16,8},{20,12},{9,17},{13,21},{17,9},{21,13},{10,18... | collective-permute-start | bytes 2764808 | tf_op jit(solution)/shard_map/ppermute | solution.py:554
  8.7 21.9 %collective-permute-start.2 = (bf16[3600,128]{1,0:T(8,128)(2,1)}, bf16[3600,128]{1,0:T(8,128)(2,1)S(1)}, u32[]{:S(2)}, u32[]{:S(2)}) collective-permute-start(bf16[3600,128]{1,0:T(8,128)(2,1)} %get-tuple-element.44.refs_15_), channel_id=1, source_target_pairs={{0,4},{4,0},{8,12},{12,8},{16,20},{20,16},{24,28},{28,24},{1,5},{5... | collective-permute-start | bytes 2764808 | tf_op jit(solution)/shard_map/ppermute | solution.py:550
  27.4 25.5 %copy-start.9 = (bf16[3600,128]{1,0:T(8,128)(2,1)}, bf16[3600,128]{1,0:T(8,128)(2,1)S(1)}, u32[]{:S(2)}) copy-start(bf16[3600,128]{1,0:T(8,128)(2,1)S(1)} %collective-permute-done.refs_17_) | copy-start | bytes 2764804
  30.6 22.4 %copy-start.10 = (bf16[3600,128]{1,0:T(8,128)(2,1)}, bf16[3600,128]{1,0:T(8,128)(2,1)S(1)}, u32[]{:S(2)}) copy-start(bf16[3600,128]{1,0:T(8,128)(2,1)S(1)} %collective-permute-done.2.refs_16_) | copy-start | bytes 2764804
  30.6 22.6 %collective-permute-start.3 = (bf16[3600,128]{1,0:T(8,128)(2,1)S(1)}, bf16[3600,128]{1,0:T(8,128)(2,1)S(1)}, u32[]{:S(2)}, u32[]{:S(2)}) collective-permute-start(bf16[3600,128]{1,0:T(8,128)(2,1)S(1)} %collective-permute-done.refs_17_), channel_id=1, source_target_pairs={{8,16},{12,20},{16,8},{20,12},{9,17},{13,21},{17,9},{21,13},{10,18... | collective-permute-start | bytes 2764808 | tf_op jit(solution)/shard_map/ppermute | solution.py:554
  32.8 20.8 %collective-permute-start.5 = (bf16[3600,128]{1,0:T(8,128)(2,1)S(1)}, bf16[3600,128]{1,0:T(8,128)(2,1)S(1)}, u32[]{:S(2)}, u32[]{:S(2)}) collective-permute-start(bf16[3600,128]{1,0:T(8,128)(2,1)S(1)} %collective-permute-done.refs_17_), channel_id=1, source_target_pairs={{0,4},{4,0},{8,12},{12,8},{16,20},{20,16},{24,28},{28,24},{1,5},{5... | collective-permute-start | bytes 2764808 | tf_op jit(solution)/shard_map/ppermute | solution.py:550
  34.3 19.5 %collective-permute-start.4 = (bf16[3600,128]{1,0:T(8,128)(2,1)S(1)}, bf16[3600,128]{1,0:T(8,128)(2,1)S(1)}, u32[]{:S(2)}, u32[]{:S(2)}) collective-permute-start(bf16[3600,128]{1,0:T(8,128)(2,1)S(1)} %collective-permute-done.1), channel_id=1, source_target_pairs={{8,0},{12,4},{16,24},{20,28},{9,1},{13,5},{17,25},{21,29},{10,2},{... | collective-permute-start | bytes 2764808 | tf_op jit(solution)/shard_map/ppermute | solution.py:554
  53.6 23.0 %copy-start.11 = (bf16[3600,128]{1,0:T(8,128)(2,1)}, bf16[3600,128]{1,0:T(8,128)(2,1)S(1)}, u32[]{:S(2)}) copy-start(bf16[3600,128]{1,0:T(8,128)(2,1)S(1)} %collective-permute-done.5.refs_18_) | copy-start | bytes 2764804
  54.1 22.5 %copy-start.4 = (bf16[3600,128]{1,0:T(8,128)(2,1)}, bf16[3600,128]{1,0:T(8,128)(2,1)S(1)}, u32[]{:S(2)}) copy-start(bf16[3600,128]{1,0:T(8,128)(2,1)S(1)} %add.89.refs_19_) | copy-start | bytes 2764804
  54.1 22.5 %collective-permute-start.7 = (bf16[3600,128]{1,0:T(8,128)(2,1)S(1)}, bf16[3600,128]{1,0:T(8,128)(2,1)S(1)}, u32[]{:S(2)}, u32[]{:S(2)}) collective-permute-start(bf16[3600,128]{1,0:T(8,128)(2,1)S(1)} %add.89.refs_19_), channel_id=1, source_target_pairs={{0,4},{4,0},{8,12},{12,8},{16,20},{20,16},{24,28},{28,24},{1,5},{5... | collective-permute-start | bytes 2764808 | tf_op jit(solution)/shard_map/ppermute | solution.py:550
  55.4 21.2 %collective-permute-start.6 = (bf16[3600,128]{1,0:T(8,128)(2,1)S(1)}, bf16[3600,128]{1,0:T(8,128)(2,1)S(1)}, u32[]{:S(2)}, u32[]{:S(2)}) collective-permute-start(bf16[3600,128]{1,0:T(8,128)(2,1)S(1)} %collective-permute-done.3), channel_id=1, source_target_pairs={{8,0},{12,4},{16,24},{20,28},{9,1},{13,5},{17,25},{21,29},{10,2},{... | collective-permute-start | bytes 2764808 | tf_op jit(solution)/shard_map/ppermute | solution.py:554
  76.9 19.3 %collective-permute-start.8 = (bf16[3600,128]{1,0:T(8,128)(2,1)S(1)}, bf16[3600,128]{1,0:T(8,128)(2,1)S(1)}, u32[]{:S(2)}, u32[]{:S(2)}) collective-permute-start(bf16[3600,128]{1,0:T(8,128)(2,1)S(1)} %add.90.refs_21_), channel_id=1, source_target_pairs={{0,4},{4,0},{8,12},{12,8},{16,20},{20,16},{24,28},{28,24},{1,5},{5... | collective-permute-start | bytes 2764808 | tf_op jit(solution)/shard_map/ppermute | solution.py:550
  122.7 13.7 %collective-permute-start.9 = (bf16[1200,128]{1,0:T(8,128)(2,1)}, bf16[1200,128]{1,0:T(8,128)(2,1)S(1)}, u32[]{:S(2)}, u32[]{:S(2)}) collective-permute-start(bf16[1200,128]{1,0:T(8,128)(2,1)} %class_sums.6), channel_id=1, source_target_pairs={{0,4},{4,0},{8,12},{12,8},{16,20},{20,16},{24,28},{28,24},{1,5},{5... | collective-permute-start | bytes 921608 | tf_op jit(solution)/shard_map/ppermute | solution.py:550
  127.4 18.8 %collective-permute-start.10 = (bf16[2400,128]{1,0:T(8,128)(2,1)}, bf16[2400,128]{1,0:T(8,128)(2,1)S(1)}, u32[]{:S(2)}, u32[]{:S(2)}) collective-permute-start(bf16[2400,128]{1,0:T(8,128)(2,1)} %class_sums.7), channel_id=1, source_target_pairs={{0,4},{4,0},{8,12},{12,8},{16,20},{20,16},{24,28},{28,24},{1,5},{5... | collective-permute-start | bytes 1843208 | tf_op jit(solution)/shard_map/ppermute | solution.py:550
  135.0 31.0 %collective-permute-start.12 = (bf16[3600,128]{1,0:T(8,128)(2,1)}, bf16[3600,128]{1,0:T(8,128)(2,1)S(1)}, u32[]{:S(2)}, u32[]{:S(2)}) collective-permute-start(bf16[3600,128]{1,0:T(8,128)(2,1)} %get-tuple-element.75), channel_id=1, source_target_pairs={{0,4},{4,0},{8,12},{12,8},{16,20},{20,16},{24,28},{28,24},{1,5},{5... | collective-permute-start | bytes 2764808 | tf_op jit(solution)/shard_map/ppermute | solution.py:550
  137.7 10.8 %collective-permute-start.11 = (bf16[1200,128]{1,0:T(8,128)(2,1)S(1)}, bf16[1200,128]{1,0:T(8,128)(2,1)S(1)}, u32[]{:S(2)}, u32[]{:S(2)}) collective-permute-start(bf16[1200,128]{1,0:T(8,128)(2,1)S(1)} %fusion.2), channel_id=1, source_target_pairs={{0,8},{4,12},{24,16},{28,20},{1,9},{5,13},{25,17},{29,21},{2,10},{... | collective-permute-start | bytes 921608 | tf_op jit(solution)/shard_map/ppermute | solution.py:554
  139.0 7.2 %copy-start.3 = (f32[3600,128]{1,0:T(8,128)S(1)}, f32[3600,128]{1,0:T(8,128)}, u32[]{:S(2)}) copy-start(f32[3600,128]{1,0:T(8,128)} %get-tuple-element.68) | copy-start | bytes 5529604
  147.2 18.8 %collective-permute-start.13 = (bf16[2400,128]{1,0:T(8,128)(2,1)}, bf16[2400,128]{1,0:T(8,128)(2,1)}, u32[]{:S(2)}, u32[]{:S(2)}) collective-permute-start(bf16[2400,128]{1,0:T(8,128)(2,1)} %fusion.1), channel_id=1, source_target_pairs={{0,8},{4,12},{24,16},{28,20},{1,9},{5,13},{25,17},{29,21},{2,10},{... | collective-permute-start | bytes 1843208 | tf_op jit(solution)/shard_map/ppermute | solution.py:554
  149.3 11.6 %collective-permute-start.14 = (bf16[1200,128]{1,0:T(8,128)(2,1)}, bf16[1200,128]{1,0:T(8,128)(2,1)}, u32[]{:S(2)}, u32[]{:S(2)}) collective-permute-start(bf16[1200,128]{1,0:T(8,128)(2,1)} %add_convert_fusion.4), channel_id=1, source_target_pairs={{8,16},{12,20},{16,8},{20,12},{9,17},{13,21},{17,9},{21,13},{10,18... | collective-permute-start | bytes 921608 | tf_op jit(solution)/shard_map/ppermute | solution.py:554
  152.5 33.3 %collective-permute-start.18 = (bf16[3600,128]{1,0:T(8,128)(2,1)}, bf16[3600,128]{1,0:T(8,128)(2,1)S(1)}, u32[]{:S(2)}, u32[]{:S(2)}) collective-permute-start(bf16[3600,128]{1,0:T(8,128)(2,1)} %get-tuple-element.83), channel_id=1, source_target_pairs={{0,4},{4,0},{8,12},{12,8},{16,20},{20,16},{24,28},{28,24},{1,5},{5... | collective-permute-start | bytes 2764808 | tf_op jit(solution)/shard_map/ppermute | solution.py:550
  160.9 9.5 %copy-start.2 = (f32[3600,128]{1,0:T(8,128)S(1)}, f32[3600,128]{1,0:T(8,128)}, u32[]{:S(2)}) copy-start(f32[3600,128]{1,0:T(8,128)} %get-tuple-element.80) | copy-start | bytes 5529604
  167.3 18.5 %copy-start.6 = (f32[3600,128]{1,0:T(8,128)S(1)}, f32[3600,128]{1,0:T(8,128)}, u32[]{:S(2)}) copy-start(f32[3600,128]{1,0:T(8,128)} %get-tuple-element.82) | copy-start | bytes 5529604
  167.3 18.5 %collective-permute-start.20 = (bf16[2400,128]{1,0:T(8,128)(2,1)S(1)}, bf16[2400,128]{1,0:T(8,128)(2,1)S(1)}, u32[]{:S(2)}, u32[]{:S(2)}) collective-permute-start(bf16[2400,128]{1,0:T(8,128)(2,1)S(1)} %add_convert_fusion.2), channel_id=1, source_target_pairs={{8,16},{12,20},{16,8},{20,12},{9,17},{13,21},{17,9},{21,13},{10,18... | collective-permute-start | bytes 1843208 | tf_op jit(solution)/shard_map/ppermute | solution.py:554
  170.7 25.3 %collective-permute-start.16 = (bf16[3600,128]{1,0:T(8,128)(2,1)S(1)}, bf16[3600,128]{1,0:T(8,128)(2,1)S(1)}, u32[]{:S(2)}, u32[]{:S(2)}) collective-permute-start(bf16[3600,128]{1,0:T(8,128)(2,1)S(1)} %fusion), channel_id=1, source_target_pairs={{0,8},{4,12},{24,16},{28,20},{1,9},{5,13},{25,17},{29,21},{2,10},{... | collective-permute-start | bytes 2764808 | tf_op jit(solution)/shard_map/ppermute | solution.py:554
  172.0 40.5 %collective-permute-start.15 = (bf16[3600,128]{1,0:T(8,128)(2,1)}, bf16[3600,128]{1,0:T(8,128)(2,1)S(1)}, u32[]{:S(2)}, u32[]{:S(2)}) collective-permute-start(bf16[3600,128]{1,0:T(8,128)(2,1)} %get-tuple-element.79), channel_id=1, source_target_pairs={{0,4},{4,0},{8,12},{12,8},{16,20},{20,16},{24,28},{28,24},{1,5},{5... | collective-permute-start | bytes 2764808 | tf_op jit(solution)/shard_map/ppermute | solution.py:550
  186.0 15.3 %copy-start.17 = (f32[56,128]{1,0:T(8,128)S(1)}, f32[56,128]{1,0:T(8,128)}, u32[]{:S(2)}) copy-start(f32[56,128]{1,0:T(8,128)} %get-tuple-element.63) | copy-start | bytes 86020
  186.0 26.5 %collective-permute-start.21 = (bf16[2400,128]{1,0:T(8,128)(2,1)S(1)}, bf16[2400,128]{1,0:T(8,128)(2,1)S(1)}, u32[]{:S(2)}, u32[]{:S(2)}) collective-permute-start(bf16[2400,128]{1,0:T(8,128)(2,1)S(1)} %add_convert_fusion.1), channel_id=1, source_target_pairs={{0,8},{4,12},{8,0},{12,4},{16,24},{20,28},{24,16},{28,20},{1,9},{5... | collective-permute-start | bytes 1843208 | tf_op jit(solution)/shard_map/ppermute | solution.py:554
  197.3 17.9 %collective-permute-start.17 = (bf16[3600,128]{1,0:T(8,128)(2,1)}, bf16[3600,128]{1,0:T(8,128)(2,1)S(1)}, u32[]{:S(2)}, u32[]{:S(2)}) collective-permute-start(bf16[3600,128]{1,0:T(8,128)(2,1)} %add_convert_fusion), channel_id=1, source_target_pairs={{8,16},{12,20},{16,8},{20,12},{9,17},{13,21},{17,9},{21,13},{10,18... | collective-permute-start | bytes 2764808 | tf_op jit(solution)/shard_map/ppermute | solution.py:554
  201.2 11.3 %collective-permute-start.19 = (bf16[1200,128]{1,0:T(8,128)(2,1)S(1)}, bf16[1200,128]{1,0:T(8,128)(2,1)}, u32[]{:S(2)}, u32[]{:S(2)}) collective-permute-start(bf16[1200,128]{1,0:T(8,128)(2,1)S(1)} %add_convert_fusion.3), channel_id=1, source_target_pairs={{0,8},{4,12},{8,0},{12,4},{16,24},{20,28},{24,16},{28,20},{1,9},{5... | collective-permute-start | bytes 921608 | tf_op jit(solution)/shard_map/ppermute | solution.py:554
  203.1 17.4 %copy-start.1 = (f32[16,128]{1,0:T(8,128)S(1)}, f32[16,128]{1,0:T(8,128)}, u32[]{:S(2)}) copy-start(f32[16,128]{1,0:T(8,128)} %param.15) | copy-start | bytes 24580
  (9 other events, 20.1 us)

commit v8 on v7

--- a/solution.py
+++ b/solution.py
@@ -586,28 +586,30 @@
     return weighted, pieces, slot_of
 
 
-def add_kernel(own_ref, *refs):
-    *whole_refs, head_ref, rest_ref, out_ref = refs
-    total = own_ref[...]
-    for ref in whole_refs:
-        total = total + ref[...].astype(f32)
-    part = jnp.where(pl.program_id(0) == 0, head_ref[...], rest_ref[...])
-    out_ref[...] = total + part.astype(f32)
-
-
-def add_pieces(own, whole, pair, block):
+def add_kernel(own_ref, whole_ref, *refs, heads):
+    pairs, out_ref = refs[:-1], refs[-1]
+    total = own_ref[...] + whole_ref[...].astype(f32)
+    for n in range(0, len(pairs), 2):
+        part = jnp.where(pl.program_id(0) < heads, pairs[n][...], pairs[n + 1][...])
+        total = total + part.astype(f32)
+    out_ref[...] = total
+
+
+def add_pieces(own, whole, pairs, block):
     rows, cycles = own.shape
+    heads = pairs[0][0].shape[0] // block
     spec = pl.BlockSpec((block, cycles), lambda g: (g, 0))
-    head = pl.BlockSpec((block, cycles), lambda g: (0, 0))
-    rest = pl.BlockSpec((block, cycles), lambda g: (jnp.maximum(g - 1, 0), 0))
+    head = pl.BlockSpec((block, cycles), lambda g: (jnp.minimum(g, heads - 1), 0))
+    rest = pl.BlockSpec((block, cycles), lambda g: (jnp.maximum(g - heads, 0), 0))
     return pl.pallas_call(
-        add_kernel,
+        functools.partial(add_kernel, heads=heads),
         grid=(rows // block,),
-        in_specs=[spec] * (1 + len(whole)) + [head, rest],
+        in_specs=[spec, spec] + [head, rest] * len(pairs),
         out_specs=spec,
         out_shape=jax.ShapeDtypeStruct(own.shape, f32),
+        compiler_params=pltpu.CompilerParams(vmem_limit_bytes=VMEM_LIMIT),
         name="add_pieces",
-    )(own, *whole, *pair)
+    )(own, whole, *[part for pair in pairs for part in pair])
 
 
 def reduce_on_line(back, weighted, offsets, classes):
@@ -616,7 +618,7 @@
     order = [jnp.where(line < 2, 3, 0), jnp.where(line < 2, 2, 1), line ^ 1, line]
     theirs = [2 * z + 1 - side for z in order]
     ours = [2 * z + side for z in order]
-    groups = ((0, 1), (1, ROTS // GROUP))
+    groups = ((0, 2), (2, ROTS // GROUP))
     block = 2 * GROUP * classes
     head, rest = [slice(a * block, b * block) for a, b in groups]
     to_middle, between = ((0, 1), (3, 2)), ((1, 2), (2, 1))
@@ -657,17 +659,23 @@
     crossed_1, first_rest, middle_head, own_2 = lax.optimization_barrier(
         (crossed_1, first_rest, middle_head, own_2)
     )
+    messages = [(own_1[r] + wide(crossed_1[r])).astype(bf16) for r in (head, rest)]
+    from_end = [along(message, to_middle) for message in messages]
+    first_rest = then(first_rest, *messages)
     message = (own_0[rest] + wide(crossed_rest) + wide(first_rest)).astype(bf16)
     middle_rest = along(message, between)
-    from_end = along((own_1 + wide(crossed_1)).astype(bf16), to_middle)
     back = then(back, message)
     (own_3,) = sums(ours[3:], [f32], back)
     message = (own_2[head] + wide(crossed_2[head]) + wide(middle_head)).astype(bf16)
     last_head = along(message, neighbours)
+    message = (own_1[head] + wide(crossed_1[head]) + wide(from_end[0])).astype(bf16)
+    third_head = along(message, between)
+    middle_rest = then(middle_rest, third_head)
     message = (own_2[rest] + wide(crossed_2[rest]) + wide(middle_rest)).astype(bf16)
     last_rest = along(message, neighbours)
-    third = along((own_1 + wide(crossed_1) + wide(from_end)).astype(bf16), between)
-    return add_pieces(own_3, (crossed_3, third), (last_head, last_rest), block)
+    message = (own_1[rest] + wide(crossed_1[rest]) + wide(from_end[1])).astype(bf16)
+    third_rest = along(message, between)
+    return add_pieces(own_3, crossed_3, ((third_head, third_rest), (last_head, last_rest)), block)
 
 
 def local(particles, references, ctf_table, rot_offset, prior_shift, defocus_group):

time: 221 us -> 227 us (1.027); the launches traced: 221 us -> 223 us
    ppermute x9, waiting for transfers between devices: 19.8 us -> 8.74 us  [across(): return lax.ppermute(piece, 'dp', [(d, d ^ 1) for d in range(8)])]
    ppermute x13 -> x15, waiting for transfers between devices: 17.5 us -> 27.3 us  [along(): lax.ppermute(piece, 'dp', [(2 * a + x, 2 * b + x) for a, b in pairs for x...]
    ppermute x13 -> x15, starting transfers between devices: 26.9 us -> 29.8 us  [along(): lax.ppermute(piece, 'dp', [(2 * a + x, 2 * b + x) for a, b in pairs for x...]
  transfers between devices with their start and end apart: 22 -> 24, of which waited for: 11 -> 14; matrix products, arithmetic and copies ran while one was open for 4% -> 4% of each run, Pallas kernels for 44% -> 44%
where the time goes in v8:
time: 227 us; the launch traced here: 223 us
  Pallas kernels  124 us (55%)
  starting transfers between devices  41.5 us (18%)
  waiting for transfers between devices  36.1 us (16%)
  other arithmetic  9.47 us (4%)
  blocking collectives  6.23 us (3%)
  local copies, waits for them, and re-layouts  3.86 us (2%)
    pallas_call x3, Pallas kernels, make_spectra(): pl.pallas_call(functools.partial(spectra_kernel, per_step=per_step), grid...  46.4 us
    pallas_call x6, Pallas kernels, class_sums_of(): pl.pallas_call(functools.partial(sums_kernel, count=count, classes=classe...  32.3 us
    ppermute x15, starting transfers between devices, along(): lax.ppermute(piece, 'dp', [(2 * a + x, 2 * b + x) for a, b in pairs for x...  29.8 us
    pallas_call x2, Pallas kernels, correlate(): pl.pallas_call(functools.partial(correlate_kernel, slots=slots, classes=c...  28.4 us
    ppermute x15, waiting for transfers between devices, along(): lax.ppermute(piece, 'dp', [(2 * a + x, 2 * b + x) for a, b in pairs for x...  27.3 us
    ppermute x9, starting transfers between devices, across(): return lax.ppermute(piece, 'dp', [(d, d ^ 1) for d in range(8)])  11.6 us
    ppermute x9, waiting for transfers between devices, across(): return lax.ppermute(piece, 'dp', [(d, d ^ 1) for d in range(8)])  8.74 us
    psum x1, blocking collectives, local(): shares = lax.psum(share, 'cls')  6.23 us
  transfers between devices with their start and end apart: 24, of which 14 were waited for; matrix products, arithmetic and copies ran while one was open for 4% of the time, Pallas kernels for 44%

profile of v8, /device:TPU:8, one launch (start us, length us, event | category | flops | bytes accessed | tf_op | source)
XLA Modules:
  0.0 223.2 jit_solution(1840330387864440404)
XLA Ops:
  0.7 3.0 %turn_references.1 = (bf16[3600,128]{1,0:T(8,128)(2,1)}, f32[56,128]{1,0:T(8,128)}) custom-call(s32[1]{0:T(128)} %bitcast.3.first_ref, s32[50]{0:T(128)} %offset_ref.1, bf16[3600,128]{1,0:T(8,128)(2,1)} %bitcast.45), custom_call_target="tpu_custom_call" | custom-call | tf_op jit(solution)/shard_map/turn_references/pallas_call | solution.py:251
  3.6 5.0 %collective-permute-start.1 = (bf16[3600,128]{1,0:T(8,128)(2,1)}, bf16[3600,128]{1,0:T(8,128)(2,1)S(1)}, u32[]{:S(2)}, u32[]{:S(2)}) collective-permute-start(bf16[3600,128]{1,0:T(8,128)(2,1)} %get-tuple-element.46.refs_15_), channel_id=1, source_target_pairs={{8,16},{12,20},{16,8},{20,12},{9,17},{13,21},{17,9},{21,13},{10,18... | collective-permute-start | bytes 2764808 | tf_op jit(solution)/shard_map/ppermute | solution.py:554
  10.2 4.6 %centre.1.base_ref = f32[8,2,288,128]{3,2,1,0:T(8,128)} custom-call(s32[2,8]{1,0:T(2,128)} %bitcast.46, bf16[8,2,288,128]{3,2,1,0:T(8,128)(2,1)} %part_ref.1, f32[2,288,128]{2,1,0:T(8,128)} %constant.49.clone.turns_ref), custom_call_target="tpu_custom_call" | custom-call | tf_op jit(solution)/shard_map/centre/pallas_call | solution.py:87
  15.7 11.9 %spectra.3.refs_4_ = bf16[288,208,256]{2,1,0:T(8,128)(2,1)} custom-call(f32[8,2,288,128]{3,2,1,0:T(8,128)} %centre.1.base_ref, f32[8,128]{1,0:T(8,128)} %fusion.4.ctf_ref.refs_6_, bf16[576,576]{1,0:T(8,128)(2,1)} %constant.50.clone.table_ref, f32[2,5,2,288,128]{4,3,2,1,0:T(8,128)} %constant.51.clone.refs_0_.refs_1_.refs_2_.refs_3_, ...), custom_call_target="tpu_custom_call" | custom-call | tf_op jit(solution)/shard_map/spectra/pallas_call | solution.py:171
  30.6 2.2 collective-permute-start.3
  35.7 17.3 %spectra.4.refs_4_ = bf16[288,208,256]{2,1,0:T(8,128)(2,1)} custom-call(f32[8,2,288,128]{3,2,1,0:T(8,128)} %centre.1.base_ref, f32[8,128]{1,0:T(8,128)} %fusion.4.ctf_ref.refs_6_, bf16[576,576]{1,0:T(8,128)(2,1)} %constant.50.clone.table_ref, f32[2,5,2,288,128]{4,3,2,1,0:T(8,128)} %constant.51.clone.refs_0_.refs_1_.refs_2_.refs_3_, ...), custom_call_target="tpu_custom_call", output_to_operand_aliasing={{}: (7, {})} | custom-call | tf_op jit(solution)/shard_map/spectra/pallas_call | solution.py:171
  55.4 3.9 %collective-permute-start.6 = (bf16[3600,128]{1,0:T(8,128)(2,1)S(1)}, bf16[3600,128]{1,0:T(8,128)(2,1)S(1)}, u32[]{:S(2)}, u32[]{:S(2)}) collective-permute-start(bf16[3600,128]{1,0:T(8,128)(2,1)S(1)} %collective-permute-done.3), channel_id=1, source_target_pairs={{8,0},{12,4},{16,24},{20,28},{9,1},{13,5},{17,25},{21,29},{10,2},{... | collective-permute-start | bytes 2764808 | tf_op jit(solution)/shard_map/ppermute | solution.py:554
  59.3 17.3 %spectra.5 = bf16[288,208,256]{2,1,0:T(8,128)(2,1)} custom-call(f32[8,2,288,128]{3,2,1,0:T(8,128)} %centre.1.base_ref, f32[8,128]{1,0:T(8,128)} %fusion.4.ctf_ref.refs_6_, bf16[576,576]{1,0:T(8,128)(2,1)} %constant.50.clone.table_ref, f32[2,5,2,288,128]{4,3,2,1,0:T(8,128)} %constant.51.clone.refs_0_.refs_1_.refs_2_.refs_3_, ...), custom_call_target="tpu_custom_call", output_to_operand_aliasing={{}: (7, {})} | custom-call | tf_op jit(solution)/shard_map/spectra/pallas_call | solution.py:171
  76.9 1.6 collective-permute-start.8
  78.5 17.1 %correlate.1 = (f32[36,112,256]{2,1,0:T(8,128)}, f32[56,128]{1,0:T(8,128)}) custom-call(s32[1]{0:T(128)} %bitcast.7.refs_0_, s32[1]{0:T(128)} %bitcast.8.refs_1_, s32[1]{0:T(128)} %bitcast.9.refs_2_.refs_0_, s32[1]{0:T(128)} %bitcast.10.refs_3_, s32[1]{0:T(128)} %bitcast.11.refs_4_.refs_0_, s32[1]{0:T(128)} %bitcast.12.refs_5_, s32[1]{0:T(128)} %bitcast.13.refs_6_.refs_0_, ...), custom_call_target="tpu_custom_call" | custom-call | tf_op jit(solution)/shard_map/correlate/pallas_call | solution.py:417
  97.1 11.3 %scores.1 = (f32[36,56,256]{2,1,0:T(8,128)}, f32[64,128]{1,0:T(8,128)}, f32[4,2,128]{2,1,0:T(2,128)}) custom-call(s32[1]{0:T(128)} %bitcast.refs_0_, s32[1]{0:T(128)} %bitcast.1.refs_7_.refs_1_, bf16[8,36,208,256]{3,2,1,0:T(8,128)(2,1)} %bitcast.34, bf16[3600,128]{1,0:T(8,128)(2,1)} %copy-done.11, f32[36,112,256]{2,1,0:T(8,128)} %get-tuple-element.58.refs_4_, ...), custom_call_target="tpu_custom_call" | custom-call | tf_op jit(solution)/shard_map/scores/pallas_call | solution.py:417
  108.4 6.2 %psum.7.share_ref = f32[4,2,128]{2,1,0:T(2,128)} all-reduce(f32[4,2,128]{2,1,0:T(2,128)} %get-tuple-element.62), channel_id=1, replica_groups=mesh['dp'=8,'cls'=4] {'cls'}, use_global_device_ids=true, to_apply=%region_0.1 | all-reduce | flops 1024 | bytes 8192 | tf_op jit(solution)/shard_map/psum | solution.py:713
  114.7 5.5 %back.1 = (bf16[36,112,208]{2,1,0:T(8,128)(2,1)}, f32[8,128]{1,0:T(8,128)}, f32[56,128]{1,0:T(8,128)}) custom-call(f32[36,56,256]{2,1,0:T(8,128)} %get-tuple-element.60.weight_ref, f32[64,128]{1,0:T(8,128)} %get-tuple-element.61.stat_ref, f32[4,2,128]{2,1,0:T(2,128)} %psum.7.share_ref, f32[56,128]{1,0:T(8,128)} %get-tuple-element.63.offset_ref.refs_3_.refs_5_), custom_call_target="tpu_custom_call" | custom-call | tf_op jit(solution)/shard_map/back/pallas_call | solution.py:483
  120.1 3.2 %class_sums.6 = bf16[2400,128]{1,0:T(8,128)(2,1)} custom-call(s32[1]{0:T(128)} %bitcast.16.refs_0_, bf16[36,112,208]{2,1,0:T(8,128)(2,1)} %get-tuple-element.83.refs_1_.refs_2_, bf16[8,36,208,256]{3,2,1,0:T(8,128)(2,1)} %bitcast.35, f32[56,128]{1,0:T(8,128)} %get-tuple-element.63.offset_ref.refs_3_.refs_5_), custom_call_target="tpu_custom_call" | custom-call | tf_op jit(solution)/shard_map/class_sums/pallas_call | solution.py:526
  124.9 2.6 %class_sums.7 = bf16[1200,128]{1,0:T(8,128)(2,1)} custom-call(s32[1]{0:T(128)} %bitcast.16.refs_0_, bf16[36,112,208]{2,1,0:T(8,128)(2,1)} %get-tuple-element.83.refs_1_.refs_2_, bf16[8,36,208,256]{3,2,1,0:T(8,128)(2,1)} %bitcast.36, f32[56,128]{1,0:T(8,128)} %get-tuple-element.63.offset_ref.refs_3_.refs_5_), custom_call_target="tpu_custom_call" | custom-call | tf_op jit(solution)/shard_map/class_sums/pallas_call | solution.py:526
  127.5 7.0 %class_sums.8 = (f32[3600,128]{1,0:T(8,128)}, bf16[3600,128]{1,0:T(8,128)(2,1)}) custom-call(s32[1]{0:T(128)} %bitcast.13.refs_6_.refs_0_, s32[1]{0:T(128)} %bitcast.17.refs_1_, bf16[36,112,208]{2,1,0:T(8,128)(2,1)} %get-tuple-element.83.refs_1_.refs_2_, bf16[8,36,208,256]{3,2,1,0:T(8,128)(2,1)} %bitcast.37, bf16[8,36,208,256]{3,2,1,0:T(8,128)(2,1)} %bitcast.38, ...), custom_call_target="tpu_custom_call" | custom-call | tf_op jit(solution)/shard_map/class_sums/pallas_call | solution.py:526
  134.4 4.8 %collective-permute-done.9 = bf16[2400,128]{1,0:T(8,128)(2,1)S(1)} collective-permute-done((bf16[2400,128]{1,0:T(8,128)(2,1)}, bf16[2400,128]{1,0:T(8,128)(2,1)S(1)}, u32[]{:S(2)}, u32[]{:S(2)}) %collective-permute-start.9) | collective-permute-done | bytes 614432 | tf_op jit(solution)/shard_map/ppermute | solution.py:550
  139.2 2.3 %fusion = bf16[2400,128]{1,0:T(8,128)(2,1)} fusion(bf16[2400,128]{1,0:T(8,128)(2,1)S(1)} %collective-permute-done.9, f32[3600,128]{1,0:T(8,128)} %get-tuple-element.70), kind=kLoop, calls=%fused_computation.5 | loop fusion | flops 921600 | bytes 2457600 | tf_op jit(solution)/shard_map/convert_element_type | solution.py:645
  144.9 7.1 %class_sums.9 = (f32[3600,128]{1,0:T(8,128)}, bf16[3600,128]{1,0:T(8,128)(2,1)}) custom-call(s32[1]{0:T(128)} %bitcast.11.refs_4_.refs_0_, s32[1]{0:T(128)} %bitcast.18.refs_1_, bf16[36,112,208]{2,1,0:T(8,128)(2,1)} %get-tuple-element.83.refs_1_.refs_2_, bf16[8,36,208,256]{3,2,1,0:T(8,128)(2,1)} %bitcast.39, bf16[8,36,208,256]{3,2,1,0:T(8,128)(2,1)} %bitcast.40, ...), custom_call_target="tpu_custom_call" | custom-call | tf_op jit(solution)/shard_map/class_sums/pallas_call | solution.py:526
  153.4 5.1 %collective-permute-done.11 = bf16[2400,128]{1,0:T(8,128)(2,1)} collective-permute-done((bf16[2400,128]{1,0:T(8,128)(2,1)}, bf16[2400,128]{1,0:T(8,128)(2,1)}, u32[]{:S(2)}, u32[]{:S(2)}) %collective-permute-start.11) | collective-permute-done | bytes 614432 | tf_op jit(solution)/shard_map/ppermute | solution.py:554
  158.5 2.1 add_convert_fusion.2
  160.6 3.0 %collective-permute-start.14 = (bf16[2400,128]{1,0:T(8,128)(2,1)}, bf16[2400,128]{1,0:T(8,128)(2,1)S(1)}, u32[]{:S(2)}, u32[]{:S(2)}) collective-permute-start(bf16[2400,128]{1,0:T(8,128)(2,1)} %add_convert_fusion.2), channel_id=1, source_target_pairs={{8,16},{12,20},{16,8},{20,12},{9,17},{13,21},{17,9},{21,13},{10,18... | collective-permute-start | bytes 1843208 | tf_op jit(solution)/shard_map/ppermute | solution.py:554
  163.6 1.8 fusion.2
  168.2 7.1 %class_sums.10 = (f32[3600,128]{1,0:T(8,128)}, bf16[3600,128]{1,0:T(8,128)(2,1)}) custom-call(s32[1]{0:T(128)} %bitcast.9.refs_2_.refs_0_, s32[1]{0:T(128)} %bitcast.19.refs_1_, bf16[36,112,208]{2,1,0:T(8,128)(2,1)} %get-tuple-element.83.refs_1_.refs_2_, bf16[8,36,208,256]{3,2,1,0:T(8,128)(2,1)} %bitcast.41, bf16[8,36,208,256]{3,2,1,0:T(8,128)(2,1)} %bitcast.42, ...), custom_call_target="tpu_custom_call" | custom-call | tf_op jit(solution)/shard_map/class_sums/pallas_call | solution.py:526
  180.5 3.2 %collective-permute-start.22 = (bf16[1200,128]{1,0:T(8,128)(2,1)S(1)}, bf16[1200,128]{1,0:T(8,128)(2,1)S(1)}, u32[]{:S(2)}, u32[]{:S(2)}) collective-permute-start(bf16[1200,128]{1,0:T(8,128)(2,1)S(1)} %add_convert_fusion.5), channel_id=1, source_target_pairs={{8,16},{12,20},{16,8},{20,12},{9,17},{13,21},{17,9},{21,13},{10,18... | collective-permute-start | bytes 921608 | tf_op jit(solution)/shard_map/ppermute | solution.py:554
  183.7 11.7 %collective-permute-done.16 = bf16[2400,128]{1,0:T(8,128)(2,1)S(1)} collective-permute-done((bf16[2400,128]{1,0:T(8,128)(2,1)S(1)}, bf16[2400,128]{1,0:T(8,128)(2,1)S(1)}, u32[]{:S(2)}, u32[]{:S(2)}) %collective-permute-start.16) | collective-permute-done | bytes 614432 | tf_op jit(solution)/shard_map/ppermute | solution.py:554
  195.7 2.9 %collective-permute-start.17 = (bf16[2400,128]{1,0:T(8,128)(2,1)S(1)}, bf16[2400,128]{1,0:T(8,128)(2,1)S(1)}, u32[]{:S(2)}, u32[]{:S(2)}) collective-permute-start(bf16[2400,128]{1,0:T(8,128)(2,1)S(1)} %add_convert_fusion.1), channel_id=1, source_target_pairs={{8,16},{12,20},{16,8},{20,12},{9,17},{13,21},{17,9},{21,13},{10,18... | collective-permute-start | bytes 1843208 | tf_op jit(solution)/shard_map/ppermute | solution.py:554
  199.0 3.1 %collective-permute-done.18 = bf16[1200,128]{1,0:T(8,128)(2,1)S(1)} collective-permute-done((bf16[1200,128]{1,0:T(8,128)(2,1)S(1)}, bf16[1200,128]{1,0:T(8,128)(2,1)S(1)}, u32[]{:S(2)}, u32[]{:S(2)}) %collective-permute-start.18) | collective-permute-done | bytes 307232 | tf_op jit(solution)/shard_map/ppermute | solution.py:554
  202.9 2.9 %collective-permute-start.19 = (bf16[1200,128]{1,0:T(8,128)(2,1)}, bf16[1200,128]{1,0:T(8,128)(2,1)S(1)}, u32[]{:S(2)}, u32[]{:S(2)}) collective-permute-start(bf16[1200,128]{1,0:T(8,128)(2,1)} %add_convert_fusion.4), channel_id=1, source_target_pairs={{8,16},{12,20},{16,8},{20,12},{9,17},{13,21},{17,9},{21,13},{10,18... | collective-permute-start | bytes 921608 | tf_op jit(solution)/shard_map/ppermute | solution.py:554
  205.8 4.3 %collective-permute-done.17.refs_0_ = bf16[2400,128]{1,0:T(8,128)(2,1)S(1)} collective-permute-done((bf16[2400,128]{1,0:T(8,128)(2,1)S(1)}, bf16[2400,128]{1,0:T(8,128)(2,1)S(1)}, u32[]{:S(2)}, u32[]{:S(2)}) %collective-permute-start.17) | collective-permute-done | bytes 614432 | tf_op jit(solution)/shard_map/ppermute | solution.py:554
  212.1 5.2 %class_sums.11.own_ref = f32[3600,128]{1,0:T(8,128)} custom-call(s32[1]{0:T(128)} %bitcast.7.refs_0_, bf16[36,112,208]{2,1,0:T(8,128)(2,1)} %get-tuple-element.83.refs_1_.refs_2_, bf16[8,36,208,256]{3,2,1,0:T(8,128)(2,1)} %bitcast.43, f32[56,128]{1,0:T(8,128)} %get-tuple-element.63.offset_ref.refs_3_.refs_5_), custom_call_target="tpu_custom_call" | custom-call | tf_op jit(solution)/shard_map/class_sums/pallas_call | solution.py:526
  219.0 4.2 %add_pieces.1 = f32[3600,128]{1,0:T(8,128)} custom-call(f32[3600,128]{1,0:T(8,128)} %class_sums.11.own_ref, bf16[3600,128]{1,0:T(8,128)(2,1)} %collective-permute-done.15.whole_ref, bf16[2400,128]{1,0:T(8,128)(2,1)} %copy-done.12, bf16[1200,128]{1,0:T(8,128)(2,1)} %copy-done.14, bf16[2400,128]{1,0:T(8,128)(2,1)} %copy-done.13, bf16[1200,128]{1,0:T(8,128)(2,1)} %copy-done.15), custom_call_target="tpu_custom_call" | custom-call | tf_op jit(solution)/shard_map/add_pieces/pallas_call | solution.py:604
  (84 shorter events, 31.8 us)
Async XLA Ops:
  0.6 14.3 %copy-start = (f32[16,128]{1,0:T(8,128)S(1)}, f32[16,128]{1,0:T(8,128)}, u32[]{:S(2)}) copy-start(f32[16,128]{1,0:T(8,128)} %param.15) | copy-start | bytes 24580
  3.6 23.9 %collective-permute-start = (bf16[3600,128]{1,0:T(8,128)(2,1)}, bf16[3600,128]{1,0:T(8,128)(2,1)S(1)}, u32[]{:S(2)}, u32[]{:S(2)}) collective-permute-start(bf16[3600,128]{1,0:T(8,128)(2,1)} %get-tuple-element.46.refs_15_), channel_id=1, source_target_pairs={{0,8},{4,12},{8,0},{12,4},{16,24},{20,28},{24,16},{28,20},{1,9},{5... | collective-permute-start | bytes 2764808 | tf_op jit(solution)/shard_map/ppermute | solution.py:554
  3.6 25.4 %collective-permute-start.1 = (bf16[3600,128]{1,0:T(8,128)(2,1)}, bf16[3600,128]{1,0:T(8,128)(2,1)S(1)}, u32[]{:S(2)}, u32[]{:S(2)}) collective-permute-start(bf16[3600,128]{1,0:T(8,128)(2,1)} %get-tuple-element.46.refs_15_), channel_id=1, source_target_pairs={{8,16},{12,20},{16,8},{20,12},{9,17},{13,21},{17,9},{21,13},{10,18... | collective-permute-start | bytes 2764808 | tf_op jit(solution)/shard_map/ppermute | solution.py:554
  8.7 21.9 %collective-permute-start.2 = (bf16[3600,128]{1,0:T(8,128)(2,1)}, bf16[3600,128]{1,0:T(8,128)(2,1)S(1)}, u32[]{:S(2)}, u32[]{:S(2)}) collective-permute-start(bf16[3600,128]{1,0:T(8,128)(2,1)} %get-tuple-element.46.refs_15_), channel_id=1, source_target_pairs={{0,4},{4,0},{8,12},{12,8},{16,20},{20,16},{24,28},{28,24},{1,5},{5... | collective-permute-start | bytes 2764808 | tf_op jit(solution)/shard_map/ppermute | solution.py:550
  27.6 25.4 %copy-start.7 = (bf16[3600,128]{1,0:T(8,128)(2,1)}, bf16[3600,128]{1,0:T(8,128)(2,1)S(1)}, u32[]{:S(2)}) copy-start(bf16[3600,128]{1,0:T(8,128)(2,1)S(1)} %collective-permute-done.refs_17_) | copy-start | bytes 2764804
  30.6 22.4 %copy-start.8 = (bf16[3600,128]{1,0:T(8,128)(2,1)}, bf16[3600,128]{1,0:T(8,128)(2,1)S(1)}, u32[]{:S(2)}) copy-start(bf16[3600,128]{1,0:T(8,128)(2,1)S(1)} %collective-permute-done.2.refs_16_) | copy-start | bytes 2764804
  30.6 22.6 %collective-permute-start.3 = (bf16[3600,128]{1,0:T(8,128)(2,1)S(1)}, bf16[3600,128]{1,0:T(8,128)(2,1)S(1)}, u32[]{:S(2)}, u32[]{:S(2)}) collective-permute-start(bf16[3600,128]{1,0:T(8,128)(2,1)S(1)} %collective-permute-done.refs_17_), channel_id=1, source_target_pairs={{8,16},{12,20},{16,8},{20,12},{9,17},{13,21},{17,9},{21,13},{10,18... | collective-permute-start | bytes 2764808 | tf_op jit(solution)/shard_map/ppermute | solution.py:554
  32.8 20.8 %collective-permute-start.5 = (bf16[3600,128]{1,0:T(8,128)(2,1)S(1)}, bf16[3600,128]{1,0:T(8,128)(2,1)S(1)}, u32[]{:S(2)}, u32[]{:S(2)}) collective-permute-start(bf16[3600,128]{1,0:T(8,128)(2,1)S(1)} %collective-permute-done.refs_17_), channel_id=1, source_target_pairs={{0,4},{4,0},{8,12},{12,8},{16,20},{20,16},{24,28},{28,24},{1,5},{5... | collective-permute-start | bytes 2764808 | tf_op jit(solution)/shard_map/ppermute | solution.py:550
  34.3 19.5 %collective-permute-start.4 = (bf16[3600,128]{1,0:T(8,128)(2,1)S(1)}, bf16[3600,128]{1,0:T(8,128)(2,1)S(1)}, u32[]{:S(2)}, u32[]{:S(2)}) collective-permute-start(bf16[3600,128]{1,0:T(8,128)(2,1)S(1)} %collective-permute-done.1), channel_id=1, source_target_pairs={{8,0},{12,4},{16,24},{20,28},{9,1},{13,5},{17,25},{21,29},{10,2},{... | collective-permute-start | bytes 2764808 | tf_op jit(solution)/shard_map/ppermute | solution.py:554
  53.6 23.0 %copy-start.9 = (bf16[3600,128]{1,0:T(8,128)(2,1)}, bf16[3600,128]{1,0:T(8,128)(2,1)S(1)}, u32[]{:S(2)}) copy-start(bf16[3600,128]{1,0:T(8,128)(2,1)S(1)} %collective-permute-done.5.refs_18_) | copy-start | bytes 2764804
  54.1 22.5 %copy-start.4 = (bf16[3600,128]{1,0:T(8,128)(2,1)}, bf16[3600,128]{1,0:T(8,128)(2,1)S(1)}, u32[]{:S(2)}) copy-start(bf16[3600,128]{1,0:T(8,128)(2,1)S(1)} %add.96.refs_19_) | copy-start | bytes 2764804
  54.1 22.5 %collective-permute-start.7 = (bf16[3600,128]{1,0:T(8,128)(2,1)S(1)}, bf16[3600,128]{1,0:T(8,128)(2,1)S(1)}, u32[]{:S(2)}, u32[]{:S(2)}) collective-permute-start(bf16[3600,128]{1,0:T(8,128)(2,1)S(1)} %add.96.refs_19_), channel_id=1, source_target_pairs={{0,4},{4,0},{8,12},{12,8},{16,20},{20,16},{24,28},{28,24},{1,5},{5... | collective-permute-start | bytes 2764808 | tf_op jit(solution)/shard_map/ppermute | solution.py:550
  55.4 21.3 %collective-permute-start.6 = (bf16[3600,128]{1,0:T(8,128)(2,1)S(1)}, bf16[3600,128]{1,0:T(8,128)(2,1)S(1)}, u32[]{:S(2)}, u32[]{:S(2)}) collective-permute-start(bf16[3600,128]{1,0:T(8,128)(2,1)S(1)} %collective-permute-done.3), channel_id=1, source_target_pairs={{8,0},{12,4},{16,24},{20,28},{9,1},{13,5},{17,25},{21,29},{10,2},{... | collective-permute-start | bytes 2764808 | tf_op jit(solution)/shard_map/ppermute | solution.py:554
  76.9 19.3 %collective-permute-start.8 = (bf16[3600,128]{1,0:T(8,128)(2,1)S(1)}, bf16[3600,128]{1,0:T(8,128)(2,1)S(1)}, u32[]{:S(2)}, u32[]{:S(2)}) collective-permute-start(bf16[3600,128]{1,0:T(8,128)(2,1)S(1)} %add.97.refs_21_), channel_id=1, source_target_pairs={{0,4},{4,0},{8,12},{12,8},{16,20},{20,16},{24,28},{28,24},{1,5},{5... | collective-permute-start | bytes 2764808 | tf_op jit(solution)/shard_map/ppermute | solution.py:550
  123.4 15.8 %collective-permute-start.9 = (bf16[2400,128]{1,0:T(8,128)(2,1)}, bf16[2400,128]{1,0:T(8,128)(2,1)S(1)}, u32[]{:S(2)}, u32[]{:S(2)}) collective-permute-start(bf16[2400,128]{1,0:T(8,128)(2,1)} %class_sums.6), channel_id=1, source_target_pairs={{0,4},{4,0},{8,12},{12,8},{16,20},{20,16},{24,28},{28,24},{1,5},{5... | collective-permute-start | bytes 1843208 | tf_op jit(solution)/shard_map/ppermute | solution.py:550
  141.5 17.0 %collective-permute-start.11 = (bf16[2400,128]{1,0:T(8,128)(2,1)}, bf16[2400,128]{1,0:T(8,128)(2,1)}, u32[]{:S(2)}, u32[]{:S(2)}) collective-permute-start(bf16[2400,128]{1,0:T(8,128)(2,1)} %fusion), channel_id=1, source_target_pairs={{0,8},{4,12},{24,16},{28,20},{1,9},{5,13},{25,17},{29,21},{2,10},{... | collective-permute-start | bytes 1843208 | tf_op jit(solution)/shard_map/ppermute | solution.py:554
  142.8 10.6 %collective-permute-start.10 = (bf16[1200,128]{1,0:T(8,128)(2,1)}, bf16[1200,128]{1,0:T(8,128)(2,1)}, u32[]{:S(2)}, u32[]{:S(2)}) collective-permute-start(bf16[1200,128]{1,0:T(8,128)(2,1)} %class_sums.7), channel_id=1, source_target_pairs={{0,4},{4,0},{8,12},{12,8},{16,20},{20,16},{24,28},{28,24},{1,5},{5... | collective-permute-start | bytes 921608 | tf_op jit(solution)/shard_map/ppermute | solution.py:550
  144.3 31.6 %collective-permute-start.12 = (bf16[3600,128]{1,0:T(8,128)(2,1)}, bf16[3600,128]{1,0:T(8,128)(2,1)S(1)}, u32[]{:S(2)}, u32[]{:S(2)}) collective-permute-start(bf16[3600,128]{1,0:T(8,128)(2,1)} %get-tuple-element.77), channel_id=1, source_target_pairs={{0,4},{4,0},{8,12},{12,8},{16,20},{20,16},{24,28},{28,24},{1,5},{5... | collective-permute-start | bytes 2764808 | tf_op jit(solution)/shard_map/ppermute | solution.py:550
  144.9 13.6 %copy-start.3 = (f32[3600,128]{1,0:T(8,128)S(1)}, f32[3600,128]{1,0:T(8,128)}, u32[]{:S(2)}) copy-start(f32[3600,128]{1,0:T(8,128)} %get-tuple-element.70) | copy-start | bytes 5529604
  160.6 15.9 %collective-permute-start.14 = (bf16[2400,128]{1,0:T(8,128)(2,1)}, bf16[2400,128]{1,0:T(8,128)(2,1)S(1)}, u32[]{:S(2)}, u32[]{:S(2)}) collective-permute-start(bf16[2400,128]{1,0:T(8,128)(2,1)} %add_convert_fusion.2), channel_id=1, source_target_pairs={{8,16},{12,20},{16,8},{20,12},{9,17},{13,21},{17,9},{21,13},{10,18... | collective-permute-start | bytes 1843208 | tf_op jit(solution)/shard_map/ppermute | solution.py:554
  165.4 10.5 %collective-permute-start.13 = (bf16[1200,128]{1,0:T(8,128)(2,1)}, bf16[1200,128]{1,0:T(8,128)(2,1)}, u32[]{:S(2)}, u32[]{:S(2)}) collective-permute-start(bf16[1200,128]{1,0:T(8,128)(2,1)} %fusion.2), channel_id=1, source_target_pairs={{0,8},{4,12},{24,16},{28,20},{1,9},{5,13},{25,17},{29,21},{2,10},{... | collective-permute-start | bytes 921608 | tf_op jit(solution)/shard_map/ppermute | solution.py:554
  166.7 32.0 %collective-permute-start.20 = (bf16[3600,128]{1,0:T(8,128)(2,1)}, bf16[3600,128]{1,0:T(8,128)(2,1)S(1)}, u32[]{:S(2)}, u32[]{:S(2)}) collective-permute-start(bf16[3600,128]{1,0:T(8,128)(2,1)} %get-tuple-element.86), channel_id=1, source_target_pairs={{0,4},{4,0},{8,12},{12,8},{16,20},{20,16},{24,28},{28,24},{1,5},{5... | collective-permute-start | bytes 2764808 | tf_op jit(solution)/shard_map/ppermute | solution.py:550
  175.3 42.0 %collective-permute-start.15 = (bf16[3600,128]{1,0:T(8,128)(2,1)}, bf16[3600,128]{1,0:T(8,128)(2,1)}, u32[]{:S(2)}, u32[]{:S(2)}) collective-permute-start(bf16[3600,128]{1,0:T(8,128)(2,1)} %get-tuple-element.84), channel_id=1, source_target_pairs={{0,4},{4,0},{8,12},{12,8},{16,20},{20,16},{24,28},{28,24},{1,5},{5... | collective-permute-start | bytes 2764808 | tf_op jit(solution)/shard_map/ppermute | solution.py:550
  176.7 18.8 %collective-permute-start.16 = (bf16[2400,128]{1,0:T(8,128)(2,1)S(1)}, bf16[2400,128]{1,0:T(8,128)(2,1)S(1)}, u32[]{:S(2)}, u32[]{:S(2)}) collective-permute-start(bf16[2400,128]{1,0:T(8,128)(2,1)S(1)} %fusion.1), channel_id=1, source_target_pairs={{0,8},{4,12},{24,16},{28,20},{1,9},{5,13},{25,17},{29,21},{2,10},{... | collective-permute-start | bytes 1843208 | tf_op jit(solution)/shard_map/ppermute | solution.py:554
  178.0 24.0 %collective-permute-start.18 = (bf16[1200,128]{1,0:T(8,128)(2,1)S(1)}, bf16[1200,128]{1,0:T(8,128)(2,1)S(1)}, u32[]{:S(2)}, u32[]{:S(2)}) collective-permute-start(bf16[1200,128]{1,0:T(8,128)(2,1)S(1)} %fusion.3), channel_id=1, source_target_pairs={{0,8},{4,12},{24,16},{28,20},{1,9},{5,13},{25,17},{29,21},{2,10},{... | collective-permute-start | bytes 921608 | tf_op jit(solution)/shard_map/ppermute | solution.py:554
  180.5 18.1 %copy-start.6 = (f32[3600,128]{1,0:T(8,128)S(1)}, f32[3600,128]{1,0:T(8,128)}, u32[]{:S(2)}) copy-start(f32[3600,128]{1,0:T(8,128)} %get-tuple-element.85) | copy-start | bytes 5529604
  180.5 25.3 %collective-permute-start.22 = (bf16[1200,128]{1,0:T(8,128)(2,1)S(1)}, bf16[1200,128]{1,0:T(8,128)(2,1)S(1)}, u32[]{:S(2)}, u32[]{:S(2)}) collective-permute-start(bf16[1200,128]{1,0:T(8,128)(2,1)S(1)} %add_convert_fusion.5), channel_id=1, source_target_pairs={{8,16},{12,20},{16,8},{20,12},{9,17},{13,21},{17,9},{21,13},{10,18... | collective-permute-start | bytes 921608 | tf_op jit(solution)/shard_map/ppermute | solution.py:554
  195.7 14.4 %collective-permute-start.17 = (bf16[2400,128]{1,0:T(8,128)(2,1)S(1)}, bf16[2400,128]{1,0:T(8,128)(2,1)S(1)}, u32[]{:S(2)}, u32[]{:S(2)}) collective-permute-start(bf16[2400,128]{1,0:T(8,128)(2,1)S(1)} %add_convert_fusion.1), channel_id=1, source_target_pairs={{8,16},{12,20},{16,8},{20,12},{9,17},{13,21},{17,9},{21,13},{10,18... | collective-permute-start | bytes 1843208 | tf_op jit(solution)/shard_map/ppermute | solution.py:554
  198.9 11.4 %copy-start.16 = (f32[56,128]{1,0:T(8,128)S(1)}, f32[56,128]{1,0:T(8,128)}, u32[]{:S(2)}) copy-start(f32[56,128]{1,0:T(8,128)} %get-tuple-element.65) | copy-start | bytes 86020
  198.9 18.5 %collective-permute-start.21 = (bf16[2400,128]{1,0:T(8,128)(2,1)S(1)}, bf16[2400,128]{1,0:T(8,128)(2,1)S(1)}, u32[]{:S(2)}, u32[]{:S(2)}) collective-permute-start(bf16[2400,128]{1,0:T(8,128)(2,1)S(1)} %add_convert_fusion), channel_id=1, source_target_pairs={{0,8},{4,12},{8,0},{12,4},{16,24},{20,28},{24,16},{28,20},{1,9},{5... | collective-permute-start | bytes 1843208 | tf_op jit(solution)/shard_map/ppermute | solution.py:554
  202.9 14.5 %collective-permute-start.19 = (bf16[1200,128]{1,0:T(8,128)(2,1)}, bf16[1200,128]{1,0:T(8,128)(2,1)S(1)}, u32[]{:S(2)}, u32[]{:S(2)}) collective-permute-start(bf16[1200,128]{1,0:T(8,128)(2,1)} %add_convert_fusion.4), channel_id=1, source_target_pairs={{8,16},{12,20},{16,8},{20,12},{9,17},{13,21},{17,9},{21,13},{10,18... | collective-permute-start | bytes 921608 | tf_op jit(solution)/shard_map/ppermute | solution.py:554
  210.2 7.8 %collective-permute-start.23 = (bf16[1200,128]{1,0:T(8,128)(2,1)S(1)}, bf16[1200,128]{1,0:T(8,128)(2,1)S(1)}, u32[]{:S(2)}, u32[]{:S(2)}) collective-permute-start(bf16[1200,128]{1,0:T(8,128)(2,1)S(1)} %add_convert_fusion.3), channel_id=1, source_target_pairs={{0,8},{4,12},{8,0},{12,4},{16,24},{20,28},{24,16},{28,20},{1,9},{5... | collective-permute-start | bytes 921608 | tf_op jit(solution)/shard_map/ppermute | solution.py:554
  (10 other events, 38.0 us)

commit v9 on v7

--- a/solution.py
+++ b/solution.py
@@ -569,9 +569,9 @@
     far_middle = along(near, ((1, 2), (2, 1)))
     end = along(middle, ((1, 0), (2, 3)))
     weighted = make_spectra(base, ctf_rows, cuts[1], cuts[2], weighted)
-    weighted, far_middle, end, near_crossed = lax.optimization_barrier(
-        (weighted, far_middle, end, near_crossed)
-    )
+    weighted, end = lax.optimization_barrier((weighted, end))
+    weighted, near_crossed = lax.optimization_barrier((weighted, near_crossed))
+    weighted, far_middle = lax.optimization_barrier((weighted, far_middle))
     third = middle + end
     third_crossed = across(third)
     far_end = along(far_middle, ((1, 0), (2, 3)))
@@ -657,16 +657,21 @@
     crossed_1, first_rest, middle_head, own_2 = lax.optimization_barrier(
         (crossed_1, first_rest, middle_head, own_2)
     )
+    message = (own_1 + wide(crossed_1)).astype(bf16)
+    from_end = along(message, to_middle)
+    first_rest = then(first_rest, message)
     message = (own_0[rest] + wide(crossed_rest) + wide(first_rest)).astype(bf16)
     middle_rest = along(message, between)
-    from_end = along((own_1 + wide(crossed_1)).astype(bf16), to_middle)
     back = then(back, message)
     (own_3,) = sums(ours[3:], [f32], back)
     message = (own_2[head] + wide(crossed_2[head]) + wide(middle_head)).astype(bf16)
     last_head = along(message, neighbours)
+    from_end = then(from_end, crossed_2)
+    message = (own_1 + wide(crossed_1) + wide(from_end)).astype(bf16)
+    third = along(message, between)
+    middle_rest = then(middle_rest, message)
     message = (own_2[rest] + wide(crossed_2[rest]) + wide(middle_rest)).astype(bf16)
     last_rest = along(message, neighbours)
-    third = along((own_1 + wide(crossed_1) + wide(from_end)).astype(bf16), between)
     return add_pieces(own_3, (crossed_3, third), (last_head, last_rest), block)
 
 

time: 221 us -> 222 us (level)
  starting transfers between devices: 39.4 us -> 32.8 us
  waiting for transfers between devices: 37.3 us -> 40.9 us
    ppermute x9, waiting for transfers between devices: 19.8 us -> 25.3 us  [across(): return lax.ppermute(piece, 'dp', [(d, d ^ 1) for d in range(8)])]
    ppermute x9, starting transfers between devices: 12.5 us -> 8.03 us  [across(): return lax.ppermute(piece, 'dp', [(d, d ^ 1) for d in range(8)])]
  transfers between devices with their start and end apart: 22 -> 22, of which waited for: 11 -> 10; matrix products, arithmetic and copies ran while one was open for 4% -> 5% of each run, Pallas kernels for 44% -> 44%
where the time goes in v9:
time: 222 us; the launch traced here: 220 us
  Pallas kernels  125 us (56%)
  waiting for transfers between devices  40.9 us (18%)
  starting transfers between devices  32.8 us (15%)
  other arithmetic  8.82 us (4%)
  blocking collectives  6.23 us (3%)
  local copies, waits for them, and re-layouts  5.05 us (2%)
    pallas_call x3, Pallas kernels, make_spectra(): pl.pallas_call(functools.partial(spectra_kernel, per_step=per_step), grid...  46.3 us
    pallas_call x6, Pallas kernels, class_sums_of(): pl.pallas_call(functools.partial(sums_kernel, count=count, classes=classe...  32.3 us
    pallas_call x2, Pallas kernels, correlate(): pl.pallas_call(functools.partial(correlate_kernel, slots=slots, classes=c...  28.4 us
    ppermute x9, waiting for transfers between devices, across(): return lax.ppermute(piece, 'dp', [(d, d ^ 1) for d in range(8)])  25.3 us
    ppermute x13, starting transfers between devices, along(): lax.ppermute(piece, 'dp', [(2 * a + x, 2 * b + x) for a, b in pairs for x...  24.7 us
    ppermute x13, waiting for transfers between devices, along(): lax.ppermute(piece, 'dp', [(2 * a + x, 2 * b + x) for a, b in pairs for x...  15.6 us
    ppermute x9, starting transfers between devices, across(): return lax.ppermute(piece, 'dp', [(d, d ^ 1) for d in range(8)])  8.03 us
    psum x1, blocking collectives, local(): shares = lax.psum(share, 'cls')  6.23 us
  transfers between devices with their start and end apart: 22, of which 10 were waited for; matrix products, arithmetic and copies ran while one was open for 5% of the time, Pallas kernels for 44%

profile of v9, /device:TPU:8, one launch (start us, length us, event | category | flops | bytes accessed | tf_op | source)
XLA Modules:
  0.0 220.0 jit_solution(6913978564018691981)
XLA Ops:
  0.7 3.0 %turn_references.1 = (bf16[3600,128]{1,0:T(8,128)(2,1)}, f32[56,128]{1,0:T(8,128)}) custom-call(s32[1]{0:T(128)} %bitcast.3.first_ref, s32[50]{0:T(128)} %offset_ref.1, bf16[3600,128]{1,0:T(8,128)(2,1)} %bitcast.45), custom_call_target="tpu_custom_call" | custom-call | tf_op jit(solution)/shard_map/turn_references/pallas_call | solution.py:251
  3.6 5.0 %collective-permute-start.1 = (bf16[3600,128]{1,0:T(8,128)(2,1)}, bf16[3600,128]{1,0:T(8,128)(2,1)S(1)}, u32[]{:S(2)}, u32[]{:S(2)}) collective-permute-start(bf16[3600,128]{1,0:T(8,128)(2,1)} %get-tuple-element.49.refs_15_), channel_id=1, source_target_pairs={{8,16},{12,20},{16,8},{20,12},{9,17},{13,21},{17,9},{21,13},{10,18... | collective-permute-start | bytes 2764808 | tf_op jit(solution)/shard_map/ppermute | solution.py:554
  8.7 1.6 collective-permute-start.2
  10.2 4.6 %centre.1.base_ref = f32[8,2,288,128]{3,2,1,0:T(8,128)} custom-call(s32[2,8]{1,0:T(2,128)} %bitcast.46, bf16[8,2,288,128]{3,2,1,0:T(8,128)(2,1)} %part_ref.1, f32[2,288,128]{2,1,0:T(8,128)} %constant.49.clone.turns_ref), custom_call_target="tpu_custom_call" | custom-call | tf_op jit(solution)/shard_map/centre/pallas_call | solution.py:87
  15.7 11.8 %spectra.3.refs_4_ = bf16[288,208,256]{2,1,0:T(8,128)(2,1)} custom-call(f32[8,2,288,128]{3,2,1,0:T(8,128)} %centre.1.base_ref, f32[8,128]{1,0:T(8,128)} %fusion.3.ctf_ref.refs_6_, bf16[576,576]{1,0:T(8,128)(2,1)} %constant.50.clone.table_ref, f32[2,5,2,288,128]{4,3,2,1,0:T(8,128)} %constant.51.clone.refs_0_.refs_1_.refs_2_.refs_3_, ...), custom_call_target="tpu_custom_call" | custom-call | tf_op jit(solution)/shard_map/spectra/pallas_call | solution.py:171
  27.4 1.6 collective-permute-done.1
  29.0 1.5 collective-permute-done.2.refs_16_
  31.9 1.6 collective-permute-start.4
  33.5 2.2 collective-permute-start.5
  35.7 17.3 %spectra.4.refs_4_ = bf16[288,208,256]{2,1,0:T(8,128)(2,1)} custom-call(f32[8,2,288,128]{3,2,1,0:T(8,128)} %centre.1.base_ref, f32[8,128]{1,0:T(8,128)} %fusion.3.ctf_ref.refs_6_, bf16[576,576]{1,0:T(8,128)(2,1)} %constant.50.clone.table_ref, f32[2,5,2,288,128]{4,3,2,1,0:T(8,128)} %constant.51.clone.refs_0_.refs_1_.refs_2_.refs_3_, ...), custom_call_target="tpu_custom_call", output_to_operand_aliasing={{}: (7, {})} | custom-call | tf_op jit(solution)/shard_map/spectra/pallas_call | solution.py:171
  53.0 2.8 %collective-permute-done.5 = bf16[3600,128]{1,0:T(8,128)(2,1)S(1)} collective-permute-done((bf16[3600,128]{1,0:T(8,128)(2,1)S(1)}, bf16[3600,128]{1,0:T(8,128)(2,1)S(1)}, u32[]{:S(2)}, u32[]{:S(2)}) %collective-permute-start.5) | collective-permute-done | bytes 921632 | tf_op jit(solution)/shard_map/ppermute | solution.py:554
  58.2 17.2 %spectra.5 = bf16[288,208,256]{2,1,0:T(8,128)(2,1)} custom-call(f32[8,2,288,128]{3,2,1,0:T(8,128)} %centre.1.base_ref, f32[8,128]{1,0:T(8,128)} %fusion.3.ctf_ref.refs_6_, bf16[576,576]{1,0:T(8,128)(2,1)} %constant.50.clone.table_ref, f32[2,5,2,288,128]{4,3,2,1,0:T(8,128)} %constant.51.clone.refs_0_.refs_1_.refs_2_.refs_3_, ...), custom_call_target="tpu_custom_call", output_to_operand_aliasing={{}: (7, {})} | custom-call | tf_op jit(solution)/shard_map/spectra/pallas_call | solution.py:171
  75.4 2.5 %collective-permute-done.7.refs_20_ = bf16[3600,128]{1,0:T(8,128)(2,1)S(1)} collective-permute-done((bf16[3600,128]{1,0:T(8,128)(2,1)S(1)}, bf16[3600,128]{1,0:T(8,128)(2,1)S(1)}, u32[]{:S(2)}, u32[]{:S(2)}) %collective-permute-start.7) | collective-permute-done | bytes 921632 | tf_op jit(solution)/shard_map/ppermute | solution.py:550
  79.1 17.1 %correlate.1 = (f32[36,112,256]{2,1,0:T(8,128)}, f32[56,128]{1,0:T(8,128)}) custom-call(s32[1]{0:T(128)} %bitcast.7.refs_0_, s32[1]{0:T(128)} %bitcast.8.refs_1_, s32[1]{0:T(128)} %bitcast.9.refs_2_.refs_0_, s32[1]{0:T(128)} %bitcast.10.refs_3_, s32[1]{0:T(128)} %bitcast.11.refs_4_.refs_0_, s32[1]{0:T(128)} %bitcast.12.refs_5_, s32[1]{0:T(128)} %bitcast.13.refs_6_.refs_0_, ...), custom_call_target="tpu_custom_call" | custom-call | tf_op jit(solution)/shard_map/correlate/pallas_call | solution.py:417
  97.8 11.3 %scores.1 = (f32[36,56,256]{2,1,0:T(8,128)}, f32[64,128]{1,0:T(8,128)}, f32[4,2,128]{2,1,0:T(2,128)}) custom-call(s32[1]{0:T(128)} %bitcast.refs_0_, s32[1]{0:T(128)} %bitcast.1.refs_7_.refs_1_, bf16[8,36,208,256]{3,2,1,0:T(8,128)(2,1)} %bitcast.34, bf16[3600,128]{1,0:T(8,128)(2,1)} %copy-done.14, f32[36,112,256]{2,1,0:T(8,128)} %get-tuple-element.63.refs_4_, ...), custom_call_target="tpu_custom_call" | custom-call | tf_op jit(solution)/shard_map/scores/pallas_call | solution.py:417
  109.1 6.2 %psum.7.share_ref = f32[4,2,128]{2,1,0:T(2,128)} all-reduce(f32[4,2,128]{2,1,0:T(2,128)} %get-tuple-element.67), channel_id=1, replica_groups=mesh['dp'=8,'cls'=4] {'cls'}, use_global_device_ids=true, to_apply=%region_0.1 | all-reduce | flops 1024 | bytes 8192 | tf_op jit(solution)/shard_map/psum | solution.py:710
  115.4 5.5 %back.1 = (bf16[36,112,208]{2,1,0:T(8,128)(2,1)}, f32[8,128]{1,0:T(8,128)}, f32[56,128]{1,0:T(8,128)}) custom-call(f32[36,56,256]{2,1,0:T(8,128)} %get-tuple-element.65.weight_ref, f32[64,128]{1,0:T(8,128)} %get-tuple-element.66.stat_ref, f32[4,2,128]{2,1,0:T(2,128)} %psum.7.share_ref, f32[56,128]{1,0:T(8,128)} %get-tuple-element.68.offset_ref.refs_3_.refs_5_), custom_call_target="tpu_custom_call" | custom-call | tf_op jit(solution)/shard_map/back/pallas_call | solution.py:483
  120.8 2.6 %class_sums.6 = bf16[1200,128]{1,0:T(8,128)(2,1)} custom-call(s32[1]{0:T(128)} %bitcast.16.refs_0_, bf16[36,112,208]{2,1,0:T(8,128)(2,1)} %get-tuple-element.88.refs_1_.refs_2_, bf16[8,36,208,256]{3,2,1,0:T(8,128)(2,1)} %bitcast.35, f32[56,128]{1,0:T(8,128)} %get-tuple-element.68.offset_ref.refs_3_.refs_5_), custom_call_target="tpu_custom_call" | custom-call | tf_op jit(solution)/shard_map/class_sums/pallas_call | solution.py:526
  124.0 3.2 %class_sums.7 = bf16[2400,128]{1,0:T(8,128)(2,1)} custom-call(s32[1]{0:T(128)} %bitcast.16.refs_0_, bf16[36,112,208]{2,1,0:T(8,128)(2,1)} %get-tuple-element.88.refs_1_.refs_2_, bf16[8,36,208,256]{3,2,1,0:T(8,128)(2,1)} %bitcast.36, f32[56,128]{1,0:T(8,128)} %get-tuple-element.68.offset_ref.refs_3_.refs_5_), custom_call_target="tpu_custom_call" | custom-call | tf_op jit(solution)/shard_map/class_sums/pallas_call | solution.py:526
  128.7 7.0 %class_sums.8 = (f32[3600,128]{1,0:T(8,128)}, bf16[3600,128]{1,0:T(8,128)(2,1)}) custom-call(s32[1]{0:T(128)} %bitcast.13.refs_6_.refs_0_, s32[1]{0:T(128)} %bitcast.17.refs_1_, bf16[36,112,208]{2,1,0:T(8,128)(2,1)} %get-tuple-element.88.refs_1_.refs_2_, bf16[8,36,208,256]{3,2,1,0:T(8,128)(2,1)} %bitcast.37, bf16[8,36,208,256]{3,2,1,0:T(8,128)(2,1)} %bitcast.38, ...), custom_call_target="tpu_custom_call" | custom-call | tf_op jit(solution)/shard_map/class_sums/pallas_call | solution.py:526
  138.8 7.2 %class_sums.9 = (f32[3600,128]{1,0:T(8,128)}, bf16[3600,128]{1,0:T(8,128)(2,1)}) custom-call(s32[1]{0:T(128)} %bitcast.11.refs_4_.refs_0_, s32[1]{0:T(128)} %bitcast.18.refs_1_, bf16[36,112,208]{2,1,0:T(8,128)(2,1)} %get-tuple-element.88.refs_1_.refs_2_, bf16[8,36,208,256]{3,2,1,0:T(8,128)(2,1)} %bitcast.39, bf16[8,36,208,256]{3,2,1,0:T(8,128)(2,1)} %bitcast.40, ...), custom_call_target="tpu_custom_call" | custom-call | tf_op jit(solution)/shard_map/class_sums/pallas_call | solution.py:526
  150.1 2.8 %collective-permute-start.14 = (bf16[1200,128]{1,0:T(8,128)(2,1)}, bf16[1200,128]{1,0:T(8,128)(2,1)}, u32[]{:S(2)}, u32[]{:S(2)}) collective-permute-start(bf16[1200,128]{1,0:T(8,128)(2,1)} %add_convert_fusion.4), channel_id=1, source_target_pairs={{8,16},{12,20},{16,8},{20,12},{9,17},{13,21},{17,9},{21,13},{10,18... | collective-permute-start | bytes 921608 | tf_op jit(solution)/shard_map/ppermute | solution.py:554
  153.5 7.1 %class_sums.10 = (f32[3600,128]{1,0:T(8,128)}, bf16[3600,128]{1,0:T(8,128)(2,1)}) custom-call(s32[1]{0:T(128)} %bitcast.9.refs_2_.refs_0_, s32[1]{0:T(128)} %bitcast.19.refs_1_, bf16[36,112,208]{2,1,0:T(8,128)(2,1)} %get-tuple-element.88.refs_1_.refs_2_, bf16[8,36,208,256]{3,2,1,0:T(8,128)(2,1)} %bitcast.41, bf16[8,36,208,256]{3,2,1,0:T(8,128)(2,1)} %bitcast.42, ...), custom_call_target="tpu_custom_call" | custom-call | tf_op jit(solution)/shard_map/class_sums/pallas_call | solution.py:526
  160.6 6.1 %collective-permute-done.12 = bf16[3600,128]{1,0:T(8,128)(2,1)S(1)} collective-permute-done((bf16[3600,128]{1,0:T(8,128)(2,1)}, bf16[3600,128]{1,0:T(8,128)(2,1)S(1)}, u32[]{:S(2)}, u32[]{:S(2)}) %collective-permute-start.12) | collective-permute-done | bytes 921632 | tf_op jit(solution)/shard_map/ppermute | solution.py:550
  170.1 2.9 %collective-permute-start.20 = (bf16[2400,128]{1,0:T(8,128)(2,1)S(1)}, bf16[2400,128]{1,0:T(8,128)(2,1)S(1)}, u32[]{:S(2)}, u32[]{:S(2)}) collective-permute-start(bf16[2400,128]{1,0:T(8,128)(2,1)S(1)} %add_convert_fusion.2), channel_id=1, source_target_pairs={{8,16},{12,20},{16,8},{20,12},{9,17},{13,21},{17,9},{21,13},{10,18... | collective-permute-start | bytes 1843208 | tf_op jit(solution)/shard_map/ppermute | solution.py:554
  173.1 13.5 %collective-permute-done.17 = bf16[3600,128]{1,0:T(8,128)(2,1)} collective-permute-done((bf16[3600,128]{1,0:T(8,128)(2,1)}, bf16[3600,128]{1,0:T(8,128)(2,1)}, u32[]{:S(2)}, u32[]{:S(2)}) %collective-permute-start.17) | collective-permute-done | bytes 921632 | tf_op jit(solution)/shard_map/ppermute | solution.py:550
  186.6 2.5 %collective-permute-done.16 = bf16[3600,128]{1,0:T(8,128)(2,1)S(1)} collective-permute-done((bf16[3600,128]{1,0:T(8,128)(2,1)S(1)}, bf16[3600,128]{1,0:T(8,128)(2,1)S(1)}, u32[]{:S(2)}, u32[]{:S(2)}) %collective-permute-start.16) | collective-permute-done | bytes 921632 | tf_op jit(solution)/shard_map/ppermute | solution.py:554
  190.3 2.9 %collective-permute-start.18 = (bf16[3600,128]{1,0:T(8,128)(2,1)}, bf16[3600,128]{1,0:T(8,128)(2,1)S(1)}, u32[]{:S(2)}, u32[]{:S(2)}) collective-permute-start(bf16[3600,128]{1,0:T(8,128)(2,1)} %add_convert_fusion), channel_id=1, source_target_pairs={{8,16},{12,20},{16,8},{20,12},{9,17},{13,21},{17,9},{21,13},{10,18... | collective-permute-start | bytes 2764808 | tf_op jit(solution)/shard_map/ppermute | solution.py:554
  195.8 2.1 collective-permute-start.19
  199.7 5.2 %class_sums.11.own_ref = f32[3600,128]{1,0:T(8,128)} custom-call(s32[1]{0:T(128)} %bitcast.7.refs_0_, bf16[36,112,208]{2,1,0:T(8,128)(2,1)} %get-tuple-element.88.refs_1_.refs_2_, bf16[8,36,208,256]{3,2,1,0:T(8,128)(2,1)} %bitcast.43, f32[56,128]{1,0:T(8,128)} %get-tuple-element.68.offset_ref.refs_3_.refs_5_), custom_call_target="tpu_custom_call" | custom-call | tf_op jit(solution)/shard_map/class_sums/pallas_call | solution.py:526
  204.9 8.8 %collective-permute-done.19.refs_2_ = bf16[1200,128]{1,0:T(8,128)(2,1)S(1)} collective-permute-done((bf16[1200,128]{1,0:T(8,128)(2,1)S(1)}, bf16[1200,128]{1,0:T(8,128)(2,1)S(1)}, u32[]{:S(2)}, u32[]{:S(2)}) %collective-permute-start.19) | collective-permute-done | bytes 307232 | tf_op jit(solution)/shard_map/ppermute | solution.py:554
  215.6 4.5 %add_pieces.1 = f32[3600,128]{1,0:T(8,128)} custom-call(f32[3600,128]{1,0:T(8,128)} %class_sums.11.own_ref, bf16[3600,128]{1,0:T(8,128)(2,1)} %collective-permute-done.15.refs_0_, bf16[3600,128]{1,0:T(8,128)(2,1)} %copy-done.13, bf16[1200,128]{1,0:T(8,128)(2,1)} %copy-done.16, bf16[2400,128]{1,0:T(8,128)(2,1)} %copy-done.15), custom_call_target="tpu_custom_call" | custom-call | tf_op jit(solution)/shard_map/add_pieces/pallas_call | solution.py:603
  (80 shorter events, 28.1 us)
Async XLA Ops:
  0.6 14.3 %copy-start = (f32[16,128]{1,0:T(8,128)S(1)}, f32[16,128]{1,0:T(8,128)}, u32[]{:S(2)}) copy-start(f32[16,128]{1,0:T(8,128)} %param.15) | copy-start | bytes 24580
  3.6 23.8 %collective-permute-start = (bf16[3600,128]{1,0:T(8,128)(2,1)}, bf16[3600,128]{1,0:T(8,128)(2,1)S(1)}, u32[]{:S(2)}, u32[]{:S(2)}) collective-permute-start(bf16[3600,128]{1,0:T(8,128)(2,1)} %get-tuple-element.49.refs_15_), channel_id=1, source_target_pairs={{0,8},{4,12},{8,0},{12,4},{16,24},{20,28},{24,16},{28,20},{1,9},{5... | collective-permute-start | bytes 2764808 | tf_op jit(solution)/shard_map/ppermute | solution.py:554
  3.6 25.4 %collective-permute-start.1 = (bf16[3600,128]{1,0:T(8,128)(2,1)}, bf16[3600,128]{1,0:T(8,128)(2,1)S(1)}, u32[]{:S(2)}, u32[]{:S(2)}) collective-permute-start(bf16[3600,128]{1,0:T(8,128)(2,1)} %get-tuple-element.49.refs_15_), channel_id=1, source_target_pairs={{8,16},{12,20},{16,8},{20,12},{9,17},{13,21},{17,9},{21,13},{10,18... | collective-permute-start | bytes 2764808 | tf_op jit(solution)/shard_map/ppermute | solution.py:554
  8.7 21.9 %collective-permute-start.2 = (bf16[3600,128]{1,0:T(8,128)(2,1)}, bf16[3600,128]{1,0:T(8,128)(2,1)S(1)}, u32[]{:S(2)}, u32[]{:S(2)}) collective-permute-start(bf16[3600,128]{1,0:T(8,128)(2,1)} %get-tuple-element.49.refs_15_), channel_id=1, source_target_pairs={{0,4},{4,0},{8,12},{12,8},{16,20},{20,16},{24,28},{28,24},{1,5},{5... | collective-permute-start | bytes 2764808 | tf_op jit(solution)/shard_map/ppermute | solution.py:550
  27.4 25.5 %copy-start.9 = (bf16[3600,128]{1,0:T(8,128)(2,1)}, bf16[3600,128]{1,0:T(8,128)(2,1)S(1)}, u32[]{:S(2)}) copy-start(bf16[3600,128]{1,0:T(8,128)(2,1)S(1)} %collective-permute-done.refs_17_) | copy-start | bytes 2764804
  30.6 22.4 %copy-start.10 = (bf16[3600,128]{1,0:T(8,128)(2,1)}, bf16[3600,128]{1,0:T(8,128)(2,1)S(1)}, u32[]{:S(2)}) copy-start(bf16[3600,128]{1,0:T(8,128)(2,1)S(1)} %collective-permute-done.2.refs_16_) | copy-start | bytes 2764804
  30.6 22.4 %collective-permute-start.3 = (bf16[3600,128]{1,0:T(8,128)(2,1)S(1)}, bf16[3600,128]{1,0:T(8,128)(2,1)S(1)}, u32[]{:S(2)}, u32[]{:S(2)}) collective-permute-start(bf16[3600,128]{1,0:T(8,128)(2,1)S(1)} %collective-permute-done.1), channel_id=1, source_target_pairs={{8,0},{12,4},{16,24},{20,28},{9,1},{13,5},{17,25},{21,29},{10,2},{... | collective-permute-start | bytes 2764808 | tf_op jit(solution)/shard_map/ppermute | solution.py:554
  31.9 21.1 %collective-permute-start.4 = (bf16[3600,128]{1,0:T(8,128)(2,1)S(1)}, bf16[3600,128]{1,0:T(8,128)(2,1)S(1)}, u32[]{:S(2)}, u32[]{:S(2)}) collective-permute-start(bf16[3600,128]{1,0:T(8,128)(2,1)S(1)} %collective-permute-done.refs_17_), channel_id=1, source_target_pairs={{0,4},{4,0},{8,12},{12,8},{16,20},{20,16},{24,28},{28,24},{1,5},{5... | collective-permute-start | bytes 2764808 | tf_op jit(solution)/shard_map/ppermute | solution.py:550
  33.5 22.3 %collective-permute-start.5 = (bf16[3600,128]{1,0:T(8,128)(2,1)S(1)}, bf16[3600,128]{1,0:T(8,128)(2,1)S(1)}, u32[]{:S(2)}, u32[]{:S(2)}) collective-permute-start(bf16[3600,128]{1,0:T(8,128)(2,1)S(1)} %collective-permute-done.refs_17_), channel_id=1, source_target_pairs={{8,16},{12,20},{16,8},{20,12},{9,17},{13,21},{17,9},{21,13},{10,18... | collective-permute-start | bytes 2764808 | tf_op jit(solution)/shard_map/ppermute | solution.py:554
  53.0 22.4 %copy-start.11 = (bf16[3600,128]{1,0:T(8,128)(2,1)}, bf16[3600,128]{1,0:T(8,128)(2,1)S(1)}, u32[]{:S(2)}) copy-start(bf16[3600,128]{1,0:T(8,128)(2,1)S(1)} %collective-permute-done.4.refs_18_) | copy-start | bytes 2764804
  55.8 19.6 %collective-permute-start.6 = (bf16[3600,128]{1,0:T(8,128)(2,1)S(1)}, bf16[3600,128]{1,0:T(8,128)(2,1)S(1)}, u32[]{:S(2)}, u32[]{:S(2)}) collective-permute-start(bf16[3600,128]{1,0:T(8,128)(2,1)S(1)} %collective-permute-done.5), channel_id=1, source_target_pairs={{8,0},{12,4},{16,24},{20,28},{9,1},{13,5},{17,25},{21,29},{10,2},{... | collective-permute-start | bytes 2764808 | tf_op jit(solution)/shard_map/ppermute | solution.py:554
  57.6 17.8 %copy-start.4 = (bf16[3600,128]{1,0:T(8,128)(2,1)}, bf16[3600,128]{1,0:T(8,128)(2,1)S(1)}, u32[]{:S(2)}) copy-start(bf16[3600,128]{1,0:T(8,128)(2,1)S(1)} %add.89.refs_19_) | copy-start | bytes 2764804
  57.6 20.3 %collective-permute-start.7 = (bf16[3600,128]{1,0:T(8,128)(2,1)S(1)}, bf16[3600,128]{1,0:T(8,128)(2,1)S(1)}, u32[]{:S(2)}, u32[]{:S(2)}) collective-permute-start(bf16[3600,128]{1,0:T(8,128)(2,1)S(1)} %add.89.refs_19_), channel_id=1, source_target_pairs={{0,4},{4,0},{8,12},{12,8},{16,20},{20,16},{24,28},{28,24},{1,5},{5... | collective-permute-start | bytes 2764808 | tf_op jit(solution)/shard_map/ppermute | solution.py:550
  78.2 18.7 %collective-permute-start.8 = (bf16[3600,128]{1,0:T(8,128)(2,1)S(1)}, bf16[3600,128]{1,0:T(8,128)(2,1)S(1)}, u32[]{:S(2)}, u32[]{:S(2)}) collective-permute-start(bf16[3600,128]{1,0:T(8,128)(2,1)S(1)} %add.90.refs_21_), channel_id=1, source_target_pairs={{0,4},{4,0},{8,12},{12,8},{16,20},{20,16},{24,28},{28,24},{1,5},{5... | collective-permute-start | bytes 2764808 | tf_op jit(solution)/shard_map/ppermute | solution.py:550
  123.4 12.8 %collective-permute-start.9 = (bf16[1200,128]{1,0:T(8,128)(2,1)}, bf16[1200,128]{1,0:T(8,128)(2,1)S(1)}, u32[]{:S(2)}, u32[]{:S(2)}) collective-permute-start(bf16[1200,128]{1,0:T(8,128)(2,1)} %class_sums.6), channel_id=1, source_target_pairs={{0,4},{4,0},{8,12},{12,8},{16,20},{20,16},{24,28},{28,24},{1,5},{5... | collective-permute-start | bytes 921608 | tf_op jit(solution)/shard_map/ppermute | solution.py:550
  127.2 19.7 %collective-permute-start.10 = (bf16[2400,128]{1,0:T(8,128)(2,1)}, bf16[2400,128]{1,0:T(8,128)(2,1)S(1)}, u32[]{:S(2)}, u32[]{:S(2)}) collective-permute-start(bf16[2400,128]{1,0:T(8,128)(2,1)} %class_sums.7), channel_id=1, source_target_pairs={{0,4},{4,0},{8,12},{12,8},{16,20},{20,16},{24,28},{28,24},{1,5},{5... | collective-permute-start | bytes 1843208 | tf_op jit(solution)/shard_map/ppermute | solution.py:550
  135.7 31.0 %collective-permute-start.12 = (bf16[3600,128]{1,0:T(8,128)(2,1)}, bf16[3600,128]{1,0:T(8,128)(2,1)S(1)}, u32[]{:S(2)}, u32[]{:S(2)}) collective-permute-start(bf16[3600,128]{1,0:T(8,128)(2,1)} %get-tuple-element.82), channel_id=1, source_target_pairs={{0,4},{4,0},{8,12},{12,8},{16,20},{20,16},{24,28},{28,24},{1,5},{5... | collective-permute-start | bytes 2764808 | tf_op jit(solution)/shard_map/ppermute | solution.py:550
  137.5 11.8 %collective-permute-start.11 = (bf16[1200,128]{1,0:T(8,128)(2,1)S(1)}, bf16[1200,128]{1,0:T(8,128)(2,1)S(1)}, u32[]{:S(2)}, u32[]{:S(2)}) collective-permute-start(bf16[1200,128]{1,0:T(8,128)(2,1)S(1)} %fusion.2), channel_id=1, source_target_pairs={{0,8},{4,12},{24,16},{28,20},{1,9},{5,13},{25,17},{29,21},{2,10},{... | collective-permute-start | bytes 921608 | tf_op jit(solution)/shard_map/ppermute | solution.py:554
  138.8 8.2 %copy-start.3 = (f32[3600,128]{1,0:T(8,128)S(1)}, f32[3600,128]{1,0:T(8,128)}, u32[]{:S(2)}) copy-start(f32[3600,128]{1,0:T(8,128)} %get-tuple-element.75) | copy-start | bytes 5529604
  147.9 18.8 %collective-permute-start.13 = (bf16[2400,128]{1,0:T(8,128)(2,1)}, bf16[2400,128]{1,0:T(8,128)(2,1)}, u32[]{:S(2)}, u32[]{:S(2)}) collective-permute-start(bf16[2400,128]{1,0:T(8,128)(2,1)} %fusion.1), channel_id=1, source_target_pairs={{0,8},{4,12},{24,16},{28,20},{1,9},{5,13},{25,17},{29,21},{2,10},{... | collective-permute-start | bytes 1843208 | tf_op jit(solution)/shard_map/ppermute | solution.py:554
  150.1 10.5 %collective-permute-start.14 = (bf16[1200,128]{1,0:T(8,128)(2,1)}, bf16[1200,128]{1,0:T(8,128)(2,1)}, u32[]{:S(2)}, u32[]{:S(2)}) collective-permute-start(bf16[1200,128]{1,0:T(8,128)(2,1)} %add_convert_fusion.4), channel_id=1, source_target_pairs={{8,16},{12,20},{16,8},{20,12},{9,17},{13,21},{17,9},{21,13},{10,18... | collective-permute-start | bytes 921608 | tf_op jit(solution)/shard_map/ppermute | solution.py:554
  152.9 33.6 %collective-permute-start.17 = (bf16[3600,128]{1,0:T(8,128)(2,1)}, bf16[3600,128]{1,0:T(8,128)(2,1)}, u32[]{:S(2)}, u32[]{:S(2)}) collective-permute-start(bf16[3600,128]{1,0:T(8,128)(2,1)} %get-tuple-element.90), channel_id=1, source_target_pairs={{0,4},{4,0},{8,12},{12,8},{16,20},{20,16},{24,28},{28,24},{1,5},{5... | collective-permute-start | bytes 2764808 | tf_op jit(solution)/shard_map/ppermute | solution.py:550
  153.5 13.2 %copy-start.2 = (f32[3600,128]{1,0:T(8,128)S(1)}, f32[3600,128]{1,0:T(8,128)}, u32[]{:S(2)}) copy-start(f32[3600,128]{1,0:T(8,128)} %get-tuple-element.85) | copy-start | bytes 5529604
  166.9 22.1 %collective-permute-start.16 = (bf16[3600,128]{1,0:T(8,128)(2,1)S(1)}, bf16[3600,128]{1,0:T(8,128)(2,1)S(1)}, u32[]{:S(2)}, u32[]{:S(2)}) collective-permute-start(bf16[3600,128]{1,0:T(8,128)(2,1)S(1)} %fusion), channel_id=1, source_target_pairs={{0,8},{4,12},{24,16},{28,20},{1,9},{5,13},{25,17},{29,21},{2,10},{... | collective-permute-start | bytes 2764808 | tf_op jit(solution)/shard_map/ppermute | solution.py:554
  168.2 45.5 %collective-permute-start.15 = (bf16[3600,128]{1,0:T(8,128)(2,1)}, bf16[3600,128]{1,0:T(8,128)(2,1)}, u32[]{:S(2)}, u32[]{:S(2)}) collective-permute-start(bf16[3600,128]{1,0:T(8,128)(2,1)} %get-tuple-element.89), channel_id=1, source_target_pairs={{0,4},{4,0},{8,12},{12,8},{16,20},{20,16},{24,28},{28,24},{1,5},{5... | collective-permute-start | bytes 2764808 | tf_op jit(solution)/shard_map/ppermute | solution.py:550
  170.1 23.1 %copy-start.6 = (f32[3600,128]{1,0:T(8,128)S(1)}, f32[3600,128]{1,0:T(8,128)}, u32[]{:S(2)}) copy-start(f32[3600,128]{1,0:T(8,128)} %get-tuple-element.92) | copy-start | bytes 5529604
  170.1 23.1 %collective-permute-start.20 = (bf16[2400,128]{1,0:T(8,128)(2,1)S(1)}, bf16[2400,128]{1,0:T(8,128)(2,1)S(1)}, u32[]{:S(2)}, u32[]{:S(2)}) collective-permute-start(bf16[2400,128]{1,0:T(8,128)(2,1)S(1)} %add_convert_fusion.2), channel_id=1, source_target_pairs={{8,16},{12,20},{16,8},{20,12},{9,17},{13,21},{17,9},{21,13},{10,18... | collective-permute-start | bytes 1843208 | tf_op jit(solution)/shard_map/ppermute | solution.py:554
  190.3 7.6 %copy-start.17 = (f32[56,128]{1,0:T(8,128)S(1)}, f32[56,128]{1,0:T(8,128)}, u32[]{:S(2)}) copy-start(f32[56,128]{1,0:T(8,128)} %get-tuple-element.70) | copy-start | bytes 86020
  190.3 23.5 %collective-permute-start.18 = (bf16[3600,128]{1,0:T(8,128)(2,1)}, bf16[3600,128]{1,0:T(8,128)(2,1)S(1)}, u32[]{:S(2)}, u32[]{:S(2)}) collective-permute-start(bf16[3600,128]{1,0:T(8,128)(2,1)} %add_convert_fusion), channel_id=1, source_target_pairs={{8,16},{12,20},{16,8},{20,12},{9,17},{13,21},{17,9},{21,13},{10,18... | collective-permute-start | bytes 2764808 | tf_op jit(solution)/shard_map/ppermute | solution.py:554
  194.5 19.2 %collective-permute-start.21 = (bf16[2400,128]{1,0:T(8,128)(2,1)S(1)}, bf16[2400,128]{1,0:T(8,128)(2,1)S(1)}, u32[]{:S(2)}, u32[]{:S(2)}) collective-permute-start(bf16[2400,128]{1,0:T(8,128)(2,1)S(1)} %add_convert_fusion.1), channel_id=1, source_target_pairs={{0,8},{4,12},{8,0},{12,4},{16,24},{20,28},{24,16},{28,20},{1,9},{5... | collective-permute-start | bytes 1843208 | tf_op jit(solution)/shard_map/ppermute | solution.py:554
  195.8 17.9 %collective-permute-start.19 = (bf16[1200,128]{1,0:T(8,128)(2,1)S(1)}, bf16[1200,128]{1,0:T(8,128)(2,1)S(1)}, u32[]{:S(2)}, u32[]{:S(2)}) collective-permute-start(bf16[1200,128]{1,0:T(8,128)(2,1)S(1)} %add_convert_fusion.3), channel_id=1, source_target_pairs={{0,8},{4,12},{8,0},{12,4},{16,24},{20,28},{24,16},{28,20},{1,9},{5... | collective-permute-start | bytes 921608 | tf_op jit(solution)/shard_map/ppermute | solution.py:554
  199.7 20.3 %copy-start.1 = (f32[16,128]{1,0:T(8,128)S(1)}, f32[16,128]{1,0:T(8,128)}, u32[]{:S(2)}) copy-start(f32[16,128]{1,0:T(8,128)} %param.15) | copy-start | bytes 24580
  (9 other events, 15.9 us)

commit v10 on v9

--- a/solution.py
+++ b/solution.py
@@ -586,30 +586,6 @@
     return weighted, pieces, slot_of
 
 
-def add_kernel(own_ref, *refs):
-    *whole_refs, head_ref, rest_ref, out_ref = refs
-    total = own_ref[...]
-    for ref in whole_refs:
-        total = total + ref[...].astype(f32)
-    part = jnp.where(pl.program_id(0) == 0, head_ref[...], rest_ref[...])
-    out_ref[...] = total + part.astype(f32)
-
-
-def add_pieces(own, whole, pair, block):
-    rows, cycles = own.shape
-    spec = pl.BlockSpec((block, cycles), lambda g: (g, 0))
-    head = pl.BlockSpec((block, cycles), lambda g: (0, 0))
-    rest = pl.BlockSpec((block, cycles), lambda g: (jnp.maximum(g - 1, 0), 0))
-    return pl.pallas_call(
-        add_kernel,
-        grid=(rows // block,),
-        in_specs=[spec] * (1 + len(whole)) + [head, rest],
-        out_specs=spec,
-        out_shape=jax.ShapeDtypeStruct(own.shape, f32),
-        name="add_pieces",
-    )(own, *whole, *pair)
-
-
 def reduce_on_line(back, weighted, offsets, classes):
     index = lax.axis_index("dp")
     line, side = index // 2, index % 2
@@ -664,15 +640,13 @@
     middle_rest = along(message, between)
     back = then(back, message)
     (own_3,) = sums(ours[3:], [f32], back)
-    message = (own_2[head] + wide(crossed_2[head]) + wide(middle_head)).astype(bf16)
-    last_head = along(message, neighbours)
     from_end = then(from_end, crossed_2)
     message = (own_1 + wide(crossed_1) + wide(from_end)).astype(bf16)
     third = along(message, between)
     middle_rest = then(middle_rest, message)
-    message = (own_2[rest] + wide(crossed_2[rest]) + wide(middle_rest)).astype(bf16)
-    last_rest = along(message, neighbours)
-    return add_pieces(own_3, (crossed_3, third), (last_head, last_rest), block)
+    middle = jnp.concatenate([middle_head, middle_rest], 0)
+    last = along((own_2 + wide(crossed_2) + wide(middle)).astype(bf16), neighbours)
+    return own_3 + wide(crossed_3) + wide(third) + wide(last)
 
 
 def local(particles, references, ctf_table, rot_offset, prior_shift, defocus_group):

time: 222 us -> 218 us (0.982)
  Pallas kernels: 125 us -> 120 us
  waiting for transfers between devices: 40.9 us -> 43.7 us
  other arithmetic: 8.82 us -> 11.3 us
  starting transfers between devices: 32.8 us -> 30.5 us
    pallas_call x1 -> x0, Pallas kernels: 4.47 us -> none  [add_pieces(): pl.pallas_call(add_kernel, grid=(rows // block,), in_specs=[spec] * (1 +...]
    add x0 -> x1, other arithmetic: none -> 3.36 us  [reduce_on_line(): return own_3 + wide(crossed_3) + wide(third) + wide(last)]
    ppermute x9, waiting for transfers between devices: 25.3 us -> 28.7 us  [across(): return lax.ppermute(piece, 'dp', [(d, d ^ 1) for d in range(8)])]
    ppermute x13 -> x12, starting transfers between devices: 24.7 us -> 22.5 us  [along(): lax.ppermute(piece, 'dp', [(2 * a + x, 2 * b + x) for a, b in pairs for x...]
    ppermute x13 -> x12, waiting for transfers between devices: 15.6 us -> 15.1 us  [along(): lax.ppermute(piece, 'dp', [(2 * a + x, 2 * b + x) for a, b in pairs for x...]
  transfers between devices with their start and end apart: 22 -> 21, of which waited for: 10 -> 12; matrix products, arithmetic and copies ran while one was open for 5% -> 5% of each run, Pallas kernels for 44% -> 45%
where the time goes in v10:
time: 218 us; the launch traced here: 217 us
  Pallas kernels  120 us (55%)
  waiting for transfers between devices  43.7 us (20%)
  starting transfers between devices  30.5 us (14%)
  other arithmetic  11.3 us (5%)
  blocking collectives  6.23 us (3%)
  local copies, waits for them, and re-layouts  3.23 us (1%)
    pallas_call x3, Pallas kernels, make_spectra(): pl.pallas_call(functools.partial(spectra_kernel, per_step=per_step), grid...  46.4 us
    pallas_call x6, Pallas kernels, class_sums_of(): pl.pallas_call(functools.partial(sums_kernel, count=count, classes=classe...  32.4 us
    ppermute x9, waiting for transfers between devices, across(): return lax.ppermute(piece, 'dp', [(d, d ^ 1) for d in range(8)])  28.7 us
    pallas_call x2, Pallas kernels, correlate(): pl.pallas_call(functools.partial(correlate_kernel, slots=slots, classes=c...  28.4 us
    ppermute x12, starting transfers between devices, along(): lax.ppermute(piece, 'dp', [(2 * a + x, 2 * b + x) for a, b in pairs for x...  22.5 us
    ppermute x12, waiting for transfers between devices, along(): lax.ppermute(piece, 'dp', [(2 * a + x, 2 * b + x) for a, b in pairs for x...  15.1 us
    ppermute x9, starting transfers between devices, across(): return lax.ppermute(piece, 'dp', [(d, d ^ 1) for d in range(8)])  8.01 us
    psum x1, blocking collectives, local(): shares = lax.psum(share, 'cls')  6.23 us
  transfers between devices with their start and end apart: 21, of which 12 were waited for; matrix products, arithmetic and copies ran while one was open for 5% of the time, Pallas kernels for 45%

profile of v10, /device:TPU:8, one launch (start us, length us, event | category | flops | bytes accessed | tf_op | source)
XLA Modules:
  0.0 216.8 jit_solution(18232189837681062355)
XLA Ops:
  0.7 3.0 %turn_references.1 = (bf16[3600,128]{1,0:T(8,128)(2,1)}, f32[56,128]{1,0:T(8,128)}) custom-call(s32[1]{0:T(128)} %bitcast.3.first_ref, s32[50]{0:T(128)} %offset_ref.1, bf16[3600,128]{1,0:T(8,128)(2,1)} %bitcast.45), custom_call_target="tpu_custom_call" | custom-call | tf_op jit(solution)/shard_map/turn_references/pallas_call | solution.py:251
  3.6 5.0 %collective-permute-start.1 = (bf16[3600,128]{1,0:T(8,128)(2,1)}, bf16[3600,128]{1,0:T(8,128)(2,1)S(1)}, u32[]{:S(2)}, u32[]{:S(2)}) collective-permute-start(bf16[3600,128]{1,0:T(8,128)(2,1)} %get-tuple-element.49.refs_15_), channel_id=1, source_target_pairs={{8,16},{12,20},{16,8},{20,12},{9,17},{13,21},{17,9},{21,13},{10,18... | collective-permute-start | bytes 2764808 | tf_op jit(solution)/shard_map/ppermute | solution.py:554
  8.7 1.6 collective-permute-start.2
  10.2 4.6 %centre.1.base_ref = f32[8,2,288,128]{3,2,1,0:T(8,128)} custom-call(s32[2,8]{1,0:T(2,128)} %bitcast.46, bf16[8,2,288,128]{3,2,1,0:T(8,128)(2,1)} %part_ref.1, f32[2,288,128]{2,1,0:T(8,128)} %constant.49.clone.turns_ref), custom_call_target="tpu_custom_call" | custom-call | tf_op jit(solution)/shard_map/centre/pallas_call | solution.py:87
  15.7 11.9 %spectra.3.refs_4_ = bf16[288,208,256]{2,1,0:T(8,128)(2,1)} custom-call(f32[8,2,288,128]{3,2,1,0:T(8,128)} %centre.1.base_ref, f32[8,128]{1,0:T(8,128)} %fusion.3.ctf_ref.refs_6_, bf16[576,576]{1,0:T(8,128)(2,1)} %constant.50.clone.table_ref, f32[2,5,2,288,128]{4,3,2,1,0:T(8,128)} %constant.51.clone.refs_0_.refs_1_.refs_2_.refs_3_, ...), custom_call_target="tpu_custom_call" | custom-call | tf_op jit(solution)/shard_map/spectra/pallas_call | solution.py:171
  31.9 1.6 collective-permute-start.4
  33.5 2.2 %collective-permute-start.5 = (bf16[3600,128]{1,0:T(8,128)(2,1)S(1)}, bf16[3600,128]{1,0:T(8,128)(2,1)S(1)}, u32[]{:S(2)}, u32[]{:S(2)}) collective-permute-start(bf16[3600,128]{1,0:T(8,128)(2,1)S(1)} %collective-permute-done.refs_17_), channel_id=1, source_target_pairs={{8,16},{12,20},{16,8},{20,12},{9,17},{13,21},{17,9},{21,13},{10,18... | collective-permute-start | bytes 2764808 | tf_op jit(solution)/shard_map/ppermute | solution.py:554
  35.7 17.2 %spectra.4.refs_4_ = bf16[288,208,256]{2,1,0:T(8,128)(2,1)} custom-call(f32[8,2,288,128]{3,2,1,0:T(8,128)} %centre.1.base_ref, f32[8,128]{1,0:T(8,128)} %fusion.3.ctf_ref.refs_6_, bf16[576,576]{1,0:T(8,128)(2,1)} %constant.50.clone.table_ref, f32[2,5,2,288,128]{4,3,2,1,0:T(8,128)} %constant.51.clone.refs_0_.refs_1_.refs_2_.refs_3_, ...), custom_call_target="tpu_custom_call", output_to_operand_aliasing={{}: (7, {})} | custom-call | tf_op jit(solution)/shard_map/spectra/pallas_call | solution.py:171
  53.0 2.8 %collective-permute-done.5 = bf16[3600,128]{1,0:T(8,128)(2,1)S(1)} collective-permute-done((bf16[3600,128]{1,0:T(8,128)(2,1)S(1)}, bf16[3600,128]{1,0:T(8,128)(2,1)S(1)}, u32[]{:S(2)}, u32[]{:S(2)}) %collective-permute-start.5) | collective-permute-done | bytes 921632 | tf_op jit(solution)/shard_map/ppermute | solution.py:554
  58.2 17.2 %spectra.5 = bf16[288,208,256]{2,1,0:T(8,128)(2,1)} custom-call(f32[8,2,288,128]{3,2,1,0:T(8,128)} %centre.1.base_ref, f32[8,128]{1,0:T(8,128)} %fusion.3.ctf_ref.refs_6_, bf16[576,576]{1,0:T(8,128)(2,1)} %constant.50.clone.table_ref, f32[2,5,2,288,128]{4,3,2,1,0:T(8,128)} %constant.51.clone.refs_0_.refs_1_.refs_2_.refs_3_, ...), custom_call_target="tpu_custom_call", output_to_operand_aliasing={{}: (7, {})} | custom-call | tf_op jit(solution)/shard_map/spectra/pallas_call | solution.py:171
  75.4 2.5 %collective-permute-done.7.refs_20_ = bf16[3600,128]{1,0:T(8,128)(2,1)S(1)} collective-permute-done((bf16[3600,128]{1,0:T(8,128)(2,1)S(1)}, bf16[3600,128]{1,0:T(8,128)(2,1)S(1)}, u32[]{:S(2)}, u32[]{:S(2)}) %collective-permute-start.7) | collective-permute-done | bytes 921632 | tf_op jit(solution)/shard_map/ppermute | solution.py:550
  79.2 17.1 %correlate.1 = (f32[36,112,256]{2,1,0:T(8,128)}, f32[56,128]{1,0:T(8,128)}) custom-call(s32[1]{0:T(128)} %bitcast.7.refs_0_, s32[1]{0:T(128)} %bitcast.8.refs_1_, s32[1]{0:T(128)} %bitcast.9.refs_2_.refs_0_, s32[1]{0:T(128)} %bitcast.10.refs_3_, s32[1]{0:T(128)} %bitcast.11.refs_4_.refs_0_, s32[1]{0:T(128)} %bitcast.12.refs_5_, s32[1]{0:T(128)} %bitcast.13.refs_6_.refs_0_, ...), custom_call_target="tpu_custom_call" | custom-call | tf_op jit(solution)/shard_map/correlate/pallas_call | solution.py:417
  97.8 11.3 %scores.1 = (f32[36,56,256]{2,1,0:T(8,128)}, f32[64,128]{1,0:T(8,128)}, f32[4,2,128]{2,1,0:T(2,128)}) custom-call(s32[1]{0:T(128)} %bitcast.refs_0_, s32[1]{0:T(128)} %bitcast.1.refs_7_.refs_1_, bf16[8,36,208,256]{3,2,1,0:T(8,128)(2,1)} %bitcast.34, bf16[3600,128]{1,0:T(8,128)(2,1)} %copy-done.13, f32[36,112,256]{2,1,0:T(8,128)} %get-tuple-element.63.refs_4_, ...), custom_call_target="tpu_custom_call" | custom-call | tf_op jit(solution)/shard_map/scores/pallas_call | solution.py:417
  109.1 6.2 %psum.7.share_ref = f32[4,2,128]{2,1,0:T(2,128)} all-reduce(f32[4,2,128]{2,1,0:T(2,128)} %get-tuple-element.67), channel_id=1, replica_groups=mesh['dp'=8,'cls'=4] {'cls'}, use_global_device_ids=true, to_apply=%region_0.1 | all-reduce | flops 1024 | bytes 8192 | tf_op jit(solution)/shard_map/psum | solution.py:684
  115.4 5.4 %back.1 = (bf16[36,112,208]{2,1,0:T(8,128)(2,1)}, f32[8,128]{1,0:T(8,128)}, f32[56,128]{1,0:T(8,128)}) custom-call(f32[36,56,256]{2,1,0:T(8,128)} %get-tuple-element.65.weight_ref, f32[64,128]{1,0:T(8,128)} %get-tuple-element.66.stat_ref, f32[4,2,128]{2,1,0:T(2,128)} %psum.7.share_ref, f32[56,128]{1,0:T(8,128)} %get-tuple-element.68.offset_ref.refs_3_.refs_5_), custom_call_target="tpu_custom_call" | custom-call | tf_op jit(solution)/shard_map/back/pallas_call | solution.py:483
  120.8 2.6 %class_sums.6 = bf16[1200,128]{1,0:T(8,128)(2,1)} custom-call(s32[1]{0:T(128)} %bitcast.16.refs_0_, bf16[36,112,208]{2,1,0:T(8,128)(2,1)} %get-tuple-element.88.refs_1_.refs_2_, bf16[8,36,208,256]{3,2,1,0:T(8,128)(2,1)} %bitcast.35, f32[56,128]{1,0:T(8,128)} %get-tuple-element.68.offset_ref.refs_3_.refs_5_), custom_call_target="tpu_custom_call" | custom-call | tf_op jit(solution)/shard_map/class_sums/pallas_call | solution.py:526
  124.0 3.2 %class_sums.7 = bf16[2400,128]{1,0:T(8,128)(2,1)} custom-call(s32[1]{0:T(128)} %bitcast.16.refs_0_, bf16[36,112,208]{2,1,0:T(8,128)(2,1)} %get-tuple-element.88.refs_1_.refs_2_, bf16[8,36,208,256]{3,2,1,0:T(8,128)(2,1)} %bitcast.36, f32[56,128]{1,0:T(8,128)} %get-tuple-element.68.offset_ref.refs_3_.refs_5_), custom_call_target="tpu_custom_call" | custom-call | tf_op jit(solution)/shard_map/class_sums/pallas_call | solution.py:526
  128.7 7.1 %class_sums.8 = (f32[3600,128]{1,0:T(8,128)}, bf16[3600,128]{1,0:T(8,128)(2,1)}) custom-call(s32[1]{0:T(128)} %bitcast.13.refs_6_.refs_0_, s32[1]{0:T(128)} %bitcast.17.refs_1_, bf16[36,112,208]{2,1,0:T(8,128)(2,1)} %get-tuple-element.88.refs_1_.refs_2_, bf16[8,36,208,256]{3,2,1,0:T(8,128)(2,1)} %bitcast.37, bf16[8,36,208,256]{3,2,1,0:T(8,128)(2,1)} %bitcast.38, ...), custom_call_target="tpu_custom_call" | custom-call | tf_op jit(solution)/shard_map/class_sums/pallas_call | solution.py:526
  138.8 7.1 %class_sums.9 = (f32[3600,128]{1,0:T(8,128)}, bf16[3600,128]{1,0:T(8,128)(2,1)}) custom-call(s32[1]{0:T(128)} %bitcast.11.refs_4_.refs_0_, s32[1]{0:T(128)} %bitcast.18.refs_1_, bf16[36,112,208]{2,1,0:T(8,128)(2,1)} %get-tuple-element.88.refs_1_.refs_2_, bf16[8,36,208,256]{3,2,1,0:T(8,128)(2,1)} %bitcast.39, bf16[8,36,208,256]{3,2,1,0:T(8,128)(2,1)} %bitcast.40, ...), custom_call_target="tpu_custom_call" | custom-call | tf_op jit(solution)/shard_map/class_sums/pallas_call | solution.py:526
  150.1 2.8 %collective-permute-start.14 = (bf16[1200,128]{1,0:T(8,128)(2,1)}, bf16[1200,128]{1,0:T(8,128)(2,1)}, u32[]{:S(2)}, u32[]{:S(2)}) collective-permute-start(bf16[1200,128]{1,0:T(8,128)(2,1)} %add_convert_fusion.3), channel_id=1, source_target_pairs={{8,16},{12,20},{16,8},{20,12},{9,17},{13,21},{17,9},{21,13},{10,18... | collective-permute-start | bytes 921608 | tf_op jit(solution)/shard_map/ppermute | solution.py:554
  153.5 7.1 %class_sums.10 = (f32[3600,128]{1,0:T(8,128)}, bf16[3600,128]{1,0:T(8,128)(2,1)}) custom-call(s32[1]{0:T(128)} %bitcast.9.refs_2_.refs_0_, s32[1]{0:T(128)} %bitcast.19.refs_1_, bf16[36,112,208]{2,1,0:T(8,128)(2,1)} %get-tuple-element.88.refs_1_.refs_2_, bf16[8,36,208,256]{3,2,1,0:T(8,128)(2,1)} %bitcast.41, bf16[8,36,208,256]{3,2,1,0:T(8,128)(2,1)} %bitcast.42, ...), custom_call_target="tpu_custom_call" | custom-call | tf_op jit(solution)/shard_map/class_sums/pallas_call | solution.py:526
  160.6 6.1 %collective-permute-done.12 = bf16[3600,128]{1,0:T(8,128)(2,1)S(1)} collective-permute-done((bf16[3600,128]{1,0:T(8,128)(2,1)}, bf16[3600,128]{1,0:T(8,128)(2,1)S(1)}, u32[]{:S(2)}, u32[]{:S(2)}) %collective-permute-start.12) | collective-permute-done | bytes 921632 | tf_op jit(solution)/shard_map/ppermute | solution.py:550
  170.1 2.9 %collective-permute-start.19 = (bf16[2400,128]{1,0:T(8,128)(2,1)S(1)}, bf16[2400,128]{1,0:T(8,128)(2,1)S(1)}, u32[]{:S(2)}, u32[]{:S(2)}) collective-permute-start(bf16[2400,128]{1,0:T(8,128)(2,1)S(1)} %add_convert_fusion.2), channel_id=1, source_target_pairs={{8,16},{12,20},{16,8},{20,12},{9,17},{13,21},{17,9},{21,13},{10,18... | collective-permute-start | bytes 1843208 | tf_op jit(solution)/shard_map/ppermute | solution.py:554
  173.1 13.5 %collective-permute-done.17 = bf16[3600,128]{1,0:T(8,128)(2,1)} collective-permute-done((bf16[3600,128]{1,0:T(8,128)(2,1)}, bf16[3600,128]{1,0:T(8,128)(2,1)}, u32[]{:S(2)}, u32[]{:S(2)}) %collective-permute-start.17) | collective-permute-done | bytes 921632 | tf_op jit(solution)/shard_map/ppermute | solution.py:550
  186.6 2.5 %collective-permute-done.16 = bf16[3600,128]{1,0:T(8,128)(2,1)S(1)} collective-permute-done((bf16[3600,128]{1,0:T(8,128)(2,1)S(1)}, bf16[3600,128]{1,0:T(8,128)(2,1)S(1)}, u32[]{:S(2)}, u32[]{:S(2)}) %collective-permute-start.16) | collective-permute-done | bytes 921632 | tf_op jit(solution)/shard_map/ppermute | solution.py:554
  190.3 1.6 add_convert_fusion
  192.0 2.8 %collective-permute-start.18 = (bf16[3600,128]{1,0:T(8,128)(2,1)}, bf16[3600,128]{1,0:T(8,128)(2,1)S(1)}, u32[]{:S(2)}, u32[]{:S(2)}) collective-permute-start(bf16[3600,128]{1,0:T(8,128)(2,1)} %add_convert_fusion.1), channel_id=1, source_target_pairs={{8,16},{12,20},{16,8},{20,12},{9,17},{13,21},{17,9},{21,13},{10,18... | collective-permute-start | bytes 2764808 | tf_op jit(solution)/shard_map/ppermute | solution.py:554
  196.6 5.2 %class_sums.11 = f32[3600,128]{1,0:T(8,128)} custom-call(s32[1]{0:T(128)} %bitcast.7.refs_0_, bf16[36,112,208]{2,1,0:T(8,128)(2,1)} %get-tuple-element.88.refs_1_.refs_2_, bf16[8,36,208,256]{3,2,1,0:T(8,128)(2,1)} %bitcast.43, f32[56,128]{1,0:T(8,128)} %get-tuple-element.68.offset_ref.refs_3_.refs_5_), custom_call_target="tpu_custom_call" | custom-call | tf_op jit(solution)/shard_map/class_sums/pallas_call | solution.py:526
  201.8 3.4 %collective-permute-done.15 = bf16[3600,128]{1,0:T(8,128)(2,1)} collective-permute-done((bf16[3600,128]{1,0:T(8,128)(2,1)}, bf16[3600,128]{1,0:T(8,128)(2,1)}, u32[]{:S(2)}, u32[]{:S(2)}) %collective-permute-start.15) | collective-permute-done | bytes 921632 | tf_op jit(solution)/shard_map/ppermute | solution.py:550
  205.2 6.2 %collective-permute-done.20 = bf16[3600,128]{1,0:T(8,128)(2,1)S(1)} collective-permute-done((bf16[3600,128]{1,0:T(8,128)(2,1)S(1)}, bf16[3600,128]{1,0:T(8,128)(2,1)S(1)}, u32[]{:S(2)}, u32[]{:S(2)}) %collective-permute-start.20) | collective-permute-done | bytes 921632 | tf_op jit(solution)/shard_map/ppermute | solution.py:554
  211.3 2.1 collective-permute-done.18
  213.5 3.4 %convert_add_fusion = f32[3600,128]{1,0:T(8,128)} fusion(bf16[3600,128]{1,0:T(8,128)(2,1)S(1)} %collective-permute-done.20, bf16[3600,128]{1,0:T(8,128)(2,1)S(1)} %collective-permute-done.18, f32[3600,128]{1,0:T(8,128)} %class_sums.11, bf16[3600,128]{1,0:T(8,128)(2,1)} %collective-permute-done.15), kind=kLoop, calls=%fused_computation | loop fusion | flops 2764800 | bytes 6451200 | tf_op jit(solution)/shard_map/add | solution.py:649
  (71 shorter events, 26.8 us)
Async XLA Ops:
  0.6 14.3 %copy-start = (f32[16,128]{1,0:T(8,128)S(1)}, f32[16,128]{1,0:T(8,128)}, u32[]{:S(2)}) copy-start(f32[16,128]{1,0:T(8,128)} %param.15) | copy-start | bytes 24580
  3.6 23.9 %collective-permute-start = (bf16[3600,128]{1,0:T(8,128)(2,1)}, bf16[3600,128]{1,0:T(8,128)(2,1)S(1)}, u32[]{:S(2)}, u32[]{:S(2)}) collective-permute-start(bf16[3600,128]{1,0:T(8,128)(2,1)} %get-tuple-element.49.refs_15_), channel_id=1, source_target_pairs={{0,8},{4,12},{8,0},{12,4},{16,24},{20,28},{24,16},{28,20},{1,9},{5... | collective-permute-start | bytes 2764808 | tf_op jit(solution)/shard_map/ppermute | solution.py:554
  3.6 25.4 %collective-permute-start.1 = (bf16[3600,128]{1,0:T(8,128)(2,1)}, bf16[3600,128]{1,0:T(8,128)(2,1)S(1)}, u32[]{:S(2)}, u32[]{:S(2)}) collective-permute-start(bf16[3600,128]{1,0:T(8,128)(2,1)} %get-tuple-element.49.refs_15_), channel_id=1, source_target_pairs={{8,16},{12,20},{16,8},{20,12},{9,17},{13,21},{17,9},{21,13},{10,18... | collective-permute-start | bytes 2764808 | tf_op jit(solution)/shard_map/ppermute | solution.py:554
  8.7 21.9 %collective-permute-start.2 = (bf16[3600,128]{1,0:T(8,128)(2,1)}, bf16[3600,128]{1,0:T(8,128)(2,1)S(1)}, u32[]{:S(2)}, u32[]{:S(2)}) collective-permute-start(bf16[3600,128]{1,0:T(8,128)(2,1)} %get-tuple-element.49.refs_15_), channel_id=1, source_target_pairs={{0,4},{4,0},{8,12},{12,8},{16,20},{20,16},{24,28},{28,24},{1,5},{5... | collective-permute-start | bytes 2764808 | tf_op jit(solution)/shard_map/ppermute | solution.py:550
  10.2 4.6 %copy-start.15 = (s32[8]{0:T(128)S(1)}, s32[8]{0:T(128)}, u32[]{:S(2)}) copy-start(s32[8]{0:T(128)} %param.18) | copy-start | bytes 100
  27.5 25.4 %copy-start.9 = (bf16[3600,128]{1,0:T(8,128)(2,1)}, bf16[3600,128]{1,0:T(8,128)(2,1)S(1)}, u32[]{:S(2)}) copy-start(bf16[3600,128]{1,0:T(8,128)(2,1)S(1)} %collective-permute-done.refs_17_) | copy-start | bytes 2764804
  30.6 22.4 %copy-start.10 = (bf16[3600,128]{1,0:T(8,128)(2,1)}, bf16[3600,128]{1,0:T(8,128)(2,1)S(1)}, u32[]{:S(2)}) copy-start(bf16[3600,128]{1,0:T(8,128)(2,1)S(1)} %collective-permute-done.2.refs_16_) | copy-start | bytes 2764804
  30.6 22.4 %collective-permute-start.3 = (bf16[3600,128]{1,0:T(8,128)(2,1)S(1)}, bf16[3600,128]{1,0:T(8,128)(2,1)S(1)}, u32[]{:S(2)}, u32[]{:S(2)}) collective-permute-start(bf16[3600,128]{1,0:T(8,128)(2,1)S(1)} %collective-permute-done.1), channel_id=1, source_target_pairs={{8,0},{12,4},{16,24},{20,28},{9,1},{13,5},{17,25},{21,29},{10,2},{... | collective-permute-start | bytes 2764808 | tf_op jit(solution)/shard_map/ppermute | solution.py:554
  31.9 21.0 %collective-permute-start.4 = (bf16[3600,128]{1,0:T(8,128)(2,1)S(1)}, bf16[3600,128]{1,0:T(8,128)(2,1)S(1)}, u32[]{:S(2)}, u32[]{:S(2)}) collective-permute-start(bf16[3600,128]{1,0:T(8,128)(2,1)S(1)} %collective-permute-done.refs_17_), channel_id=1, source_target_pairs={{0,4},{4,0},{8,12},{12,8},{16,20},{20,16},{24,28},{28,24},{1,5},{5... | collective-permute-start | bytes 2764808 | tf_op jit(solution)/shard_map/ppermute | solution.py:550
  33.5 22.3 %collective-permute-start.5 = (bf16[3600,128]{1,0:T(8,128)(2,1)S(1)}, bf16[3600,128]{1,0:T(8,128)(2,1)S(1)}, u32[]{:S(2)}, u32[]{:S(2)}) collective-permute-start(bf16[3600,128]{1,0:T(8,128)(2,1)S(1)} %collective-permute-done.refs_17_), channel_id=1, source_target_pairs={{8,16},{12,20},{16,8},{20,12},{9,17},{13,21},{17,9},{21,13},{10,18... | collective-permute-start | bytes 2764808 | tf_op jit(solution)/shard_map/ppermute | solution.py:554
  53.0 22.5 %copy-start.11 = (bf16[3600,128]{1,0:T(8,128)(2,1)}, bf16[3600,128]{1,0:T(8,128)(2,1)S(1)}, u32[]{:S(2)}) copy-start(bf16[3600,128]{1,0:T(8,128)(2,1)S(1)} %collective-permute-done.4.refs_18_) | copy-start | bytes 2764804
  55.8 19.6 %collective-permute-start.6 = (bf16[3600,128]{1,0:T(8,128)(2,1)S(1)}, bf16[3600,128]{1,0:T(8,128)(2,1)S(1)}, u32[]{:S(2)}, u32[]{:S(2)}) collective-permute-start(bf16[3600,128]{1,0:T(8,128)(2,1)S(1)} %collective-permute-done.5), channel_id=1, source_target_pairs={{8,0},{12,4},{16,24},{20,28},{9,1},{13,5},{17,25},{21,29},{10,2},{... | collective-permute-start | bytes 2764808 | tf_op jit(solution)/shard_map/ppermute | solution.py:554
  57.6 17.9 %copy-start.4 = (bf16[3600,128]{1,0:T(8,128)(2,1)}, bf16[3600,128]{1,0:T(8,128)(2,1)S(1)}, u32[]{:S(2)}) copy-start(bf16[3600,128]{1,0:T(8,128)(2,1)S(1)} %add.92.refs_19_) | copy-start | bytes 2764804
  57.6 20.3 %collective-permute-start.7 = (bf16[3600,128]{1,0:T(8,128)(2,1)S(1)}, bf16[3600,128]{1,0:T(8,128)(2,1)S(1)}, u32[]{:S(2)}, u32[]{:S(2)}) collective-permute-start(bf16[3600,128]{1,0:T(8,128)(2,1)S(1)} %add.92.refs_19_), channel_id=1, source_target_pairs={{0,4},{4,0},{8,12},{12,8},{16,20},{20,16},{24,28},{28,24},{1,5},{5... | collective-permute-start | bytes 2764808 | tf_op jit(solution)/shard_map/ppermute | solution.py:550
  78.2 18.7 %collective-permute-start.8 = (bf16[3600,128]{1,0:T(8,128)(2,1)S(1)}, bf16[3600,128]{1,0:T(8,128)(2,1)S(1)}, u32[]{:S(2)}, u32[]{:S(2)}) collective-permute-start(bf16[3600,128]{1,0:T(8,128)(2,1)S(1)} %add.93.refs_21_), channel_id=1, source_target_pairs={{0,4},{4,0},{8,12},{12,8},{16,20},{20,16},{24,28},{28,24},{1,5},{5... | collective-permute-start | bytes 2764808 | tf_op jit(solution)/shard_map/ppermute | solution.py:550
  123.4 12.8 %collective-permute-start.9 = (bf16[1200,128]{1,0:T(8,128)(2,1)}, bf16[1200,128]{1,0:T(8,128)(2,1)S(1)}, u32[]{:S(2)}, u32[]{:S(2)}) collective-permute-start(bf16[1200,128]{1,0:T(8,128)(2,1)} %class_sums.6), channel_id=1, source_target_pairs={{0,4},{4,0},{8,12},{12,8},{16,20},{20,16},{24,28},{28,24},{1,5},{5... | collective-permute-start | bytes 921608 | tf_op jit(solution)/shard_map/ppermute | solution.py:550
  127.2 19.8 %collective-permute-start.10 = (bf16[2400,128]{1,0:T(8,128)(2,1)}, bf16[2400,128]{1,0:T(8,128)(2,1)S(1)}, u32[]{:S(2)}, u32[]{:S(2)}) collective-permute-start(bf16[2400,128]{1,0:T(8,128)(2,1)} %class_sums.7), channel_id=1, source_target_pairs={{0,4},{4,0},{8,12},{12,8},{16,20},{20,16},{24,28},{28,24},{1,5},{5... | collective-permute-start | bytes 1843208 | tf_op jit(solution)/shard_map/ppermute | solution.py:550
  135.8 31.0 %collective-permute-start.12 = (bf16[3600,128]{1,0:T(8,128)(2,1)}, bf16[3600,128]{1,0:T(8,128)(2,1)S(1)}, u32[]{:S(2)}, u32[]{:S(2)}) collective-permute-start(bf16[3600,128]{1,0:T(8,128)(2,1)} %get-tuple-element.82), channel_id=1, source_target_pairs={{0,4},{4,0},{8,12},{12,8},{16,20},{20,16},{24,28},{28,24},{1,5},{5... | collective-permute-start | bytes 2764808 | tf_op jit(solution)/shard_map/ppermute | solution.py:550
  137.5 11.7 %collective-permute-start.11 = (bf16[1200,128]{1,0:T(8,128)(2,1)S(1)}, bf16[1200,128]{1,0:T(8,128)(2,1)S(1)}, u32[]{:S(2)}, u32[]{:S(2)}) collective-permute-start(bf16[1200,128]{1,0:T(8,128)(2,1)S(1)} %fusion.2), channel_id=1, source_target_pairs={{0,8},{4,12},{24,16},{28,20},{1,9},{5,13},{25,17},{29,21},{2,10},{... | collective-permute-start | bytes 921608 | tf_op jit(solution)/shard_map/ppermute | solution.py:554
  138.8 8.1 %copy-start.3 = (f32[3600,128]{1,0:T(8,128)S(1)}, f32[3600,128]{1,0:T(8,128)}, u32[]{:S(2)}) copy-start(f32[3600,128]{1,0:T(8,128)} %get-tuple-element.75) | copy-start | bytes 5529604
  147.9 18.8 %collective-permute-start.13 = (bf16[2400,128]{1,0:T(8,128)(2,1)}, bf16[2400,128]{1,0:T(8,128)(2,1)}, u32[]{:S(2)}, u32[]{:S(2)}) collective-permute-start(bf16[2400,128]{1,0:T(8,128)(2,1)} %fusion.1), channel_id=1, source_target_pairs={{0,8},{4,12},{24,16},{28,20},{1,9},{5,13},{25,17},{29,21},{2,10},{... | collective-permute-start | bytes 1843208 | tf_op jit(solution)/shard_map/ppermute | solution.py:554
  150.1 10.5 %collective-permute-start.14 = (bf16[1200,128]{1,0:T(8,128)(2,1)}, bf16[1200,128]{1,0:T(8,128)(2,1)}, u32[]{:S(2)}, u32[]{:S(2)}) collective-permute-start(bf16[1200,128]{1,0:T(8,128)(2,1)} %add_convert_fusion.3), channel_id=1, source_target_pairs={{8,16},{12,20},{16,8},{20,12},{9,17},{13,21},{17,9},{21,13},{10,18... | collective-permute-start | bytes 921608 | tf_op jit(solution)/shard_map/ppermute | solution.py:554
  152.9 33.7 %collective-permute-start.17 = (bf16[3600,128]{1,0:T(8,128)(2,1)}, bf16[3600,128]{1,0:T(8,128)(2,1)}, u32[]{:S(2)}, u32[]{:S(2)}) collective-permute-start(bf16[3600,128]{1,0:T(8,128)(2,1)} %get-tuple-element.90), channel_id=1, source_target_pairs={{0,4},{4,0},{8,12},{12,8},{16,20},{20,16},{24,28},{28,24},{1,5},{5... | collective-permute-start | bytes 2764808 | tf_op jit(solution)/shard_map/ppermute | solution.py:550
  153.5 13.2 %copy-start.2 = (f32[3600,128]{1,0:T(8,128)S(1)}, f32[3600,128]{1,0:T(8,128)}, u32[]{:S(2)}) copy-start(f32[3600,128]{1,0:T(8,128)} %get-tuple-element.85) | copy-start | bytes 5529604
  166.9 22.1 %collective-permute-start.16 = (bf16[3600,128]{1,0:T(8,128)(2,1)S(1)}, bf16[3600,128]{1,0:T(8,128)(2,1)S(1)}, u32[]{:S(2)}, u32[]{:S(2)}) collective-permute-start(bf16[3600,128]{1,0:T(8,128)(2,1)S(1)} %fusion), channel_id=1, source_target_pairs={{0,8},{4,12},{24,16},{28,20},{1,9},{5,13},{25,17},{29,21},{2,10},{... | collective-permute-start | bytes 2764808 | tf_op jit(solution)/shard_map/ppermute | solution.py:554
  168.2 37.0 %collective-permute-start.15 = (bf16[3600,128]{1,0:T(8,128)(2,1)}, bf16[3600,128]{1,0:T(8,128)(2,1)}, u32[]{:S(2)}, u32[]{:S(2)}) collective-permute-start(bf16[3600,128]{1,0:T(8,128)(2,1)} %get-tuple-element.89), channel_id=1, source_target_pairs={{0,4},{4,0},{8,12},{12,8},{16,20},{20,16},{24,28},{28,24},{1,5},{5... | collective-permute-start | bytes 2764808 | tf_op jit(solution)/shard_map/ppermute | solution.py:550
  170.1 20.2 %copy-start.6 = (f32[3600,128]{1,0:T(8,128)S(1)}, f32[3600,128]{1,0:T(8,128)}, u32[]{:S(2)}) copy-start(f32[3600,128]{1,0:T(8,128)} %get-tuple-element.92) | copy-start | bytes 5529604
  170.1 20.2 %collective-permute-start.19 = (bf16[2400,128]{1,0:T(8,128)(2,1)S(1)}, bf16[2400,128]{1,0:T(8,128)(2,1)S(1)}, u32[]{:S(2)}, u32[]{:S(2)}) collective-permute-start(bf16[2400,128]{1,0:T(8,128)(2,1)S(1)} %add_convert_fusion.2), channel_id=1, source_target_pairs={{8,16},{12,20},{16,8},{20,12},{9,17},{13,21},{17,9},{21,13},{10,18... | collective-permute-start | bytes 1843208 | tf_op jit(solution)/shard_map/ppermute | solution.py:554
  190.3 4.4 %copy-start.14 = (f32[56,128]{1,0:T(8,128)S(1)}, f32[56,128]{1,0:T(8,128)}, u32[]{:S(2)}) copy-start(f32[56,128]{1,0:T(8,128)} %get-tuple-element.70) | copy-start | bytes 86020
  191.9 19.5 %collective-permute-start.20 = (bf16[3600,128]{1,0:T(8,128)(2,1)S(1)}, bf16[3600,128]{1,0:T(8,128)(2,1)S(1)}, u32[]{:S(2)}, u32[]{:S(2)}) collective-permute-start(bf16[3600,128]{1,0:T(8,128)(2,1)S(1)} %add_convert_fusion), channel_id=1, source_target_pairs={{0,8},{4,12},{8,0},{12,4},{16,24},{20,28},{24,16},{28,20},{1,9},{5... | collective-permute-start | bytes 2764808 | tf_op jit(solution)/shard_map/ppermute | solution.py:554
  192.0 21.5 %collective-permute-start.18 = (bf16[3600,128]{1,0:T(8,128)(2,1)}, bf16[3600,128]{1,0:T(8,128)(2,1)S(1)}, u32[]{:S(2)}, u32[]{:S(2)}) collective-permute-start(bf16[3600,128]{1,0:T(8,128)(2,1)} %add_convert_fusion.1), channel_id=1, source_target_pairs={{8,16},{12,20},{16,8},{20,12},{9,17},{13,21},{17,9},{21,13},{10,18... | collective-permute-start | bytes 2764808 | tf_op jit(solution)/shard_map/ppermute | solution.py:554
  196.6 20.2 %copy-start.1 = (f32[16,128]{1,0:T(8,128)S(1)}, f32[16,128]{1,0:T(8,128)}, u32[]{:S(2)}) copy-start(f32[16,128]{1,0:T(8,128)} %param.15) | copy-start | bytes 24580
  (5 other events, 8.7 us)

commit v11 on v10

--- a/solution.py
+++ b/solution.py
@@ -564,7 +564,8 @@
     near = along(piece, ((0, 1), (1, 0), (2, 3), (3, 2)))
     middle = along(piece, ((1, 2), (2, 1)))
     weighted = make_spectra(base, ctf_rows, cuts[0], cuts[1])
-    weighted, near, middle, own_crossed = lax.optimization_barrier((weighted, near, middle, own_crossed))
+    weighted, own_crossed = lax.optimization_barrier((weighted, own_crossed))
+    weighted, near, middle = lax.optimization_barrier((weighted, near, middle))
     near_crossed = across(near)
     far_middle = along(near, ((1, 2), (2, 1)))
     end = along(middle, ((1, 0), (2, 3)))
@@ -625,14 +626,13 @@
     message = (own_0[rest] + wide(crossed_rest)).astype(bf16)
     first_rest = along(message, to_middle)
     back = then(back, message)
+    first_head = then(first_head, message)
     message = (own_0[head] + wide(crossed_head) + wide(first_head)).astype(bf16)
     middle_head = along(message, between)
     back = then(back, message)
     own_2, away = sums([ours[2], theirs[3]], [f32, bf16], back)
     crossed_3 = across(away)
-    crossed_1, first_rest, middle_head, own_2 = lax.optimization_barrier(
-        (crossed_1, first_rest, middle_head, own_2)
-    )
+    crossed_1, middle_head, own_2 = lax.optimization_barrier((crossed_1, middle_head, own_2))
     message = (own_1 + wide(crossed_1)).astype(bf16)
     from_end = along(message, to_middle)
     first_rest = then(first_rest, message)

time: 218 us -> 217 us (level)
  starting transfers between devices: 30.5 us -> 35.9 us
  waiting for transfers between devices: 43.7 us -> 39 us
    ppermute x9, waiting for transfers between devices: 28.7 us -> 23.2 us  [across(): return lax.ppermute(piece, 'dp', [(d, d ^ 1) for d in range(8)])]
    ppermute x9, starting transfers between devices: 8.01 us -> 11.1 us  [across(): return lax.ppermute(piece, 'dp', [(d, d ^ 1) for d in range(8)])]
    ppermute x12, starting transfers between devices: 22.5 us -> 24.8 us  [along(): lax.ppermute(piece, 'dp', [(2 * a + x, 2 * b + x) for a, b in pairs for x...]
  transfers between devices with their start and end apart: 21 -> 21, of which waited for: 12 -> 11; matrix products, arithmetic and copies ran while one was open for 5% -> 4% of each run, Pallas kernels for 45% -> 45%
where the time goes in v11:
time: 217 us; the launch traced here: 216 us
  Pallas kernels  120 us (55%)
  waiting for transfers between devices  39 us (18%)
  starting transfers between devices  35.9 us (17%)
  other arithmetic  10.3 us (5%)
  blocking collectives  6.23 us (3%)
  local copies, waits for them, and re-layouts  2.86 us (1%)
    pallas_call x3, Pallas kernels, make_spectra(): pl.pallas_call(functools.partial(spectra_kernel, per_step=per_step), grid...  46.4 us
    pallas_call x6, Pallas kernels, class_sums_of(): pl.pallas_call(functools.partial(sums_kernel, count=count, classes=classe...  32.4 us
    pallas_call x2, Pallas kernels, correlate(): pl.pallas_call(functools.partial(correlate_kernel, slots=slots, classes=c...  28.4 us
    ppermute x12, starting transfers between devices, along(): lax.ppermute(piece, 'dp', [(2 * a + x, 2 * b + x) for a, b in pairs for x...  24.8 us
    ppermute x9, waiting for transfers between devices, across(): return lax.ppermute(piece, 'dp', [(d, d ^ 1) for d in range(8)])  23.2 us
    ppermute x12, waiting for transfers between devices, along(): lax.ppermute(piece, 'dp', [(2 * a + x, 2 * b + x) for a, b in pairs for x...  15.8 us
    ppermute x9, starting transfers between devices, across(): return lax.ppermute(piece, 'dp', [(d, d ^ 1) for d in range(8)])  11.1 us
    psum x1, blocking collectives, local(): shares = lax.psum(share, 'cls')  6.23 us
  transfers between devices with their start and end apart: 21, of which 11 were waited for; matrix products, arithmetic and copies ran while one was open for 4% of the time, Pallas kernels for 45%

profile of v11, /device:TPU:8, one launch (start us, length us, event | category | flops | bytes accessed | tf_op | source)
XLA Modules:
  0.0 216.2 jit_solution(12354235728299011489)
XLA Ops:
  0.7 3.0 %turn_references.1 = (bf16[3600,128]{1,0:T(8,128)(2,1)}, f32[56,128]{1,0:T(8,128)}) custom-call(s32[1]{0:T(128)} %bitcast.3.first_ref, s32[50]{0:T(128)} %offset_ref.1, bf16[3600,128]{1,0:T(8,128)(2,1)} %bitcast.45), custom_call_target="tpu_custom_call" | custom-call | tf_op jit(solution)/shard_map/turn_references/pallas_call | solution.py:251
  5.6 4.6 %collective-permute-start.2 = (bf16[3600,128]{1,0:T(8,128)(2,1)}, bf16[3600,128]{1,0:T(8,128)(2,1)S(1)}, u32[]{:S(2)}, u32[]{:S(2)}) collective-permute-start(bf16[3600,128]{1,0:T(8,128)(2,1)} %get-tuple-element.50.refs_15_), channel_id=1, source_target_pairs={{8,16},{12,20},{16,8},{20,12},{9,17},{13,21},{17,9},{21,13},{10,18... | collective-permute-start | bytes 2764808 | tf_op jit(solution)/shard_map/ppermute | solution.py:554
  10.2 4.6 %centre.1.base_ref = f32[8,2,288,128]{3,2,1,0:T(8,128)} custom-call(s32[2,8]{1,0:T(2,128)} %bitcast.46, bf16[8,2,288,128]{3,2,1,0:T(8,128)(2,1)} %part_ref.1, f32[2,288,128]{2,1,0:T(8,128)} %constant.49.clone.turns_ref), custom_call_target="tpu_custom_call" | custom-call | tf_op jit(solution)/shard_map/centre/pallas_call | solution.py:87
  15.6 11.9 %spectra.3.refs_4_ = bf16[288,208,256]{2,1,0:T(8,128)(2,1)} custom-call(f32[8,2,288,128]{3,2,1,0:T(8,128)} %centre.1.base_ref, f32[8,128]{1,0:T(8,128)} %fusion.3.ctf_ref.refs_6_, bf16[576,576]{1,0:T(8,128)(2,1)} %constant.50.clone.table_ref, f32[2,5,2,288,128]{4,3,2,1,0:T(8,128)} %constant.51.clone.refs_0_.refs_1_.refs_2_.refs_3_, ...), custom_call_target="tpu_custom_call" | custom-call | tf_op jit(solution)/shard_map/spectra/pallas_call | solution.py:171
  27.5 2.7 %collective-permute-done.2 = bf16[3600,128]{1,0:T(8,128)(2,1)S(1)} collective-permute-done((bf16[3600,128]{1,0:T(8,128)(2,1)}, bf16[3600,128]{1,0:T(8,128)(2,1)S(1)}, u32[]{:S(2)}, u32[]{:S(2)}) %collective-permute-start.2) | collective-permute-done | bytes 921632 | tf_op jit(solution)/shard_map/ppermute | solution.py:554
  32.2 3.6 %collective-permute-start.5 = (bf16[3600,128]{1,0:T(8,128)(2,1)S(1)}, bf16[3600,128]{1,0:T(8,128)(2,1)S(1)}, u32[]{:S(2)}, u32[]{:S(2)}) collective-permute-start(bf16[3600,128]{1,0:T(8,128)(2,1)S(1)} %collective-permute-done.1.refs_17_), channel_id=1, source_target_pairs={{8,16},{12,20},{16,8},{20,12},{9,17},{13,21},{17,9},{21,13},{10,18... | collective-permute-start | bytes 2764808 | tf_op jit(solution)/shard_map/ppermute | solution.py:554
  35.8 17.3 %spectra.4.refs_4_ = bf16[288,208,256]{2,1,0:T(8,128)(2,1)} custom-call(f32[8,2,288,128]{3,2,1,0:T(8,128)} %centre.1.base_ref, f32[8,128]{1,0:T(8,128)} %fusion.3.ctf_ref.refs_6_, bf16[576,576]{1,0:T(8,128)(2,1)} %constant.50.clone.table_ref, f32[2,5,2,288,128]{4,3,2,1,0:T(8,128)} %constant.51.clone.refs_0_.refs_1_.refs_2_.refs_3_, ...), custom_call_target="tpu_custom_call", output_to_operand_aliasing={{}: (7, {})} | custom-call | tf_op jit(solution)/shard_map/spectra/pallas_call | solution.py:171
  53.1 1.7 collective-permute-done.5
  56.6 1.6 collective-permute-start.7
  58.1 17.2 %spectra.5 = bf16[288,208,256]{2,1,0:T(8,128)(2,1)} custom-call(f32[8,2,288,128]{3,2,1,0:T(8,128)} %centre.1.base_ref, f32[8,128]{1,0:T(8,128)} %fusion.3.ctf_ref.refs_6_, bf16[576,576]{1,0:T(8,128)(2,1)} %constant.50.clone.table_ref, f32[2,5,2,288,128]{4,3,2,1,0:T(8,128)} %constant.51.clone.refs_0_.refs_1_.refs_2_.refs_3_, ...), custom_call_target="tpu_custom_call", output_to_operand_aliasing={{}: (7, {})} | custom-call | tf_op jit(solution)/shard_map/spectra/pallas_call | solution.py:171
  77.2 1.6 collective-permute-start.8
  78.7 17.1 %correlate.1 = (f32[36,112,256]{2,1,0:T(8,128)}, f32[56,128]{1,0:T(8,128)}) custom-call(s32[1]{0:T(128)} %bitcast.7.refs_0_, s32[1]{0:T(128)} %bitcast.8.refs_1_, s32[1]{0:T(128)} %bitcast.9.refs_2_.refs_0_, s32[1]{0:T(128)} %bitcast.10.refs_3_, s32[1]{0:T(128)} %bitcast.11.refs_4_.refs_0_, s32[1]{0:T(128)} %bitcast.12.refs_5_, s32[1]{0:T(128)} %bitcast.13.refs_6_.refs_0_, ...), custom_call_target="tpu_custom_call" | custom-call | tf_op jit(solution)/shard_map/correlate/pallas_call | solution.py:417
  97.1 11.3 %scores.1 = (f32[36,56,256]{2,1,0:T(8,128)}, f32[64,128]{1,0:T(8,128)}, f32[4,2,128]{2,1,0:T(2,128)}) custom-call(s32[1]{0:T(128)} %bitcast.refs_0_, s32[1]{0:T(128)} %bitcast.1.refs_7_.refs_1_, bf16[8,36,208,256]{3,2,1,0:T(8,128)(2,1)} %bitcast.34, bf16[3600,128]{1,0:T(8,128)(2,1)} %copy-done.13, f32[36,112,256]{2,1,0:T(8,128)} %get-tuple-element.65.refs_4_, ...), custom_call_target="tpu_custom_call" | custom-call | tf_op jit(solution)/shard_map/scores/pallas_call | solution.py:417
  108.4 6.2 %psum.7.share_ref = f32[4,2,128]{2,1,0:T(2,128)} all-reduce(f32[4,2,128]{2,1,0:T(2,128)} %get-tuple-element.69), channel_id=1, replica_groups=mesh['dp'=8,'cls'=4] {'cls'}, use_global_device_ids=true, to_apply=%region_0.1 | all-reduce | flops 1024 | bytes 8192 | tf_op jit(solution)/shard_map/psum | solution.py:684
  114.7 5.4 %back.1 = (bf16[36,112,208]{2,1,0:T(8,128)(2,1)}, f32[8,128]{1,0:T(8,128)}, f32[56,128]{1,0:T(8,128)}) custom-call(f32[36,56,256]{2,1,0:T(8,128)} %get-tuple-element.67.weight_ref, f32[64,128]{1,0:T(8,128)} %get-tuple-element.68.stat_ref, f32[4,2,128]{2,1,0:T(2,128)} %psum.7.share_ref, f32[56,128]{1,0:T(8,128)} %get-tuple-element.70.offset_ref.refs_3_.refs_5_), custom_call_target="tpu_custom_call" | custom-call | tf_op jit(solution)/shard_map/back/pallas_call | solution.py:483
  120.1 2.6 %class_sums.6 = bf16[1200,128]{1,0:T(8,128)(2,1)} custom-call(s32[1]{0:T(128)} %bitcast.16.refs_0_, bf16[36,112,208]{2,1,0:T(8,128)(2,1)} %get-tuple-element.90.refs_1_.refs_2_, bf16[8,36,208,256]{3,2,1,0:T(8,128)(2,1)} %bitcast.35, f32[56,128]{1,0:T(8,128)} %get-tuple-element.70.offset_ref.refs_3_.refs_5_), custom_call_target="tpu_custom_call" | custom-call | tf_op jit(solution)/shard_map/class_sums/pallas_call | solution.py:526
  124.2 3.2 %class_sums.7 = bf16[2400,128]{1,0:T(8,128)(2,1)} custom-call(s32[1]{0:T(128)} %bitcast.16.refs_0_, bf16[36,112,208]{2,1,0:T(8,128)(2,1)} %get-tuple-element.90.refs_1_.refs_2_, bf16[8,36,208,256]{3,2,1,0:T(8,128)(2,1)} %bitcast.36, f32[56,128]{1,0:T(8,128)} %get-tuple-element.70.offset_ref.refs_3_.refs_5_), custom_call_target="tpu_custom_call" | custom-call | tf_op jit(solution)/shard_map/class_sums/pallas_call | solution.py:526
  128.0 7.0 %class_sums.8 = (f32[3600,128]{1,0:T(8,128)}, bf16[3600,128]{1,0:T(8,128)(2,1)}) custom-call(s32[1]{0:T(128)} %bitcast.13.refs_6_.refs_0_, s32[1]{0:T(128)} %bitcast.17.refs_1_, bf16[36,112,208]{2,1,0:T(8,128)(2,1)} %get-tuple-element.90.refs_1_.refs_2_, bf16[8,36,208,256]{3,2,1,0:T(8,128)(2,1)} %bitcast.37, bf16[8,36,208,256]{3,2,1,0:T(8,128)(2,1)} %bitcast.38, ...), custom_call_target="tpu_custom_call" | custom-call | tf_op jit(solution)/shard_map/class_sums/pallas_call | solution.py:526
  139.1 7.2 %class_sums.9 = (f32[3600,128]{1,0:T(8,128)}, bf16[3600,128]{1,0:T(8,128)(2,1)}) custom-call(s32[1]{0:T(128)} %bitcast.11.refs_4_.refs_0_, s32[1]{0:T(128)} %bitcast.18.refs_1_, bf16[36,112,208]{2,1,0:T(8,128)(2,1)} %get-tuple-element.90.refs_1_.refs_2_, bf16[8,36,208,256]{3,2,1,0:T(8,128)(2,1)} %bitcast.39, bf16[8,36,208,256]{3,2,1,0:T(8,128)(2,1)} %bitcast.40, ...), custom_call_target="tpu_custom_call" | custom-call | tf_op jit(solution)/shard_map/class_sums/pallas_call | solution.py:526
  148.7 3.1 %collective-permute-start.14 = (bf16[1200,128]{1,0:T(8,128)(2,1)}, bf16[1200,128]{1,0:T(8,128)(2,1)}, u32[]{:S(2)}, u32[]{:S(2)}) collective-permute-start(bf16[1200,128]{1,0:T(8,128)(2,1)} %add_convert_fusion.3), channel_id=1, source_target_pairs={{8,16},{12,20},{16,8},{20,12},{9,17},{13,21},{17,9},{21,13},{10,18... | collective-permute-start | bytes 921608 | tf_op jit(solution)/shard_map/ppermute | solution.py:554
  154.0 7.1 %class_sums.10 = (f32[3600,128]{1,0:T(8,128)}, bf16[3600,128]{1,0:T(8,128)(2,1)}) custom-call(s32[1]{0:T(128)} %bitcast.9.refs_2_.refs_0_, s32[1]{0:T(128)} %bitcast.19.refs_1_, bf16[36,112,208]{2,1,0:T(8,128)(2,1)} %get-tuple-element.90.refs_1_.refs_2_, bf16[8,36,208,256]{3,2,1,0:T(8,128)(2,1)} %bitcast.41, bf16[8,36,208,256]{3,2,1,0:T(8,128)(2,1)} %bitcast.42, ...), custom_call_target="tpu_custom_call" | custom-call | tf_op jit(solution)/shard_map/class_sums/pallas_call | solution.py:526
  161.2 4.9 %collective-permute-done.13 = bf16[3600,128]{1,0:T(8,128)(2,1)S(1)} collective-permute-done((bf16[3600,128]{1,0:T(8,128)(2,1)}, bf16[3600,128]{1,0:T(8,128)(2,1)S(1)}, u32[]{:S(2)}, u32[]{:S(2)}) %collective-permute-start.13) | collective-permute-done | bytes 921632 | tf_op jit(solution)/shard_map/ppermute | solution.py:550
  167.5 1.6 collective-permute-start.15
  169.3 3.2 %collective-permute-start.19 = (bf16[2400,128]{1,0:T(8,128)(2,1)S(1)}, bf16[2400,128]{1,0:T(8,128)(2,1)S(1)}, u32[]{:S(2)}, u32[]{:S(2)}) collective-permute-start(bf16[2400,128]{1,0:T(8,128)(2,1)S(1)} %add_convert_fusion.2), channel_id=1, source_target_pairs={{8,16},{12,20},{16,8},{20,12},{9,17},{13,21},{17,9},{21,13},{10,18... | collective-permute-start | bytes 1843208 | tf_op jit(solution)/shard_map/ppermute | solution.py:554
  172.5 13.3 %collective-permute-done.17 = bf16[3600,128]{1,0:T(8,128)(2,1)} collective-permute-done((bf16[3600,128]{1,0:T(8,128)(2,1)}, bf16[3600,128]{1,0:T(8,128)(2,1)}, u32[]{:S(2)}, u32[]{:S(2)}) %collective-permute-start.17) | collective-permute-done | bytes 921632 | tf_op jit(solution)/shard_map/ppermute | solution.py:550
  185.9 2.5 %collective-permute-done.16 = bf16[3600,128]{1,0:T(8,128)(2,1)S(1)} collective-permute-done((bf16[3600,128]{1,0:T(8,128)(2,1)S(1)}, bf16[3600,128]{1,0:T(8,128)(2,1)S(1)}, u32[]{:S(2)}, u32[]{:S(2)}) %collective-permute-start.16) | collective-permute-done | bytes 921632 | tf_op jit(solution)/shard_map/ppermute | solution.py:554
  191.3 3.1 %collective-permute-start.18 = (bf16[3600,128]{1,0:T(8,128)(2,1)}, bf16[3600,128]{1,0:T(8,128)(2,1)S(1)}, u32[]{:S(2)}, u32[]{:S(2)}) collective-permute-start(bf16[3600,128]{1,0:T(8,128)(2,1)} %add_convert_fusion.1), channel_id=1, source_target_pairs={{8,16},{12,20},{16,8},{20,12},{9,17},{13,21},{17,9},{21,13},{10,18... | collective-permute-start | bytes 2764808 | tf_op jit(solution)/shard_map/ppermute | solution.py:554
  196.2 5.2 %class_sums.11 = f32[3600,128]{1,0:T(8,128)} custom-call(s32[1]{0:T(128)} %bitcast.7.refs_0_, bf16[36,112,208]{2,1,0:T(8,128)(2,1)} %get-tuple-element.90.refs_1_.refs_2_, bf16[8,36,208,256]{3,2,1,0:T(8,128)(2,1)} %bitcast.43, f32[56,128]{1,0:T(8,128)} %get-tuple-element.70.offset_ref.refs_3_.refs_5_), custom_call_target="tpu_custom_call" | custom-call | tf_op jit(solution)/shard_map/class_sums/pallas_call | solution.py:526
  201.4 3.1 %collective-permute-done.15 = bf16[3600,128]{1,0:T(8,128)(2,1)} collective-permute-done((bf16[3600,128]{1,0:T(8,128)(2,1)}, bf16[3600,128]{1,0:T(8,128)(2,1)}, u32[]{:S(2)}, u32[]{:S(2)}) %collective-permute-start.15) | collective-permute-done | bytes 921632 | tf_op jit(solution)/shard_map/ppermute | solution.py:550
  204.5 6.2 %collective-permute-done.20 = bf16[3600,128]{1,0:T(8,128)(2,1)S(1)} collective-permute-done((bf16[3600,128]{1,0:T(8,128)(2,1)S(1)}, bf16[3600,128]{1,0:T(8,128)(2,1)S(1)}, u32[]{:S(2)}, u32[]{:S(2)}) %collective-permute-start.20) | collective-permute-done | bytes 921632 | tf_op jit(solution)/shard_map/ppermute | solution.py:554
  210.7 2.1 collective-permute-done.18
  212.8 3.4 %convert_add_fusion = f32[3600,128]{1,0:T(8,128)} fusion(bf16[3600,128]{1,0:T(8,128)(2,1)S(1)} %collective-permute-done.20, bf16[3600,128]{1,0:T(8,128)(2,1)S(1)} %collective-permute-done.18, f32[3600,128]{1,0:T(8,128)} %class_sums.11, bf16[3600,128]{1,0:T(8,128)(2,1)} %collective-permute-done.15), kind=kLoop, calls=%fused_computation | loop fusion | flops 2764800 | bytes 6451200 | tf_op jit(solution)/shard_map/add | solution.py:649
  (71 shorter events, 26.8 us)
Async XLA Ops:
  0.6 14.2 %copy-start = (f32[16,128]{1,0:T(8,128)S(1)}, f32[16,128]{1,0:T(8,128)}, u32[]{:S(2)}) copy-start(f32[16,128]{1,0:T(8,128)} %param.15) | copy-start | bytes 24580
  3.6 23.9 %collective-permute-start = (bf16[3600,128]{1,0:T(8,128)(2,1)}, bf16[3600,128]{1,0:T(8,128)(2,1)S(1)}, u32[]{:S(2)}, u32[]{:S(2)}) collective-permute-start(bf16[3600,128]{1,0:T(8,128)(2,1)} %get-tuple-element.50.refs_15_), channel_id=1, source_target_pairs={{0,4},{4,0},{8,12},{12,8},{16,20},{20,16},{24,28},{28,24},{1,5},{5... | collective-permute-start | bytes 2764808 | tf_op jit(solution)/shard_map/ppermute | solution.py:550
  5.1 22.4 %collective-permute-start.1 = (bf16[3600,128]{1,0:T(8,128)(2,1)}, bf16[3600,128]{1,0:T(8,128)(2,1)S(1)}, u32[]{:S(2)}, u32[]{:S(2)}) collective-permute-start(bf16[3600,128]{1,0:T(8,128)(2,1)} %get-tuple-element.50.refs_15_), channel_id=1, source_target_pairs={{0,8},{4,12},{8,0},{12,4},{16,24},{20,28},{24,16},{28,20},{1,9},{5... | collective-permute-start | bytes 2764808 | tf_op jit(solution)/shard_map/ppermute | solution.py:554
  5.6 24.7 %collective-permute-start.2 = (bf16[3600,128]{1,0:T(8,128)(2,1)}, bf16[3600,128]{1,0:T(8,128)(2,1)S(1)}, u32[]{:S(2)}, u32[]{:S(2)}) collective-permute-start(bf16[3600,128]{1,0:T(8,128)(2,1)} %get-tuple-element.50.refs_15_), channel_id=1, source_target_pairs={{8,16},{12,20},{16,8},{20,12},{9,17},{13,21},{17,9},{21,13},{10,18... | collective-permute-start | bytes 2764808 | tf_op jit(solution)/shard_map/ppermute | solution.py:554
  10.2 4.7 %copy-start.15 = (s32[8]{0:T(128)S(1)}, s32[8]{0:T(128)}, u32[]{:S(2)}) copy-start(s32[8]{0:T(128)} %param.18) | copy-start | bytes 100
  27.5 25.6 %copy-start.9 = (bf16[3600,128]{1,0:T(8,128)(2,1)}, bf16[3600,128]{1,0:T(8,128)(2,1)S(1)}, u32[]{:S(2)}) copy-start(bf16[3600,128]{1,0:T(8,128)(2,1)S(1)} %collective-permute-done.refs_16_) | copy-start | bytes 2764804
  27.5 25.6 %copy-start.10 = (bf16[3600,128]{1,0:T(8,128)(2,1)}, bf16[3600,128]{1,0:T(8,128)(2,1)S(1)}, u32[]{:S(2)}) copy-start(bf16[3600,128]{1,0:T(8,128)(2,1)S(1)} %collective-permute-done.1.refs_17_) | copy-start | bytes 2764804
  30.3 22.8 %collective-permute-start.3 = (bf16[3600,128]{1,0:T(8,128)(2,1)S(1)}, bf16[3600,128]{1,0:T(8,128)(2,1)S(1)}, u32[]{:S(2)}, u32[]{:S(2)}) collective-permute-start(bf16[3600,128]{1,0:T(8,128)(2,1)S(1)} %collective-permute-done.2), channel_id=1, source_target_pairs={{8,0},{12,4},{16,24},{20,28},{9,1},{13,5},{17,25},{21,29},{10,2},{... | collective-permute-start | bytes 2764808 | tf_op jit(solution)/shard_map/ppermute | solution.py:554
  31.6 21.5 %collective-permute-start.4 = (bf16[3600,128]{1,0:T(8,128)(2,1)S(1)}, bf16[3600,128]{1,0:T(8,128)(2,1)S(1)}, u32[]{:S(2)}, u32[]{:S(2)}) collective-permute-start(bf16[3600,128]{1,0:T(8,128)(2,1)S(1)} %collective-permute-done.1.refs_17_), channel_id=1, source_target_pairs={{0,4},{4,0},{8,12},{12,8},{16,20},{20,16},{24,28},{28,24},{1,5},{5... | collective-permute-start | bytes 2764808 | tf_op jit(solution)/shard_map/ppermute | solution.py:550
  32.2 22.6 %collective-permute-start.5 = (bf16[3600,128]{1,0:T(8,128)(2,1)S(1)}, bf16[3600,128]{1,0:T(8,128)(2,1)S(1)}, u32[]{:S(2)}, u32[]{:S(2)}) collective-permute-start(bf16[3600,128]{1,0:T(8,128)(2,1)S(1)} %collective-permute-done.1.refs_17_), channel_id=1, source_target_pairs={{8,16},{12,20},{16,8},{20,12},{9,17},{13,21},{17,9},{21,13},{10,18... | collective-permute-start | bytes 2764808 | tf_op jit(solution)/shard_map/ppermute | solution.py:554
  53.1 22.3 %copy-start.11 = (bf16[3600,128]{1,0:T(8,128)(2,1)}, bf16[3600,128]{1,0:T(8,128)(2,1)S(1)}, u32[]{:S(2)}) copy-start(bf16[3600,128]{1,0:T(8,128)(2,1)S(1)} %collective-permute-done.4.refs_18_) | copy-start | bytes 2764804
  54.8 20.6 %collective-permute-start.6 = (bf16[3600,128]{1,0:T(8,128)(2,1)S(1)}, bf16[3600,128]{1,0:T(8,128)(2,1)S(1)}, u32[]{:S(2)}, u32[]{:S(2)}) collective-permute-start(bf16[3600,128]{1,0:T(8,128)(2,1)S(1)} %collective-permute-done.5), channel_id=1, source_target_pairs={{8,0},{12,4},{16,24},{20,28},{9,1},{13,5},{17,25},{21,29},{10,2},{... | collective-permute-start | bytes 2764808 | tf_op jit(solution)/shard_map/ppermute | solution.py:554
  56.6 18.8 %copy-start.4 = (bf16[3600,128]{1,0:T(8,128)(2,1)}, bf16[3600,128]{1,0:T(8,128)(2,1)S(1)}, u32[]{:S(2)}) copy-start(bf16[3600,128]{1,0:T(8,128)(2,1)S(1)} %add.92.refs_19_) | copy-start | bytes 2764804
  56.6 20.3 %collective-permute-start.7 = (bf16[3600,128]{1,0:T(8,128)(2,1)S(1)}, bf16[3600,128]{1,0:T(8,128)(2,1)S(1)}, u32[]{:S(2)}, u32[]{:S(2)}) collective-permute-start(bf16[3600,128]{1,0:T(8,128)(2,1)S(1)} %add.92.refs_19_), channel_id=1, source_target_pairs={{0,4},{4,0},{8,12},{12,8},{16,20},{20,16},{24,28},{28,24},{1,5},{5... | collective-permute-start | bytes 2764808 | tf_op jit(solution)/shard_map/ppermute | solution.py:550
  77.2 19.0 %collective-permute-start.8 = (bf16[3600,128]{1,0:T(8,128)(2,1)S(1)}, bf16[3600,128]{1,0:T(8,128)(2,1)S(1)}, u32[]{:S(2)}, u32[]{:S(2)}) collective-permute-start(bf16[3600,128]{1,0:T(8,128)(2,1)S(1)} %add.93.refs_21_), channel_id=1, source_target_pairs={{0,4},{4,0},{8,12},{12,8},{16,20},{20,16},{24,28},{28,24},{1,5},{5... | collective-permute-start | bytes 2764808 | tf_op jit(solution)/shard_map/ppermute | solution.py:550
  122.7 13.8 %collective-permute-start.9 = (bf16[1200,128]{1,0:T(8,128)(2,1)}, bf16[1200,128]{1,0:T(8,128)(2,1)S(1)}, u32[]{:S(2)}, u32[]{:S(2)}) collective-permute-start(bf16[1200,128]{1,0:T(8,128)(2,1)} %class_sums.6), channel_id=1, source_target_pairs={{0,4},{4,0},{8,12},{12,8},{16,20},{20,16},{24,28},{28,24},{1,5},{5... | collective-permute-start | bytes 921608 | tf_op jit(solution)/shard_map/ppermute | solution.py:550
  127.5 18.8 %collective-permute-start.10 = (bf16[2400,128]{1,0:T(8,128)(2,1)}, bf16[2400,128]{1,0:T(8,128)(2,1)S(1)}, u32[]{:S(2)}, u32[]{:S(2)}) collective-permute-start(bf16[2400,128]{1,0:T(8,128)(2,1)} %class_sums.7), channel_id=1, source_target_pairs={{0,4},{4,0},{8,12},{12,8},{16,20},{20,16},{24,28},{28,24},{1,5},{5... | collective-permute-start | bytes 1843208 | tf_op jit(solution)/shard_map/ppermute | solution.py:550
  135.0 31.0 %collective-permute-start.13 = (bf16[3600,128]{1,0:T(8,128)(2,1)}, bf16[3600,128]{1,0:T(8,128)(2,1)S(1)}, u32[]{:S(2)}, u32[]{:S(2)}) collective-permute-start(bf16[3600,128]{1,0:T(8,128)(2,1)} %get-tuple-element.86), channel_id=1, source_target_pairs={{0,4},{4,0},{8,12},{12,8},{16,20},{20,16},{24,28},{28,24},{1,5},{5... | collective-permute-start | bytes 2764808 | tf_op jit(solution)/shard_map/ppermute | solution.py:550
  137.7 10.1 %collective-permute-start.11 = (bf16[1200,128]{1,0:T(8,128)(2,1)S(1)}, bf16[1200,128]{1,0:T(8,128)(2,1)S(1)}, u32[]{:S(2)}, u32[]{:S(2)}) collective-permute-start(bf16[1200,128]{1,0:T(8,128)(2,1)S(1)} %fusion.2), channel_id=1, source_target_pairs={{0,8},{4,12},{24,16},{28,20},{1,9},{5,13},{25,17},{29,21},{2,10},{... | collective-permute-start | bytes 921608 | tf_op jit(solution)/shard_map/ppermute | solution.py:554
  139.1 7.2 %copy-start.3 = (f32[3600,128]{1,0:T(8,128)S(1)}, f32[3600,128]{1,0:T(8,128)}, u32[]{:S(2)}) copy-start(f32[3600,128]{1,0:T(8,128)} %get-tuple-element.77) | copy-start | bytes 5529604
  148.7 12.5 %collective-permute-start.14 = (bf16[1200,128]{1,0:T(8,128)(2,1)}, bf16[1200,128]{1,0:T(8,128)(2,1)}, u32[]{:S(2)}, u32[]{:S(2)}) collective-permute-start(bf16[1200,128]{1,0:T(8,128)(2,1)} %add_convert_fusion.3), channel_id=1, source_target_pairs={{8,16},{12,20},{16,8},{20,12},{9,17},{13,21},{17,9},{21,13},{10,18... | collective-permute-start | bytes 921608 | tf_op jit(solution)/shard_map/ppermute | solution.py:554
  151.8 34.0 %collective-permute-start.17 = (bf16[3600,128]{1,0:T(8,128)(2,1)}, bf16[3600,128]{1,0:T(8,128)(2,1)}, u32[]{:S(2)}, u32[]{:S(2)}) collective-permute-start(bf16[3600,128]{1,0:T(8,128)(2,1)} %get-tuple-element.92), channel_id=1, source_target_pairs={{0,4},{4,0},{8,12},{12,8},{16,20},{20,16},{24,28},{28,24},{1,5},{5... | collective-permute-start | bytes 2764808 | tf_op jit(solution)/shard_map/ppermute | solution.py:550
  152.7 16.3 %collective-permute-start.12 = (bf16[2400,128]{1,0:T(8,128)(2,1)}, bf16[2400,128]{1,0:T(8,128)(2,1)S(1)}, u32[]{:S(2)}, u32[]{:S(2)}) collective-permute-start(bf16[2400,128]{1,0:T(8,128)(2,1)} %fusion.1), channel_id=1, source_target_pairs={{0,8},{4,12},{24,16},{28,20},{1,9},{5,13},{25,17},{29,21},{2,10},{... | collective-permute-start | bytes 1843208 | tf_op jit(solution)/shard_map/ppermute | solution.py:554
  154.0 12.0 %copy-start.2 = (f32[3600,128]{1,0:T(8,128)S(1)}, f32[3600,128]{1,0:T(8,128)}, u32[]{:S(2)}) copy-start(f32[3600,128]{1,0:T(8,128)} %get-tuple-element.85) | copy-start | bytes 5529604
  166.2 22.1 %collective-permute-start.16 = (bf16[3600,128]{1,0:T(8,128)(2,1)S(1)}, bf16[3600,128]{1,0:T(8,128)(2,1)S(1)}, u32[]{:S(2)}, u32[]{:S(2)}) collective-permute-start(bf16[3600,128]{1,0:T(8,128)(2,1)S(1)} %fusion), channel_id=1, source_target_pairs={{0,8},{4,12},{24,16},{28,20},{1,9},{5,13},{25,17},{29,21},{2,10},{... | collective-permute-start | bytes 2764808 | tf_op jit(solution)/shard_map/ppermute | solution.py:554
  167.5 37.0 %collective-permute-start.15 = (bf16[3600,128]{1,0:T(8,128)(2,1)}, bf16[3600,128]{1,0:T(8,128)(2,1)}, u32[]{:S(2)}, u32[]{:S(2)}) collective-permute-start(bf16[3600,128]{1,0:T(8,128)(2,1)} %get-tuple-element.91), channel_id=1, source_target_pairs={{0,4},{4,0},{8,12},{12,8},{16,20},{20,16},{24,28},{28,24},{1,5},{5... | collective-permute-start | bytes 2764808 | tf_op jit(solution)/shard_map/ppermute | solution.py:550
  169.3 20.3 %copy-start.6 = (f32[3600,128]{1,0:T(8,128)S(1)}, f32[3600,128]{1,0:T(8,128)}, u32[]{:S(2)}) copy-start(f32[3600,128]{1,0:T(8,128)} %get-tuple-element.94) | copy-start | bytes 5529604
  169.3 20.3 %collective-permute-start.19 = (bf16[2400,128]{1,0:T(8,128)(2,1)S(1)}, bf16[2400,128]{1,0:T(8,128)(2,1)S(1)}, u32[]{:S(2)}, u32[]{:S(2)}) collective-permute-start(bf16[2400,128]{1,0:T(8,128)(2,1)S(1)} %add_convert_fusion.2), channel_id=1, source_target_pairs={{8,16},{12,20},{16,8},{20,12},{9,17},{13,21},{17,9},{21,13},{10,18... | collective-permute-start | bytes 1843208 | tf_op jit(solution)/shard_map/ppermute | solution.py:554
  189.7 4.7 %copy-start.14 = (f32[56,128]{1,0:T(8,128)S(1)}, f32[56,128]{1,0:T(8,128)}, u32[]{:S(2)}) copy-start(f32[56,128]{1,0:T(8,128)} %get-tuple-element.72) | copy-start | bytes 86020
  191.2 19.5 %collective-permute-start.20 = (bf16[3600,128]{1,0:T(8,128)(2,1)S(1)}, bf16[3600,128]{1,0:T(8,128)(2,1)S(1)}, u32[]{:S(2)}, u32[]{:S(2)}) collective-permute-start(bf16[3600,128]{1,0:T(8,128)(2,1)S(1)} %add_convert_fusion), channel_id=1, source_target_pairs={{0,8},{4,12},{8,0},{12,4},{16,24},{20,28},{24,16},{28,20},{1,9},{5... | collective-permute-start | bytes 2764808 | tf_op jit(solution)/shard_map/ppermute | solution.py:554
  191.3 21.5 %collective-permute-start.18 = (bf16[3600,128]{1,0:T(8,128)(2,1)}, bf16[3600,128]{1,0:T(8,128)(2,1)S(1)}, u32[]{:S(2)}, u32[]{:S(2)}) collective-permute-start(bf16[3600,128]{1,0:T(8,128)(2,1)} %add_convert_fusion.1), channel_id=1, source_target_pairs={{8,16},{12,20},{16,8},{20,12},{9,17},{13,21},{17,9},{21,13},{10,18... | collective-permute-start | bytes 2764808 | tf_op jit(solution)/shard_map/ppermute | solution.py:554
  196.2 19.9 %copy-start.1 = (f32[16,128]{1,0:T(8,128)S(1)}, f32[16,128]{1,0:T(8,128)}, u32[]{:S(2)}) copy-start(f32[16,128]{1,0:T(8,128)} %param.15) | copy-start | bytes 24580
  (5 other events, 8.5 us)

commit v12 on v11

--- a/solution.py
+++ b/solution.py
@@ -564,8 +564,9 @@
     near = along(piece, ((0, 1), (1, 0), (2, 3), (3, 2)))
     middle = along(piece, ((1, 2), (2, 1)))
     weighted = make_spectra(base, ctf_rows, cuts[0], cuts[1])
+    weighted, middle = lax.optimization_barrier((weighted, middle))
     weighted, own_crossed = lax.optimization_barrier((weighted, own_crossed))
-    weighted, near, middle = lax.optimization_barrier((weighted, near, middle))
+    weighted, near = lax.optimization_barrier((weighted, near))
     near_crossed = across(near)
     far_middle = along(near, ((1, 2), (2, 1)))
     end = along(middle, ((1, 0), (2, 3)))
@@ -626,7 +627,6 @@
     message = (own_0[rest] + wide(crossed_rest)).astype(bf16)
     first_rest = along(message, to_middle)
     back = then(back, message)
-    first_head = then(first_head, message)
     message = (own_0[head] + wide(crossed_head) + wide(first_head)).astype(bf16)
     middle_head = along(message, between)
     back = then(back, message)

time: 217 us -> 222 us (1.023)
  waiting for transfers between devices: 39 us -> 47.2 us
    ppermute x9, waiting for transfers between devices: 23.2 us -> 33.5 us  [across(): return lax.ppermute(piece, 'dp', [(d, d ^ 1) for d in range(8)])]
  transfers between devices with their start and end apart: 21 -> 21, of which waited for: 11 -> 12; matrix products, arithmetic and copies ran while one was open for 4% -> 3% of each run, Pallas kernels for 45% -> 44%
where the time goes in v12:
time: 222 us; the launch traced here: 221 us
  Pallas kernels  120 us (54%)
  waiting for transfers between devices  47.2 us (21%)
  starting transfers between devices  34 us (15%)
  other arithmetic  9.01 us (4%)
  blocking collectives  6.22 us (3%)
  local copies, waits for them, and re-layouts  3.22 us (1%)
    pallas_call x3, Pallas kernels, make_spectra(): pl.pallas_call(functools.partial(spectra_kernel, per_step=per_step), grid...  46.3 us
    ppermute x9, waiting for transfers between devices, across(): return lax.ppermute(piece, 'dp', [(d, d ^ 1) for d in range(8)])  33.5 us
    pallas_call x6, Pallas kernels, class_sums_of(): pl.pallas_call(functools.partial(sums_kernel, count=count, classes=classe...  32.3 us
    pallas_call x2, Pallas kernels, correlate(): pl.pallas_call(functools.partial(correlate_kernel, slots=slots, classes=c...  28.4 us
    ppermute x12, starting transfers between devices, along(): lax.ppermute(piece, 'dp', [(2 * a + x, 2 * b + x) for a, b in pairs for x...  24.1 us
    ppermute x12, waiting for transfers between devices, along(): lax.ppermute(piece, 'dp', [(2 * a + x, 2 * b + x) for a, b in pairs for x...  13.6 us
    ppermute x9, starting transfers between devices, across(): return lax.ppermute(piece, 'dp', [(d, d ^ 1) for d in range(8)])  9.96 us
    psum x1, blocking collectives, local(): shares = lax.psum(share, 'cls')  6.22 us
  transfers between devices with their start and end apart: 21, of which 12 were waited for; matrix products, arithmetic and copies ran while one was open for 3% of the time, Pallas kernels for 44%

profile of v12, /device:TPU:8, one launch (start us, length us, event | category | flops | bytes accessed | tf_op | source)
XLA Modules:
  0.0 221.4 jit_solution(12479053727393156333)
XLA Ops:
  0.7 3.0 %turn_references.1 = (bf16[3600,128]{1,0:T(8,128)(2,1)}, f32[56,128]{1,0:T(8,128)}) custom-call(s32[1]{0:T(128)} %bitcast.3.first_ref, s32[50]{0:T(128)} %offset_ref.1, bf16[3600,128]{1,0:T(8,128)(2,1)} %bitcast.45), custom_call_target="tpu_custom_call" | custom-call | tf_op jit(solution)/shard_map/turn_references/pallas_call | solution.py:251
  3.6 3.5 %collective-permute-start = (bf16[3600,128]{1,0:T(8,128)(2,1)}, bf16[3600,128]{1,0:T(8,128)(2,1)S(1)}, u32[]{:S(2)}, u32[]{:S(2)}) collective-permute-start(bf16[3600,128]{1,0:T(8,128)(2,1)} %get-tuple-element.50.refs_15_), channel_id=1, source_target_pairs={{8,16},{12,20},{16,8},{20,12},{9,17},{13,21},{17,9},{21,13},{10,18... | collective-permute-start | bytes 2764808 | tf_op jit(solution)/shard_map/ppermute | solution.py:554
  7.1 1.6 collective-permute-start.1
  8.7 4.7 %centre.1.base_ref = f32[8,2,288,128]{3,2,1,0:T(8,128)} custom-call(s32[2,8]{1,0:T(2,128)} %bitcast.46, bf16[8,2,288,128]{3,2,1,0:T(8,128)(2,1)} %part_ref.1, f32[2,288,128]{2,1,0:T(8,128)} %constant.49.clone.turns_ref), custom_call_target="tpu_custom_call" | custom-call | tf_op jit(solution)/shard_map/centre/pallas_call | solution.py:87
  14.1 11.8 %spectra.3.refs_4_ = bf16[288,208,256]{2,1,0:T(8,128)(2,1)} custom-call(f32[8,2,288,128]{3,2,1,0:T(8,128)} %centre.1.base_ref, f32[8,128]{1,0:T(8,128)} %fusion.3.ctf_ref.refs_6_, bf16[576,576]{1,0:T(8,128)(2,1)} %constant.50.clone.table_ref, f32[2,5,2,288,128]{4,3,2,1,0:T(8,128)} %constant.51.clone.refs_0_.refs_1_.refs_2_.refs_3_, ...), custom_call_target="tpu_custom_call" | custom-call | tf_op jit(solution)/shard_map/spectra/pallas_call | solution.py:171
  25.9 2.0 collective-permute-done
  32.2 3.2 %collective-permute-start.5 = (bf16[3600,128]{1,0:T(8,128)(2,1)S(1)}, bf16[3600,128]{1,0:T(8,128)(2,1)S(1)}, u32[]{:S(2)}, u32[]{:S(2)}) collective-permute-start(bf16[3600,128]{1,0:T(8,128)(2,1)S(1)} %collective-permute-done.2.refs_17_), channel_id=1, source_target_pairs={{8,16},{12,20},{16,8},{20,12},{9,17},{13,21},{17,9},{21,13},{10,18... | collective-permute-start | bytes 2764808 | tf_op jit(solution)/shard_map/ppermute | solution.py:554
  35.4 17.3 %spectra.4.refs_4_ = bf16[288,208,256]{2,1,0:T(8,128)(2,1)} custom-call(f32[8,2,288,128]{3,2,1,0:T(8,128)} %centre.1.base_ref, f32[8,128]{1,0:T(8,128)} %fusion.3.ctf_ref.refs_6_, bf16[576,576]{1,0:T(8,128)(2,1)} %constant.50.clone.table_ref, f32[2,5,2,288,128]{4,3,2,1,0:T(8,128)} %constant.51.clone.refs_0_.refs_1_.refs_2_.refs_3_, ...), custom_call_target="tpu_custom_call", output_to_operand_aliasing={{}: (7, {})} | custom-call | tf_op jit(solution)/shard_map/spectra/pallas_call | solution.py:171
  53.0 1.8 collective-permute-done.5
  56.9 17.2 %spectra.5 = bf16[288,208,256]{2,1,0:T(8,128)(2,1)} custom-call(f32[8,2,288,128]{3,2,1,0:T(8,128)} %centre.1.base_ref, f32[8,128]{1,0:T(8,128)} %fusion.3.ctf_ref.refs_6_, bf16[576,576]{1,0:T(8,128)(2,1)} %constant.50.clone.table_ref, f32[2,5,2,288,128]{4,3,2,1,0:T(8,128)} %constant.51.clone.refs_0_.refs_1_.refs_2_.refs_3_, ...), custom_call_target="tpu_custom_call", output_to_operand_aliasing={{}: (7, {})} | custom-call | tf_op jit(solution)/shard_map/spectra/pallas_call | solution.py:171
  74.1 2.6 %collective-permute-done.7.refs_20_ = bf16[3600,128]{1,0:T(8,128)(2,1)S(1)} collective-permute-done((bf16[3600,128]{1,0:T(8,128)(2,1)S(1)}, bf16[3600,128]{1,0:T(8,128)(2,1)S(1)}, u32[]{:S(2)}, u32[]{:S(2)}) %collective-permute-start.7) | collective-permute-done | bytes 921632 | tf_op jit(solution)/shard_map/ppermute | solution.py:550
  77.9 17.1 %correlate.1 = (f32[36,112,256]{2,1,0:T(8,128)}, f32[56,128]{1,0:T(8,128)}) custom-call(s32[1]{0:T(128)} %bitcast.7.refs_0_, s32[1]{0:T(128)} %bitcast.8.refs_1_, s32[1]{0:T(128)} %bitcast.9.refs_2_.refs_0_, s32[1]{0:T(128)} %bitcast.10.refs_3_, s32[1]{0:T(128)} %bitcast.11.refs_4_.refs_0_, s32[1]{0:T(128)} %bitcast.12.refs_5_, s32[1]{0:T(128)} %bitcast.13.refs_6_.refs_0_, ...), custom_call_target="tpu_custom_call" | custom-call | tf_op jit(solution)/shard_map/correlate/pallas_call | solution.py:417
  96.9 11.3 %scores.1 = (f32[36,56,256]{2,1,0:T(8,128)}, f32[64,128]{1,0:T(8,128)}, f32[4,2,128]{2,1,0:T(2,128)}) custom-call(s32[1]{0:T(128)} %bitcast.refs_0_, s32[1]{0:T(128)} %bitcast.1.refs_7_.refs_1_, bf16[8,36,208,256]{3,2,1,0:T(8,128)(2,1)} %bitcast.34, bf16[3600,128]{1,0:T(8,128)(2,1)} %copy-done.11, f32[36,112,256]{2,1,0:T(8,128)} %get-tuple-element.66.refs_4_, ...), custom_call_target="tpu_custom_call" | custom-call | tf_op jit(solution)/shard_map/scores/pallas_call | solution.py:417
  108.2 6.2 %psum.7.share_ref = f32[4,2,128]{2,1,0:T(2,128)} all-reduce(f32[4,2,128]{2,1,0:T(2,128)} %get-tuple-element.70), channel_id=1, replica_groups=mesh['dp'=8,'cls'=4] {'cls'}, use_global_device_ids=true, to_apply=%region_0.1 | all-reduce | flops 1024 | bytes 8192 | tf_op jit(solution)/shard_map/psum | solution.py:684
  114.4 5.4 %back.1 = (bf16[36,112,208]{2,1,0:T(8,128)(2,1)}, f32[8,128]{1,0:T(8,128)}, f32[56,128]{1,0:T(8,128)}) custom-call(f32[36,56,256]{2,1,0:T(8,128)} %get-tuple-element.68.weight_ref, f32[64,128]{1,0:T(8,128)} %get-tuple-element.69.stat_ref, f32[4,2,128]{2,1,0:T(2,128)} %psum.7.share_ref, f32[56,128]{1,0:T(8,128)} %get-tuple-element.71.offset_ref.refs_3_.refs_5_), custom_call_target="tpu_custom_call" | custom-call | tf_op jit(solution)/shard_map/back/pallas_call | solution.py:483
  119.9 2.6 %class_sums.6 = bf16[1200,128]{1,0:T(8,128)(2,1)} custom-call(s32[1]{0:T(128)} %bitcast.16.refs_0_, bf16[36,112,208]{2,1,0:T(8,128)(2,1)} %get-tuple-element.90.refs_1_.refs_2_, bf16[8,36,208,256]{3,2,1,0:T(8,128)(2,1)} %bitcast.35, f32[56,128]{1,0:T(8,128)} %get-tuple-element.71.offset_ref.refs_3_.refs_5_), custom_call_target="tpu_custom_call" | custom-call | tf_op jit(solution)/shard_map/class_sums/pallas_call | solution.py:526
  123.0 3.3 %class_sums.7 = bf16[2400,128]{1,0:T(8,128)(2,1)} custom-call(s32[1]{0:T(128)} %bitcast.16.refs_0_, bf16[36,112,208]{2,1,0:T(8,128)(2,1)} %get-tuple-element.90.refs_1_.refs_2_, bf16[8,36,208,256]{3,2,1,0:T(8,128)(2,1)} %bitcast.36, f32[56,128]{1,0:T(8,128)} %get-tuple-element.71.offset_ref.refs_3_.refs_5_), custom_call_target="tpu_custom_call" | custom-call | tf_op jit(solution)/shard_map/class_sums/pallas_call | solution.py:526
  126.2 7.1 %class_sums.8 = (f32[3600,128]{1,0:T(8,128)}, bf16[3600,128]{1,0:T(8,128)(2,1)}) custom-call(s32[1]{0:T(128)} %bitcast.13.refs_6_.refs_0_, s32[1]{0:T(128)} %bitcast.17.refs_1_, bf16[36,112,208]{2,1,0:T(8,128)(2,1)} %get-tuple-element.90.refs_1_.refs_2_, bf16[8,36,208,256]{3,2,1,0:T(8,128)(2,1)} %bitcast.37, bf16[8,36,208,256]{3,2,1,0:T(8,128)(2,1)} %bitcast.38, ...), custom_call_target="tpu_custom_call" | custom-call | tf_op jit(solution)/shard_map/class_sums/pallas_call | solution.py:526
  137.8 7.1 %class_sums.9 = (f32[3600,128]{1,0:T(8,128)}, bf16[3600,128]{1,0:T(8,128)(2,1)}) custom-call(s32[1]{0:T(128)} %bitcast.11.refs_4_.refs_0_, s32[1]{0:T(128)} %bitcast.18.refs_1_, bf16[36,112,208]{2,1,0:T(8,128)(2,1)} %get-tuple-element.90.refs_1_.refs_2_, bf16[8,36,208,256]{3,2,1,0:T(8,128)(2,1)} %bitcast.39, bf16[8,36,208,256]{3,2,1,0:T(8,128)(2,1)} %bitcast.40, ...), custom_call_target="tpu_custom_call" | custom-call | tf_op jit(solution)/shard_map/class_sums/pallas_call | solution.py:526
  146.6 3.3 %collective-permute-start.14 = (bf16[1200,128]{1,0:T(8,128)(2,1)S(1)}, bf16[1200,128]{1,0:T(8,128)(2,1)S(1)}, u32[]{:S(2)}, u32[]{:S(2)}) collective-permute-start(bf16[1200,128]{1,0:T(8,128)(2,1)S(1)} %add_convert_fusion.3), channel_id=1, source_target_pairs={{8,16},{12,20},{16,8},{20,12},{9,17},{13,21},{17,9},{21,13},{10,18... | collective-permute-start | bytes 921608 | tf_op jit(solution)/shard_map/ppermute | solution.py:554
  149.9 2.7 %collective-permute-done.10 = bf16[2400,128]{1,0:T(8,128)(2,1)S(1)} collective-permute-done((bf16[2400,128]{1,0:T(8,128)(2,1)S(1)}, bf16[2400,128]{1,0:T(8,128)(2,1)S(1)}, u32[]{:S(2)}, u32[]{:S(2)}) %collective-permute-start.10) | collective-permute-done | bytes 614432 | tf_op jit(solution)/shard_map/ppermute | solution.py:550
  154.8 7.1 %class_sums.10 = (f32[3600,128]{1,0:T(8,128)}, bf16[3600,128]{1,0:T(8,128)(2,1)}) custom-call(s32[1]{0:T(128)} %bitcast.9.refs_2_.refs_0_, s32[1]{0:T(128)} %bitcast.19.refs_1_, bf16[36,112,208]{2,1,0:T(8,128)(2,1)} %get-tuple-element.90.refs_1_.refs_2_, bf16[8,36,208,256]{3,2,1,0:T(8,128)(2,1)} %bitcast.41, bf16[8,36,208,256]{3,2,1,0:T(8,128)(2,1)} %bitcast.42, ...), custom_call_target="tpu_custom_call" | custom-call | tf_op jit(solution)/shard_map/class_sums/pallas_call | solution.py:526
  162.0 10.3 %collective-permute-done.13 = bf16[3600,128]{1,0:T(8,128)(2,1)S(1)} collective-permute-done((bf16[3600,128]{1,0:T(8,128)(2,1)}, bf16[3600,128]{1,0:T(8,128)(2,1)S(1)}, u32[]{:S(2)}, u32[]{:S(2)}) %collective-permute-start.13) | collective-permute-done | bytes 921632 | tf_op jit(solution)/shard_map/ppermute | solution.py:550
  175.7 3.4 %collective-permute-start.19 = (bf16[2400,128]{1,0:T(8,128)(2,1)S(1)}, bf16[2400,128]{1,0:T(8,128)(2,1)S(1)}, u32[]{:S(2)}, u32[]{:S(2)}) collective-permute-start(bf16[2400,128]{1,0:T(8,128)(2,1)S(1)} %add_convert_fusion.2), channel_id=1, source_target_pairs={{8,16},{12,20},{16,8},{20,12},{9,17},{13,21},{17,9},{21,13},{10,18... | collective-permute-start | bytes 1843208 | tf_op jit(solution)/shard_map/ppermute | solution.py:554
  179.1 13.0 %collective-permute-done.17 = bf16[3600,128]{1,0:T(8,128)(2,1)S(1)} collective-permute-done((bf16[3600,128]{1,0:T(8,128)(2,1)}, bf16[3600,128]{1,0:T(8,128)(2,1)S(1)}, u32[]{:S(2)}, u32[]{:S(2)}) %collective-permute-start.17) | collective-permute-done | bytes 921632 | tf_op jit(solution)/shard_map/ppermute | solution.py:550
  192.1 2.0 collective-permute-done.16
  197.5 3.2 %collective-permute-start.18 = (bf16[3600,128]{1,0:T(8,128)(2,1)}, bf16[3600,128]{1,0:T(8,128)(2,1)S(1)}, u32[]{:S(2)}, u32[]{:S(2)}) collective-permute-start(bf16[3600,128]{1,0:T(8,128)(2,1)} %add_convert_fusion.1), channel_id=1, source_target_pairs={{8,16},{12,20},{16,8},{20,12},{9,17},{13,21},{17,9},{21,13},{10,18... | collective-permute-start | bytes 2764808 | tf_op jit(solution)/shard_map/ppermute | solution.py:554
  202.6 5.2 %class_sums.11 = f32[3600,128]{1,0:T(8,128)} custom-call(s32[1]{0:T(128)} %bitcast.7.refs_0_, bf16[36,112,208]{2,1,0:T(8,128)(2,1)} %get-tuple-element.90.refs_1_.refs_2_, bf16[8,36,208,256]{3,2,1,0:T(8,128)(2,1)} %bitcast.43, f32[56,128]{1,0:T(8,128)} %get-tuple-element.71.offset_ref.refs_3_.refs_5_), custom_call_target="tpu_custom_call" | custom-call | tf_op jit(solution)/shard_map/class_sums/pallas_call | solution.py:526
  207.7 2.7 %collective-permute-done.15 = bf16[3600,128]{1,0:T(8,128)(2,1)S(1)} collective-permute-done((bf16[3600,128]{1,0:T(8,128)(2,1)}, bf16[3600,128]{1,0:T(8,128)(2,1)S(1)}, u32[]{:S(2)}, u32[]{:S(2)}) %collective-permute-start.15) | collective-permute-done | bytes 921632 | tf_op jit(solution)/shard_map/ppermute | solution.py:550
  210.4 5.2 %collective-permute-done.20 = bf16[3600,128]{1,0:T(8,128)(2,1)S(1)} collective-permute-done((bf16[3600,128]{1,0:T(8,128)(2,1)}, bf16[3600,128]{1,0:T(8,128)(2,1)S(1)}, u32[]{:S(2)}, u32[]{:S(2)}) %collective-permute-start.20) | collective-permute-done | bytes 921632 | tf_op jit(solution)/shard_map/ppermute | solution.py:554
  215.6 2.7 %collective-permute-done.18 = bf16[3600,128]{1,0:T(8,128)(2,1)S(1)} collective-permute-done((bf16[3600,128]{1,0:T(8,128)(2,1)}, bf16[3600,128]{1,0:T(8,128)(2,1)S(1)}, u32[]{:S(2)}, u32[]{:S(2)}) %collective-permute-start.18) | collective-permute-done | bytes 921632 | tf_op jit(solution)/shard_map/ppermute | solution.py:554
  218.3 3.2 %convert_add_fusion = f32[3600,128]{1,0:T(8,128)} fusion(bf16[3600,128]{1,0:T(8,128)(2,1)S(1)} %collective-permute-done.20, bf16[3600,128]{1,0:T(8,128)(2,1)S(1)} %collective-permute-done.18, f32[3600,128]{1,0:T(8,128)} %class_sums.11, bf16[3600,128]{1,0:T(8,128)(2,1)S(1)} %collective-permute-done.15), kind=kLoop, calls=%fused_computation | loop fusion | flops 2764800 | bytes 6451200 | tf_op jit(solution)/shard_map/add | solution.py:649
  (73 shorter events, 28.0 us)
Async XLA Ops:
  0.6 12.7 %copy-start = (f32[16,128]{1,0:T(8,128)S(1)}, f32[16,128]{1,0:T(8,128)}, u32[]{:S(2)}) copy-start(f32[16,128]{1,0:T(8,128)} %param.15) | copy-start | bytes 24580
  3.6 24.3 %collective-permute-start = (bf16[3600,128]{1,0:T(8,128)(2,1)}, bf16[3600,128]{1,0:T(8,128)(2,1)S(1)}, u32[]{:S(2)}, u32[]{:S(2)}) collective-permute-start(bf16[3600,128]{1,0:T(8,128)(2,1)} %get-tuple-element.50.refs_15_), channel_id=1, source_target_pairs={{8,16},{12,20},{16,8},{20,12},{9,17},{13,21},{17,9},{21,13},{10,18... | collective-permute-start | bytes 2764808 | tf_op jit(solution)/shard_map/ppermute | solution.py:554
  7.1 22.2 %collective-permute-start.1 = (bf16[3600,128]{1,0:T(8,128)(2,1)}, bf16[3600,128]{1,0:T(8,128)(2,1)S(1)}, u32[]{:S(2)}, u32[]{:S(2)}) collective-permute-start(bf16[3600,128]{1,0:T(8,128)(2,1)} %get-tuple-element.50.refs_15_), channel_id=1, source_target_pairs={{0,4},{4,0},{8,12},{12,8},{16,20},{20,16},{24,28},{28,24},{1,5},{5... | collective-permute-start | bytes 2764808 | tf_op jit(solution)/shard_map/ppermute | solution.py:550
  8.7 22.0 %collective-permute-start.2 = (bf16[3600,128]{1,0:T(8,128)(2,1)}, bf16[3600,128]{1,0:T(8,128)(2,1)S(1)}, u32[]{:S(2)}, u32[]{:S(2)}) collective-permute-start(bf16[3600,128]{1,0:T(8,128)(2,1)} %get-tuple-element.50.refs_15_), channel_id=1, source_target_pairs={{0,8},{4,12},{8,0},{12,4},{16,24},{20,28},{24,16},{28,20},{1,9},{5... | collective-permute-start | bytes 2764808 | tf_op jit(solution)/shard_map/ppermute | solution.py:554
  29.3 23.4 %copy-start.7 = (bf16[3600,128]{1,0:T(8,128)(2,1)}, bf16[3600,128]{1,0:T(8,128)(2,1)S(1)}, u32[]{:S(2)}) copy-start(bf16[3600,128]{1,0:T(8,128)(2,1)S(1)} %collective-permute-done.1.refs_16_) | copy-start | bytes 2764804
  29.3 23.4 %collective-permute-start.3 = (bf16[3600,128]{1,0:T(8,128)(2,1)S(1)}, bf16[3600,128]{1,0:T(8,128)(2,1)S(1)}, u32[]{:S(2)}, u32[]{:S(2)}) collective-permute-start(bf16[3600,128]{1,0:T(8,128)(2,1)S(1)} %collective-permute-done), channel_id=1, source_target_pairs={{8,0},{12,4},{16,24},{20,28},{9,1},{13,5},{17,25},{21,29},{10,2},{... | collective-permute-start | bytes 2764808 | tf_op jit(solution)/shard_map/ppermute | solution.py:554
  30.6 22.0 %copy-start.8 = (bf16[3600,128]{1,0:T(8,128)(2,1)}, bf16[3600,128]{1,0:T(8,128)(2,1)S(1)}, u32[]{:S(2)}) copy-start(bf16[3600,128]{1,0:T(8,128)(2,1)S(1)} %collective-permute-done.2.refs_17_) | copy-start | bytes 2764804
  30.7 22.3 %collective-permute-start.4 = (bf16[3600,128]{1,0:T(8,128)(2,1)S(1)}, bf16[3600,128]{1,0:T(8,128)(2,1)S(1)}, u32[]{:S(2)}, u32[]{:S(2)}) collective-permute-start(bf16[3600,128]{1,0:T(8,128)(2,1)S(1)} %collective-permute-done.2.refs_17_), channel_id=1, source_target_pairs={{0,4},{4,0},{8,12},{12,8},{16,20},{20,16},{24,28},{28,24},{1,5},{5... | collective-permute-start | bytes 2764808 | tf_op jit(solution)/shard_map/ppermute | solution.py:550
  32.2 22.6 %collective-permute-start.5 = (bf16[3600,128]{1,0:T(8,128)(2,1)S(1)}, bf16[3600,128]{1,0:T(8,128)(2,1)S(1)}, u32[]{:S(2)}, u32[]{:S(2)}) collective-permute-start(bf16[3600,128]{1,0:T(8,128)(2,1)S(1)} %collective-permute-done.2.refs_17_), channel_id=1, source_target_pairs={{8,16},{12,20},{16,8},{20,12},{9,17},{13,21},{17,9},{21,13},{10,18... | collective-permute-start | bytes 2764808 | tf_op jit(solution)/shard_map/ppermute | solution.py:554
  53.0 21.1 %copy-start.4 = (bf16[3600,128]{1,0:T(8,128)(2,1)}, bf16[3600,128]{1,0:T(8,128)(2,1)S(1)}, u32[]{:S(2)}) copy-start(bf16[3600,128]{1,0:T(8,128)(2,1)S(1)} %add.92.refs_19_) | copy-start | bytes 2764804
  53.0 21.1 %copy-start.9 = (bf16[3600,128]{1,0:T(8,128)(2,1)}, bf16[3600,128]{1,0:T(8,128)(2,1)S(1)}, u32[]{:S(2)}) copy-start(bf16[3600,128]{1,0:T(8,128)(2,1)S(1)} %collective-permute-done.4.refs_18_) | copy-start | bytes 2764804
  54.8 19.3 %collective-permute-start.6 = (bf16[3600,128]{1,0:T(8,128)(2,1)S(1)}, bf16[3600,128]{1,0:T(8,128)(2,1)S(1)}, u32[]{:S(2)}, u32[]{:S(2)}) collective-permute-start(bf16[3600,128]{1,0:T(8,128)(2,1)S(1)} %collective-permute-done.5), channel_id=1, source_target_pairs={{8,0},{12,4},{16,24},{20,28},{9,1},{13,5},{17,25},{21,29},{10,2},{... | collective-permute-start | bytes 2764808 | tf_op jit(solution)/shard_map/ppermute | solution.py:554
  56.3 20.3 %collective-permute-start.7 = (bf16[3600,128]{1,0:T(8,128)(2,1)S(1)}, bf16[3600,128]{1,0:T(8,128)(2,1)S(1)}, u32[]{:S(2)}, u32[]{:S(2)}) collective-permute-start(bf16[3600,128]{1,0:T(8,128)(2,1)S(1)} %add.92.refs_19_), channel_id=1, source_target_pairs={{0,4},{4,0},{8,12},{12,8},{16,20},{20,16},{24,28},{28,24},{1,5},{5... | collective-permute-start | bytes 2764808 | tf_op jit(solution)/shard_map/ppermute | solution.py:550
  76.9 19.0 %collective-permute-start.8 = (bf16[3600,128]{1,0:T(8,128)(2,1)S(1)}, bf16[3600,128]{1,0:T(8,128)(2,1)S(1)}, u32[]{:S(2)}, u32[]{:S(2)}) collective-permute-start(bf16[3600,128]{1,0:T(8,128)(2,1)S(1)} %add.93.refs_21_), channel_id=1, source_target_pairs={{0,4},{4,0},{8,12},{12,8},{16,20},{20,16},{24,28},{28,24},{1,5},{5... | collective-permute-start | bytes 2764808 | tf_op jit(solution)/shard_map/ppermute | solution.py:550
  122.4 10.9 %collective-permute-start.9 = (bf16[1200,128]{1,0:T(8,128)(2,1)}, bf16[1200,128]{1,0:T(8,128)(2,1)S(1)}, u32[]{:S(2)}, u32[]{:S(2)}) collective-permute-start(bf16[1200,128]{1,0:T(8,128)(2,1)} %class_sums.6), channel_id=1, source_target_pairs={{0,4},{4,0},{8,12},{12,8},{16,20},{20,16},{24,28},{28,24},{1,5},{5... | collective-permute-start | bytes 921608 | tf_op jit(solution)/shard_map/ppermute | solution.py:550
  126.2 9.5 %copy-start.12 = (bf16[2400,128]{1,0:T(8,128)(2,1)S(1)}, bf16[2400,128]{1,0:T(8,128)(2,1)}, u32[]{:S(2)}) copy-start(bf16[2400,128]{1,0:T(8,128)(2,1)} %class_sums.7) | copy-start | bytes 1843204
  134.4 12.0 %collective-permute-start.11 = (bf16[1200,128]{1,0:T(8,128)(2,1)S(1)}, bf16[1200,128]{1,0:T(8,128)(2,1)S(1)}, u32[]{:S(2)}, u32[]{:S(2)}) collective-permute-start(bf16[1200,128]{1,0:T(8,128)(2,1)S(1)} %fusion.2), channel_id=1, source_target_pairs={{0,8},{4,12},{24,16},{28,20},{1,9},{5,13},{25,17},{29,21},{2,10},{... | collective-permute-start | bytes 921608 | tf_op jit(solution)/shard_map/ppermute | solution.py:554
  135.7 16.8 %collective-permute-start.10 = (bf16[2400,128]{1,0:T(8,128)(2,1)S(1)}, bf16[2400,128]{1,0:T(8,128)(2,1)S(1)}, u32[]{:S(2)}, u32[]{:S(2)}) collective-permute-start(bf16[2400,128]{1,0:T(8,128)(2,1)S(1)} %copy-done.12), channel_id=1, source_target_pairs={{0,4},{4,0},{8,12},{12,8},{16,20},{20,16},{24,28},{28,24},{1,5},{5... | collective-permute-start | bytes 1843208 | tf_op jit(solution)/shard_map/ppermute | solution.py:550
  137.3 35.1 %collective-permute-start.13 = (bf16[3600,128]{1,0:T(8,128)(2,1)}, bf16[3600,128]{1,0:T(8,128)(2,1)S(1)}, u32[]{:S(2)}, u32[]{:S(2)}) collective-permute-start(bf16[3600,128]{1,0:T(8,128)(2,1)} %get-tuple-element.86), channel_id=1, source_target_pairs={{0,4},{4,0},{8,12},{12,8},{16,20},{20,16},{24,28},{28,24},{1,5},{5... | collective-permute-start | bytes 2764808 | tf_op jit(solution)/shard_map/ppermute | solution.py:550
  145.0 47.1 %collective-permute-start.17 = (bf16[3600,128]{1,0:T(8,128)(2,1)}, bf16[3600,128]{1,0:T(8,128)(2,1)S(1)}, u32[]{:S(2)}, u32[]{:S(2)}) collective-permute-start(bf16[3600,128]{1,0:T(8,128)(2,1)} %get-tuple-element.92), channel_id=1, source_target_pairs={{0,4},{4,0},{8,12},{12,8},{16,20},{20,16},{24,28},{28,24},{1,5},{5... | collective-permute-start | bytes 2764808 | tf_op jit(solution)/shard_map/ppermute | solution.py:550
  146.6 15.4 %collective-permute-start.14 = (bf16[1200,128]{1,0:T(8,128)(2,1)S(1)}, bf16[1200,128]{1,0:T(8,128)(2,1)S(1)}, u32[]{:S(2)}, u32[]{:S(2)}) collective-permute-start(bf16[1200,128]{1,0:T(8,128)(2,1)S(1)} %add_convert_fusion.3), channel_id=1, source_target_pairs={{8,16},{12,20},{16,8},{20,12},{9,17},{13,21},{17,9},{21,13},{10,18... | collective-permute-start | bytes 921608 | tf_op jit(solution)/shard_map/ppermute | solution.py:554
  153.5 21.9 %collective-permute-start.12 = (bf16[2400,128]{1,0:T(8,128)(2,1)}, bf16[2400,128]{1,0:T(8,128)(2,1)S(1)}, u32[]{:S(2)}, u32[]{:S(2)}) collective-permute-start(bf16[2400,128]{1,0:T(8,128)(2,1)} %fusion.1), channel_id=1, source_target_pairs={{0,8},{4,12},{24,16},{28,20},{1,9},{5,13},{25,17},{29,21},{2,10},{... | collective-permute-start | bytes 1843208 | tf_op jit(solution)/shard_map/ppermute | solution.py:554
  154.8 17.5 %copy-start.2 = (f32[3600,128]{1,0:T(8,128)S(1)}, f32[3600,128]{1,0:T(8,128)}, u32[]{:S(2)}) copy-start(f32[3600,128]{1,0:T(8,128)} %get-tuple-element.85) | copy-start | bytes 5529604
  162.0 10.6 %copy-start.13 = (bf16[1200,128]{1,0:T(8,128)(2,1)}, bf16[1200,128]{1,0:T(8,128)(2,1)S(1)}, u32[]{:S(2)}) copy-start(bf16[1200,128]{1,0:T(8,128)(2,1)S(1)} %collective-permute-done.14) | copy-start | bytes 921604
  172.6 21.5 %collective-permute-start.16 = (bf16[3600,128]{1,0:T(8,128)(2,1)S(1)}, bf16[3600,128]{1,0:T(8,128)(2,1)S(1)}, u32[]{:S(2)}, u32[]{:S(2)}) collective-permute-start(bf16[3600,128]{1,0:T(8,128)(2,1)S(1)} %fusion), channel_id=1, source_target_pairs={{0,8},{4,12},{24,16},{28,20},{1,9},{5,13},{25,17},{29,21},{2,10},{... | collective-permute-start | bytes 2764808 | tf_op jit(solution)/shard_map/ppermute | solution.py:554
  173.9 36.5 %collective-permute-start.15 = (bf16[3600,128]{1,0:T(8,128)(2,1)}, bf16[3600,128]{1,0:T(8,128)(2,1)S(1)}, u32[]{:S(2)}, u32[]{:S(2)}) collective-permute-start(bf16[3600,128]{1,0:T(8,128)(2,1)} %get-tuple-element.91), channel_id=1, source_target_pairs={{0,4},{4,0},{8,12},{12,8},{16,20},{20,16},{24,28},{28,24},{1,5},{5... | collective-permute-start | bytes 2764808 | tf_op jit(solution)/shard_map/ppermute | solution.py:550
  175.6 19.8 %copy-start.6 = (f32[3600,128]{1,0:T(8,128)S(1)}, f32[3600,128]{1,0:T(8,128)}, u32[]{:S(2)}) copy-start(f32[3600,128]{1,0:T(8,128)} %get-tuple-element.94) | copy-start | bytes 5529604
  175.7 19.8 %copy-start.14 = (bf16[1200,128]{1,0:T(8,128)(2,1)S(1)}, bf16[1200,128]{1,0:T(8,128)(2,1)}, u32[]{:S(2)}) copy-start(bf16[1200,128]{1,0:T(8,128)(2,1)} %copy-done.13) | copy-start | bytes 921604
  175.7 19.7 %collective-permute-start.19 = (bf16[2400,128]{1,0:T(8,128)(2,1)S(1)}, bf16[2400,128]{1,0:T(8,128)(2,1)S(1)}, u32[]{:S(2)}, u32[]{:S(2)}) collective-permute-start(bf16[2400,128]{1,0:T(8,128)(2,1)S(1)} %add_convert_fusion.2), channel_id=1, source_target_pairs={{8,16},{12,20},{16,8},{20,12},{9,17},{13,21},{17,9},{21,13},{10,18... | collective-permute-start | bytes 1843208 | tf_op jit(solution)/shard_map/ppermute | solution.py:554
  196.8 18.8 %collective-permute-start.20 = (bf16[3600,128]{1,0:T(8,128)(2,1)}, bf16[3600,128]{1,0:T(8,128)(2,1)S(1)}, u32[]{:S(2)}, u32[]{:S(2)}) collective-permute-start(bf16[3600,128]{1,0:T(8,128)(2,1)} %add_convert_fusion), channel_id=1, source_target_pairs={{0,8},{4,12},{8,0},{12,4},{16,24},{20,28},{24,16},{28,20},{1,9},{5... | collective-permute-start | bytes 2764808 | tf_op jit(solution)/shard_map/ppermute | solution.py:554
  197.5 20.8 %collective-permute-start.18 = (bf16[3600,128]{1,0:T(8,128)(2,1)}, bf16[3600,128]{1,0:T(8,128)(2,1)S(1)}, u32[]{:S(2)}, u32[]{:S(2)}) collective-permute-start(bf16[3600,128]{1,0:T(8,128)(2,1)} %add_convert_fusion.1), channel_id=1, source_target_pairs={{8,16},{12,20},{16,8},{20,12},{9,17},{13,21},{17,9},{21,13},{10,18... | collective-permute-start | bytes 2764808 | tf_op jit(solution)/shard_map/ppermute | solution.py:554
  202.6 18.9 %copy-start.1 = (f32[16,128]{1,0:T(8,128)S(1)}, f32[16,128]{1,0:T(8,128)}, u32[]{:S(2)}) copy-start(f32[16,128]{1,0:T(8,128)} %param.15) | copy-start | bytes 24580
  (6 other events, 21.4 us)

commit v13 on v11

--- a/solution.py
+++ b/solution.py
@@ -456,9 +456,6 @@
                 sine_part = jnp.zeros_like(scale) if m in (0, FOLD - 1) else sin_sums[m]
                 sum_ref[m, rows, lanes] = cos_sums[m]
                 sum_ref[m, low, lanes] = sine_part
-                if m not in (0, FOLD - 1):
-                    sum_ref[ROTS - m, rows, lanes] = cos_sums[m]
-                    sum_ref[ROTS - m, low, lanes] = -sine_part
             return carry
 
         lax.fori_loop(0, padded // 8, transform, 0)
@@ -467,10 +464,12 @@
 
     def turn(m, carry):
         cosine, sine_part = carry
+        place = jnp.minimum(m, ROTS - m)
+        sign = jnp.where(m < FOLD, 1.0, -1.0).astype(f32)
         for tile in range(weight_ref.shape[2] // LANES):
             lanes = slice(tile * LANES, (tile + 1) * LANES)
             kept = slice(tile * LANES, min((tile + 1) * LANES, queries))
-            re, im = sum_ref[m, :padded, lanes], sum_ref[m, padded:, lanes]
+            re, im = sum_ref[place, :padded, lanes], sum_ref[place, padded:, lanes] * sign
             turned = jnp.concatenate([re * cosine - im * sine_part, re * sine_part + im * cosine], 0)
             out_ref[m, :, kept] = turned[:, : kept.stop - kept.start].astype(bf16)
         return cosine * step_cos - sine_part * step_sin, sine_part * step_cos + cosine * step_sin
@@ -487,7 +486,7 @@
             jax.ShapeDtypeStruct((8, LANES), f32),
             jax.ShapeDtypeStruct((padded, LANES), f32),
         ],
-        scratch_shapes=[pltpu.VMEM((ROTS, 2 * padded, wide_lanes), f32)],
+        scratch_shapes=[pltpu.VMEM((FOLD, 2 * padded, wide_lanes), f32)],
         compiler_params=pltpu.CompilerParams(vmem_limit_bytes=VMEM_LIMIT),
         name="back",
     )(weights, stat, shares, offsets)

time: 217 us -> 217 us (level)
  no operation moved by 1% of the time
where the time goes in v13:
time: 217 us; the launch traced here: 216 us
  Pallas kernels  120 us (55%)
  waiting for transfers between devices  39 us (18%)
  starting transfers between devices  35.9 us (17%)
  other arithmetic  10.3 us (5%)
  blocking collectives  6.23 us (3%)
  local copies, waits for them, and re-layouts  2.86 us (1%)
    pallas_call x3, Pallas kernels, make_spectra(): pl.pallas_call(functools.partial(spectra_kernel, per_step=per_step), grid...  46.4 us
    pallas_call x6, Pallas kernels, class_sums_of(): pl.pallas_call(functools.partial(sums_kernel, count=count, classes=classe...  32.4 us
    pallas_call x2, Pallas kernels, correlate(): pl.pallas_call(functools.partial(correlate_kernel, slots=slots, classes=c...  28.4 us
    ppermute x12, starting transfers between devices, along(): lax.ppermute(piece, 'dp', [(2 * a + x, 2 * b + x) for a, b in pairs for x...  24.8 us
    ppermute x9, waiting for transfers between devices, across(): return lax.ppermute(piece, 'dp', [(d, d ^ 1) for d in range(8)])  23.2 us
    ppermute x12, waiting for transfers between devices, along(): lax.ppermute(piece, 'dp', [(2 * a + x, 2 * b + x) for a, b in pairs for x...  15.8 us
    ppermute x9, starting transfers between devices, across(): return lax.ppermute(piece, 'dp', [(d, d ^ 1) for d in range(8)])  11.1 us
    psum x1, blocking collectives, local(): shares = lax.psum(share, 'cls')  6.23 us
  transfers between devices with their start and end apart: 21, of which 11 were waited for; matrix products, arithmetic and copies ran while one was open for 4% of the time, Pallas kernels for 45%

profile of v13, /device:TPU:8, one launch (start us, length us, event | category | flops | bytes accessed | tf_op | source)
XLA Modules:
  0.0 216.1 jit_solution(618106655254042823)
XLA Ops:
  0.7 3.0 %turn_references.1 = (bf16[3600,128]{1,0:T(8,128)(2,1)}, f32[56,128]{1,0:T(8,128)}) custom-call(s32[1]{0:T(128)} %bitcast.3.first_ref, s32[50]{0:T(128)} %offset_ref.1, bf16[3600,128]{1,0:T(8,128)(2,1)} %bitcast.45), custom_call_target="tpu_custom_call" | custom-call | tf_op jit(solution)/shard_map/turn_references/pallas_call | solution.py:251
  5.6 4.6 %collective-permute-start.2 = (bf16[3600,128]{1,0:T(8,128)(2,1)}, bf16[3600,128]{1,0:T(8,128)(2,1)S(1)}, u32[]{:S(2)}, u32[]{:S(2)}) collective-permute-start(bf16[3600,128]{1,0:T(8,128)(2,1)} %get-tuple-element.50.refs_15_), channel_id=1, source_target_pairs={{8,16},{12,20},{16,8},{20,12},{9,17},{13,21},{17,9},{21,13},{10,18... | collective-permute-start | bytes 2764808 | tf_op jit(solution)/shard_map/ppermute | solution.py:553
  10.2 4.6 %centre.1.base_ref = f32[8,2,288,128]{3,2,1,0:T(8,128)} custom-call(s32[2,8]{1,0:T(2,128)} %bitcast.46, bf16[8,2,288,128]{3,2,1,0:T(8,128)(2,1)} %part_ref.1, f32[2,288,128]{2,1,0:T(8,128)} %constant.49.clone.turns_ref), custom_call_target="tpu_custom_call" | custom-call | tf_op jit(solution)/shard_map/centre/pallas_call | solution.py:87
  15.6 11.9 %spectra.3.refs_4_ = bf16[288,208,256]{2,1,0:T(8,128)(2,1)} custom-call(f32[8,2,288,128]{3,2,1,0:T(8,128)} %centre.1.base_ref, f32[8,128]{1,0:T(8,128)} %fusion.3.ctf_ref.refs_6_, bf16[576,576]{1,0:T(8,128)(2,1)} %constant.50.clone.table_ref, f32[2,5,2,288,128]{4,3,2,1,0:T(8,128)} %constant.51.clone.refs_0_.refs_1_.refs_2_.refs_3_, ...), custom_call_target="tpu_custom_call" | custom-call | tf_op jit(solution)/shard_map/spectra/pallas_call | solution.py:171
  27.5 2.7 %collective-permute-done.2 = bf16[3600,128]{1,0:T(8,128)(2,1)S(1)} collective-permute-done((bf16[3600,128]{1,0:T(8,128)(2,1)}, bf16[3600,128]{1,0:T(8,128)(2,1)S(1)}, u32[]{:S(2)}, u32[]{:S(2)}) %collective-permute-start.2) | collective-permute-done | bytes 921632 | tf_op jit(solution)/shard_map/ppermute | solution.py:553
  32.2 3.6 %collective-permute-start.5 = (bf16[3600,128]{1,0:T(8,128)(2,1)S(1)}, bf16[3600,128]{1,0:T(8,128)(2,1)S(1)}, u32[]{:S(2)}, u32[]{:S(2)}) collective-permute-start(bf16[3600,128]{1,0:T(8,128)(2,1)S(1)} %collective-permute-done.1.refs_17_), channel_id=1, source_target_pairs={{8,16},{12,20},{16,8},{20,12},{9,17},{13,21},{17,9},{21,13},{10,18... | collective-permute-start | bytes 2764808 | tf_op jit(solution)/shard_map/ppermute | solution.py:553
  35.8 17.3 %spectra.4.refs_4_ = bf16[288,208,256]{2,1,0:T(8,128)(2,1)} custom-call(f32[8,2,288,128]{3,2,1,0:T(8,128)} %centre.1.base_ref, f32[8,128]{1,0:T(8,128)} %fusion.3.ctf_ref.refs_6_, bf16[576,576]{1,0:T(8,128)(2,1)} %constant.50.clone.table_ref, f32[2,5,2,288,128]{4,3,2,1,0:T(8,128)} %constant.51.clone.refs_0_.refs_1_.refs_2_.refs_3_, ...), custom_call_target="tpu_custom_call", output_to_operand_aliasing={{}: (7, {})} | custom-call | tf_op jit(solution)/shard_map/spectra/pallas_call | solution.py:171
  53.1 1.7 collective-permute-done.5
  56.6 1.6 collective-permute-start.7
  58.1 17.2 %spectra.5 = bf16[288,208,256]{2,1,0:T(8,128)(2,1)} custom-call(f32[8,2,288,128]{3,2,1,0:T(8,128)} %centre.1.base_ref, f32[8,128]{1,0:T(8,128)} %fusion.3.ctf_ref.refs_6_, bf16[576,576]{1,0:T(8,128)(2,1)} %constant.50.clone.table_ref, f32[2,5,2,288,128]{4,3,2,1,0:T(8,128)} %constant.51.clone.refs_0_.refs_1_.refs_2_.refs_3_, ...), custom_call_target="tpu_custom_call", output_to_operand_aliasing={{}: (7, {})} | custom-call | tf_op jit(solution)/shard_map/spectra/pallas_call | solution.py:171
  77.2 1.6 collective-permute-start.8
  78.7 17.1 %correlate.1 = (f32[36,112,256]{2,1,0:T(8,128)}, f32[56,128]{1,0:T(8,128)}) custom-call(s32[1]{0:T(128)} %bitcast.7.refs_0_, s32[1]{0:T(128)} %bitcast.8.refs_1_, s32[1]{0:T(128)} %bitcast.9.refs_2_.refs_0_, s32[1]{0:T(128)} %bitcast.10.refs_3_, s32[1]{0:T(128)} %bitcast.11.refs_4_.refs_0_, s32[1]{0:T(128)} %bitcast.12.refs_5_, s32[1]{0:T(128)} %bitcast.13.refs_6_.refs_0_, ...), custom_call_target="tpu_custom_call" | custom-call | tf_op jit(solution)/shard_map/correlate/pallas_call | solution.py:417
  97.1 11.3 %scores.1 = (f32[36,56,256]{2,1,0:T(8,128)}, f32[64,128]{1,0:T(8,128)}, f32[4,2,128]{2,1,0:T(2,128)}) custom-call(s32[1]{0:T(128)} %bitcast.refs_0_, s32[1]{0:T(128)} %bitcast.1.refs_7_.refs_1_, bf16[8,36,208,256]{3,2,1,0:T(8,128)(2,1)} %bitcast.34, bf16[3600,128]{1,0:T(8,128)(2,1)} %copy-done.13, f32[36,112,256]{2,1,0:T(8,128)} %get-tuple-element.65.refs_4_, ...), custom_call_target="tpu_custom_call" | custom-call | tf_op jit(solution)/shard_map/scores/pallas_call | solution.py:417
  108.4 6.2 %psum.7.share_ref = f32[4,2,128]{2,1,0:T(2,128)} all-reduce(f32[4,2,128]{2,1,0:T(2,128)} %get-tuple-element.69), channel_id=1, replica_groups=mesh['dp'=8,'cls'=4] {'cls'}, use_global_device_ids=true, to_apply=%region_0.1 | all-reduce | flops 1024 | bytes 8192 | tf_op jit(solution)/shard_map/psum | solution.py:683
  114.7 5.4 %back.1 = (bf16[36,112,208]{2,1,0:T(8,128)(2,1)}, f32[8,128]{1,0:T(8,128)}, f32[56,128]{1,0:T(8,128)}) custom-call(f32[36,56,256]{2,1,0:T(8,128)} %get-tuple-element.67.weight_ref, f32[64,128]{1,0:T(8,128)} %get-tuple-element.68.stat_ref, f32[4,2,128]{2,1,0:T(2,128)} %psum.7.share_ref, f32[56,128]{1,0:T(8,128)} %get-tuple-element.70.offset_ref.refs_3_.refs_5_), custom_call_target="tpu_custom_call" | custom-call | tf_op jit(solution)/shard_map/back/pallas_call | solution.py:482
  120.0 2.6 %class_sums.6 = bf16[1200,128]{1,0:T(8,128)(2,1)} custom-call(s32[1]{0:T(128)} %bitcast.16.refs_0_, bf16[36,112,208]{2,1,0:T(8,128)(2,1)} %get-tuple-element.90.refs_1_.refs_2_, bf16[8,36,208,256]{3,2,1,0:T(8,128)(2,1)} %bitcast.35, f32[56,128]{1,0:T(8,128)} %get-tuple-element.70.offset_ref.refs_3_.refs_5_), custom_call_target="tpu_custom_call" | custom-call | tf_op jit(solution)/shard_map/class_sums/pallas_call | solution.py:525
  124.2 3.2 %class_sums.7 = bf16[2400,128]{1,0:T(8,128)(2,1)} custom-call(s32[1]{0:T(128)} %bitcast.16.refs_0_, bf16[36,112,208]{2,1,0:T(8,128)(2,1)} %get-tuple-element.90.refs_1_.refs_2_, bf16[8,36,208,256]{3,2,1,0:T(8,128)(2,1)} %bitcast.36, f32[56,128]{1,0:T(8,128)} %get-tuple-element.70.offset_ref.refs_3_.refs_5_), custom_call_target="tpu_custom_call" | custom-call | tf_op jit(solution)/shard_map/class_sums/pallas_call | solution.py:525
  127.9 7.0 %class_sums.8 = (f32[3600,128]{1,0:T(8,128)}, bf16[3600,128]{1,0:T(8,128)(2,1)}) custom-call(s32[1]{0:T(128)} %bitcast.13.refs_6_.refs_0_, s32[1]{0:T(128)} %bitcast.17.refs_1_, bf16[36,112,208]{2,1,0:T(8,128)(2,1)} %get-tuple-element.90.refs_1_.refs_2_, bf16[8,36,208,256]{3,2,1,0:T(8,128)(2,1)} %bitcast.37, bf16[8,36,208,256]{3,2,1,0:T(8,128)(2,1)} %bitcast.38, ...), custom_call_target="tpu_custom_call" | custom-call | tf_op jit(solution)/shard_map/class_sums/pallas_call | solution.py:525
  139.0 7.2 %class_sums.9 = (f32[3600,128]{1,0:T(8,128)}, bf16[3600,128]{1,0:T(8,128)(2,1)}) custom-call(s32[1]{0:T(128)} %bitcast.11.refs_4_.refs_0_, s32[1]{0:T(128)} %bitcast.18.refs_1_, bf16[36,112,208]{2,1,0:T(8,128)(2,1)} %get-tuple-element.90.refs_1_.refs_2_, bf16[8,36,208,256]{3,2,1,0:T(8,128)(2,1)} %bitcast.39, bf16[8,36,208,256]{3,2,1,0:T(8,128)(2,1)} %bitcast.40, ...), custom_call_target="tpu_custom_call" | custom-call | tf_op jit(solution)/shard_map/class_sums/pallas_call | solution.py:525
  148.6 3.1 %collective-permute-start.14 = (bf16[1200,128]{1,0:T(8,128)(2,1)}, bf16[1200,128]{1,0:T(8,128)(2,1)}, u32[]{:S(2)}, u32[]{:S(2)}) collective-permute-start(bf16[1200,128]{1,0:T(8,128)(2,1)} %add_convert_fusion.3), channel_id=1, source_target_pairs={{8,16},{12,20},{16,8},{20,12},{9,17},{13,21},{17,9},{21,13},{10,18... | collective-permute-start | bytes 921608 | tf_op jit(solution)/shard_map/ppermute | solution.py:553
  154.0 7.1 %class_sums.10 = (f32[3600,128]{1,0:T(8,128)}, bf16[3600,128]{1,0:T(8,128)(2,1)}) custom-call(s32[1]{0:T(128)} %bitcast.9.refs_2_.refs_0_, s32[1]{0:T(128)} %bitcast.19.refs_1_, bf16[36,112,208]{2,1,0:T(8,128)(2,1)} %get-tuple-element.90.refs_1_.refs_2_, bf16[8,36,208,256]{3,2,1,0:T(8,128)(2,1)} %bitcast.41, bf16[8,36,208,256]{3,2,1,0:T(8,128)(2,1)} %bitcast.42, ...), custom_call_target="tpu_custom_call" | custom-call | tf_op jit(solution)/shard_map/class_sums/pallas_call | solution.py:525
  161.1 4.8 %collective-permute-done.13 = bf16[3600,128]{1,0:T(8,128)(2,1)S(1)} collective-permute-done((bf16[3600,128]{1,0:T(8,128)(2,1)}, bf16[3600,128]{1,0:T(8,128)(2,1)S(1)}, u32[]{:S(2)}, u32[]{:S(2)}) %collective-permute-start.13) | collective-permute-done | bytes 921632 | tf_op jit(solution)/shard_map/ppermute | solution.py:549
  167.4 1.6 collective-permute-start.15
  169.3 3.2 %collective-permute-start.19 = (bf16[2400,128]{1,0:T(8,128)(2,1)S(1)}, bf16[2400,128]{1,0:T(8,128)(2,1)S(1)}, u32[]{:S(2)}, u32[]{:S(2)}) collective-permute-start(bf16[2400,128]{1,0:T(8,128)(2,1)S(1)} %add_convert_fusion.2), channel_id=1, source_target_pairs={{8,16},{12,20},{16,8},{20,12},{9,17},{13,21},{17,9},{21,13},{10,18... | collective-permute-start | bytes 1843208 | tf_op jit(solution)/shard_map/ppermute | solution.py:553
  172.5 13.3 %collective-permute-done.17 = bf16[3600,128]{1,0:T(8,128)(2,1)} collective-permute-done((bf16[3600,128]{1,0:T(8,128)(2,1)}, bf16[3600,128]{1,0:T(8,128)(2,1)}, u32[]{:S(2)}, u32[]{:S(2)}) %collective-permute-start.17) | collective-permute-done | bytes 921632 | tf_op jit(solution)/shard_map/ppermute | solution.py:549
  185.8 2.5 %collective-permute-done.16 = bf16[3600,128]{1,0:T(8,128)(2,1)S(1)} collective-permute-done((bf16[3600,128]{1,0:T(8,128)(2,1)S(1)}, bf16[3600,128]{1,0:T(8,128)(2,1)S(1)}, u32[]{:S(2)}, u32[]{:S(2)}) %collective-permute-start.16) | collective-permute-done | bytes 921632 | tf_op jit(solution)/shard_map/ppermute | solution.py:553
  191.2 3.1 %collective-permute-start.18 = (bf16[3600,128]{1,0:T(8,128)(2,1)}, bf16[3600,128]{1,0:T(8,128)(2,1)S(1)}, u32[]{:S(2)}, u32[]{:S(2)}) collective-permute-start(bf16[3600,128]{1,0:T(8,128)(2,1)} %add_convert_fusion.1), channel_id=1, source_target_pairs={{8,16},{12,20},{16,8},{20,12},{9,17},{13,21},{17,9},{21,13},{10,18... | collective-permute-start | bytes 2764808 | tf_op jit(solution)/shard_map/ppermute | solution.py:553
  196.2 5.2 %class_sums.11 = f32[3600,128]{1,0:T(8,128)} custom-call(s32[1]{0:T(128)} %bitcast.7.refs_0_, bf16[36,112,208]{2,1,0:T(8,128)(2,1)} %get-tuple-element.90.refs_1_.refs_2_, bf16[8,36,208,256]{3,2,1,0:T(8,128)(2,1)} %bitcast.43, f32[56,128]{1,0:T(8,128)} %get-tuple-element.70.offset_ref.refs_3_.refs_5_), custom_call_target="tpu_custom_call" | custom-call | tf_op jit(solution)/shard_map/class_sums/pallas_call | solution.py:525
  201.4 3.1 %collective-permute-done.15 = bf16[3600,128]{1,0:T(8,128)(2,1)} collective-permute-done((bf16[3600,128]{1,0:T(8,128)(2,1)}, bf16[3600,128]{1,0:T(8,128)(2,1)}, u32[]{:S(2)}, u32[]{:S(2)}) %collective-permute-start.15) | collective-permute-done | bytes 921632 | tf_op jit(solution)/shard_map/ppermute | solution.py:549
  204.4 6.2 %collective-permute-done.20 = bf16[3600,128]{1,0:T(8,128)(2,1)S(1)} collective-permute-done((bf16[3600,128]{1,0:T(8,128)(2,1)S(1)}, bf16[3600,128]{1,0:T(8,128)(2,1)S(1)}, u32[]{:S(2)}, u32[]{:S(2)}) %collective-permute-start.20) | collective-permute-done | bytes 921632 | tf_op jit(solution)/shard_map/ppermute | solution.py:553
  210.6 2.1 collective-permute-done.18
  212.8 3.4 %convert_add_fusion = f32[3600,128]{1,0:T(8,128)} fusion(bf16[3600,128]{1,0:T(8,128)(2,1)S(1)} %collective-permute-done.20, bf16[3600,128]{1,0:T(8,128)(2,1)S(1)} %collective-permute-done.18, f32[3600,128]{1,0:T(8,128)} %class_sums.11, bf16[3600,128]{1,0:T(8,128)(2,1)} %collective-permute-done.15), kind=kLoop, calls=%fused_computation | loop fusion | flops 2764800 | bytes 6451200 | tf_op jit(solution)/shard_map/add | solution.py:648
  (71 shorter events, 26.8 us)
Async XLA Ops:
  0.6 14.2 %copy-start = (f32[16,128]{1,0:T(8,128)S(1)}, f32[16,128]{1,0:T(8,128)}, u32[]{:S(2)}) copy-start(f32[16,128]{1,0:T(8,128)} %param.15) | copy-start | bytes 24580
  3.6 23.9 %collective-permute-start = (bf16[3600,128]{1,0:T(8,128)(2,1)}, bf16[3600,128]{1,0:T(8,128)(2,1)S(1)}, u32[]{:S(2)}, u32[]{:S(2)}) collective-permute-start(bf16[3600,128]{1,0:T(8,128)(2,1)} %get-tuple-element.50.refs_15_), channel_id=1, source_target_pairs={{0,4},{4,0},{8,12},{12,8},{16,20},{20,16},{24,28},{28,24},{1,5},{5... | collective-permute-start | bytes 2764808 | tf_op jit(solution)/shard_map/ppermute | solution.py:549
  5.1 22.4 %collective-permute-start.1 = (bf16[3600,128]{1,0:T(8,128)(2,1)}, bf16[3600,128]{1,0:T(8,128)(2,1)S(1)}, u32[]{:S(2)}, u32[]{:S(2)}) collective-permute-start(bf16[3600,128]{1,0:T(8,128)(2,1)} %get-tuple-element.50.refs_15_), channel_id=1, source_target_pairs={{0,8},{4,12},{8,0},{12,4},{16,24},{20,28},{24,16},{28,20},{1,9},{5... | collective-permute-start | bytes 2764808 | tf_op jit(solution)/shard_map/ppermute | solution.py:553
  5.6 24.7 %collective-permute-start.2 = (bf16[3600,128]{1,0:T(8,128)(2,1)}, bf16[3600,128]{1,0:T(8,128)(2,1)S(1)}, u32[]{:S(2)}, u32[]{:S(2)}) collective-permute-start(bf16[3600,128]{1,0:T(8,128)(2,1)} %get-tuple-element.50.refs_15_), channel_id=1, source_target_pairs={{8,16},{12,20},{16,8},{20,12},{9,17},{13,21},{17,9},{21,13},{10,18... | collective-permute-start | bytes 2764808 | tf_op jit(solution)/shard_map/ppermute | solution.py:553
  10.2 4.7 %copy-start.15 = (s32[8]{0:T(128)S(1)}, s32[8]{0:T(128)}, u32[]{:S(2)}) copy-start(s32[8]{0:T(128)} %param.18) | copy-start | bytes 100
  27.5 25.6 %copy-start.9 = (bf16[3600,128]{1,0:T(8,128)(2,1)}, bf16[3600,128]{1,0:T(8,128)(2,1)S(1)}, u32[]{:S(2)}) copy-start(bf16[3600,128]{1,0:T(8,128)(2,1)S(1)} %collective-permute-done.refs_16_) | copy-start | bytes 2764804
  27.5 25.6 %copy-start.10 = (bf16[3600,128]{1,0:T(8,128)(2,1)}, bf16[3600,128]{1,0:T(8,128)(2,1)S(1)}, u32[]{:S(2)}) copy-start(bf16[3600,128]{1,0:T(8,128)(2,1)S(1)} %collective-permute-done.1.refs_17_) | copy-start | bytes 2764804
  30.3 22.8 %collective-permute-start.3 = (bf16[3600,128]{1,0:T(8,128)(2,1)S(1)}, bf16[3600,128]{1,0:T(8,128)(2,1)S(1)}, u32[]{:S(2)}, u32[]{:S(2)}) collective-permute-start(bf16[3600,128]{1,0:T(8,128)(2,1)S(1)} %collective-permute-done.2), channel_id=1, source_target_pairs={{8,0},{12,4},{16,24},{20,28},{9,1},{13,5},{17,25},{21,29},{10,2},{... | collective-permute-start | bytes 2764808 | tf_op jit(solution)/shard_map/ppermute | solution.py:553
  31.6 21.5 %collective-permute-start.4 = (bf16[3600,128]{1,0:T(8,128)(2,1)S(1)}, bf16[3600,128]{1,0:T(8,128)(2,1)S(1)}, u32[]{:S(2)}, u32[]{:S(2)}) collective-permute-start(bf16[3600,128]{1,0:T(8,128)(2,1)S(1)} %collective-permute-done.1.refs_17_), channel_id=1, source_target_pairs={{0,4},{4,0},{8,12},{12,8},{16,20},{20,16},{24,28},{28,24},{1,5},{5... | collective-permute-start | bytes 2764808 | tf_op jit(solution)/shard_map/ppermute | solution.py:549
  32.2 22.6 %collective-permute-start.5 = (bf16[3600,128]{1,0:T(8,128)(2,1)S(1)}, bf16[3600,128]{1,0:T(8,128)(2,1)S(1)}, u32[]{:S(2)}, u32[]{:S(2)}) collective-permute-start(bf16[3600,128]{1,0:T(8,128)(2,1)S(1)} %collective-permute-done.1.refs_17_), channel_id=1, source_target_pairs={{8,16},{12,20},{16,8},{20,12},{9,17},{13,21},{17,9},{21,13},{10,18... | collective-permute-start | bytes 2764808 | tf_op jit(solution)/shard_map/ppermute | solution.py:553
  53.1 22.3 %copy-start.11 = (bf16[3600,128]{1,0:T(8,128)(2,1)}, bf16[3600,128]{1,0:T(8,128)(2,1)S(1)}, u32[]{:S(2)}) copy-start(bf16[3600,128]{1,0:T(8,128)(2,1)S(1)} %collective-permute-done.4.refs_18_) | copy-start | bytes 2764804
  54.8 20.6 %collective-permute-start.6 = (bf16[3600,128]{1,0:T(8,128)(2,1)S(1)}, bf16[3600,128]{1,0:T(8,128)(2,1)S(1)}, u32[]{:S(2)}, u32[]{:S(2)}) collective-permute-start(bf16[3600,128]{1,0:T(8,128)(2,1)S(1)} %collective-permute-done.5), channel_id=1, source_target_pairs={{8,0},{12,4},{16,24},{20,28},{9,1},{13,5},{17,25},{21,29},{10,2},{... | collective-permute-start | bytes 2764808 | tf_op jit(solution)/shard_map/ppermute | solution.py:553
  56.6 18.8 %copy-start.4 = (bf16[3600,128]{1,0:T(8,128)(2,1)}, bf16[3600,128]{1,0:T(8,128)(2,1)S(1)}, u32[]{:S(2)}) copy-start(bf16[3600,128]{1,0:T(8,128)(2,1)S(1)} %add.92.refs_19_) | copy-start | bytes 2764804
  56.6 20.3 %collective-permute-start.7 = (bf16[3600,128]{1,0:T(8,128)(2,1)S(1)}, bf16[3600,128]{1,0:T(8,128)(2,1)S(1)}, u32[]{:S(2)}, u32[]{:S(2)}) collective-permute-start(bf16[3600,128]{1,0:T(8,128)(2,1)S(1)} %add.92.refs_19_), channel_id=1, source_target_pairs={{0,4},{4,0},{8,12},{12,8},{16,20},{20,16},{24,28},{28,24},{1,5},{5... | collective-permute-start | bytes 2764808 | tf_op jit(solution)/shard_map/ppermute | solution.py:549
  77.2 19.0 %collective-permute-start.8 = (bf16[3600,128]{1,0:T(8,128)(2,1)S(1)}, bf16[3600,128]{1,0:T(8,128)(2,1)S(1)}, u32[]{:S(2)}, u32[]{:S(2)}) collective-permute-start(bf16[3600,128]{1,0:T(8,128)(2,1)S(1)} %add.93.refs_21_), channel_id=1, source_target_pairs={{0,4},{4,0},{8,12},{12,8},{16,20},{20,16},{24,28},{28,24},{1,5},{5... | collective-permute-start | bytes 2764808 | tf_op jit(solution)/shard_map/ppermute | solution.py:549
  122.7 13.8 %collective-permute-start.9 = (bf16[1200,128]{1,0:T(8,128)(2,1)}, bf16[1200,128]{1,0:T(8,128)(2,1)S(1)}, u32[]{:S(2)}, u32[]{:S(2)}) collective-permute-start(bf16[1200,128]{1,0:T(8,128)(2,1)} %class_sums.6), channel_id=1, source_target_pairs={{0,4},{4,0},{8,12},{12,8},{16,20},{20,16},{24,28},{28,24},{1,5},{5... | collective-permute-start | bytes 921608 | tf_op jit(solution)/shard_map/ppermute | solution.py:549
  127.4 18.8 %collective-permute-start.10 = (bf16[2400,128]{1,0:T(8,128)(2,1)}, bf16[2400,128]{1,0:T(8,128)(2,1)S(1)}, u32[]{:S(2)}, u32[]{:S(2)}) collective-permute-start(bf16[2400,128]{1,0:T(8,128)(2,1)} %class_sums.7), channel_id=1, source_target_pairs={{0,4},{4,0},{8,12},{12,8},{16,20},{20,16},{24,28},{28,24},{1,5},{5... | collective-permute-start | bytes 1843208 | tf_op jit(solution)/shard_map/ppermute | solution.py:549
  135.0 31.0 %collective-permute-start.13 = (bf16[3600,128]{1,0:T(8,128)(2,1)}, bf16[3600,128]{1,0:T(8,128)(2,1)S(1)}, u32[]{:S(2)}, u32[]{:S(2)}) collective-permute-start(bf16[3600,128]{1,0:T(8,128)(2,1)} %get-tuple-element.86), channel_id=1, source_target_pairs={{0,4},{4,0},{8,12},{12,8},{16,20},{20,16},{24,28},{28,24},{1,5},{5... | collective-permute-start | bytes 2764808 | tf_op jit(solution)/shard_map/ppermute | solution.py:549
  137.7 10.1 %collective-permute-start.11 = (bf16[1200,128]{1,0:T(8,128)(2,1)S(1)}, bf16[1200,128]{1,0:T(8,128)(2,1)S(1)}, u32[]{:S(2)}, u32[]{:S(2)}) collective-permute-start(bf16[1200,128]{1,0:T(8,128)(2,1)S(1)} %fusion.2), channel_id=1, source_target_pairs={{0,8},{4,12},{24,16},{28,20},{1,9},{5,13},{25,17},{29,21},{2,10},{... | collective-permute-start | bytes 921608 | tf_op jit(solution)/shard_map/ppermute | solution.py:553
  139.0 7.2 %copy-start.3 = (f32[3600,128]{1,0:T(8,128)S(1)}, f32[3600,128]{1,0:T(8,128)}, u32[]{:S(2)}) copy-start(f32[3600,128]{1,0:T(8,128)} %get-tuple-element.77) | copy-start | bytes 5529604
  148.6 12.5 %collective-permute-start.14 = (bf16[1200,128]{1,0:T(8,128)(2,1)}, bf16[1200,128]{1,0:T(8,128)(2,1)}, u32[]{:S(2)}, u32[]{:S(2)}) collective-permute-start(bf16[1200,128]{1,0:T(8,128)(2,1)} %add_convert_fusion.3), channel_id=1, source_target_pairs={{8,16},{12,20},{16,8},{20,12},{9,17},{13,21},{17,9},{21,13},{10,18... | collective-permute-start | bytes 921608 | tf_op jit(solution)/shard_map/ppermute | solution.py:553
  151.8 34.0 %collective-permute-start.17 = (bf16[3600,128]{1,0:T(8,128)(2,1)}, bf16[3600,128]{1,0:T(8,128)(2,1)}, u32[]{:S(2)}, u32[]{:S(2)}) collective-permute-start(bf16[3600,128]{1,0:T(8,128)(2,1)} %get-tuple-element.92), channel_id=1, source_target_pairs={{0,4},{4,0},{8,12},{12,8},{16,20},{20,16},{24,28},{28,24},{1,5},{5... | collective-permute-start | bytes 2764808 | tf_op jit(solution)/shard_map/ppermute | solution.py:549
  152.7 16.3 %collective-permute-start.12 = (bf16[2400,128]{1,0:T(8,128)(2,1)}, bf16[2400,128]{1,0:T(8,128)(2,1)S(1)}, u32[]{:S(2)}, u32[]{:S(2)}) collective-permute-start(bf16[2400,128]{1,0:T(8,128)(2,1)} %fusion.1), channel_id=1, source_target_pairs={{0,8},{4,12},{24,16},{28,20},{1,9},{5,13},{25,17},{29,21},{2,10},{... | collective-permute-start | bytes 1843208 | tf_op jit(solution)/shard_map/ppermute | solution.py:553
  154.0 12.0 %copy-start.2 = (f32[3600,128]{1,0:T(8,128)S(1)}, f32[3600,128]{1,0:T(8,128)}, u32[]{:S(2)}) copy-start(f32[3600,128]{1,0:T(8,128)} %get-tuple-element.85) | copy-start | bytes 5529604
  166.1 22.1 %collective-permute-start.16 = (bf16[3600,128]{1,0:T(8,128)(2,1)S(1)}, bf16[3600,128]{1,0:T(8,128)(2,1)S(1)}, u32[]{:S(2)}, u32[]{:S(2)}) collective-permute-start(bf16[3600,128]{1,0:T(8,128)(2,1)S(1)} %fusion), channel_id=1, source_target_pairs={{0,8},{4,12},{24,16},{28,20},{1,9},{5,13},{25,17},{29,21},{2,10},{... | collective-permute-start | bytes 2764808 | tf_op jit(solution)/shard_map/ppermute | solution.py:553
  167.4 37.0 %collective-permute-start.15 = (bf16[3600,128]{1,0:T(8,128)(2,1)}, bf16[3600,128]{1,0:T(8,128)(2,1)}, u32[]{:S(2)}, u32[]{:S(2)}) collective-permute-start(bf16[3600,128]{1,0:T(8,128)(2,1)} %get-tuple-element.91), channel_id=1, source_target_pairs={{0,4},{4,0},{8,12},{12,8},{16,20},{20,16},{24,28},{28,24},{1,5},{5... | collective-permute-start | bytes 2764808 | tf_op jit(solution)/shard_map/ppermute | solution.py:549
  169.3 20.3 %copy-start.6 = (f32[3600,128]{1,0:T(8,128)S(1)}, f32[3600,128]{1,0:T(8,128)}, u32[]{:S(2)}) copy-start(f32[3600,128]{1,0:T(8,128)} %get-tuple-element.94) | copy-start | bytes 5529604
  169.3 20.3 %collective-permute-start.19 = (bf16[2400,128]{1,0:T(8,128)(2,1)S(1)}, bf16[2400,128]{1,0:T(8,128)(2,1)S(1)}, u32[]{:S(2)}, u32[]{:S(2)}) collective-permute-start(bf16[2400,128]{1,0:T(8,128)(2,1)S(1)} %add_convert_fusion.2), channel_id=1, source_target_pairs={{8,16},{12,20},{16,8},{20,12},{9,17},{13,21},{17,9},{21,13},{10,18... | collective-permute-start | bytes 1843208 | tf_op jit(solution)/shard_map/ppermute | solution.py:553
  189.6 4.7 %copy-start.14 = (f32[56,128]{1,0:T(8,128)S(1)}, f32[56,128]{1,0:T(8,128)}, u32[]{:S(2)}) copy-start(f32[56,128]{1,0:T(8,128)} %get-tuple-element.72) | copy-start | bytes 86020
  191.2 19.5 %collective-permute-start.20 = (bf16[3600,128]{1,0:T(8,128)(2,1)S(1)}, bf16[3600,128]{1,0:T(8,128)(2,1)S(1)}, u32[]{:S(2)}, u32[]{:S(2)}) collective-permute-start(bf16[3600,128]{1,0:T(8,128)(2,1)S(1)} %add_convert_fusion), channel_id=1, source_target_pairs={{0,8},{4,12},{8,0},{12,4},{16,24},{20,28},{24,16},{28,20},{1,9},{5... | collective-permute-start | bytes 2764808 | tf_op jit(solution)/shard_map/ppermute | solution.py:553
  191.2 21.5 %collective-permute-start.18 = (bf16[3600,128]{1,0:T(8,128)(2,1)}, bf16[3600,128]{1,0:T(8,128)(2,1)S(1)}, u32[]{:S(2)}, u32[]{:S(2)}) collective-permute-start(bf16[3600,128]{1,0:T(8,128)(2,1)} %add_convert_fusion.1), channel_id=1, source_target_pairs={{8,16},{12,20},{16,8},{20,12},{9,17},{13,21},{17,9},{21,13},{10,18... | collective-permute-start | bytes 2764808 | tf_op jit(solution)/shard_map/ppermute | solution.py:553
  196.2 19.9 %copy-start.1 = (f32[16,128]{1,0:T(8,128)S(1)}, f32[16,128]{1,0:T(8,128)}, u32[]{:S(2)}) copy-start(f32[16,128]{1,0:T(8,128)} %param.15) | copy-start | bytes 24580
  (5 other events, 8.5 us)
